TPU v7x, 32 devices: a whole 2x2x4 slice. The times are simulated.
32 devices in a mesh: leaf: 8 (over z, x), front: 4 (over y, core).
Axes of the slice: x: 2, y: 2, z: 4, core: 2. Of those that a mesh axis runs over, the one named last changes fastest.
Arguments:
- rhs_zero: float32 [64, 4096], P(None, 'leaf'), may hold values from -6 to 6
- rhs_one: float32 [64, 8192], P(None, 'leaf'), may hold values from -6 to 6
- rhs_two: float32 [64, 16384], P(None, 'leaf'), may hold values from -6 to 6
- pivot_zero: bfloat16 [4096, 4096], P('leaf', 'front'), may hold values from -0.09375 to 0.09375
- pivot_one: bfloat16 [8192, 4096], P('leaf', 'front'), may hold values from -0.09375 to 0.09375
- pivot_two: bfloat16 [16384, 4096], P('leaf', 'front'), may hold values from -0.09375 to 0.09375
- lower_one: bfloat16 [4096, 8192], P('front', 'leaf'), may hold values from -0.09375 to 0.09375
- lower_two: bfloat16 [4096, 16384], P('front', 'leaf'), may hold values from -0.09375 to 0.09375
- upper_one: bfloat16 [8192, 4096], P('leaf', 'front'), may hold values from -0.09375 to 0.09375
- upper_two: bfloat16 [16384, 4096], P('leaf', 'front'), may hold values from -0.09375 to 0.09375
- back_zero: bfloat16 [4096, 4096], P('front', 'leaf'), may hold values from -0.09375 to 0.09375
- back_one: bfloat16 [4096, 8192], P('front', 'leaf'), may hold values from -0.09375 to 0.09375
- back_two: bfloat16 [4096, 16384], P('front', 'leaf'), may hold values from -0.09375 to 0.09375
- index_one: int32 [2, 4096], replicated, may hold values from 0 to 4095, as said below
- index_two: int32 [4, 4096], replicated, may hold values from 0 to 8191
Outputs:
- solution_zero: float32 [64, 4096], P(None, 'leaf')
- solution_one: float32 [64, 8192], P(None, 'leaf')
- solution_two: float32 [64, 16384], P(None, 'leaf')
Inputs may be any that keep to these rules, and one draw needn't show every extreme that they name: `index_one`: each row holds 4096 different columns of the root separator.
All inputs are finite; a program needn't handle non-finite values.
Results may differ from a plain program's by a relative error of at most 0.013.
Values may be sent and summed in bfloat16 or wider, within the bound.
No kernel may reach another device: no remote copies, remote signals or barrier semaphores. Data moves between devices by JAX's collectives and lax.ppermute only.
A program may use at most 128 MiB of HBM per device.

v0:
```python
import jax
import jax.numpy as jnp
from jax import lax
from jax.sharding import PartitionSpec as P

SEP = 4096
UPD = 4096
RHS = 64


def swapped(x, axis, bit):
    return lax.ppermute(x, axis, [(i, i ^ 1 << bit) for i in range(lax.axis_size(axis))])


def mat_product(left, right):
    return jnp.dot(
        left.astype(jnp.float32),
        right.astype(jnp.float32),
        precision=lax.Precision.HIGHEST,
        preferred_element_type=jnp.float32,
    )


def subtree_rows(segment, group_bits, leaf_pos):
    current = segment
    for bit_pos in reversed(range(group_bits)):
        midpoint = current.shape[1] // 2
        lower_half = current[:, :midpoint]
        upper_half = current[:, midpoint:]
        parity = leaf_pos >> bit_pos & 1
        retained = jnp.where(parity == 1, upper_half, lower_half)
        outgoing = jnp.where(parity == 1, lower_half, upper_half)
        current = retained + swapped(outgoing, "leaf", bit_pos)
    return current


def group_total(partial_value, group_bits, for_pivot):
    current = partial_value
    for bit_pos in range(group_bits):
        if for_pivot:
            incoming = swapped(current, "leaf", bit_pos)
        else:
            incoming = swapped(current, "leaf", bit_pos)
        current = current + incoming
    return current


def group_values(values, group_bits, leaf_pos):
    current = values
    for bit_pos in range(group_bits):
        incoming = swapped(current, "leaf", bit_pos)
        parity = leaf_pos >> bit_pos & 1
        current = jnp.where(
            parity == 1,
            jnp.concatenate([incoming, current], axis=1),
            jnp.concatenate([current, incoming], axis=1),
        )
    return current


def update_rows(index_table, front_id, member, width):
    return lax.dynamic_slice(index_table, (front_id, member * width), (1, width))[0]


def per_device(
    rhs_zero,
    rhs_one,
    rhs_two,
    pivot_zero,
    pivot_one,
    pivot_two,
    lower_one,
    lower_two,
    upper_one,
    upper_two,
    back_zero,
    back_one,
    back_two,
    index_one,
    index_two,
):
    leaf_count = lax.axis_size("leaf")
    leaf_pos = lax.axis_index("leaf")
    rhs_list = (rhs_zero, rhs_one, rhs_two)
    pivot_list = (pivot_zero, pivot_one, pivot_two)
    lower_list = (None, lower_one, lower_two)
    upper_list = (None, upper_one, upper_two)
    back_list = (back_zero, back_one, back_two)
    index_list = (None, index_one, index_two)
    pending = jnp.zeros((RHS, 2 * SEP), jnp.float32)
    solved_list = [None, None, None]
    for tier_index in (2, 1, 0):
        group_width = leaf_count >> tier_index
        group_bits = group_width.bit_length() - 1
        front_id = leaf_pos >> group_bits
        member = leaf_pos & group_width - 1
        reduced = rhs_list[tier_index]
        if tier_index < 2:
            segment = pending[:, tier_index * SEP : (tier_index + 1) * SEP]
            reduced = reduced - subtree_rows(segment, group_bits, leaf_pos)
        partial_value = mat_product(reduced.astype(jnp.bfloat16), pivot_list[tier_index])
        result = group_total(partial_value, group_bits, True)
        solved_list[tier_index] = result
        if tier_index > 0:
            update_part = mat_product(result.astype(jnp.bfloat16), lower_list[tier_index])
            lifted = lax.psum(update_part, "front")
            targets = update_rows(index_list[tier_index], front_id, member, UPD // group_width)
            pending = pending.at[:, targets].add(lifted)
    ancestors = None
    answers = []
    for tier_index in (0, 1, 2):
        group_width = leaf_count >> tier_index
        group_bits = group_width.bit_length() - 1
        front_id = leaf_pos >> group_bits
        member = leaf_pos & group_width - 1
        remaining = solved_list[tier_index]
        if tier_index > 0:
            targets = update_rows(index_list[tier_index], front_id, member, UPD // group_width)
            picked = ancestors[:, targets]
            coupling = mat_product(picked, upper_list[tier_index])
            remaining = remaining - group_total(coupling, group_bits, False)
        answer_part = mat_product(remaining.astype(jnp.bfloat16), back_list[tier_index])
        answer = lax.psum(answer_part, "front")
        answers.append(answer)
        if tier_index < 2:
            full_block = group_values(answer.astype(jnp.bfloat16), group_bits, leaf_pos)
            if ancestors is None:
                ancestors = full_block
            else:
                ancestors = jnp.concatenate([ancestors, full_block], axis=1)
    return (answers[0], answers[1], answers[2])


def solution(mesh):
    placed = (
        P(None, "leaf"),
        P(None, "leaf"),
        P(None, "leaf"),
        P("leaf", "front"),
        P("leaf", "front"),
        P("leaf", "front"),
        P("front", "leaf"),
        P("front", "leaf"),
        P("leaf", "front"),
        P("leaf", "front"),
        P("front", "leaf"),
        P("front", "leaf"),
        P("front", "leaf"),
        P(),
        P(),
    )
    return jax.shard_map(
        per_device,
        mesh=mesh,
        in_specs=placed,
        out_specs=(P(None, "leaf"), P(None, "leaf"), P(None, "leaf")),
        check_vma=False,
    )
```

profile of v0, /device:TPU:0, one launch (start us, length us, event | category | flops | bytes accessed | tf_op | source)
XLA Modules:
  0.0 424.6 jit_solution(3506596753880053965)
XLA Ops:
  7.2 3.3 fusion.2
  10.6 3.0 collective-permute-start
  13.6 6.3 %collective-permute-done = f32[64,1024]{1,0:T(8,128)S(1)} collective-permute-done((f32[64,1024]{1,0:T(8,128)S(1)}, f32[64,1024]{1,0:T(8,128)S(1)}, u32[]{:S(2)}, u32[]{:S(2)}) %collective-permute-start) | collective-permute-done | bytes 262176 | tf_op jit(solution)/shard_map/ppermute | solution.py:12
  20.6 1.6 fusion.11
  23.2 33.9 %all-reduce.6.cloned.1.call-done = f32[64,2048]{1,0:T(8,128)} async-done(((f32[64,2048]{1,0:T(8,128)}), f32[64,2048]{1,0:T(8,128)}) %all-reduce.6.cloned.1.call-update) | async-done | bytes 524304 | tf_op jit(solution)/shard_map/psum | solution.py:106
  57.2 1.4 copy.32
  58.5 13.6 %scatter_custom_fusion = f32[64,8192]{0,1:T(8,128)} fusion(s32[2048]{0:T(1024)S(1)} %bitcast.24, f32[2048,64]{1,0:T(8,128)S(1)} %copy.32, f32[]{:T(128)} %constant.3.clone.1), kind=kCustom, calls=%fused_computation.4 | custom fusion | flops 131072 | bytes 2097156 | tf_op jit(solution)/shard_map/scatter-add | solution.py:108
  72.2 3.0 fusion.15
  75.2 1.6 copy.41
  76.8 1.5 copy.42
  79.2 1.5 collective-permute-start.1
  80.7 11.3 %collective-permute-done.1 = f32[64,2048]{1,0:T(8,128)} collective-permute-done((f32[64,2048]{1,0:T(8,128)}, f32[64,2048]{1,0:T(8,128)}, u32[]{:S(2)}, u32[]{:S(2)}) %collective-permute-start.1) | collective-permute-done | bytes 524320 | tf_op jit(solution)/shard_map/ppermute | solution.py:12
  93.1 1.8 collective-permute-start.2
  94.9 4.6 %collective-permute-done.2 = f32[64,1024]{1,0:T(8,128)S(1)} collective-permute-done((f32[64,1024]{1,0:T(8,128)S(1)}, f32[64,1024]{1,0:T(8,128)S(1)}, u32[]{:S(2)}, u32[]{:S(2)}) %collective-permute-start.2) | collective-permute-done | bytes 262176 | tf_op jit(solution)/shard_map/ppermute | solution.py:12
  100.1 1.8 collective-permute-start.3
  101.8 4.6 %collective-permute-done.3 = f32[64,1024]{1,0:T(8,128)S(1)} collective-permute-done((f32[64,1024]{1,0:T(8,128)S(1)}, f32[64,1024]{1,0:T(8,128)S(1)}, u32[]{:S(2)}, u32[]{:S(2)}) %collective-permute-start.3) | collective-permute-done | bytes 262176 | tf_op jit(solution)/shard_map/ppermute | solution.py:12
  106.5 1.8 collective-permute-start.4
  108.3 4.6 %collective-permute-done.4 = f32[64,1024]{1,0:T(8,128)S(1)} collective-permute-done((f32[64,1024]{1,0:T(8,128)S(1)}, f32[64,1024]{1,0:T(8,128)S(1)}, u32[]{:S(2)}, u32[]{:S(2)}) %collective-permute-start.4) | collective-permute-done | bytes 262176 | tf_op jit(solution)/shard_map/ppermute | solution.py:12
  113.0 1.2 fusion.9
  115.1 31.5 %all-reduce.8.cloned.1.call-done = f32[64,1024]{1,0:T(8,128)} async-done(((f32[64,1024]{1,0:T(8,128)}), f32[64,1024]{1,0:T(8,128)}) %all-reduce.8.cloned.1.call-update) | async-done | bytes 262160 | tf_op jit(solution)/shard_map/psum | solution.py:106
  147.8 9.5 %scatter_fusion = f32[64,8192]{0,1:T(8,128)} fusion(f32[64,8192]{0,1:T(8,128)} %scatter_custom_fusion, s32[1024]{0:T(1024)S(1)} %bitcast.26, f32[1024,64]{1,0:T(8,128)S(1)} %copy.35), kind=kCustom, calls=%fused_computation.3 | custom fusion | flops 65536 | bytes 790528 | tf_op jit(solution)/shard_map/scatter-add | solution.py:108
  157.3 1.7 slice_select_fusion
  160.1 2.4 collective-permute-start.5
  162.5 22.3 %collective-permute-done.5 = f32[64,2048]{1,0:T(8,128)} collective-permute-done((f32[64,2048]{1,0:T(8,128)}, f32[64,2048]{1,0:T(8,128)}, u32[]{:S(2)}, u32[]{:S(2)}) %collective-permute-start.5) | collective-permute-done | bytes 524320 | tf_op jit(solution)/shard_map/ppermute | solution.py:12
  184.8 1.4 copy.37
  186.2 1.7 select_add_fusion
  188.8 12.1 %collective-permute-done.6 = f32[64,1024]{0,1:T(8,128)S(1)} collective-permute-done((f32[64,1024]{0,1:T(8,128)S(1)}, f32[64,1024]{0,1:T(8,128)S(1)}, u32[]{:S(2)}, u32[]{:S(2)}) %collective-permute-start.6) | collective-permute-done | bytes 262176 | tf_op jit(solution)/shard_map/ppermute | solution.py:12
  201.0 1.8 collective-permute-start.7
  202.9 4.9 %collective-permute-done.7 = f32[64,512]{0,1:T(8,128)} collective-permute-done((f32[64,512]{0,1:T(8,128)S(1)}, f32[64,512]{0,1:T(8,128)}, u32[]{:S(2)}, u32[]{:S(2)}) %collective-permute-start.7) | collective-permute-done | bytes 131104 | tf_op jit(solution)/shard_map/ppermute | solution.py:12
  207.8 1.6 fusion.5
  209.5 1.5 collective-permute-start.8
  211.0 4.9 %collective-permute-done.8 = f32[64,1024]{1,0:T(8,128)S(1)} collective-permute-done((f32[64,1024]{1,0:T(8,128)S(1)}, f32[64,1024]{1,0:T(8,128)S(1)}, u32[]{:S(2)}, u32[]{:S(2)}) %collective-permute-start.8) | collective-permute-done | bytes 262176 | tf_op jit(solution)/shard_map/ppermute | solution.py:12
  216.0 2.6 collective-permute-start.9
  218.6 4.4 %collective-permute-done.9 = f32[64,1024]{1,0:T(8,128)S(1)} collective-permute-done((f32[64,1024]{1,0:T(8,128)S(1)}, f32[64,1024]{1,0:T(8,128)S(1)}, u32[]{:S(2)}, u32[]{:S(2)}) %collective-permute-start.9) | collective-permute-done | bytes 262176 | tf_op jit(solution)/shard_map/ppermute | solution.py:12
  223.0 6.1 %collective-permute-start.10 = (f32[64,1024]{1,0:T(8,128)S(1)}, f32[64,1024]{1,0:T(8,128)S(1)}, u32[]{:S(2)}, u32[]{:S(2)}) collective-permute-start(f32[64,1024]{1,0:T(8,128)S(1)} %add.125), channel_id=1, source_target_pairs={{0,16},{4,20},{8,24},{12,28},{16,0},{20,4},{24,8},{28,12},{1,17},{... | collective-permute-start | bytes 786440 | tf_op jit(solution)/shard_map/ppermute | solution.py:12
  229.1 6.8 %collective-permute-done.10 = f32[64,1024]{1,0:T(8,128)S(1)} collective-permute-done((f32[64,1024]{1,0:T(8,128)S(1)}, f32[64,1024]{1,0:T(8,128)S(1)}, u32[]{:S(2)}, u32[]{:S(2)}) %collective-permute-start.10) | collective-permute-done | bytes 262176 | tf_op jit(solution)/shard_map/ppermute | solution.py:12
  235.9 2.2 fusion.6
  238.4 31.2 %all-reduce.10.cloned.1.call-done = f32[64,512]{1,0:T(8,128)} async-done(((f32[64,512]{1,0:T(8,128)}), f32[64,512]{1,0:T(8,128)}) %all-reduce.10.cloned.1.call-update) | async-done | bytes 131088 | tf_op jit(solution)/shard_map/psum | solution.py:123
  270.5 1.5 collective-permute-start.11
  272.0 2.8 collective-permute-done.11
  274.8 1.6 collective-permute-start.12
  276.4 3.5 collective-permute-done.12
  280.0 3.3 collective-permute-start.13
  283.2 7.8 %collective-permute-done.13 = bf16[64,2048]{1,0:T(8,128)(2,1)S(1)} collective-permute-done((bf16[64,2048]{1,0:T(8,128)(2,1)S(1)}, bf16[64,2048]{1,0:T(8,128)(2,1)S(1)}, u32[]{:S(2)}, u32[]{:S(2)}) %collective-permute-start.13) | collective-permute-done | bytes 262176 | tf_op jit(solution)/shard_map/ppermute | solution.py:12
  291.2 1.4 copy.39
  292.5 4.2 gather_fusion
  296.8 2.2 fusion.16
  299.0 1.7 collective-permute-start.14
  300.8 4.7 %collective-permute-done.14 = f32[64,1024]{1,0:T(8,128)S(1)} collective-permute-done((f32[64,1024]{1,0:T(8,128)S(1)}, f32[64,1024]{1,0:T(8,128)S(1)}, u32[]{:S(2)}, u32[]{:S(2)}) %collective-permute-start.14) | collective-permute-done | bytes 262176 | tf_op jit(solution)/shard_map/ppermute | solution.py:12
  306.5 5.5 %collective-permute-done.15 = f32[64,1024]{1,0:T(8,128)S(1)} collective-permute-done((f32[64,1024]{1,0:T(8,128)S(1)}, f32[64,1024]{1,0:T(8,128)S(1)}, u32[]{:S(2)}, u32[]{:S(2)}) %collective-permute-start.15) | collective-permute-done | bytes 262176 | tf_op jit(solution)/shard_map/ppermute | solution.py:12
  311.9 1.2 fusion.7
  313.2 33.0 %all-reduce.12.cloned.1.call-done = f32[64,1024]{1,0:T(8,128)} async-done(((f32[64,1024]{1,0:T(8,128)}), f32[64,1024]{1,0:T(8,128)}) %all-reduce.12.cloned.1.call-update) | async-done | bytes 262160 | tf_op jit(solution)/shard_map/psum | solution.py:123
  347.2 1.5 collective-permute-start.16
  348.7 3.5 collective-permute-done.16
  352.3 1.6 collective-permute-start.17
  353.9 4.9 %collective-permute-done.17 = bf16[64,2048]{1,0:T(8,128)(2,1)S(1)} collective-permute-done((bf16[64,2048]{1,0:T(8,128)(2,1)S(1)}, bf16[64,2048]{1,0:T(8,128)(2,1)S(1)}, u32[]{:S(2)}, u32[]{:S(2)}) %collective-permute-start.17) | collective-permute-done | bytes 262176 | tf_op jit(solution)/shard_map/ppermute | solution.py:12
  359.9 2.7 copy.40
  362.7 7.5 %gather_fusion.1 = bf16[2048,64]{1,0:T(8,128)(2,1)S(1)} fusion(bf16[64,8192]{0,1:T(8,128)(2,1)} %copy.40, s32[2048]{0:T(1024)S(1)} %broadcast_clamp_fusion), kind=kCustom, calls=%fused_computation.1 | custom fusion | bytes 532480 | tf_op jit(solution)/shard_map/gather | solution.py:119
  370.2 3.2 fusion.17
  373.4 1.5 collective-permute-start.18
  374.9 4.9 %collective-permute-done.18 = f32[64,1024]{1,0:T(8,128)S(1)} collective-permute-done((f32[64,1024]{1,0:T(8,128)S(1)}, f32[64,1024]{1,0:T(8,128)S(1)}, u32[]{:S(2)}, u32[]{:S(2)}) %collective-permute-start.18) | collective-permute-done | bytes 262176 | tf_op jit(solution)/shard_map/ppermute | solution.py:12
  379.9 1.6 fusion.8
  381.5 33.3 %all-reduce.14.cloned.1.call-done = f32[64,2048]{1,0:T(8,128)} async-done(((f32[64,2048]{1,0:T(8,128)}), f32[64,2048]{1,0:T(8,128)}) %all-reduce.14.cloned.1.call-update) | async-done | bytes 524304 | tf_op jit(solution)/shard_map/psum | solution.py:123
  416.2 1.9 copy.51
  (64 shorter events, 14.6 us)
Async XLA Ops:
  7.2 92.4 %copy-start = (bf16[1024,1024]{1,0:T(8,128)(2,1)S(1)}, bf16[1024,1024]{1,0:T(8,128)(2,1)}, u32[]{:S(2)}) copy-start(bf16[1024,1024]{1,0:T(8,128)(2,1)} %param.19) | copy-start | bytes 6291460
  7.2 50.0 %all-reduce.6.cloned.1.call-start = ((), (), s32[]{:S(2)}) async-start(), calls=%async_computation | async-start | bytes 1048576 | tf_op jit(solution)/shard_map/psum | solution.py:106
  7.2 13.4 %copy-start.1 = (bf16[1024,2048]{1,0:T(8,128)(2,1)S(1)}, bf16[1024,2048]{1,0:T(8,128)(2,1)}, u32[]{:S(2)}) copy-start(bf16[1024,2048]{1,0:T(8,128)(2,1)} %param.22) | copy-start | bytes 12582916
  10.6 9.3 %collective-permute-start = (f32[64,1024]{1,0:T(8,128)S(1)}, f32[64,1024]{1,0:T(8,128)S(1)}, u32[]{:S(2)}, u32[]{:S(2)}) collective-permute-start(f32[64,1024]{1,0:T(8,128)S(1)} %fusion.2), channel_id=1, source_target_pairs={{0,4},{4,0},{8,12},{12,8},{16,20},{20,16},{24,28},{28,24},{1,5},{5... | collective-permute-start | bytes 786440 | tf_op jit(solution)/shard_map/ppermute | solution.py:12
  19.9 0.7 copy-start.3
  22.3 124.3 %all-reduce.8.cloned.1.call-start = ((), (), s32[]{:S(2)}) async-start(), calls=%async_computation.1 | async-start | bytes 524288 | tf_op jit(solution)/shard_map/psum | solution.py:106
  75.2 24.4 %copy-start.9 = (f32[64,1024]{1,0:T(8,128)S(1)}, f32[64,1024]{1,0:T(8,128)}, u32[]{:S(2)}) copy-start(f32[64,1024]{1,0:T(8,128)} %param.16) | copy-start | bytes 786436
  79.2 12.8 %collective-permute-start.1 = (f32[64,2048]{1,0:T(8,128)}, f32[64,2048]{1,0:T(8,128)}, u32[]{:S(2)}, u32[]{:S(2)}) collective-permute-start(f32[64,2048]{1,0:T(8,128)} %broadcast_select_fusion), channel_id=1, source_target_pairs={{0,8},{4,12},{8,0},{12,4},{16,24},{20,28},{24,16},{28,20},{1,9},{5... | collective-permute-start | bytes 1572872 | tf_op jit(solution)/shard_map/ppermute | solution.py:12
  80.7 32.3 %copy-start.5 = (bf16[1024,1024]{1,0:T(8,128)(2,1)S(1)}, bf16[1024,1024]{1,0:T(8,128)(2,1)}, u32[]{:S(2)}) copy-start(bf16[1024,1024]{1,0:T(8,128)(2,1)} %param.21) | copy-start | bytes 6291460
  93.1 6.4 %collective-permute-start.2 = (f32[64,1024]{1,0:T(8,128)S(1)}, f32[64,1024]{1,0:T(8,128)S(1)}, u32[]{:S(2)}, u32[]{:S(2)}) collective-permute-start(f32[64,1024]{1,0:T(8,128)S(1)} %slice_select_fusion.3), channel_id=1, source_target_pairs={{0,4},{4,0},{8,12},{12,8},{16,20},{20,16},{24,28},{28,24},{1,5},{5... | collective-permute-start | bytes 786440 | tf_op jit(solution)/shard_map/ppermute | solution.py:12
  100.1 6.4 %collective-permute-start.3 = (f32[64,1024]{1,0:T(8,128)S(1)}, f32[64,1024]{1,0:T(8,128)S(1)}, u32[]{:S(2)}, u32[]{:S(2)}) collective-permute-start(f32[64,1024]{1,0:T(8,128)S(1)} %fusion.4), channel_id=1, source_target_pairs={{0,4},{4,0},{8,12},{12,8},{16,20},{20,16},{24,28},{28,24},{1,5},{5... | collective-permute-start | bytes 786440 | tf_op jit(solution)/shard_map/ppermute | solution.py:12
  106.5 6.4 %collective-permute-start.4 = (f32[64,1024]{1,0:T(8,128)S(1)}, f32[64,1024]{1,0:T(8,128)S(1)}, u32[]{:S(2)}, u32[]{:S(2)}) collective-permute-start(f32[64,1024]{1,0:T(8,128)S(1)} %add.119), channel_id=1, source_target_pairs={{0,8},{4,12},{8,0},{12,4},{16,24},{20,28},{24,16},{28,20},{1,9},{5... | collective-permute-start | bytes 786440 | tf_op jit(solution)/shard_map/ppermute | solution.py:12
  114.2 155.3 %all-reduce.10.cloned.1.call-start = ((), (), s32[]{:S(2)}) async-start(), calls=%async_computation.2 | async-start | bytes 262144 | tf_op jit(solution)/shard_map/psum | solution.py:123
  160.1 24.7 %collective-permute-start.5 = (f32[64,2048]{1,0:T(8,128)}, f32[64,2048]{1,0:T(8,128)}, u32[]{:S(2)}, u32[]{:S(2)}) collective-permute-start(f32[64,2048]{1,0:T(8,128)} %copy.36), channel_id=1, source_target_pairs={{0,16},{4,20},{8,24},{12,28},{16,0},{20,4},{24,8},{28,12},{1,17},{... | collective-permute-start | bytes 1572872 | tf_op jit(solution)/shard_map/ppermute | solution.py:12
  186.2 16.6 %copy-start.10 = (f32[64,512]{1,0:T(8,128)S(1)}, f32[64,512]{1,0:T(8,128)}, u32[]{:S(2)}) copy-start(f32[64,512]{1,0:T(8,128)} %param.15) | copy-start | bytes 393220
  188.0 12.9 %collective-permute-start.6 = (f32[64,1024]{0,1:T(8,128)S(1)}, f32[64,1024]{0,1:T(8,128)S(1)}, u32[]{:S(2)}, u32[]{:S(2)}) collective-permute-start(f32[64,1024]{0,1:T(8,128)S(1)} %slice_select_fusion.1), channel_id=1, source_target_pairs={{0,8},{4,12},{8,0},{12,4},{16,24},{20,28},{24,16},{28,20},{1,9},{5... | collective-permute-start | bytes 786440 | tf_op jit(solution)/shard_map/ppermute | solution.py:12
  201.0 6.8 %collective-permute-start.7 = (f32[64,512]{0,1:T(8,128)S(1)}, f32[64,512]{0,1:T(8,128)}, u32[]{:S(2)}, u32[]{:S(2)}) collective-permute-start(f32[64,512]{0,1:T(8,128)S(1)} %slice_select_fusion.2), channel_id=1, source_target_pairs={{0,4},{4,0},{8,12},{12,8},{16,20},{20,16},{24,28},{28,24},{1,5},{5... | collective-permute-start | bytes 393224 | tf_op jit(solution)/shard_map/ppermute | solution.py:12
  209.5 6.4 %collective-permute-start.8 = (f32[64,1024]{1,0:T(8,128)S(1)}, f32[64,1024]{1,0:T(8,128)S(1)}, u32[]{:S(2)}, u32[]{:S(2)}) collective-permute-start(f32[64,1024]{1,0:T(8,128)S(1)} %fusion.5), channel_id=1, source_target_pairs={{0,4},{4,0},{8,12},{12,8},{16,20},{20,16},{24,28},{28,24},{1,5},{5... | collective-permute-start | bytes 786440 | tf_op jit(solution)/shard_map/ppermute | solution.py:12
  216.0 7.0 %collective-permute-start.9 = (f32[64,1024]{1,0:T(8,128)S(1)}, f32[64,1024]{1,0:T(8,128)S(1)}, u32[]{:S(2)}, u32[]{:S(2)}) collective-permute-start(f32[64,1024]{1,0:T(8,128)S(1)} %add.124), channel_id=1, source_target_pairs={{0,8},{4,12},{8,0},{12,4},{16,24},{20,28},{24,16},{28,20},{1,9},{5... | collective-permute-start | bytes 786440 | tf_op jit(solution)/shard_map/ppermute | solution.py:12
  223.0 12.9 %collective-permute-start.10 = (f32[64,1024]{1,0:T(8,128)S(1)}, f32[64,1024]{1,0:T(8,128)S(1)}, u32[]{:S(2)}, u32[]{:S(2)}) collective-permute-start(f32[64,1024]{1,0:T(8,128)S(1)} %add.125), channel_id=1, source_target_pairs={{0,16},{4,20},{8,24},{12,28},{16,0},{20,4},{24,8},{28,12},{1,17},{... | collective-permute-start | bytes 786440 | tf_op jit(solution)/shard_map/ppermute | solution.py:12
  238.1 108.1 %all-reduce.12.cloned.1.call-start = ((), (), s32[]{:S(2)}) async-start(), calls=%async_computation.3 | async-start | bytes 524288 | tf_op jit(solution)/shard_map/psum | solution.py:123
  270.5 4.3 %collective-permute-start.11 = (bf16[64,512]{1,0:T(8,128)(2,1)S(1)}, bf16[64,512]{1,0:T(8,128)(2,1)S(1)}, u32[]{:S(2)}, u32[]{:S(2)}) collective-permute-start(bf16[64,512]{1,0:T(8,128)(2,1)S(1)} %convert_element_type.26), channel_id=1, source_target_pairs={{0,4},{4,0},{8,12},{12,8},{16,20},{20,16},{24,28},{28,24},{1,5},{5... | collective-permute-start | bytes 196616 | tf_op jit(solution)/shard_map/ppermute | solution.py:12
  274.8 5.0 %collective-permute-start.12 = (bf16[64,1024]{1,0:T(8,128)(2,1)S(1)}, bf16[64,1024]{1,0:T(8,128)(2,1)S(1)}, u32[]{:S(2)}, u32[]{:S(2)}) collective-permute-start(bf16[64,1024]{1,0:T(8,128)(2,1)S(1)} %maximum_select_fusion.4), channel_id=1, source_target_pairs={{0,8},{4,12},{8,0},{12,4},{16,24},{20,28},{24,16},{28,20},{1,9},{5... | collective-permute-start | bytes 393224 | tf_op jit(solution)/shard_map/ppermute | solution.py:12
  280.0 11.1 %collective-permute-start.13 = (bf16[64,2048]{1,0:T(8,128)(2,1)S(1)}, bf16[64,2048]{1,0:T(8,128)(2,1)S(1)}, u32[]{:S(2)}, u32[]{:S(2)}) collective-permute-start(bf16[64,2048]{1,0:T(8,128)(2,1)S(1)} %maximum_select_fusion.2), channel_id=1, source_target_pairs={{0,16},{4,20},{8,24},{12,28},{16,0},{20,4},{24,8},{28,12},{1,17},{... | collective-permute-start | bytes 786440 | tf_op jit(solution)/shard_map/ppermute | solution.py:12
  296.8 15.2 %copy-start.6 = (bf16[1024,1024]{1,0:T(8,128)(2,1)S(1)}, bf16[1024,1024]{1,0:T(8,128)(2,1)}, u32[]{:S(2)}) copy-start(bf16[1024,1024]{1,0:T(8,128)(2,1)} %param.26) | copy-start | bytes 6291460
  299.0 6.4 %collective-permute-start.14 = (f32[64,1024]{1,0:T(8,128)S(1)}, f32[64,1024]{1,0:T(8,128)S(1)}, u32[]{:S(2)}, u32[]{:S(2)}) collective-permute-start(f32[64,1024]{1,0:T(8,128)S(1)} %fusion.16), channel_id=1, source_target_pairs={{0,4},{4,0},{8,12},{12,8},{16,20},{20,16},{24,28},{28,24},{1,5},{5... | collective-permute-start | bytes 786440 | tf_op jit(solution)/shard_map/ppermute | solution.py:12
  305.5 6.4 %collective-permute-start.15 = (f32[64,1024]{1,0:T(8,128)S(1)}, f32[64,1024]{1,0:T(8,128)S(1)}, u32[]{:S(2)}, u32[]{:S(2)}) collective-permute-start(f32[64,1024]{1,0:T(8,128)S(1)} %add.129), channel_id=1, source_target_pairs={{0,8},{4,12},{8,0},{12,4},{16,24},{20,28},{24,16},{28,20},{1,9},{5... | collective-permute-start | bytes 786440 | tf_op jit(solution)/shard_map/ppermute | solution.py:12
  313.2 101.7 %all-reduce.14.cloned.1.call-start = ((), (), s32[]{:S(2)}) async-start(), calls=%async_computation.4 | async-start | bytes 1048576 | tf_op jit(solution)/shard_map/psum | solution.py:123
  347.2 5.0 %collective-permute-start.16 = (bf16[64,1024]{1,0:T(8,128)(2,1)S(1)}, bf16[64,1024]{1,0:T(8,128)(2,1)S(1)}, u32[]{:S(2)}, u32[]{:S(2)}) collective-permute-start(bf16[64,1024]{1,0:T(8,128)(2,1)S(1)} %convert_element_type.28), channel_id=1, source_target_pairs={{0,4},{4,0},{8,12},{12,8},{16,20},{20,16},{24,28},{28,24},{1,5},{5... | collective-permute-start | bytes 393224 | tf_op jit(solution)/shard_map/ppermute | solution.py:12
  352.3 6.4 %collective-permute-start.17 = (bf16[64,2048]{1,0:T(8,128)(2,1)S(1)}, bf16[64,2048]{1,0:T(8,128)(2,1)S(1)}, u32[]{:S(2)}, u32[]{:S(2)}) collective-permute-start(bf16[64,2048]{1,0:T(8,128)(2,1)S(1)} %maximum_select_fusion.3), channel_id=1, source_target_pairs={{0,8},{4,12},{8,0},{12,4},{16,24},{20,28},{24,16},{28,20},{1,9},{5... | collective-permute-start | bytes 786440 | tf_op jit(solution)/shard_map/ppermute | solution.py:12
  362.7 17.2 %copy-start.4 = (f32[64,1024]{1,0:T(8,128)S(1)}, f32[64,1024]{1,0:T(8,128)}, u32[]{:S(2)}) copy-start(f32[64,1024]{1,0:T(8,128)} %copy-done.3) | copy-start | bytes 786436
  370.2 9.7 %copy-start.2 = (bf16[1024,2048]{1,0:T(8,128)(2,1)S(1)}, bf16[1024,2048]{1,0:T(8,128)(2,1)}, u32[]{:S(2)}) copy-start(bf16[1024,2048]{1,0:T(8,128)(2,1)} %param.27) | copy-start | bytes 12582916
  373.4 41.5 %copy-start.8 = (f32[64,512]{1,0:T(8,128)S(1)}, f32[64,512]{1,0:T(8,128)}, u32[]{:S(2)}) copy-start(f32[64,512]{1,0:T(8,128)} %all-reduce.10.cloned.1.call-done) | copy-start | bytes 393220
  373.4 42.1 %copy-start.7 = (f32[64,1024]{1,0:T(8,128)S(1)}, f32[64,1024]{1,0:T(8,128)}, u32[]{:S(2)}) copy-start(f32[64,1024]{1,0:T(8,128)} %all-reduce.12.cloned.1.call-done) | copy-start | bytes 786436
  373.4 6.4 %collective-permute-start.18 = (f32[64,1024]{1,0:T(8,128)S(1)}, f32[64,1024]{1,0:T(8,128)S(1)}, u32[]{:S(2)}, u32[]{:S(2)}) collective-permute-start(f32[64,1024]{1,0:T(8,128)S(1)} %fusion.17), channel_id=1, source_target_pairs={{0,4},{4,0},{8,12},{12,8},{16,20},{20,16},{24,28},{28,24},{1,5},{5... | collective-permute-start | bytes 786440 | tf_op jit(solution)/shard_map/ppermute | solution.py:12
Sparse Core Ops, SparseCore 0:
  22.4 34.6 all-reduce.5
  114.3 32.2 all-reduce.7
  238.3 31.2 all-reduce.9
  313.3 32.9 all-reduce.11
  381.6 33.1 all-reduce.13
where the time goes:
time: 425 us
  waiting for transfers between devices  288 us (68%)
  starting transfers between devices  39.2 us (9%)
  other arithmetic  34 us (8%)
  local copies, waits for them, and re-layouts  31.1 us (7%)
  matrix products  18.7 us (4%)
  between operations  14.1 us (3%)
    ppermute x19, waiting for transfers between devices, swapped(): lax.ppermute(x, axis, [(i, i ^ 1 << bit) for i in range(lax.axis_size(axi...  124 us
    psum x3, waiting for transfers between devices, per_device(): answer = lax.psum(answer_part, 'front')  97.5 us
    psum x2, waiting for transfers between devices, per_device(): lifted = lax.psum(update_part, 'front')  65.5 us
    ppermute x19, starting transfers between devices, swapped(): lax.ppermute(x, axis, [(i, i ^ 1 << bit) for i in range(lax.axis_size(axi...  38.8 us
    scatter-add x2, other arithmetic, per_device(): pending = pending.at[:, targets].add(lifted)  23.2 us
    dot_general x10, matrix products, mat_product(): jnp.dot(left.astype(jnp.float32), right.astype(jnp.float32), precision=la...  18.7 us
    gather x2, local copies, waits for them, and re-layouts, per_device(): picked = ancestors[:, targets]  11.7 us
  transfers between devices with their start and end apart: 24, of which 24 were waited for; matrix products, arithmetic and copies ran while one was open for 0% of the time, Pallas kernels for 0%

commit v1 on v0

v1 whole, which is shorter than its diff:
```python
import jax
import jax.numpy as jnp
from jax import lax
from jax.sharding import PartitionSpec as P

BF16 = jnp.bfloat16
F32 = jnp.float32


def dot(left, right):
    return jnp.dot(left, right, preferred_element_type=F32)


def bit_groups(bits):
    bits = list(bits)
    return [bits[i : i + 2] for i in range(0, len(bits), 2)]


def partner(x, axis, mask):
    return lax.ppermute(x, axis, [(i, i ^ mask) for i in range(lax.axis_size(axis))])


def exchange_sum(x, axis, groups):
    for group in groups:
        low = x.astype(BF16)
        parts = [low] + [partner(low, axis, m << group[0]) for m in range(1, 1 << len(group))]
        parts = [p.astype(F32) for p in parts]
        while len(parts) > 1:
            parts = [parts[i] + parts[i + 1] for i in range(0, len(parts), 2)]
        x = parts[0]
    return x


def scatter_sum(x, axis, groups):
    for group in groups:
        count = 1 << len(group)
        width = x.shape[1] // count
        total = x[:, :width]
        for m in range(1, count):
            piece = x[:, m * width : (m + 1) * width].astype(BF16)
            total = total + partner(piece, axis, m << group[0]).astype(F32)
        x = total
    return x


def gather_blocks(x, axis, groups):
    for group in reversed(groups):
        x = jnp.concatenate([x] + [partner(x, axis, m << group[0]) for m in range(1, 1 << len(group))], axis=1)
    return x


def relative_block(owner, me, groups):
    rel = owner ^ me
    place = jnp.zeros_like(rel)
    for group in groups:
        place = (place << len(group)) | (rel >> group[0] & ((1 << len(group)) - 1))
    return place


def one_hot_rows(place, width):
    hot = place[:, None] == lax.broadcasted_iota(jnp.int32, (place.shape[0], width), 1)
    return lax.optimization_barrier(hot.astype(BF16))


def one_hot_columns(place, height):
    hot = place[None, :] == lax.broadcasted_iota(jnp.int32, (height, place.shape[0]), 0)
    return lax.optimization_barrier(hot.astype(BF16))


def per_device(
    rhs_zero, rhs_one, rhs_two,
    pivot_zero, pivot_one, pivot_two,
    lower_one, lower_two,
    upper_one, upper_two,
    back_zero, back_one, back_two,
    index_one, index_two,
):
    sep = lower_one.shape[0] * lax.axis_size("front")
    leaves = lax.axis_size("leaf")
    me = lax.axis_index("leaf")
    front_pos = lax.axis_index("front")
    core = front_pos & 1
    leaf_bits = leaves.bit_length() - 1
    front_bits = lax.axis_size("front").bit_length() - 1
    groups = [bit_groups(range(leaf_bits - level)) for level in range(3)]
    away = bit_groups(range(1, front_bits))
    rhs = (rhs_zero, rhs_one, rhs_two)
    pivot = (pivot_zero, pivot_one, pivot_two)
    lower = (None, lower_one, lower_two)
    upper = (None, upper_one, upper_two)
    back = (back_zero, back_one, back_two)

    def own_index(level):
        table = index_one if level == 1 else index_two
        width = leaves >> level
        chunk = table.shape[1] // width
        start = (me & width - 1) * chunk
        return lax.dynamic_slice(table, (me >> (leaf_bits - level), start), (1, chunk))[0]

    def split_place(column, level):
        block = sep // (leaves >> level)
        half = block // 2
        owner = column // block
        mine = me & (leaves >> level) - 1
        rel = relative_block(owner, mine, groups[level])
        return ((column // half & 1) ^ core) * (sep // 2) + rel * half + column % half

    def whole_place(column, level):
        block = sep // (leaves >> level)
        mine = me & (leaves >> level) - 1
        rel = relative_block(column // block, mine, groups[level])
        return rel * block + column % block

    def both_halves(own):
        other = partner(own, "front", 1)
        return jnp.concatenate([jnp.where(core == 0, own, other), jnp.where(core == 0, other, own)], axis=1)

    def front_half(x):
        width = x.shape[1] // 2
        keep = jnp.where(core == 0, x[:, :width], x[:, width:])
        send = jnp.where(core == 0, x[:, width:], x[:, :width])
        return exchange_sum(keep + partner(send, "front", 1), "front", away)

    def front_sum(x):
        return exchange_sum(x + partner(x, "front", 1), "front", away)

    def row_total(pending, level):
        width = sep // 2
        total = pending[:, :width] + partner(pending[:, width:], "front", 1)
        return scatter_sum(total, "leaf", groups[level])

    def half_columns(x):
        width = x.shape[1] // 2
        return jnp.where(core == 0, x[:, :width], x[:, width:])

    def core_slice(index):
        half = index.shape[0] // 2
        return lax.dynamic_slice(index, (core * half,), (half,))

    index = core_slice(own_index(2))
    is_root = index < sep
    place_one = jnp.where(is_root, -1, split_place(index - sep, 1))
    place_root = jnp.where(is_root, split_place(index, 0), -1)
    y_two = exchange_sum(dot(rhs_two.astype(BF16), pivot_two), "leaf", groups[2])
    hot_one = one_hot_rows(place_one, sep)
    hot_root = one_hot_rows(place_root, sep)
    update = front_half(dot(y_two.astype(BF16), lower_two)).astype(BF16)
    pending_one = dot(update, hot_one)
    pending_root = dot(update, hot_root)

    own_rhs = half_columns(rhs_one)
    reduced = both_halves((own_rhs - row_total(pending_one, 1)).astype(BF16))
    y_one = exchange_sum(dot(reduced, pivot_one), "leaf", groups[1])
    hot_up = one_hot_rows(split_place(core_slice(own_index(1)), 0), sep)
    update = front_half(dot(y_one.astype(BF16), lower_one)).astype(BF16)
    pending_root = pending_root + dot(update, hot_up)

    own_rhs = half_columns(rhs_zero)
    reduced = both_halves((own_rhs - row_total(pending_root, 0)).astype(BF16))
    y_zero = exchange_sum(dot(reduced, pivot_zero), "leaf", groups[0])
    x_zero = front_sum(dot(y_zero.astype(BF16), back_zero))
    known_zero = gather_blocks(x_zero.astype(BF16), "leaf", groups[0])

    pick_one = one_hot_columns(whole_place(own_index(1), 0), sep)
    index = own_index(2)
    is_root = index < sep
    pick_root = one_hot_columns(jnp.where(is_root, whole_place(index, 0), -1), sep)
    pick_mid = one_hot_columns(jnp.where(is_root, -1, whole_place(index - sep, 1)), sep)
    picked = dot(known_zero, pick_one).astype(BF16)
    z_one = y_one - exchange_sum(dot(picked, upper_one), "leaf", groups[1])
    x_one = front_sum(dot(z_one.astype(BF16), back_one))
    known_one = gather_blocks(x_one.astype(BF16), "leaf", groups[1])

    picked = (dot(known_zero, pick_root) + dot(known_one, pick_mid)).astype(BF16)
    z_two = y_two - exchange_sum(dot(picked, upper_two), "leaf", groups[2])
    x_two = front_sum(dot(z_two.astype(BF16), back_two))
    return x_zero, x_one, x_two


def solution(mesh):
    by_leaf = P(None, "leaf")
    rows = P("leaf", "front")
    columns = P("front", "leaf")
    return jax.shard_map(
        per_device,
        mesh=mesh,
        in_specs=(by_leaf,) * 3 + (rows,) * 3 + (columns,) * 2 + (rows,) * 2 + (columns,) * 3 + (P(), P()),
        out_specs=(by_leaf,) * 3,
        check_vma=False,
    )
```

time: 425 us -> 195 us (0.46)
  waiting for transfers between devices: 288 us -> 66.5 us
  local copies, waits for them, and re-layouts: 31.1 us -> 1.93 us
  matrix products: 18.7 us -> 38.2 us
  between operations: 14.1 us -> 1.12 us
  other arithmetic: 34 us -> 44.7 us
    psum x5 -> x0, waiting for transfers between devices: 163 us -> none  [the longest x3 97.5 us: per_device(): answer = lax.psum(answer_part, 'front')]
    ppermute x19 -> x40, waiting for transfers between devices: 124 us -> 66.5 us  [partner(): lax.ppermute(x, axis, [(i, i ^ mask) for i in range(lax.axis_size(axis))])]
    convert_element_type x2 -> x15, other arithmetic: 1.88 us -> 40.4 us  [the longest x3 26.9 us: one_hot_columns(): return lax.optimization_barrier(hot.astype(BF16))]
    scatter-add x2 -> x0, other arithmetic: 23.2 us -> none  [per_device(): pending = pending.at[:, targets].add(lifted)]
    dot_general x10 -> x14, matrix products: 18.7 us -> 38.2 us  [dot(): return jnp.dot(left, right, preferred_element_type=F32)]
    gather x2 -> x0, local copies, waits for them, and re-layouts: 11.7 us -> none  [per_device(): picked = ancestors[:, targets]]
    unnamed x28 -> x27, local copies, waits for them, and re-layouts: 7.22 us -> 0.09 us
    ppermute x19 -> x40, starting transfers between devices: 38.8 us -> 41.8 us  [partner(): lax.ppermute(x, axis, [(i, i ^ mask) for i in range(lax.axis_size(axis))])]
  transfers between devices with their start and end apart: 24 -> 40, of which waited for: 24 -> 32; matrix products, arithmetic and copies ran while one was open for 0% -> 22% of each run, Pallas kernels for 0% -> 0%
where the time goes in v1:
time: 195 us; the launch traced here: 194 us
  waiting for transfers between devices  66.5 us (34%)
  other arithmetic  44.7 us (23%)
  starting transfers between devices  41.8 us (21%)
  matrix products  38.2 us (20%)
    ppermute x40, waiting for transfers between devices, partner(): lax.ppermute(x, axis, [(i, i ^ mask) for i in range(lax.axis_size(axis))])  66.5 us
    ppermute x40, starting transfers between devices, partner(): lax.ppermute(x, axis, [(i, i ^ mask) for i in range(lax.axis_size(axis))])  41.8 us
    dot_general x14, matrix products, dot(): return jnp.dot(left, right, preferred_element_type=F32)  38.2 us
    convert_element_type x3, other arithmetic, one_hot_columns(): return lax.optimization_barrier(hot.astype(BF16))  26.9 us
    convert_element_type x3, other arithmetic, one_hot_rows(): return lax.optimization_barrier(hot.astype(BF16))  12.5 us
  transfers between devices with their start and end apart: 40, of which 32 were waited for; matrix products, arithmetic and copies ran while one was open for 22% of the time, Pallas kernels for 0%

profile of v1, /device:TPU:0, one launch (start us, length us, event | category | flops | bytes accessed | tf_op | source)
XLA Modules:
  0.0 194.2 jit_solution(12141741435178551584)
XLA Ops:
  0.6 3.3 %convolution_convert_fusion.3 = bf16[64,1024]{1,0:T(8,128)(2,1)S(1)} fusion(bf16[2048,1024]{1,0:T(8,128)(2,1)} %param.20, f32[64,2048]{1,0:T(8,128)} %param.17), kind=kOutput, calls=%fused_computation.18 | convolution fusion | flops 268632064 | bytes 4849664 | tf_op jit(solution)/shard_map/dot_general | solution.py:11
  4.0 3.0 %collective-permute-start = (bf16[64,1024]{1,0:T(8,128)(2,1)S(1)}, bf16[64,1024]{1,0:T(8,128)(2,1)S(1)}, u32[]{:S(2)}, u32[]{:S(2)}) collective-permute-start(bf16[64,1024]{1,0:T(8,128)(2,1)S(1)} %convolution_convert_fusion.3), channel_id=1, source_target_pairs={{0,4},{4,0},{8,12},{12,8},{16,20},{20,16},{24,28},{28,24},{1,5},{5... | collective-permute-start | bytes 393224 | tf_op jit(solution)/shard_map/ppermute | solution.py:20
  7.0 3.5 %collective-permute-done = bf16[64,1024]{1,0:T(8,128)(2,1)S(1)} collective-permute-done((bf16[64,1024]{1,0:T(8,128)(2,1)S(1)}, bf16[64,1024]{1,0:T(8,128)(2,1)S(1)}, u32[]{:S(2)}, u32[]{:S(2)}) %collective-permute-start) | collective-permute-done | bytes 131104 | tf_op jit(solution)/shard_map/ppermute | solution.py:20
  10.5 3.0 %fusion.17 = f32[64,2048]{1,0:T(8,128)S(1)} fusion(bf16[1024,2048]{1,0:T(8,128)(2,1)} %param.22, bf16[64,1024]{1,0:T(8,128)(2,1)S(1)} %collective-permute-done, bf16[64,1024]{1,0:T(8,128)(2,1)S(1)} %convolution_convert_fusion.3), kind=kOutput, calls=%fused_computation.46 | convolution fusion | flops 268697600 | bytes 4980736 | tf_op jit(solution)/shard_map/dot_general | solution.py:11
  15.1 0.9 collective-permute-done.1
  16.1 1.8 collective-permute-start.2
  17.9 3.7 %fusion.3 = bf16[1024,4096]{1,0:T(8,128)(2,1)S(1)} fusion(s32[1024]{0:T(1024)S(1)} %get-tuple-element.25), kind=kLoop, calls=%fused_computation.8 | loop fusion | flops 8388608 | bytes 8392704 | tf_op jit(solution)/shard_map/convert_element_type | solution.py:62
  21.7 1.6 fusion.39
  23.4 1.9 collective-permute-done.3
  25.4 2.8 %collective-permute-start.6 = (bf16[64,512]{1,0:T(8,128)(2,1)S(1)}, bf16[64,512]{1,0:T(8,128)(2,1)S(1)}, u32[]{:S(2)}, u32[]{:S(2)}) collective-permute-start(bf16[64,512]{1,0:T(8,128)(2,1)S(1)} %get-tuple-element.16), channel_id=1, source_target_pairs={{0,12},{4,8},{8,4},{12,0},{16,28},{20,24},{24,20},{28,16},{1,13},{... | collective-permute-start | bytes 196616 | tf_op jit(solution)/shard_map/ppermute | solution.py:20
  28.9 1.7 collective-permute-done.6
  30.7 1.8 collective-permute-done.5
  33.0 1.2 collective-permute-done.7
  34.8 1.8 collective-permute-start.10
  37.0 1.3 collective-permute-start.8
  38.3 7.0 %fusion.2 = bf16[1024,4096]{1,0:T(8,128)(2,1)} fusion(s32[1024]{0:T(1024)S(1)} %get-tuple-element.24), kind=kLoop, calls=%fused_computation.7 | loop fusion | flops 8388608 | bytes 8392704 | tf_op jit(solution)/shard_map/convert_element_type | solution.py:62
  45.3 0.9 dynamic_slice.26
  46.3 2.4 %fusion.31 = f32[64,1024]{1,0:T(8,128)S(1)} fusion(bf16[1024,1024]{1,0:T(8,128)(2,1)} %param.21, bf16[64,1024]{1,0:T(8,128)(2,1)S(1)} %collective-permute-done.10, bf16[64,1024]{1,0:T(8,128)(2,1)S(1)} %collective-permute-done.9, bf16[64,1024]{1,0:T(8,128)(2,1)S(1)} %collective-permute-done.8, bf16[64,1024]{1,0:T(8,128)(2,1)S(1)} %convolution_convert_fusion.5), kind=kOutput, calls=%fused_computation.66 | convolution fusion | flops 134742016 | bytes 2883584 | tf_op jit(solution)/shard_map/dot_general | solution.py:11
  48.8 1.3 collective-permute-done.11
  50.2 1.6 collective-permute-start.12
  51.8 1.8 fusion.5
  53.6 1.0 collective-permute-done.12
  55.4 1.6 convolution_add_fusion
  57.1 1.9 collective-permute-done.13
  59.1 1.8 collective-permute-start.16
  61.4 1.3 collective-permute-start.14
  62.7 2.0 %collective-permute-done.16 = bf16[64,512]{1,0:T(8,128)(2,1)S(1)} collective-permute-done((bf16[64,512]{1,0:T(8,128)(2,1)S(1)}, bf16[64,512]{1,0:T(8,128)(2,1)S(1)}, u32[]{:S(2)}, u32[]{:S(2)}) %collective-permute-start.16) | collective-permute-done | bytes 65568 | tf_op jit(solution)/shard_map/ppermute | solution.py:20
  65.7 2.7 %collective-permute-start.17 = (bf16[64,256]{1,0:T(8,128)(2,1)S(1)}, bf16[64,256]{1,0:T(8,128)(2,1)S(1)}, u32[]{:S(2)}, u32[]{:S(2)}) collective-permute-start(bf16[64,256]{1,0:T(8,128)(2,1)S(1)} %slice.151), channel_id=1, source_target_pairs={{0,16},{4,20},{8,24},{12,28},{16,0},{20,4},{24,8},{28,12},{1,17},{... | collective-permute-start | bytes 98312 | tf_op jit(solution)/shard_map/ppermute | solution.py:20
  68.3 2.2 %collective-permute-done.17 = bf16[64,256]{1,0:T(8,128)(2,1)S(1)} collective-permute-done((bf16[64,256]{1,0:T(8,128)(2,1)S(1)}, bf16[64,256]{1,0:T(8,128)(2,1)S(1)}, u32[]{:S(2)}, u32[]{:S(2)}) %collective-permute-start.17) | collective-permute-done | bytes 32800 | tf_op jit(solution)/shard_map/ppermute | solution.py:20
  70.7 1.2 collective-permute-done.18
  72.2 2.4 %collective-permute-start.21 = (bf16[64,1024]{1,0:T(8,128)(2,1)S(1)}, bf16[64,1024]{1,0:T(8,128)(2,1)S(1)}, u32[]{:S(2)}, u32[]{:S(2)}) collective-permute-start(bf16[64,1024]{1,0:T(8,128)(2,1)S(1)} %convolution_convert_fusion.2), channel_id=1, source_target_pairs={{0,12},{4,8},{8,4},{12,0},{16,28},{20,24},{24,20},{28,16},{1,13},{... | collective-permute-start | bytes 393224 | tf_op jit(solution)/shard_map/ppermute | solution.py:20
  75.7 3.8 %collective-permute-done.21 = bf16[64,1024]{1,0:T(8,128)(2,1)S(1)} collective-permute-done((bf16[64,1024]{1,0:T(8,128)(2,1)S(1)}, bf16[64,1024]{1,0:T(8,128)(2,1)S(1)}, u32[]{:S(2)}, u32[]{:S(2)}) %collective-permute-start.21) | collective-permute-done | bytes 131104 | tf_op jit(solution)/shard_map/ppermute | solution.py:20
  79.5 1.9 collective-permute-done.20
  81.6 2.7 %collective-permute-start.22 = (bf16[64,1024]{1,0:T(8,128)(2,1)S(1)}, bf16[64,1024]{1,0:T(8,128)(2,1)S(1)}, u32[]{:S(2)}, u32[]{:S(2)}) collective-permute-start(bf16[64,1024]{1,0:T(8,128)(2,1)S(1)} %add_convert_fusion.3), channel_id=1, source_target_pairs={{0,16},{4,20},{8,24},{12,28},{16,0},{20,4},{24,8},{28,12},{1,17},{... | collective-permute-start | bytes 393224 | tf_op jit(solution)/shard_map/ppermute | solution.py:20
  84.3 6.3 %collective-permute-done.22 = bf16[64,1024]{1,0:T(8,128)(2,1)S(1)} collective-permute-done((bf16[64,1024]{1,0:T(8,128)(2,1)S(1)}, bf16[64,1024]{1,0:T(8,128)(2,1)S(1)}, u32[]{:S(2)}, u32[]{:S(2)}) %collective-permute-start.22) | collective-permute-done | bytes 131104 | tf_op jit(solution)/shard_map/ppermute | solution.py:20
  90.9 1.3 collective-permute-done.23
  92.3 1.6 collective-permute-start.24
  93.9 2.7 %collective-permute-done.24 = bf16[64,512]{1,0:T(8,128)(2,1)S(1)} collective-permute-done((bf16[64,512]{1,0:T(8,128)(2,1)S(1)}, bf16[64,512]{1,0:T(8,128)(2,1)S(1)}, u32[]{:S(2)}, u32[]{:S(2)}) %collective-permute-start.24) | collective-permute-done | bytes 65568 | tf_op jit(solution)/shard_map/ppermute | solution.py:20
  98.1 5.1 %collective-permute-done.25 = bf16[64,512]{1,0:T(8,128)(2,1)S(1)} collective-permute-done((bf16[64,512]{1,0:T(8,128)(2,1)S(1)}, bf16[64,512]{1,0:T(8,128)(2,1)S(1)}, u32[]{:S(2)}, u32[]{:S(2)}) %collective-permute-start.25) | collective-permute-done | bytes 65568 | tf_op jit(solution)/shard_map/ppermute | solution.py:20
  103.2 1.6 collective-permute-start.26
  104.8 7.8 %fusion.4 = bf16[4096,1024]{1,0:T(8,128)(2,1)} fusion(s32[1024]{0:T(1024)S(1)} %bitcast.25), kind=kLoop, calls=%fused_computation.9 | loop fusion | flops 8388608 | bytes 8392704 | tf_op jit(solution)/shard_map/convert_element_type | solution.py:67
  113.1 1.4 collective-permute-start.28
  114.6 3.0 %collective-permute-done.27 = bf16[64,1024]{1,0:T(8,128)(2,1)S(1)} collective-permute-done((bf16[64,1024]{1,0:T(8,128)(2,1)S(1)}, bf16[64,1024]{1,0:T(8,128)(2,1)S(1)}, u32[]{:S(2)}, u32[]{:S(2)}) %collective-permute-start.27) | collective-permute-done | bytes 131104 | tf_op jit(solution)/shard_map/ppermute | solution.py:20
  117.6 1.4 collective-permute-done.28
  119.0 5.9 %convolution_convert_fusion.4 = bf16[64,1024]{1,0:T(8,128)(2,1)S(1)} fusion(bf16[1024,1024]{1,0:T(8,128)(2,1)} %param.23, bf16[64,4096]{1,0:T(8,128)(2,1)S(1)} %constant_dynamic-update-slice_fusion, bf16[4096,1024]{1,0:T(8,128)(2,1)} %fusion.4), kind=kOutput, calls=%fused_computation.19 | convolution fusion | flops 671219712 | bytes 11141120 | tf_op jit(solution)/shard_map/dot_general | solution.py:11
  125.0 1.5 collective-permute-start.31
  126.4 1.5 collective-permute-start.30
  128.5 2.4 %collective-permute-done.31 = bf16[64,1024]{1,0:T(8,128)(2,1)S(1)} collective-permute-done((bf16[64,1024]{1,0:T(8,128)(2,1)S(1)}, bf16[64,1024]{1,0:T(8,128)(2,1)S(1)}, u32[]{:S(2)}, u32[]{:S(2)}) %collective-permute-start.31) | collective-permute-done | bytes 131104 | tf_op jit(solution)/shard_map/ppermute | solution.py:20
  130.9 1.4 collective-permute-done.30
  132.9 1.5 fusion.20
  134.4 1.0 compare_select_fusion.7
  136.0 1.6 collective-permute-start.33
  137.6 9.0 %fusion.1 = bf16[4096,2048]{1,0:T(8,128)(2,1)S(1)} fusion(s32[2048]{0:T(1024)S(1)} %bitcast.24), kind=kLoop, calls=%fused_computation.3 | loop fusion | flops 16777216 | bytes 16785408 | tf_op jit(solution)/shard_map/convert_element_type | solution.py:67
  147.4 1.5 collective-permute-start.36
  149.7 1.2 collective-permute-start.34
  150.9 10.0 %fusion = bf16[4096,2048]{1,0:T(8,128)(2,1)} fusion(s32[2048]{0:T(1024)S(1)} %bitcast.23), kind=kLoop, calls=%fused_computation.2 | loop fusion | flops 16777216 | bytes 16785408 | tf_op jit(solution)/shard_map/convert_element_type | solution.py:67
  160.9 3.1 %fusion.7 = f32[64,2048]{1,0:T(8,128)S(1)} fusion(bf16[4096,2048]{1,0:T(8,128)(2,1)S(1)} %fusion.1, bf16[64,1024]{1,0:T(8,128)(2,1)S(1)} %collective-permute-done.36, bf16[64,1024]{1,0:T(8,128)(2,1)S(1)} %collective-permute-done.35, bf16[64,1024]{1,0:T(8,128)(2,1)S(1)} %collective-permute-done.34, bf16[64,1024]{1,0:T(8,128)(2,1)S(1)} %get-tuple-element.3), kind=kOutput, calls=%fused_computation.23 | convolution fusion | flops 1075838976 | bytes 17825792 | tf_op jit(solution)/shard_map/dot_general | solution.py:11
  164.0 10.9 %convolution_convert_fusion = bf16[64,1024]{1,0:T(8,128)(2,1)S(1)} fusion(bf16[2048,1024]{1,0:T(8,128)(2,1)} %param.24, f32[64,2048]{1,0:T(8,128)S(1)} %fusion.7, bf16[64,4096]{1,0:T(8,128)(2,1)S(1)} %constant_dynamic-update-slice_fusion, bf16[4096,2048]{1,0:T(8,128)(2,1)} %fusion), kind=kOutput, calls=%fused_computation.15 | convolution fusion | flops 1342504960 | bytes 22151168 | tf_op jit(solution)/shard_map/dot_general | solution.py:11
  174.9 0.9 collective-permute-start.37
  175.8 4.1 %collective-permute-done.37 = bf16[64,1024]{1,0:T(8,128)(2,1)S(1)} collective-permute-done((bf16[64,1024]{1,0:T(8,128)(2,1)S(1)}, bf16[64,1024]{1,0:T(8,128)(2,1)S(1)}, u32[]{:S(2)}, u32[]{:S(2)}) %collective-permute-start.37) | collective-permute-done | bytes 131104 | tf_op jit(solution)/shard_map/ppermute | solution.py:20
  179.9 3.0 %fusion.21 = f32[64,2048]{1,0:T(8,128)S(1)} fusion(bf16[1024,2048]{1,0:T(8,128)(2,1)} %param.27, bf16[64,1024]{1,0:T(8,128)(2,1)S(1)} %collective-permute-done.37, bf16[64,1024]{1,0:T(8,128)(2,1)S(1)} %convolution_convert_fusion, bf16[64,1024]{1,0:T(8,128)(2,1)S(1)} %collective-permute-done, bf16[64,1024]{1,0:T(8,128)(2,1)S(1)} %convolution_convert_fusion.3), kind=kOutput, calls=%fused_computation.49 | convolution fusion | flops 268959744 | bytes 5242880 | tf_op jit(solution)/shard_map/dot_general | solution.py:11
  183.0 1.9 collective-permute-done.38
  185.6 7.8 %collective-permute-done.39 = bf16[64,2048]{1,0:T(8,128)(2,1)S(1)} collective-permute-done((bf16[64,2048]{1,0:T(8,128)(2,1)S(1)}, bf16[64,2048]{1,0:T(8,128)(2,1)S(1)}, u32[]{:S(2)}, u32[]{:S(2)}) %collective-permute-start.39) | collective-permute-done | bytes 262176 | tf_op jit(solution)/shard_map/ppermute | solution.py:20
  193.4 0.8 convert_add_fusion
  (94 shorter events, 15.2 us)
Async XLA Ops:
  0.6 33.7 %copy-start = (bf16[1024,1024]{1,0:T(8,128)(2,1)S(1)}, bf16[1024,1024]{1,0:T(8,128)(2,1)}, u32[]{:S(2)}) copy-start(bf16[1024,1024]{1,0:T(8,128)(2,1)} %param.19) | copy-start | bytes 6291460
  4.0 6.5 %collective-permute-start = (bf16[64,1024]{1,0:T(8,128)(2,1)S(1)}, bf16[64,1024]{1,0:T(8,128)(2,1)S(1)}, u32[]{:S(2)}, u32[]{:S(2)}) collective-permute-start(bf16[64,1024]{1,0:T(8,128)(2,1)S(1)} %convolution_convert_fusion.3), channel_id=1, source_target_pairs={{0,4},{4,0},{8,12},{12,8},{16,20},{20,16},{24,28},{28,24},{1,5},{5... | collective-permute-start | bytes 393224 | tf_op jit(solution)/shard_map/ppermute | solution.py:20
  14.3 1.7 collective-permute-start.1
  16.1 5.6 %collective-permute-start.2 = (bf16[64,1024]{1,0:T(8,128)(2,1)S(1)}, bf16[64,1024]{1,0:T(8,128)(2,1)S(1)}, u32[]{:S(2)}, u32[]{:S(2)}) collective-permute-start(bf16[64,1024]{1,0:T(8,128)(2,1)S(1)} %add_convert_fusion.5), channel_id=1, source_target_pairs={{0,2},{1,3},{2,0},{3,1},{4,6},{5,7},{6,4},{7,5},{8,10},{9,11},{10,... | collective-permute-start | bytes 393224 | tf_op jit(solution)/shard_map/ppermute | solution.py:20
  21.6 11.3 %copy-start.10 = (f32[64,1024]{1,0:T(8,128)S(1)}, f32[64,1024]{1,0:T(8,128)}, u32[]{:S(2)}) copy-start(f32[64,1024]{1,0:T(8,128)} %param.16) | copy-start | bytes 786436
  23.3 2.0 %collective-permute-start.3 = (f32[64,2048]{1,0:T(8,128)S(1)}, f32[64,2048]{1,0:T(8,128)S(1)}, u32[]{:S(2)}, u32[]{:S(2)}) collective-permute-start(f32[64,2048]{1,0:T(8,128)S(1)} %slice.102), channel_id=1, source_target_pairs={{0,1},{1,0},{2,3},{3,2},{4,5},{5,4},{6,7},{7,6},{8,9},{9,8},{10,11... | collective-permute-start | bytes 1572872 | tf_op jit(solution)/shard_map/ppermute | solution.py:20
  25.4 5.3 %collective-permute-start.6 = (bf16[64,512]{1,0:T(8,128)(2,1)S(1)}, bf16[64,512]{1,0:T(8,128)(2,1)S(1)}, u32[]{:S(2)}, u32[]{:S(2)}) collective-permute-start(bf16[64,512]{1,0:T(8,128)(2,1)S(1)} %get-tuple-element.16), channel_id=1, source_target_pairs={{0,12},{4,8},{8,4},{12,0},{16,28},{20,24},{24,20},{28,16},{1,13},{... | collective-permute-start | bytes 196616 | tf_op jit(solution)/shard_map/ppermute | solution.py:20
  28.2 4.3 %collective-permute-start.5 = (bf16[64,512]{1,0:T(8,128)(2,1)S(1)}, bf16[64,512]{1,0:T(8,128)(2,1)S(1)}, u32[]{:S(2)}, u32[]{:S(2)}) collective-permute-start(bf16[64,512]{1,0:T(8,128)(2,1)S(1)} %get-tuple-element.17), channel_id=1, source_target_pairs={{0,8},{4,12},{8,0},{12,4},{16,24},{20,28},{24,16},{28,20},{1,9},{5... | collective-permute-start | bytes 196616 | tf_op jit(solution)/shard_map/ppermute | solution.py:20
  28.6 4.3 %collective-permute-start.4 = (bf16[64,512]{1,0:T(8,128)(2,1)S(1)}, bf16[64,512]{1,0:T(8,128)(2,1)S(1)}, u32[]{:S(2)}, u32[]{:S(2)}) collective-permute-start(bf16[64,512]{1,0:T(8,128)(2,1)S(1)} %get-tuple-element.15), channel_id=1, source_target_pairs={{0,4},{4,0},{8,12},{12,8},{16,20},{20,16},{24,28},{28,24},{1,5},{5... | collective-permute-start | bytes 196616 | tf_op jit(solution)/shard_map/ppermute | solution.py:20
  33.0 1.3 collective-permute-start.7
  34.8 11.5 %collective-permute-start.10 = (bf16[64,1024]{1,0:T(8,128)(2,1)S(1)}, bf16[64,1024]{1,0:T(8,128)(2,1)S(1)}, u32[]{:S(2)}, u32[]{:S(2)}) collective-permute-start(bf16[64,1024]{1,0:T(8,128)(2,1)S(1)} %convolution_convert_fusion.5), channel_id=1, source_target_pairs={{0,12},{4,8},{8,4},{12,0},{16,28},{20,24},{24,20},{28,16},{1,13},{... | collective-permute-start | bytes 393224 | tf_op jit(solution)/shard_map/ppermute | solution.py:20
  36.6 9.7 %collective-permute-start.9 = (bf16[64,1024]{1,0:T(8,128)(2,1)S(1)}, bf16[64,1024]{1,0:T(8,128)(2,1)S(1)}, u32[]{:S(2)}, u32[]{:S(2)}) collective-permute-start(bf16[64,1024]{1,0:T(8,128)(2,1)S(1)} %convolution_convert_fusion.5), channel_id=1, source_target_pairs={{0,8},{4,12},{8,0},{12,4},{16,24},{20,28},{24,16},{28,20},{1,9},{5... | collective-permute-start | bytes 393224 | tf_op jit(solution)/shard_map/ppermute | solution.py:20
  37.0 9.3 %collective-permute-start.8 = (bf16[64,1024]{1,0:T(8,128)(2,1)S(1)}, bf16[64,1024]{1,0:T(8,128)(2,1)S(1)}, u32[]{:S(2)}, u32[]{:S(2)}) collective-permute-start(bf16[64,1024]{1,0:T(8,128)(2,1)S(1)} %convolution_convert_fusion.5), channel_id=1, source_target_pairs={{0,4},{4,0},{8,12},{12,8},{16,20},{20,16},{24,28},{28,24},{1,5},{5... | collective-permute-start | bytes 393224 | tf_op jit(solution)/shard_map/ppermute | solution.py:20
  45.3 10.0 %copy-start.2 = (bf16[1024,4096]{1,0:T(8,128)(2,1)S(1)}, bf16[1024,4096]{1,0:T(8,128)(2,1)}, u32[]{:S(2)}) copy-start(bf16[1024,4096]{1,0:T(8,128)(2,1)} %fusion.2) | copy-start | bytes 25165828
  46.3 10.7 %copy-start.6 = (bf16[64,1024]{1,0:T(8,128)(2,1)}, bf16[64,1024]{1,0:T(8,128)(2,1)S(1)}, u32[]{:S(2)}) copy-start(bf16[64,1024]{1,0:T(8,128)(2,1)S(1)} %collective-permute-done.10) | copy-start | bytes 393220
  46.3 10.7 %copy-start.8 = (bf16[64,1024]{1,0:T(8,128)(2,1)}, bf16[64,1024]{1,0:T(8,128)(2,1)S(1)}, u32[]{:S(2)}) copy-start(bf16[64,1024]{1,0:T(8,128)(2,1)S(1)} %collective-permute-done.9) | copy-start | bytes 393220
  46.3 10.7 %copy-start.9 = (bf16[64,1024]{1,0:T(8,128)(2,1)}, bf16[64,1024]{1,0:T(8,128)(2,1)S(1)}, u32[]{:S(2)}) copy-start(bf16[64,1024]{1,0:T(8,128)(2,1)S(1)} %collective-permute-done.8) | copy-start | bytes 393220
  48.7 1.4 collective-permute-start.11
  50.2 4.3 %collective-permute-start.12 = (bf16[64,512]{1,0:T(8,128)(2,1)S(1)}, bf16[64,512]{1,0:T(8,128)(2,1)S(1)}, u32[]{:S(2)}, u32[]{:S(2)}) collective-permute-start(bf16[64,512]{1,0:T(8,128)(2,1)S(1)} %add_convert_fusion.9), channel_id=1, source_target_pairs={{0,2},{1,3},{2,0},{3,1},{4,6},{5,7},{6,4},{7,5},{8,10},{9,11},{10,... | collective-permute-start | bytes 196616 | tf_op jit(solution)/shard_map/ppermute | solution.py:20
  55.4 15.2 %copy-start.11 = (f32[64,512]{1,0:T(8,128)S(1)}, f32[64,512]{1,0:T(8,128)}, u32[]{:S(2)}) copy-start(f32[64,512]{1,0:T(8,128)} %param.15) | copy-start | bytes 393220
  55.4 16.5 %copy-start.4 = (bf16[512,1024]{1,0:T(8,128)(2,1)S(1)}, bf16[512,1024]{1,0:T(8,128)(2,1)}, u32[]{:S(2)}) copy-start(bf16[512,1024]{1,0:T(8,128)(2,1)} %param.18) | copy-start | bytes 3145732
  55.4 35.2 %copy-start.5 = (bf16[1024,512]{1,0:T(8,128)(2,1)S(1)}, bf16[1024,512]{1,0:T(8,128)(2,1)}, u32[]{:S(2)}) copy-start(bf16[1024,512]{1,0:T(8,128)(2,1)} %param.25) | copy-start | bytes 3145732
  57.0 2.0 %collective-permute-start.13 = (f32[64,2048]{1,0:T(8,128)S(1)}, f32[64,2048]{1,0:T(8,128)S(1)}, u32[]{:S(2)}, u32[]{:S(2)}) collective-permute-start(f32[64,2048]{1,0:T(8,128)S(1)} %slice.110), channel_id=1, source_target_pairs={{0,1},{1,0},{2,3},{3,2},{4,5},{5,4},{6,7},{7,6},{8,9},{9,8},{10,11... | collective-permute-start | bytes 1572872 | tf_op jit(solution)/shard_map/ppermute | solution.py:20
  59.1 5.5 %collective-permute-start.16 = (bf16[64,512]{1,0:T(8,128)(2,1)S(1)}, bf16[64,512]{1,0:T(8,128)(2,1)S(1)}, u32[]{:S(2)}, u32[]{:S(2)}) collective-permute-start(bf16[64,512]{1,0:T(8,128)(2,1)S(1)} %get-tuple-element.13), channel_id=1, source_target_pairs={{0,12},{4,8},{8,4},{12,0},{16,28},{20,24},{24,20},{28,16},{1,13},{... | collective-permute-start | bytes 196616 | tf_op jit(solution)/shard_map/ppermute | solution.py:20
  60.9 4.3 %collective-permute-start.15 = (bf16[64,512]{1,0:T(8,128)(2,1)S(1)}, bf16[64,512]{1,0:T(8,128)(2,1)S(1)}, u32[]{:S(2)}, u32[]{:S(2)}) collective-permute-start(bf16[64,512]{1,0:T(8,128)(2,1)S(1)} %get-tuple-element.14), channel_id=1, source_target_pairs={{0,8},{4,12},{8,0},{12,4},{16,24},{20,28},{24,16},{28,20},{1,9},{5... | collective-permute-start | bytes 196616 | tf_op jit(solution)/shard_map/ppermute | solution.py:20
  61.4 4.3 %collective-permute-start.14 = (bf16[64,512]{1,0:T(8,128)(2,1)S(1)}, bf16[64,512]{1,0:T(8,128)(2,1)S(1)}, u32[]{:S(2)}, u32[]{:S(2)}) collective-permute-start(bf16[64,512]{1,0:T(8,128)(2,1)S(1)} %get-tuple-element.12), channel_id=1, source_target_pairs={{0,4},{4,0},{8,12},{12,8},{16,20},{20,16},{24,28},{28,24},{1,5},{5... | collective-permute-start | bytes 196616 | tf_op jit(solution)/shard_map/ppermute | solution.py:20
  65.7 4.9 %collective-permute-start.17 = (bf16[64,256]{1,0:T(8,128)(2,1)S(1)}, bf16[64,256]{1,0:T(8,128)(2,1)S(1)}, u32[]{:S(2)}, u32[]{:S(2)}) collective-permute-start(bf16[64,256]{1,0:T(8,128)(2,1)S(1)} %slice.151), channel_id=1, source_target_pairs={{0,16},{4,20},{8,24},{12,28},{16,0},{20,4},{24,8},{28,12},{1,17},{... | collective-permute-start | bytes 98312 | tf_op jit(solution)/shard_map/ppermute | solution.py:20
  70.6 1.3 collective-permute-start.18
  72.2 7.3 %collective-permute-start.21 = (bf16[64,1024]{1,0:T(8,128)(2,1)S(1)}, bf16[64,1024]{1,0:T(8,128)(2,1)S(1)}, u32[]{:S(2)}, u32[]{:S(2)}) collective-permute-start(bf16[64,1024]{1,0:T(8,128)(2,1)S(1)} %convolution_convert_fusion.2), channel_id=1, source_target_pairs={{0,12},{4,8},{8,4},{12,0},{16,28},{20,24},{24,20},{28,16},{1,13},{... | collective-permute-start | bytes 393224 | tf_op jit(solution)/shard_map/ppermute | solution.py:20
  74.6 6.8 %collective-permute-start.20 = (bf16[64,1024]{1,0:T(8,128)(2,1)S(1)}, bf16[64,1024]{1,0:T(8,128)(2,1)S(1)}, u32[]{:S(2)}, u32[]{:S(2)}) collective-permute-start(bf16[64,1024]{1,0:T(8,128)(2,1)S(1)} %convolution_convert_fusion.2), channel_id=1, source_target_pairs={{0,8},{4,12},{8,0},{12,4},{16,24},{20,28},{24,16},{28,20},{1,9},{5... | collective-permute-start | bytes 393224 | tf_op jit(solution)/shard_map/ppermute | solution.py:20
  75.0 6.5 %collective-permute-start.19 = (bf16[64,1024]{1,0:T(8,128)(2,1)S(1)}, bf16[64,1024]{1,0:T(8,128)(2,1)S(1)}, u32[]{:S(2)}, u32[]{:S(2)}) collective-permute-start(bf16[64,1024]{1,0:T(8,128)(2,1)S(1)} %convolution_convert_fusion.2), channel_id=1, source_target_pairs={{0,4},{4,0},{8,12},{12,8},{16,20},{20,16},{24,28},{28,24},{1,5},{5... | collective-permute-start | bytes 393224 | tf_op jit(solution)/shard_map/ppermute | solution.py:20
  81.6 9.0 %collective-permute-start.22 = (bf16[64,1024]{1,0:T(8,128)(2,1)S(1)}, bf16[64,1024]{1,0:T(8,128)(2,1)S(1)}, u32[]{:S(2)}, u32[]{:S(2)}) collective-permute-start(bf16[64,1024]{1,0:T(8,128)(2,1)S(1)} %add_convert_fusion.3), channel_id=1, source_target_pairs={{0,16},{4,20},{8,24},{12,28},{16,0},{20,4},{24,8},{28,12},{1,17},{... | collective-permute-start | bytes 393224 | tf_op jit(solution)/shard_map/ppermute | solution.py:20
  90.8 1.4 collective-permute-start.23
  92.3 4.3 %collective-permute-start.24 = (bf16[64,512]{1,0:T(8,128)(2,1)S(1)}, bf16[64,512]{1,0:T(8,128)(2,1)S(1)}, u32[]{:S(2)}, u32[]{:S(2)}) collective-permute-start(bf16[64,512]{1,0:T(8,128)(2,1)S(1)} %add_convert_fusion.7), channel_id=1, source_target_pairs={{0,2},{1,3},{2,0},{3,1},{4,6},{5,7},{6,4},{7,5},{8,10},{9,11},{10,... | collective-permute-start | bytes 196616 | tf_op jit(solution)/shard_map/ppermute | solution.py:20
  97.3 5.9 %collective-permute-start.25 = (bf16[64,512]{1,0:T(8,128)(2,1)S(1)}, bf16[64,512]{1,0:T(8,128)(2,1)S(1)}, u32[]{:S(2)}, u32[]{:S(2)}) collective-permute-start(bf16[64,512]{1,0:T(8,128)(2,1)S(1)} %get-tuple-element.6), channel_id=1, source_target_pairs={{0,16},{4,20},{8,24},{12,28},{16,0},{20,4},{24,8},{28,12},{1,17},{... | collective-permute-start | bytes 196616 | tf_op jit(solution)/shard_map/ppermute | solution.py:20
  103.2 11.4 %collective-permute-start.26 = (bf16[64,1024]{1,0:T(8,128)(2,1)S(1)}, bf16[64,1024]{1,0:T(8,128)(2,1)S(1)}, u32[]{:S(2)}, u32[]{:S(2)}) collective-permute-start(bf16[64,1024]{1,0:T(8,128)(2,1)S(1)} %pad_maximum_fusion), channel_id=1, source_target_pairs={{0,4},{4,0},{8,12},{12,8},{16,20},{20,16},{24,28},{28,24},{1,5},{5... | collective-permute-start | bytes 393224 | tf_op jit(solution)/shard_map/ppermute | solution.py:20
  104.8 28.1 %copy-start.3 = (bf16[1024,1024]{1,0:T(8,128)(2,1)S(1)}, bf16[1024,1024]{1,0:T(8,128)(2,1)}, u32[]{:S(2)}) copy-start(bf16[1024,1024]{1,0:T(8,128)(2,1)} %param.26) | copy-start | bytes 6291460
  104.8 28.1 %copy-start.7 = (bf16[64,1024]{1,0:T(8,128)(2,1)S(1)}, bf16[64,1024]{1,0:T(8,128)(2,1)}, u32[]{:S(2)}) copy-start(bf16[64,1024]{1,0:T(8,128)(2,1)} %copy-done.6) | copy-start | bytes 393220
  112.6 5.0 %collective-permute-start.27 = (bf16[64,1024]{1,0:T(8,128)(2,1)S(1)}, bf16[64,1024]{1,0:T(8,128)(2,1)S(1)}, u32[]{:S(2)}, u32[]{:S(2)}) collective-permute-start(bf16[64,1024]{1,0:T(8,128)(2,1)S(1)} %pad_maximum_fusion), channel_id=1, source_target_pairs={{0,8},{4,12},{8,0},{12,4},{16,24},{20,28},{24,16},{28,20},{1,9},{5... | collective-permute-start | bytes 393224 | tf_op jit(solution)/shard_map/ppermute | solution.py:20
  113.1 5.9 %collective-permute-start.28 = (bf16[64,1024]{1,0:T(8,128)(2,1)S(1)}, bf16[64,1024]{1,0:T(8,128)(2,1)S(1)}, u32[]{:S(2)}, u32[]{:S(2)}) collective-permute-start(bf16[64,1024]{1,0:T(8,128)(2,1)S(1)} %pad_maximum_fusion), channel_id=1, source_target_pairs={{0,12},{4,8},{8,4},{12,0},{16,28},{20,24},{24,20},{28,16},{1,13},{... | collective-permute-start | bytes 393224 | tf_op jit(solution)/shard_map/ppermute | solution.py:20
  125.0 5.9 %collective-permute-start.31 = (bf16[64,1024]{1,0:T(8,128)(2,1)S(1)}, bf16[64,1024]{1,0:T(8,128)(2,1)S(1)}, u32[]{:S(2)}, u32[]{:S(2)}) collective-permute-start(bf16[64,1024]{1,0:T(8,128)(2,1)S(1)} %convolution_convert_fusion.4), channel_id=1, source_target_pairs={{0,12},{4,8},{8,4},{12,0},{16,28},{20,24},{24,20},{28,16},{1,13},{... | collective-permute-start | bytes 393224 | tf_op jit(solution)/shard_map/ppermute | solution.py:20
  126.4 5.8 %collective-permute-start.30 = (bf16[64,1024]{1,0:T(8,128)(2,1)S(1)}, bf16[64,1024]{1,0:T(8,128)(2,1)S(1)}, u32[]{:S(2)}, u32[]{:S(2)}) collective-permute-start(bf16[64,1024]{1,0:T(8,128)(2,1)S(1)} %convolution_convert_fusion.4), channel_id=1, source_target_pairs={{0,8},{4,12},{8,0},{12,4},{16,24},{20,28},{24,16},{28,20},{1,9},{5... | collective-permute-start | bytes 393224 | tf_op jit(solution)/shard_map/ppermute | solution.py:20
  127.9 5.0 %collective-permute-start.29 = (bf16[64,1024]{1,0:T(8,128)(2,1)S(1)}, bf16[64,1024]{1,0:T(8,128)(2,1)S(1)}, u32[]{:S(2)}, u32[]{:S(2)}) collective-permute-start(bf16[64,1024]{1,0:T(8,128)(2,1)S(1)} %convolution_convert_fusion.4), channel_id=1, source_target_pairs={{0,4},{4,0},{8,12},{12,8},{16,20},{20,16},{24,28},{28,24},{1,5},{5... | collective-permute-start | bytes 393224 | tf_op jit(solution)/shard_map/ppermute | solution.py:20
  134.4 1.6 collective-permute-start.32
  136.0 10.6 %collective-permute-start.33 = (bf16[64,1024]{1,0:T(8,128)(2,1)S(1)}, bf16[64,1024]{1,0:T(8,128)(2,1)S(1)}, u32[]{:S(2)}, u32[]{:S(2)}) collective-permute-start(bf16[64,1024]{1,0:T(8,128)(2,1)S(1)} %add_convert_fusion.1), channel_id=1, source_target_pairs={{0,2},{1,3},{2,0},{3,1},{4,6},{5,7},{6,4},{7,5},{8,10},{9,11},{10,... | collective-permute-start | bytes 393224 | tf_op jit(solution)/shard_map/ppermute | solution.py:20
  147.4 13.5 %collective-permute-start.36 = (bf16[64,1024]{1,0:T(8,128)(2,1)S(1)}, bf16[64,1024]{1,0:T(8,128)(2,1)S(1)}, u32[]{:S(2)}, u32[]{:S(2)}) collective-permute-start(bf16[64,1024]{1,0:T(8,128)(2,1)S(1)} %get-tuple-element.3), channel_id=1, source_target_pairs={{0,12},{4,8},{8,4},{12,0},{16,28},{20,24},{24,20},{28,16},{1,13},{... | collective-permute-start | bytes 393224 | tf_op jit(solution)/shard_map/ppermute | solution.py:20
  148.9 12.0 %collective-permute-start.35 = (bf16[64,1024]{1,0:T(8,128)(2,1)S(1)}, bf16[64,1024]{1,0:T(8,128)(2,1)S(1)}, u32[]{:S(2)}, u32[]{:S(2)}) collective-permute-start(bf16[64,1024]{1,0:T(8,128)(2,1)S(1)} %get-tuple-element.3), channel_id=1, source_target_pairs={{0,8},{4,12},{8,0},{12,4},{16,24},{20,28},{24,16},{28,20},{1,9},{5... | collective-permute-start | bytes 393224 | tf_op jit(solution)/shard_map/ppermute | solution.py:20
  149.7 11.2 %collective-permute-start.34 = (bf16[64,1024]{1,0:T(8,128)(2,1)S(1)}, bf16[64,1024]{1,0:T(8,128)(2,1)S(1)}, u32[]{:S(2)}, u32[]{:S(2)}) collective-permute-start(bf16[64,1024]{1,0:T(8,128)(2,1)S(1)} %get-tuple-element.3), channel_id=1, source_target_pairs={{0,4},{4,0},{8,12},{12,8},{16,20},{20,16},{24,28},{28,24},{1,5},{5... | collective-permute-start | bytes 393224 | tf_op jit(solution)/shard_map/ppermute | solution.py:20
  164.0 30.3 %copy-start.1 = (bf16[1024,1024]{1,0:T(8,128)(2,1)S(1)}, bf16[1024,1024]{1,0:T(8,128)(2,1)}, u32[]{:S(2)}) copy-start(bf16[1024,1024]{1,0:T(8,128)(2,1)} %param.19) | copy-start | bytes 6291460
  174.9 5.0 %collective-permute-start.37 = (bf16[64,1024]{1,0:T(8,128)(2,1)S(1)}, bf16[64,1024]{1,0:T(8,128)(2,1)S(1)}, u32[]{:S(2)}, u32[]{:S(2)}) collective-permute-start(bf16[64,1024]{1,0:T(8,128)(2,1)S(1)} %convolution_convert_fusion), channel_id=1, source_target_pairs={{0,4},{4,0},{8,12},{12,8},{16,20},{20,16},{24,28},{28,24},{1,5},{5... | collective-permute-start | bytes 393224 | tf_op jit(solution)/shard_map/ppermute | solution.py:20
  182.9 2.0 %collective-permute-start.38 = (f32[64,2048]{1,0:T(8,128)S(1)}, f32[64,2048]{1,0:T(8,128)S(1)}, u32[]{:S(2)}, u32[]{:S(2)}) collective-permute-start(f32[64,2048]{1,0:T(8,128)S(1)} %fusion.21), channel_id=1, source_target_pairs={{0,1},{1,0},{2,3},{3,2},{4,5},{5,4},{6,7},{7,6},{8,9},{9,8},{10,11... | collective-permute-start | bytes 1572872 | tf_op jit(solution)/shard_map/ppermute | solution.py:20
  185.0 8.4 %collective-permute-start.39 = (bf16[64,2048]{1,0:T(8,128)(2,1)S(1)}, bf16[64,2048]{1,0:T(8,128)(2,1)S(1)}, u32[]{:S(2)}, u32[]{:S(2)}) collective-permute-start(bf16[64,2048]{1,0:T(8,128)(2,1)S(1)} %add_convert_fusion), channel_id=1, source_target_pairs={{0,2},{1,3},{2,0},{3,1},{4,6},{5,7},{6,4},{7,5},{8,10},{9,11},{10,... | collective-permute-start | bytes 786440 | tf_op jit(solution)/shard_map/ppermute | solution.py:20

commit v2 on v1

--- a/solution.py
+++ b/solution.py
@@ -1,6 +1,8 @@
 import jax
 import jax.numpy as jnp
 from jax import lax
+from jax.experimental import pallas as pl
+from jax.experimental.pallas import tpu as pltpu
 from jax.sharding import PartitionSpec as P
 
 BF16 = jnp.bfloat16
@@ -44,9 +46,11 @@
 
 
 def gather_blocks(x, axis, groups):
-    for group in reversed(groups):
+    for group in groups[:0:-1]:
         x = jnp.concatenate([x] + [partner(x, axis, m << group[0]) for m in range(1, 1 << len(group))], axis=1)
-    return x
+    if not groups:
+        return [x]
+    return [x] + [partner(x, axis, m << groups[0][0]) for m in range(1, 1 << len(groups[0]))]
 
 
 def relative_block(owner, me, groups):
@@ -62,9 +66,77 @@
     return lax.optimization_barrier(hot.astype(BF16))
 
 
-def one_hot_columns(place, height):
-    hot = place[None, :] == lax.broadcasted_iota(jnp.int32, (height, place.shape[0]), 0)
-    return lax.optimization_barrier(hot.astype(BF16))
+TILE = 256
+
+
+def hot_tile(place, start, rows):
+    rel = place - start
+    rel = jnp.where((rel >= 0) & (rel < rows), rel, -1).astype(F32).astype(BF16)
+    row = lax.broadcasted_iota(jnp.int32, (rows, place.shape[1]), 0).astype(F32).astype(BF16)
+    return jnp.where(row == rel, jnp.ones((), BF16), jnp.zeros((), BF16))
+
+
+def pick_kernel(*refs):
+    pieces, (place_ref, block_ref, out_ref) = refs[:-3], refs[-3:]
+
+    @pl.when(pl.program_id(0) == 0)
+    def _():
+        out_ref[...] = jnp.zeros_like(out_ref)
+
+    place = place_ref[...]
+    picked = jnp.zeros((out_ref.shape[0], place.shape[1]), F32)
+    start = 0
+    for piece in pieces:
+        width = piece.shape[1]
+        tile = min(TILE, width)
+        for k in range(0, width, tile):
+            picked += dot(piece[:, k : k + tile], hot_tile(place, start + k, tile))
+        start += width
+    out_ref[...] += dot(picked.astype(BF16), block_ref[...])
+
+
+def picked_product(pieces, place, block):
+    if pieces[0].shape[1] % TILE:
+        pieces = [jnp.concatenate(pieces, axis=1)]
+    rows, count, width = pieces[0].shape[0], place.shape[0], block.shape[1]
+    step = min(count, 1024)
+    extent = sum(p.shape[1] for p in pieces)
+    return pl.pallas_call(
+        pick_kernel,
+        grid=(count // step,),
+        in_specs=[pl.BlockSpec(p.shape, lambda i: (0, 0)) for p in pieces]
+        + [pl.BlockSpec((1, step), lambda i: (0, i)), pl.BlockSpec((step, width), lambda i: (i, 0))],
+        out_specs=pl.BlockSpec((rows, width), lambda i: (0, 0)),
+        out_shape=jax.ShapeDtypeStruct((rows, width), F32),
+        compiler_params=pltpu.CompilerParams(vmem_limit_bytes=16 << 20),
+        cost_estimate=pl.CostEstimate(
+            flops=2 * rows * count * (extent + width), bytes_accessed=2 * count * (width + 2 * extent), transcendentals=0
+        ),
+    )(*pieces, place[None, :], block)
+
+
+def put_kernel(update_ref, place_ref, out_ref):
+    update, place = update_ref[...], place_ref[...]
+    step = out_ref.shape[1]
+    base = pl.program_id(0) * step
+    tile = min(TILE, step)
+    for n in range(0, step, tile):
+        hot = hot_tile(place, base + n, tile)
+        out_ref[:, n : n + tile] = lax.dot_general(update, hot, (((1,), (1,)), ((), ())), preferred_element_type=F32)
+
+
+def put_columns(update, place, width):
+    rows, count = update.shape
+    step = min(width, 2048)
+    return pl.pallas_call(
+        put_kernel,
+        grid=(width // step,),
+        in_specs=[pl.BlockSpec((rows, count), lambda i: (0, 0)), pl.BlockSpec((1, count), lambda i: (0, 0))],
+        out_specs=pl.BlockSpec((rows, step), lambda i: (0, i)),
+        out_shape=jax.ShapeDtypeStruct((rows, width), F32),
+        compiler_params=pltpu.CompilerParams(vmem_limit_bytes=16 << 20),
+        cost_estimate=pl.CostEstimate(flops=2 * rows * count * width, bytes_accessed=4 * count * width, transcendentals=0),
+    )(update, place[None, :])
 
 
 def per_device(
@@ -84,11 +156,6 @@
     front_bits = lax.axis_size("front").bit_length() - 1
     groups = [bit_groups(range(leaf_bits - level)) for level in range(3)]
     away = bit_groups(range(1, front_bits))
-    rhs = (rhs_zero, rhs_one, rhs_two)
-    pivot = (pivot_zero, pivot_one, pivot_two)
-    lower = (None, lower_one, lower_two)
-    upper = (None, upper_one, upper_two)
-    back = (back_zero, back_one, back_two)
 
     def own_index(level):
         table = index_one if level == 1 else index_two
@@ -105,15 +172,9 @@
         rel = relative_block(owner, mine, groups[level])
         return ((column // half & 1) ^ core) * (sep // 2) + rel * half + column % half
 
-    def whole_place(column, level):
-        block = sep // (leaves >> level)
-        mine = me & (leaves >> level) - 1
-        rel = relative_block(column // block, mine, groups[level])
-        return rel * block + column % block
-
     def both_halves(own):
         other = partner(own, "front", 1)
-        return jnp.concatenate([jnp.where(core == 0, own, other), jnp.where(core == 0, other, own)], axis=1)
+        return in_order(own, other)
 
     def front_half(x):
         width = x.shape[1] // 2
@@ -121,8 +182,12 @@
         send = jnp.where(core == 0, x[:, width:], x[:, :width])
         return exchange_sum(keep + partner(send, "front", 1), "front", away)
 
-    def front_sum(x):
-        return exchange_sum(x + partner(x, "front", 1), "front", away)
+    def in_order(own, other):
+        return jnp.concatenate([jnp.where(core == 0, own, other), jnp.where(core == 0, other, own)], axis=1)
+
+    def known_pieces(half, level):
+        own = gather_blocks(half.astype(BF16), "leaf", groups[level])
+        return own + [partner(piece, "front", 1) for piece in own]
 
     def row_total(pending, level):
         width = sep // 2
@@ -137,44 +202,46 @@
         half = index.shape[0] // 2
         return lax.dynamic_slice(index, (core * half,), (half,))
 
-    index = core_slice(own_index(2))
+    index = own_index(2)
     is_root = index < sep
     place_one = jnp.where(is_root, -1, split_place(index - sep, 1))
     place_root = jnp.where(is_root, split_place(index, 0), -1)
     y_two = exchange_sum(dot(rhs_two.astype(BF16), pivot_two), "leaf", groups[2])
-    hot_one = one_hot_rows(place_one, sep)
-    hot_root = one_hot_rows(place_root, sep)
+    hot_one = one_hot_rows(core_slice(place_one), sep)
     update = front_half(dot(y_two.astype(BF16), lower_two)).astype(BF16)
     pending_one = dot(update, hot_one)
-    pending_root = dot(update, hot_root)
-
+    pending_root = put_columns(update, core_slice(place_root), sep)
+
+    place_up = split_place(own_index(1), 0)
     own_rhs = half_columns(rhs_one)
     reduced = both_halves((own_rhs - row_total(pending_one, 1)).astype(BF16))
     y_one = exchange_sum(dot(reduced, pivot_one), "leaf", groups[1])
-    hot_up = one_hot_rows(split_place(core_slice(own_index(1)), 0), sep)
+    hot_up = one_hot_rows(core_slice(place_up), sep)
     update = front_half(dot(y_one.astype(BF16), lower_one)).astype(BF16)
     pending_root = pending_root + dot(update, hot_up)
 
+    near, far = groups[0][:1], groups[0][1:]
+    count = 1 << len(near[0])
+    block = pivot_zero.shape[1] // count
+    starts = [((me & count - 1) ^ m) * block for m in range(count)]
+    pivot_rel = jnp.concatenate([lax.dynamic_slice_in_dim(pivot_zero, at, block, 1) for at in starts], axis=1)
+    back_rel = jnp.concatenate([lax.dynamic_slice_in_dim(back_zero, at, block, 0) for at in starts], axis=0)
     own_rhs = half_columns(rhs_zero)
     reduced = both_halves((own_rhs - row_total(pending_root, 0)).astype(BF16))
-    y_zero = exchange_sum(dot(reduced, pivot_zero), "leaf", groups[0])
-    x_zero = front_sum(dot(y_zero.astype(BF16), back_zero))
-    known_zero = gather_blocks(x_zero.astype(BF16), "leaf", groups[0])
-
-    pick_one = one_hot_columns(whole_place(own_index(1), 0), sep)
-    index = own_index(2)
-    is_root = index < sep
-    pick_root = one_hot_columns(jnp.where(is_root, whole_place(index, 0), -1), sep)
-    pick_mid = one_hot_columns(jnp.where(is_root, -1, whole_place(index - sep, 1)), sep)
-    picked = dot(known_zero, pick_one).astype(BF16)
-    z_one = y_one - exchange_sum(dot(picked, upper_one), "leaf", groups[1])
-    x_one = front_sum(dot(z_one.astype(BF16), back_one))
-    known_one = gather_blocks(x_one.astype(BF16), "leaf", groups[1])
-
-    picked = (dot(known_zero, pick_root) + dot(known_one, pick_mid)).astype(BF16)
-    z_two = y_two - exchange_sum(dot(picked, upper_two), "leaf", groups[2])
-    x_two = front_sum(dot(z_two.astype(BF16), back_two))
-    return x_zero, x_one, x_two
+    y_zero = exchange_sum(scatter_sum(dot(reduced, pivot_rel), "leaf", near), "leaf", far)
+    y_zero = jnp.concatenate(gather_blocks(y_zero.astype(BF16), "leaf", near), axis=1)
+    x_zero = front_half(dot(y_zero, back_rel))
+    known_zero = known_pieces(x_zero, 0)
+
+    coupling = picked_product(known_zero, place_up, upper_one)
+    z_one = y_one - exchange_sum(coupling, "leaf", groups[1])
+    x_one = front_half(dot(z_one.astype(BF16), back_one))
+    known_one = known_pieces(x_one, 1)
+
+    coupling = picked_product(known_zero, place_root, upper_two) + picked_product(known_one, place_one, upper_two)
+    z_two = y_two - exchange_sum(coupling, "leaf", groups[2])
+    x_two = front_half(dot(z_two.astype(BF16), back_two))
+    return both_halves(x_zero), both_halves(x_one), both_halves(x_two)
 
 
 def solution(mesh):

time: 195 us -> 164 us (0.84)
  other arithmetic: 44.7 us -> 11.3 us
  matrix products: 38.2 us -> 13.5 us
  Pallas kernels: 0 us -> 13 us
  waiting for transfers between devices: 66.5 us -> 76.5 us
  starting transfers between devices: 41.8 us -> 46.6 us
    convert_element_type x4 -> x2, other arithmetic: 27.6 us -> 0.05 us  [the longest x1 0.03 us: per_device(): update = front_half(dot(y_two.astype(BF16), lower_two)).astype(BF16)]
    dot_general x14 -> x10, matrix products: 38.2 us -> 13.5 us  [dot(): return jnp.dot(left, right, preferred_element_type=F32)]
    pallas_call x0 -> x4, Pallas kernels: none -> 13 us  [the longest x3 9.95 us: picked_product(): pl.pallas_call(pick_kernel, grid=(count // step,), in_specs=[pl.BlockSpec...]
    ppermute x40 -> x54, waiting for transfers between devices: 66.5 us -> 76.5 us  [partner(): lax.ppermute(x, axis, [(i, i ^ mask) for i in range(lax.axis_size(axis))])]
    convert_element_type x3 -> x2, other arithmetic: 12.5 us -> 5.31 us  [one_hot_rows(): return lax.optimization_barrier(hot.astype(BF16))]
    ppermute x40 -> x54, starting transfers between devices: 41.8 us -> 46.6 us  [partner(): lax.ppermute(x, axis, [(i, i ^ mask) for i in range(lax.axis_size(axis))])]
    concatenate x0 -> x3, other arithmetic: none -> 2.22 us  [in_order(): jnp.concatenate([jnp.where(core == 0, own, other), jnp.where(core == 0, o...]
  transfers between devices with their start and end apart: 40 -> 54, of which waited for: 32 -> 45; matrix products, arithmetic and copies ran while one was open for 22% -> 5% of each run, Pallas kernels for 0% -> 4%
where the time goes in v2:
time: 164 us; the launch traced here: 163 us
  waiting for transfers between devices  76.5 us (47%)
  starting transfers between devices  46.6 us (28%)
  matrix products  13.5 us (8%)
  Pallas kernels  13 us (8%)
  other arithmetic  11.3 us (7%)
    ppermute x54, waiting for transfers between devices, partner(): lax.ppermute(x, axis, [(i, i ^ mask) for i in range(lax.axis_size(axis))])  76.5 us
    ppermute x54, starting transfers between devices, partner(): lax.ppermute(x, axis, [(i, i ^ mask) for i in range(lax.axis_size(axis))])  46.6 us
    dot_general x10, matrix products, dot(): return jnp.dot(left, right, preferred_element_type=F32)  13.5 us
    pallas_call x3, Pallas kernels, picked_product(): pl.pallas_call(pick_kernel, grid=(count // step,), in_specs=[pl.BlockSpec...  9.95 us
    convert_element_type x2, other arithmetic, one_hot_rows(): return lax.optimization_barrier(hot.astype(BF16))  5.31 us
  transfers between devices with their start and end apart: 54, of which 45 were waited for; matrix products, arithmetic and copies ran while one was open for 5% of the time, Pallas kernels for 4%

profile of v2, /device:TPU:0, one launch (start us, length us, event | category | flops | bytes accessed | tf_op | source)
XLA Modules:
  0.0 163.3 jit_solution(4931482477017406342)
XLA Ops:
  0.6 3.3 %convolution_convert_fusion = bf16[64,1024]{1,0:T(8,128)(2,1)S(1)} fusion(bf16[2048,1024]{1,0:T(8,128)(2,1)} %param.20, f32[64,2048]{1,0:T(8,128)} %param.17), kind=kOutput, calls=%fused_computation.4 | convolution fusion | flops 268632064 | bytes 4849664 | tf_op jit(solution)/shard_map/dot_general | solution.py:13
  4.0 3.0 %collective-permute-start = (bf16[64,1024]{1,0:T(8,128)(2,1)S(1)}, bf16[64,1024]{1,0:T(8,128)(2,1)S(1)}, u32[]{:S(2)}, u32[]{:S(2)}) collective-permute-start(bf16[64,1024]{1,0:T(8,128)(2,1)S(1)} %convolution_convert_fusion), channel_id=1, source_target_pairs={{0,4},{4,0},{8,12},{12,8},{16,20},{20,16},{24,28},{28,24},{1,5},{5... | collective-permute-start | bytes 393224 | tf_op jit(solution)/shard_map/ppermute | solution.py:22
  8.0 2.5 %collective-permute-done = bf16[64,1024]{1,0:T(8,128)(2,1)S(1)} collective-permute-done((bf16[64,1024]{1,0:T(8,128)(2,1)S(1)}, bf16[64,1024]{1,0:T(8,128)(2,1)S(1)}, u32[]{:S(2)}, u32[]{:S(2)}) %collective-permute-start) | collective-permute-done | bytes 131104 | tf_op jit(solution)/shard_map/ppermute | solution.py:22
  10.5 3.1 %fusion.20 = f32[64,2048]{1,0:T(8,128)S(1)} fusion(bf16[1024,2048]{1,0:T(8,128)(2,1)} %param.22, bf16[64,1024]{1,0:T(8,128)(2,1)S(1)} %collective-permute-done, bf16[64,1024]{1,0:T(8,128)(2,1)S(1)} %convolution_convert_fusion), kind=kOutput, calls=%fused_computation.39 | convolution fusion | flops 268697600 | bytes 4980736 | tf_op jit(solution)/shard_map/dot_general | solution.py:13
  13.8 1.5 collective-permute-done.1
  15.3 1.8 %collective-permute-start.2 = (bf16[64,1024]{1,0:T(8,128)(2,1)S(1)}, bf16[64,1024]{1,0:T(8,128)(2,1)S(1)}, u32[]{:S(2)}, u32[]{:S(2)}) collective-permute-start(bf16[64,1024]{1,0:T(8,128)(2,1)S(1)} %add_convert_fusion.3), channel_id=1, source_target_pairs={{0,2},{1,3},{2,0},{3,1},{4,6},{5,7},{6,4},{7,5},{8,10},{9,11},{10,... | collective-permute-start | bytes 393224 | tf_op jit(solution)/shard_map/ppermute | solution.py:22
  17.1 3.7 %fusion = bf16[1024,4096]{1,0:T(8,128)(2,1)S(1)} fusion(s32[1024]{0:T(1024)S(1)} %get-tuple-element.50), kind=kLoop, calls=%fused_computation.1 | loop fusion | flops 8388608 | bytes 8392704 | tf_op jit(solution)/shard_map/convert_element_type | solution.py:66
  21.0 1.6 fusion.96
  22.7 1.9 %collective-permute-done.3 = f32[64,2048]{1,0:T(8,128)S(1)} collective-permute-done((f32[64,2048]{1,0:T(8,128)S(1)}, f32[64,2048]{1,0:T(8,128)S(1)}, u32[]{:S(2)}, u32[]{:S(2)}) %collective-permute-start.3) | collective-permute-done | bytes 524320 | tf_op jit(solution)/shard_map/ppermute | solution.py:22
  24.7 1.8 %collective-permute-start.4 = (bf16[64,512]{1,0:T(8,128)(2,1)S(1)}, bf16[64,512]{1,0:T(8,128)(2,1)S(1)}, u32[]{:S(2)}, u32[]{:S(2)}) collective-permute-start(bf16[64,512]{1,0:T(8,128)(2,1)S(1)} %get-tuple-element.26), channel_id=1, source_target_pairs={{0,4},{4,0},{8,12},{12,8},{16,20},{20,16},{24,28},{28,24},{1,5},{5... | collective-permute-start | bytes 196616 | tf_op jit(solution)/shard_map/ppermute | solution.py:22
  26.4 1.6 collective-permute-start.5
  29.0 2.3 %collective-permute-done.5 = bf16[64,512]{1,0:T(8,128)(2,1)S(1)} collective-permute-done((bf16[64,512]{1,0:T(8,128)(2,1)S(1)}, bf16[64,512]{1,0:T(8,128)(2,1)S(1)}, u32[]{:S(2)}, u32[]{:S(2)}) %collective-permute-start.5) | collective-permute-done | bytes 65568 | tf_op jit(solution)/shard_map/ppermute | solution.py:22
  31.2 1.9 %collective-permute-done.6 = bf16[64,512]{1,0:T(8,128)(2,1)S(1)} collective-permute-done((bf16[64,512]{1,0:T(8,128)(2,1)S(1)}, bf16[64,512]{1,0:T(8,128)(2,1)S(1)}, u32[]{:S(2)}, u32[]{:S(2)}) %collective-permute-start.6) | collective-permute-done | bytes 65568 | tf_op jit(solution)/shard_map/ppermute | solution.py:22
  33.3 1.2 collective-permute-done.7
  35.1 1.1 collective-permute-start.10
  37.1 1.6 collective-permute-start.9
  39.5 3.0 %collective-permute-done.10 = bf16[64,1024]{1,0:T(8,128)(2,1)S(1)} collective-permute-done((bf16[64,1024]{1,0:T(8,128)(2,1)S(1)}, bf16[64,1024]{1,0:T(8,128)(2,1)S(1)}, u32[]{:S(2)}, u32[]{:S(2)}) %collective-permute-start.10) | collective-permute-done | bytes 131104 | tf_op jit(solution)/shard_map/ppermute | solution.py:22
  42.4 1.8 %collective-permute-done.8 = bf16[64,1024]{1,0:T(8,128)(2,1)S(1)} collective-permute-done((bf16[64,1024]{1,0:T(8,128)(2,1)S(1)}, bf16[64,1024]{1,0:T(8,128)(2,1)S(1)}, u32[]{:S(2)}, u32[]{:S(2)}) %collective-permute-start.8) | collective-permute-done | bytes 131104 | tf_op jit(solution)/shard_map/ppermute | solution.py:22
  44.2 2.2 %fusion.40 = f32[64,1024]{1,0:T(8,128)S(1)} fusion(bf16[1024,1024]{1,0:T(8,128)(2,1)} %param.21, bf16[64,1024]{1,0:T(8,128)(2,1)S(1)} %collective-permute-done.10, bf16[64,1024]{1,0:T(8,128)(2,1)S(1)} %collective-permute-done.9, bf16[64,1024]{1,0:T(8,128)(2,1)S(1)} %collective-permute-done.8, bf16[64,1024]{1,0:T(8,128)(2,1)S(1)} %convolution_convert_fusion.1), kind=kOutput, calls=%fused_computation.65 | convolution fusion | flops 134742016 | bytes 2883584 | tf_op jit(solution)/shard_map/dot_general | solution.py:13
  46.6 1.2 collective-permute-done.11
  47.9 1.6 collective-permute-start.12
  49.5 1.6 fusion.1
  51.1 3.0 %shard_map.166 = f32[64,4096]{1,0:T(8,128)S(1)} custom-call(bf16[64,1024]{1,0:T(8,128)(2,1)S(1)} %add_convert_fusion.2.update_ref, s32[1,1024]{1,0:T(1,128)S(1)} %bitcast.12), custom_call_target="tpu_custom_call" | custom-call | flops 536870912 | bytes 16777216 | tf_op jit(solution)/shard_map/pallas_call | solution.py:131
  55.3 1.9 %collective-permute-done.13 = f32[64,2048]{1,0:T(8,128)S(1)} collective-permute-done((f32[64,2048]{1,0:T(8,128)S(1)}, f32[64,2048]{1,0:T(8,128)S(1)}, u32[]{:S(2)}, u32[]{:S(2)}) %collective-permute-start.13) | collective-permute-done | bytes 524320 | tf_op jit(solution)/shard_map/ppermute | solution.py:22
  59.1 1.7 %collective-permute-start.16 = (bf16[64,512]{1,0:T(8,128)(2,1)S(1)}, bf16[64,512]{1,0:T(8,128)(2,1)S(1)}, u32[]{:S(2)}, u32[]{:S(2)}) collective-permute-start(bf16[64,512]{1,0:T(8,128)(2,1)S(1)} %get-tuple-element.24), channel_id=1, source_target_pairs={{0,12},{4,8},{8,4},{12,0},{16,28},{20,24},{24,20},{28,16},{1,13},{... | collective-permute-start | bytes 196616 | tf_op jit(solution)/shard_map/ppermute | solution.py:22
  61.6 1.4 collective-permute-done.15
  63.0 1.2 collective-permute-done.16
  64.9 2.6 %collective-permute-start.17 = (bf16[64,256]{1,0:T(8,128)(2,1)}, bf16[64,256]{1,0:T(8,128)(2,1)}, u32[]{:S(2)}, u32[]{:S(2)}) collective-permute-start(bf16[64,256]{1,0:T(8,128)(2,1)} %slice.229), channel_id=1, source_target_pairs={{0,16},{4,20},{8,24},{12,28},{16,0},{20,4},{24,8},{28,12},{1,17},{... | collective-permute-start | bytes 98312 | tf_op jit(solution)/shard_map/ppermute | solution.py:22
  67.5 2.5 %collective-permute-done.17 = bf16[64,256]{1,0:T(8,128)(2,1)} collective-permute-done((bf16[64,256]{1,0:T(8,128)(2,1)}, bf16[64,256]{1,0:T(8,128)(2,1)}, u32[]{:S(2)}, u32[]{:S(2)}) %collective-permute-start.17) | collective-permute-done | bytes 32800 | tf_op jit(solution)/shard_map/ppermute | solution.py:22
  71.2 1.0 collective-permute-done.18
  73.5 1.4 collective-permute-start.20
  74.9 1.2 collective-permute-start.21
  76.5 1.1 collective-permute-done.20
  77.6 2.1 %collective-permute-done.21 = bf16[64,256]{1,0:T(8,128)(2,1)S(1)} collective-permute-done((bf16[64,256]{1,0:T(8,128)(2,1)S(1)}, bf16[64,256]{1,0:T(8,128)(2,1)S(1)}, u32[]{:S(2)}, u32[]{:S(2)}) %collective-permute-start.21) | collective-permute-done | bytes 32800 | tf_op jit(solution)/shard_map/ppermute | solution.py:22
  79.7 3.0 %collective-permute-start.22 = (bf16[64,256]{1,0:T(8,128)(2,1)S(1)}, bf16[64,256]{1,0:T(8,128)(2,1)S(1)}, u32[]{:S(2)}, u32[]{:S(2)}) collective-permute-start(bf16[64,256]{1,0:T(8,128)(2,1)S(1)} %fusion.45), channel_id=1, source_target_pairs={{0,16},{4,20},{8,24},{12,28},{16,0},{20,4},{24,8},{28,12},{1,17},{... | collective-permute-start | bytes 98312 | tf_op jit(solution)/shard_map/ppermute | solution.py:22
  82.8 2.2 %collective-permute-done.22 = bf16[64,256]{1,0:T(8,128)(2,1)S(1)} collective-permute-done((bf16[64,256]{1,0:T(8,128)(2,1)S(1)}, bf16[64,256]{1,0:T(8,128)(2,1)S(1)}, u32[]{:S(2)}, u32[]{:S(2)}) %collective-permute-start.22) | collective-permute-done | bytes 32800 | tf_op jit(solution)/shard_map/ppermute | solution.py:22
  86.5 2.1 %collective-permute-start.25 = (bf16[64,256]{1,0:T(8,128)(2,1)S(1)}, bf16[64,256]{1,0:T(8,128)(2,1)S(1)}, u32[]{:S(2)}, u32[]{:S(2)}) collective-permute-start(bf16[64,256]{1,0:T(8,128)(2,1)S(1)} %add_convert_fusion.9), channel_id=1, source_target_pairs={{0,12},{4,8},{8,4},{12,0},{16,28},{20,24},{24,20},{28,16},{1,13},{... | collective-permute-start | bytes 98312 | tf_op jit(solution)/shard_map/ppermute | solution.py:22
  89.4 1.9 %collective-permute-done.25 = bf16[64,256]{1,0:T(8,128)(2,1)S(1)} collective-permute-done((bf16[64,256]{1,0:T(8,128)(2,1)S(1)}, bf16[64,256]{1,0:T(8,128)(2,1)S(1)}, u32[]{:S(2)}, u32[]{:S(2)}) %collective-permute-start.25) | collective-permute-done | bytes 32800 | tf_op jit(solution)/shard_map/ppermute | solution.py:22
  91.7 1.2 collective-permute-done.26
  93.5 3.4 %collective-permute-done.27 = bf16[64,256]{1,0:T(8,128)(2,1)S(1)} collective-permute-done((bf16[64,256]{1,0:T(8,128)(2,1)S(1)}, bf16[64,256]{1,0:T(8,128)(2,1)S(1)}, u32[]{:S(2)}, u32[]{:S(2)}) %collective-permute-start.27) | collective-permute-done | bytes 32800 | tf_op jit(solution)/shard_map/ppermute | solution.py:22
  97.0 1.2 collective-permute-done.28
  98.3 2.7 %collective-permute-start.29 = (bf16[64,256]{1,0:T(8,128)(2,1)S(1)}, bf16[64,256]{1,0:T(8,128)(2,1)S(1)}, u32[]{:S(2)}, u32[]{:S(2)}) collective-permute-start(bf16[64,256]{1,0:T(8,128)(2,1)S(1)} %get-tuple-element.37), channel_id=1, source_target_pairs={{0,16},{4,20},{8,24},{12,28},{16,0},{20,4},{24,8},{28,12},{1,17},{... | collective-permute-start | bytes 98312 | tf_op jit(solution)/shard_map/ppermute | solution.py:22
  100.9 2.2 %collective-permute-done.29 = bf16[64,256]{1,0:T(8,128)(2,1)S(1)} collective-permute-done((bf16[64,256]{1,0:T(8,128)(2,1)S(1)}, bf16[64,256]{1,0:T(8,128)(2,1)S(1)}, u32[]{:S(2)}, u32[]{:S(2)}) %collective-permute-start.29) | collective-permute-done | bytes 32800 | tf_op jit(solution)/shard_map/ppermute | solution.py:22
  103.2 1.0 collective-permute-start.30
  104.2 1.6 %collective-permute-start.31 = (bf16[64,512]{1,0:T(8,128)(2,1)S(1)}, bf16[64,512]{1,0:T(8,128)(2,1)S(1)}, u32[]{:S(2)}, u32[]{:S(2)}) collective-permute-start(bf16[64,512]{1,0:T(8,128)(2,1)S(1)} %pad_maximum_fusion.3.refs_0_), channel_id=1, source_target_pairs={{0,8},{4,12},{8,0},{12,4},{16,24},{20,28},{24,16},{28,20},{1,9},{5... | collective-permute-start | bytes 196616 | tf_op jit(solution)/shard_map/ppermute | solution.py:22
  107.4 1.0 collective-permute-done.31.refs_2_
  108.5 2.5 %collective-permute-done.32.refs_3_ = bf16[64,512]{1,0:T(8,128)(2,1)S(1)} collective-permute-done((bf16[64,512]{1,0:T(8,128)(2,1)S(1)}, bf16[64,512]{1,0:T(8,128)(2,1)S(1)}, u32[]{:S(2)}, u32[]{:S(2)}) %collective-permute-start.32) | collective-permute-done | bytes 65568 | tf_op jit(solution)/shard_map/ppermute | solution.py:22
  111.0 1.2 collective-permute-done.36.refs_7_
  112.3 2.0 %shard_map.167 = f32[64,1024]{1,0:T(8,128)S(1)} custom-call(bf16[64,512]{1,0:T(8,128)(2,1)S(1)} %pad_maximum_fusion.3.refs_0_, bf16[64,512]{1,0:T(8,128)(2,1)S(1)} %collective-permute-done.30.refs_1_, bf16[64,512]{1,0:T(8,128)(2,1)S(1)} %collective-permute-done.31.refs_2_, bf16[64,512]{1,0:T(8,128)(2,1)S(1)} %collective-permute-done.32.refs_3_, ...), custom_call_target="tpu_custom_call" | custom-call | flops 671088640 | bytes 18874368 | tf_op jit(solution)/shard_map/pallas_call | solution.py:104
  115.7 2.1 %collective-permute-start.39 = (bf16[64,1024]{1,0:T(8,128)(2,1)S(1)}, bf16[64,1024]{1,0:T(8,128)(2,1)S(1)}, u32[]{:S(2)}, u32[]{:S(2)}) collective-permute-start(bf16[64,1024]{1,0:T(8,128)(2,1)S(1)} %convert_element_type.225), channel_id=1, source_target_pairs={{0,12},{4,8},{8,4},{12,0},{16,28},{20,24},{24,20},{28,16},{1,13},{... | collective-permute-start | bytes 393224 | tf_op jit(solution)/shard_map/ppermute | solution.py:22
  117.8 2.1 %collective-permute-done.37 = bf16[64,1024]{1,0:T(8,128)(2,1)S(1)} collective-permute-done((bf16[64,1024]{1,0:T(8,128)(2,1)S(1)}, bf16[64,1024]{1,0:T(8,128)(2,1)S(1)}, u32[]{:S(2)}, u32[]{:S(2)}) %collective-permute-start.37) | collective-permute-done | bytes 131104 | tf_op jit(solution)/shard_map/ppermute | solution.py:22
  119.9 1.2 collective-permute-done.38
  121.1 2.8 %collective-permute-done.39 = bf16[64,1024]{1,0:T(8,128)(2,1)S(1)} collective-permute-done((bf16[64,1024]{1,0:T(8,128)(2,1)S(1)}, bf16[64,1024]{1,0:T(8,128)(2,1)S(1)}, u32[]{:S(2)}, u32[]{:S(2)}) %collective-permute-start.39) | collective-permute-done | bytes 131104 | tf_op jit(solution)/shard_map/ppermute | solution.py:22
  124.5 1.3 collective-permute-done.40
  126.5 3.8 %collective-permute-done.41 = bf16[64,512]{1,0:T(8,128)(2,1)S(1)} collective-permute-done((bf16[64,512]{1,0:T(8,128)(2,1)S(1)}, bf16[64,512]{1,0:T(8,128)(2,1)S(1)}, u32[]{:S(2)}, u32[]{:S(2)}) %collective-permute-start.41) | collective-permute-done | bytes 65568 | tf_op jit(solution)/shard_map/ppermute | solution.py:22
  130.3 1.3 collective-permute-done.42
  132.2 1.0 collective-permute-start.44
  133.2 2.1 %collective-permute-start.45 = (bf16[64,512]{1,0:T(8,128)(2,1)S(1)}, bf16[64,512]{1,0:T(8,128)(2,1)S(1)}, u32[]{:S(2)}, u32[]{:S(2)}) collective-permute-start(bf16[64,512]{1,0:T(8,128)(2,1)S(1)} %get-tuple-element.29.refs_0_), channel_id=1, source_target_pairs={{0,12},{4,8},{8,4},{12,0},{16,28},{20,24},{24,20},{28,16},{1,13},{... | collective-permute-start | bytes 196616 | tf_op jit(solution)/shard_map/ppermute | solution.py:22
  137.0 1.5 collective-permute-done.45.refs_3_
  138.5 4.0 %shard_map.168 = f32[64,1024]{1,0:T(8,128)S(1)} custom-call(bf16[64,512]{1,0:T(8,128)(2,1)S(1)} %pad_maximum_fusion.3.refs_0_, bf16[64,512]{1,0:T(8,128)(2,1)S(1)} %collective-permute-done.30.refs_1_, bf16[64,512]{1,0:T(8,128)(2,1)S(1)} %collective-permute-done.31.refs_2_, bf16[64,512]{1,0:T(8,128)(2,1)S(1)} %collective-permute-done.32.refs_3_, ...), custom_call_target="tpu_custom_call" | custom-call | flops 1342177280 | bytes 37748736 | tf_op jit(solution)/shard_map/pallas_call | solution.py:104
  142.6 4.0 %shard_map.169 = f32[64,1024]{1,0:T(8,128)S(1)} custom-call(bf16[64,512]{1,0:T(8,128)(2,1)S(1)} %get-tuple-element.29.refs_0_, bf16[64,512]{1,0:T(8,128)(2,1)S(1)} %collective-permute-done.43.refs_1_, bf16[64,512]{1,0:T(8,128)(2,1)S(1)} %collective-permute-done.44.refs_2_, bf16[64,512]{1,0:T(8,128)(2,1)S(1)} %collective-permute-done.45.refs_3_, ...), custom_call_target="tpu_custom_call" | custom-call | flops 1342177280 | bytes 37748736 | tf_op jit(solution)/shard_map/pallas_call | solution.py:104
  147.5 5.1 %collective-permute-done.50 = bf16[64,1024]{1,0:T(8,128)(2,1)S(1)} collective-permute-done((bf16[64,1024]{1,0:T(8,128)(2,1)S(1)}, bf16[64,1024]{1,0:T(8,128)(2,1)S(1)}, u32[]{:S(2)}, u32[]{:S(2)}) %collective-permute-start.50) | collective-permute-done | bytes 131104 | tf_op jit(solution)/shard_map/ppermute | solution.py:22
  153.6 1.5 collective-permute-done.51
  155.7 5.0 %collective-permute-done.52 = bf16[64,1024]{1,0:T(8,128)(2,1)S(1)} collective-permute-done((bf16[64,1024]{1,0:T(8,128)(2,1)S(1)}, bf16[64,1024]{1,0:T(8,128)(2,1)S(1)}, u32[]{:S(2)}, u32[]{:S(2)}) %collective-permute-start.52) | collective-permute-done | bytes 131104 | tf_op jit(solution)/shard_map/ppermute | solution.py:22
  (145 shorter events, 27.3 us)
Async XLA Ops:
  0.6 34.0 %copy-start = (bf16[1024,1024]{1,0:T(8,128)(2,1)S(1)}, bf16[1024,1024]{1,0:T(8,128)(2,1)}, u32[]{:S(2)}) copy-start(bf16[1024,1024]{1,0:T(8,128)(2,1)} %param.19) | copy-start | bytes 6291460
  4.0 6.5 %collective-permute-start = (bf16[64,1024]{1,0:T(8,128)(2,1)S(1)}, bf16[64,1024]{1,0:T(8,128)(2,1)S(1)}, u32[]{:S(2)}, u32[]{:S(2)}) collective-permute-start(bf16[64,1024]{1,0:T(8,128)(2,1)S(1)} %convolution_convert_fusion), channel_id=1, source_target_pairs={{0,4},{4,0},{8,12},{12,8},{16,20},{20,16},{24,28},{28,24},{1,5},{5... | collective-permute-start | bytes 393224 | tf_op jit(solution)/shard_map/ppermute | solution.py:22
  13.6 1.6 collective-permute-start.1
  15.3 5.6 %collective-permute-start.2 = (bf16[64,1024]{1,0:T(8,128)(2,1)S(1)}, bf16[64,1024]{1,0:T(8,128)(2,1)S(1)}, u32[]{:S(2)}, u32[]{:S(2)}) collective-permute-start(bf16[64,1024]{1,0:T(8,128)(2,1)S(1)} %add_convert_fusion.3), channel_id=1, source_target_pairs={{0,2},{1,3},{2,0},{3,1},{4,6},{5,7},{6,4},{7,5},{8,10},{9,11},{10,... | collective-permute-start | bytes 393224 | tf_op jit(solution)/shard_map/ppermute | solution.py:22
  22.6 2.0 %collective-permute-start.3 = (f32[64,2048]{1,0:T(8,128)S(1)}, f32[64,2048]{1,0:T(8,128)S(1)}, u32[]{:S(2)}, u32[]{:S(2)}) collective-permute-start(f32[64,2048]{1,0:T(8,128)S(1)} %slice.151), channel_id=1, source_target_pairs={{0,1},{1,0},{2,3},{3,2},{4,5},{5,4},{6,7},{7,6},{8,9},{9,8},{10,11... | collective-permute-start | bytes 1572872 | tf_op jit(solution)/shard_map/ppermute | solution.py:22
  24.7 4.3 %collective-permute-start.4 = (bf16[64,512]{1,0:T(8,128)(2,1)S(1)}, bf16[64,512]{1,0:T(8,128)(2,1)S(1)}, u32[]{:S(2)}, u32[]{:S(2)}) collective-permute-start(bf16[64,512]{1,0:T(8,128)(2,1)S(1)} %get-tuple-element.26), channel_id=1, source_target_pairs={{0,4},{4,0},{8,12},{12,8},{16,20},{20,16},{24,28},{28,24},{1,5},{5... | collective-permute-start | bytes 196616 | tf_op jit(solution)/shard_map/ppermute | solution.py:22
  26.4 4.8 %collective-permute-start.5 = (bf16[64,512]{1,0:T(8,128)(2,1)S(1)}, bf16[64,512]{1,0:T(8,128)(2,1)S(1)}, u32[]{:S(2)}, u32[]{:S(2)}) collective-permute-start(bf16[64,512]{1,0:T(8,128)(2,1)S(1)} %get-tuple-element.28), channel_id=1, source_target_pairs={{0,8},{4,12},{8,0},{12,4},{16,24},{20,28},{24,16},{28,20},{1,9},{5... | collective-permute-start | bytes 196616 | tf_op jit(solution)/shard_map/ppermute | solution.py:22
  28.0 5.2 %collective-permute-start.6 = (bf16[64,512]{1,0:T(8,128)(2,1)S(1)}, bf16[64,512]{1,0:T(8,128)(2,1)S(1)}, u32[]{:S(2)}, u32[]{:S(2)}) collective-permute-start(bf16[64,512]{1,0:T(8,128)(2,1)S(1)} %get-tuple-element.27), channel_id=1, source_target_pairs={{0,12},{4,8},{8,4},{12,0},{16,28},{20,24},{24,20},{28,16},{1,13},{... | collective-permute-start | bytes 196616 | tf_op jit(solution)/shard_map/ppermute | solution.py:22
  33.2 1.3 collective-permute-start.7
  35.1 7.4 %collective-permute-start.10 = (bf16[64,1024]{1,0:T(8,128)(2,1)S(1)}, bf16[64,1024]{1,0:T(8,128)(2,1)S(1)}, u32[]{:S(2)}, u32[]{:S(2)}) collective-permute-start(bf16[64,1024]{1,0:T(8,128)(2,1)S(1)} %convolution_convert_fusion.1), channel_id=1, source_target_pairs={{0,12},{4,8},{8,4},{12,0},{16,28},{20,24},{24,20},{28,16},{1,13},{... | collective-permute-start | bytes 393224 | tf_op jit(solution)/shard_map/ppermute | solution.py:22
  36.1 8.1 %collective-permute-start.8 = (bf16[64,1024]{1,0:T(8,128)(2,1)S(1)}, bf16[64,1024]{1,0:T(8,128)(2,1)S(1)}, u32[]{:S(2)}, u32[]{:S(2)}) collective-permute-start(bf16[64,1024]{1,0:T(8,128)(2,1)S(1)} %convolution_convert_fusion.1), channel_id=1, source_target_pairs={{0,4},{4,0},{8,12},{12,8},{16,20},{20,16},{24,28},{28,24},{1,5},{5... | collective-permute-start | bytes 393224 | tf_op jit(solution)/shard_map/ppermute | solution.py:22
  37.1 7.2 %collective-permute-start.9 = (bf16[64,1024]{1,0:T(8,128)(2,1)S(1)}, bf16[64,1024]{1,0:T(8,128)(2,1)S(1)}, u32[]{:S(2)}, u32[]{:S(2)}) collective-permute-start(bf16[64,1024]{1,0:T(8,128)(2,1)S(1)} %convolution_convert_fusion.1), channel_id=1, source_target_pairs={{0,8},{4,12},{8,0},{12,4},{16,24},{20,28},{24,16},{28,20},{1,9},{5... | collective-permute-start | bytes 393224 | tf_op jit(solution)/shard_map/ppermute | solution.py:22
  46.4 1.4 collective-permute-start.11
  47.9 6.3 %collective-permute-start.12 = (bf16[64,512]{1,0:T(8,128)(2,1)S(1)}, bf16[64,512]{1,0:T(8,128)(2,1)S(1)}, u32[]{:S(2)}, u32[]{:S(2)}) collective-permute-start(bf16[64,512]{1,0:T(8,128)(2,1)S(1)} %add_convert_fusion.6), channel_id=1, source_target_pairs={{0,2},{1,3},{2,0},{3,1},{4,6},{5,7},{6,4},{7,5},{8,10},{9,11},{10,... | collective-permute-start | bytes 196616 | tf_op jit(solution)/shard_map/ppermute | solution.py:22
  55.2 2.0 %collective-permute-start.13 = (f32[64,2048]{1,0:T(8,128)S(1)}, f32[64,2048]{1,0:T(8,128)S(1)}, u32[]{:S(2)}, u32[]{:S(2)}) collective-permute-start(f32[64,2048]{1,0:T(8,128)S(1)} %slice.159), channel_id=1, source_target_pairs={{0,1},{1,0},{2,3},{3,2},{4,5},{5,4},{6,7},{7,6},{8,9},{9,8},{10,11... | collective-permute-start | bytes 1572872 | tf_op jit(solution)/shard_map/ppermute | solution.py:22
  57.2 4.3 %collective-permute-start.14 = (bf16[64,512]{1,0:T(8,128)(2,1)S(1)}, bf16[64,512]{1,0:T(8,128)(2,1)S(1)}, u32[]{:S(2)}, u32[]{:S(2)}) collective-permute-start(bf16[64,512]{1,0:T(8,128)(2,1)S(1)} %get-tuple-element.23), channel_id=1, source_target_pairs={{0,4},{4,0},{8,12},{12,8},{16,20},{20,16},{24,28},{28,24},{1,5},{5... | collective-permute-start | bytes 196616 | tf_op jit(solution)/shard_map/ppermute | solution.py:22
  58.1 4.9 %collective-permute-start.15 = (bf16[64,512]{1,0:T(8,128)(2,1)S(1)}, bf16[64,512]{1,0:T(8,128)(2,1)S(1)}, u32[]{:S(2)}, u32[]{:S(2)}) collective-permute-start(bf16[64,512]{1,0:T(8,128)(2,1)S(1)} %get-tuple-element.25), channel_id=1, source_target_pairs={{0,8},{4,12},{8,0},{12,4},{16,24},{20,28},{24,16},{28,20},{1,9},{5... | collective-permute-start | bytes 196616 | tf_op jit(solution)/shard_map/ppermute | solution.py:22
  59.1 5.2 %collective-permute-start.16 = (bf16[64,512]{1,0:T(8,128)(2,1)S(1)}, bf16[64,512]{1,0:T(8,128)(2,1)S(1)}, u32[]{:S(2)}, u32[]{:S(2)}) collective-permute-start(bf16[64,512]{1,0:T(8,128)(2,1)S(1)} %get-tuple-element.24), channel_id=1, source_target_pairs={{0,12},{4,8},{8,4},{12,0},{16,28},{20,24},{24,20},{28,16},{1,13},{... | collective-permute-start | bytes 196616 | tf_op jit(solution)/shard_map/ppermute | solution.py:22
  64.9 5.1 %collective-permute-start.17 = (bf16[64,256]{1,0:T(8,128)(2,1)}, bf16[64,256]{1,0:T(8,128)(2,1)}, u32[]{:S(2)}, u32[]{:S(2)}) collective-permute-start(bf16[64,256]{1,0:T(8,128)(2,1)} %slice.229), channel_id=1, source_target_pairs={{0,16},{4,20},{8,24},{12,28},{16,0},{20,4},{24,8},{28,12},{1,17},{... | collective-permute-start | bytes 98312 | tf_op jit(solution)/shard_map/ppermute | solution.py:22
  67.5 21.1 %copy-start.6 = (bf16[1024,512]{1,0:T(8,128)(2,1)S(1)}, bf16[1024,512]{1,0:T(8,128)(2,1)}, u32[]{:S(2)}) copy-start(bf16[1024,512]{1,0:T(8,128)(2,1)} %param.25) | copy-start | bytes 3145732
  70.9 1.3 collective-permute-start.18
  72.5 39.7 %copy-start.2 = (bf16[1024,1024]{1,0:T(8,128)(2,1)S(1)}, bf16[1024,1024]{1,0:T(8,128)(2,1)}, u32[]{:S(2)}) copy-start(bf16[1024,1024]{1,0:T(8,128)(2,1)} %refs_9_.3) | copy-start | bytes 6291460
  72.5 4.0 %collective-permute-start.19 = (bf16[64,256]{1,0:T(8,128)(2,1)S(1)}, bf16[64,256]{1,0:T(8,128)(2,1)S(1)}, u32[]{:S(2)}, u32[]{:S(2)}) collective-permute-start(bf16[64,256]{1,0:T(8,128)(2,1)S(1)} %get-tuple-element.32), channel_id=1, source_target_pairs={{0,4},{4,0},{8,12},{12,8},{16,20},{20,16},{24,28},{28,24},{1,5},{5... | collective-permute-start | bytes 98312 | tf_op jit(solution)/shard_map/ppermute | solution.py:22
  73.5 4.1 %collective-permute-start.20 = (bf16[64,256]{1,0:T(8,128)(2,1)S(1)}, bf16[64,256]{1,0:T(8,128)(2,1)S(1)}, u32[]{:S(2)}, u32[]{:S(2)}) collective-permute-start(bf16[64,256]{1,0:T(8,128)(2,1)S(1)} %get-tuple-element.34), channel_id=1, source_target_pairs={{0,8},{4,12},{8,0},{12,4},{16,24},{20,28},{24,16},{28,20},{1,9},{5... | collective-permute-start | bytes 98312 | tf_op jit(solution)/shard_map/ppermute | solution.py:22
  74.9 4.8 %collective-permute-start.21 = (bf16[64,256]{1,0:T(8,128)(2,1)S(1)}, bf16[64,256]{1,0:T(8,128)(2,1)S(1)}, u32[]{:S(2)}, u32[]{:S(2)}) collective-permute-start(bf16[64,256]{1,0:T(8,128)(2,1)S(1)} %get-tuple-element.33), channel_id=1, source_target_pairs={{0,12},{4,8},{8,4},{12,0},{16,28},{20,24},{24,20},{28,16},{1,13},{... | collective-permute-start | bytes 98312 | tf_op jit(solution)/shard_map/ppermute | solution.py:22
  79.7 5.3 %collective-permute-start.22 = (bf16[64,256]{1,0:T(8,128)(2,1)S(1)}, bf16[64,256]{1,0:T(8,128)(2,1)S(1)}, u32[]{:S(2)}, u32[]{:S(2)}) collective-permute-start(bf16[64,256]{1,0:T(8,128)(2,1)S(1)} %fusion.45), channel_id=1, source_target_pairs={{0,16},{4,20},{8,24},{12,28},{16,0},{20,4},{24,8},{28,12},{1,17},{... | collective-permute-start | bytes 98312 | tf_op jit(solution)/shard_map/ppermute | solution.py:22
  85.0 4.0 %collective-permute-start.23 = (bf16[64,256]{1,0:T(8,128)(2,1)S(1)}, bf16[64,256]{1,0:T(8,128)(2,1)S(1)}, u32[]{:S(2)}, u32[]{:S(2)}) collective-permute-start(bf16[64,256]{1,0:T(8,128)(2,1)S(1)} %add_convert_fusion.9), channel_id=1, source_target_pairs={{0,4},{4,0},{8,12},{12,8},{16,20},{20,16},{24,28},{28,24},{1,5},{5... | collective-permute-start | bytes 98312 | tf_op jit(solution)/shard_map/ppermute | solution.py:22
  85.5 3.9 %collective-permute-start.24 = (bf16[64,256]{1,0:T(8,128)(2,1)S(1)}, bf16[64,256]{1,0:T(8,128)(2,1)S(1)}, u32[]{:S(2)}, u32[]{:S(2)}) collective-permute-start(bf16[64,256]{1,0:T(8,128)(2,1)S(1)} %add_convert_fusion.9), channel_id=1, source_target_pairs={{0,8},{4,12},{8,0},{12,4},{16,24},{20,28},{24,16},{28,20},{1,9},{5... | collective-permute-start | bytes 98312 | tf_op jit(solution)/shard_map/ppermute | solution.py:22
  86.5 4.8 %collective-permute-start.25 = (bf16[64,256]{1,0:T(8,128)(2,1)S(1)}, bf16[64,256]{1,0:T(8,128)(2,1)S(1)}, u32[]{:S(2)}, u32[]{:S(2)}) collective-permute-start(bf16[64,256]{1,0:T(8,128)(2,1)S(1)} %add_convert_fusion.9), channel_id=1, source_target_pairs={{0,12},{4,8},{8,4},{12,0},{16,28},{20,24},{24,20},{28,16},{1,13},{... | collective-permute-start | bytes 98312 | tf_op jit(solution)/shard_map/ppermute | solution.py:22
  91.3 32.6 %copy-start.4 = (bf16[1024,1024]{1,0:T(8,128)(2,1)S(1)}, bf16[1024,1024]{1,0:T(8,128)(2,1)}, u32[]{:S(2)}) copy-start(bf16[1024,1024]{1,0:T(8,128)(2,1)} %param.26) | copy-start | bytes 6291460
  91.3 32.6 %copy-start.10 = (bf16[64,1024]{1,0:T(8,128)(2,1)S(1)}, bf16[64,1024]{1,0:T(8,128)(2,1)}, u32[]{:S(2)}) copy-start(bf16[64,1024]{1,0:T(8,128)(2,1)} %copy-done.9) | copy-start | bytes 393220
  91.3 32.6 %copy-start.12 = (bf16[64,1024]{1,0:T(8,128)(2,1)S(1)}, bf16[64,1024]{1,0:T(8,128)(2,1)}, u32[]{:S(2)}) copy-start(bf16[64,1024]{1,0:T(8,128)(2,1)} %copy-done.11) | copy-start | bytes 393220
  91.3 32.6 %copy-start.14 = (bf16[64,1024]{1,0:T(8,128)(2,1)S(1)}, bf16[64,1024]{1,0:T(8,128)(2,1)}, u32[]{:S(2)}) copy-start(bf16[64,1024]{1,0:T(8,128)(2,1)} %copy-done.13) | copy-start | bytes 393220
  91.6 1.3 collective-permute-start.26
  92.9 4.0 %collective-permute-start.27 = (bf16[64,256]{1,0:T(8,128)(2,1)S(1)}, bf16[64,256]{1,0:T(8,128)(2,1)S(1)}, u32[]{:S(2)}, u32[]{:S(2)}) collective-permute-start(bf16[64,256]{1,0:T(8,128)(2,1)S(1)} %add_convert_fusion.8), channel_id=1, source_target_pairs={{0,2},{1,3},{2,0},{3,1},{4,6},{5,7},{6,4},{7,5},{8,10},{9,11},{10,... | collective-permute-start | bytes 98312 | tf_op jit(solution)/shard_map/ppermute | solution.py:22
  96.9 1.3 collective-permute-start.28
  98.3 4.9 %collective-permute-start.29 = (bf16[64,256]{1,0:T(8,128)(2,1)S(1)}, bf16[64,256]{1,0:T(8,128)(2,1)S(1)}, u32[]{:S(2)}, u32[]{:S(2)}) collective-permute-start(bf16[64,256]{1,0:T(8,128)(2,1)S(1)} %get-tuple-element.37), channel_id=1, source_target_pairs={{0,16},{4,20},{8,24},{12,28},{16,0},{20,4},{24,8},{28,12},{1,17},{... | collective-permute-start | bytes 98312 | tf_op jit(solution)/shard_map/ppermute | solution.py:22
  103.2 4.3 %collective-permute-start.30 = (bf16[64,512]{1,0:T(8,128)(2,1)S(1)}, bf16[64,512]{1,0:T(8,128)(2,1)S(1)}, u32[]{:S(2)}, u32[]{:S(2)}) collective-permute-start(bf16[64,512]{1,0:T(8,128)(2,1)S(1)} %pad_maximum_fusion.3.refs_0_), channel_id=1, source_target_pairs={{0,4},{4,0},{8,12},{12,8},{16,20},{20,16},{24,28},{28,24},{1,5},{5... | collective-permute-start | bytes 196616 | tf_op jit(solution)/shard_map/ppermute | solution.py:22
  104.2 4.3 %collective-permute-start.31 = (bf16[64,512]{1,0:T(8,128)(2,1)S(1)}, bf16[64,512]{1,0:T(8,128)(2,1)S(1)}, u32[]{:S(2)}, u32[]{:S(2)}) collective-permute-start(bf16[64,512]{1,0:T(8,128)(2,1)S(1)} %pad_maximum_fusion.3.refs_0_), channel_id=1, source_target_pairs={{0,8},{4,12},{8,0},{12,4},{16,24},{20,28},{24,16},{28,20},{1,9},{5... | collective-permute-start | bytes 196616 | tf_op jit(solution)/shard_map/ppermute | solution.py:22
  105.8 5.2 %collective-permute-start.32 = (bf16[64,512]{1,0:T(8,128)(2,1)S(1)}, bf16[64,512]{1,0:T(8,128)(2,1)S(1)}, u32[]{:S(2)}, u32[]{:S(2)}) collective-permute-start(bf16[64,512]{1,0:T(8,128)(2,1)S(1)} %pad_maximum_fusion.3.refs_0_), channel_id=1, source_target_pairs={{0,12},{4,8},{8,4},{12,0},{16,28},{20,24},{24,20},{28,16},{1,13},{... | collective-permute-start | bytes 196616 | tf_op jit(solution)/shard_map/ppermute | solution.py:22
  106.6 4.4 %collective-permute-start.33 = (bf16[64,512]{1,0:T(8,128)(2,1)S(1)}, bf16[64,512]{1,0:T(8,128)(2,1)S(1)}, u32[]{:S(2)}, u32[]{:S(2)}) collective-permute-start(bf16[64,512]{1,0:T(8,128)(2,1)S(1)} %pad_maximum_fusion.3.refs_0_), channel_id=1, source_target_pairs={{0,1},{1,0},{2,3},{3,2},{4,5},{5,4},{6,7},{7,6},{8,9},{9,8},{10,11... | collective-permute-start | bytes 196616 | tf_op jit(solution)/shard_map/ppermute | solution.py:22
  107.4 3.6 %collective-permute-start.34 = (bf16[64,512]{1,0:T(8,128)(2,1)S(1)}, bf16[64,512]{1,0:T(8,128)(2,1)S(1)}, u32[]{:S(2)}, u32[]{:S(2)}) collective-permute-start(bf16[64,512]{1,0:T(8,128)(2,1)S(1)} %collective-permute-done.30.refs_1_), channel_id=1, source_target_pairs={{0,1},{1,0},{2,3},{3,2},{4,5},{5,4},{6,7},{7,6},{8,9},{9,8},{10,11... | collective-permute-start | bytes 196616 | tf_op jit(solution)/shard_map/ppermute | solution.py:22
  108.5 2.6 %collective-permute-start.35 = (bf16[64,512]{1,0:T(8,128)(2,1)S(1)}, bf16[64,512]{1,0:T(8,128)(2,1)S(1)}, u32[]{:S(2)}, u32[]{:S(2)}) collective-permute-start(bf16[64,512]{1,0:T(8,128)(2,1)S(1)} %collective-permute-done.31.refs_2_), channel_id=1, source_target_pairs={{0,1},{1,0},{2,3},{3,2},{4,5},{5,4},{6,7},{7,6},{8,9},{9,8},{10,11... | collective-permute-start | bytes 196616 | tf_op jit(solution)/shard_map/ppermute | solution.py:22
  111.0 1.3 collective-permute-start.36
  112.2 23.0 %copy-start.17 = (s32[1,2048]{1,0:T(1,128)S(1)}, s32[1,2048]{1,0:T(1,128)}, u32[]{:S(2)}) copy-start(s32[1,2048]{1,0:T(1,128)} %copy-done.16) | copy-start | bytes 24580
  112.3 26.3 %copy-start.1 = (bf16[2048,1024]{1,0:T(8,128)(2,1)S(1)}, bf16[2048,1024]{1,0:T(8,128)(2,1)}, u32[]{:S(2)}) copy-start(bf16[2048,1024]{1,0:T(8,128)(2,1)} %refs_9_.5) | copy-start | bytes 12582916
  114.2 5.6 %collective-permute-start.37 = (bf16[64,1024]{1,0:T(8,128)(2,1)S(1)}, bf16[64,1024]{1,0:T(8,128)(2,1)S(1)}, u32[]{:S(2)}, u32[]{:S(2)}) collective-permute-start(bf16[64,1024]{1,0:T(8,128)(2,1)S(1)} %convert_element_type.225), channel_id=1, source_target_pairs={{0,4},{4,0},{8,12},{12,8},{16,20},{20,16},{24,28},{28,24},{1,5},{5... | collective-permute-start | bytes 393224 | tf_op jit(solution)/shard_map/ppermute | solution.py:22
  114.7 6.4 %collective-permute-start.38 = (bf16[64,1024]{1,0:T(8,128)(2,1)S(1)}, bf16[64,1024]{1,0:T(8,128)(2,1)S(1)}, u32[]{:S(2)}, u32[]{:S(2)}) collective-permute-start(bf16[64,1024]{1,0:T(8,128)(2,1)S(1)} %convert_element_type.225), channel_id=1, source_target_pairs={{0,8},{4,12},{8,0},{12,4},{16,24},{20,28},{24,16},{28,20},{1,9},{5... | collective-permute-start | bytes 393224 | tf_op jit(solution)/shard_map/ppermute | solution.py:22
  115.7 8.2 %collective-permute-start.39 = (bf16[64,1024]{1,0:T(8,128)(2,1)S(1)}, bf16[64,1024]{1,0:T(8,128)(2,1)S(1)}, u32[]{:S(2)}, u32[]{:S(2)}) collective-permute-start(bf16[64,1024]{1,0:T(8,128)(2,1)S(1)} %convert_element_type.225), channel_id=1, source_target_pairs={{0,12},{4,8},{8,4},{12,0},{16,28},{20,24},{24,20},{28,16},{1,13},{... | collective-permute-start | bytes 393224 | tf_op jit(solution)/shard_map/ppermute | solution.py:22
  124.5 1.4 collective-permute-start.40
  125.9 4.3 %collective-permute-start.41 = (bf16[64,512]{1,0:T(8,128)(2,1)S(1)}, bf16[64,512]{1,0:T(8,128)(2,1)S(1)}, u32[]{:S(2)}, u32[]{:S(2)}) collective-permute-start(bf16[64,512]{1,0:T(8,128)(2,1)S(1)} %add_convert_fusion.4), channel_id=1, source_target_pairs={{0,2},{1,3},{2,0},{3,1},{4,6},{5,7},{6,4},{7,5},{8,10},{9,11},{10,... | collective-permute-start | bytes 196616 | tf_op jit(solution)/shard_map/ppermute | solution.py:22
  130.3 1.4 collective-permute-start.42
  131.7 4.3 %collective-permute-start.43 = (bf16[64,512]{1,0:T(8,128)(2,1)S(1)}, bf16[64,512]{1,0:T(8,128)(2,1)S(1)}, u32[]{:S(2)}, u32[]{:S(2)}) collective-permute-start(bf16[64,512]{1,0:T(8,128)(2,1)S(1)} %get-tuple-element.29.refs_0_), channel_id=1, source_target_pairs={{0,4},{4,0},{8,12},{12,8},{16,20},{20,16},{24,28},{28,24},{1,5},{5... | collective-permute-start | bytes 196616 | tf_op jit(solution)/shard_map/ppermute | solution.py:22
  132.2 4.9 %collective-permute-start.44 = (bf16[64,512]{1,0:T(8,128)(2,1)S(1)}, bf16[64,512]{1,0:T(8,128)(2,1)S(1)}, u32[]{:S(2)}, u32[]{:S(2)}) collective-permute-start(bf16[64,512]{1,0:T(8,128)(2,1)S(1)} %get-tuple-element.29.refs_0_), channel_id=1, source_target_pairs={{0,8},{4,12},{8,0},{12,4},{16,24},{20,28},{24,16},{28,20},{1,9},{5... | collective-permute-start | bytes 196616 | tf_op jit(solution)/shard_map/ppermute | solution.py:22
  133.2 5.3 %collective-permute-start.45 = (bf16[64,512]{1,0:T(8,128)(2,1)S(1)}, bf16[64,512]{1,0:T(8,128)(2,1)S(1)}, u32[]{:S(2)}, u32[]{:S(2)}) collective-permute-start(bf16[64,512]{1,0:T(8,128)(2,1)S(1)} %get-tuple-element.29.refs_0_), channel_id=1, source_target_pairs={{0,12},{4,8},{8,4},{12,0},{16,28},{20,24},{24,20},{28,16},{1,13},{... | collective-permute-start | bytes 196616 | tf_op jit(solution)/shard_map/ppermute | solution.py:22
  135.4 17.2 %copy-start.3 = (bf16[1024,2048]{1,0:T(8,128)(2,1)S(1)}, bf16[1024,2048]{1,0:T(8,128)(2,1)}, u32[]{:S(2)}) copy-start(bf16[1024,2048]{1,0:T(8,128)(2,1)} %param.27) | copy-start | bytes 12582916
  135.4 7.1 %collective-permute-start.46 = (bf16[64,512]{1,0:T(8,128)(2,1)S(1)}, bf16[64,512]{1,0:T(8,128)(2,1)S(1)}, u32[]{:S(2)}, u32[]{:S(2)}) collective-permute-start(bf16[64,512]{1,0:T(8,128)(2,1)S(1)} %get-tuple-element.29.refs_0_), channel_id=1, source_target_pairs={{0,1},{1,0},{2,3},{3,2},{4,5},{5,4},{6,7},{7,6},{8,9},{9,8},{10,11... | collective-permute-start | bytes 196616 | tf_op jit(solution)/shard_map/ppermute | solution.py:22
  136.1 6.5 %collective-permute-start.47 = (bf16[64,512]{1,0:T(8,128)(2,1)S(1)}, bf16[64,512]{1,0:T(8,128)(2,1)S(1)}, u32[]{:S(2)}, u32[]{:S(2)}) collective-permute-start(bf16[64,512]{1,0:T(8,128)(2,1)S(1)} %collective-permute-done.43.refs_1_), channel_id=1, source_target_pairs={{0,1},{1,0},{2,3},{3,2},{4,5},{5,4},{6,7},{7,6},{8,9},{9,8},{10,11... | collective-permute-start | bytes 196616 | tf_op jit(solution)/shard_map/ppermute | solution.py:22
  137.0 5.5 %collective-permute-start.48 = (bf16[64,512]{1,0:T(8,128)(2,1)S(1)}, bf16[64,512]{1,0:T(8,128)(2,1)S(1)}, u32[]{:S(2)}, u32[]{:S(2)}) collective-permute-start(bf16[64,512]{1,0:T(8,128)(2,1)S(1)} %collective-permute-done.44.refs_2_), channel_id=1, source_target_pairs={{0,1},{1,0},{2,3},{3,2},{4,5},{5,4},{6,7},{7,6},{8,9},{9,8},{10,11... | collective-permute-start | bytes 196616 | tf_op jit(solution)/shard_map/ppermute | solution.py:22
  138.5 4.0 %collective-permute-start.49 = (bf16[64,512]{1,0:T(8,128)(2,1)S(1)}, bf16[64,512]{1,0:T(8,128)(2,1)S(1)}, u32[]{:S(2)}, u32[]{:S(2)}) collective-permute-start(bf16[64,512]{1,0:T(8,128)(2,1)S(1)} %collective-permute-done.45.refs_3_), channel_id=1, source_target_pairs={{0,1},{1,0},{2,3},{3,2},{4,5},{5,4},{6,7},{7,6},{8,9},{9,8},{10,11... | collective-permute-start | bytes 196616 | tf_op jit(solution)/shard_map/ppermute | solution.py:22
  146.6 6.0 %collective-permute-start.50 = (bf16[64,1024]{1,0:T(8,128)(2,1)S(1)}, bf16[64,1024]{1,0:T(8,128)(2,1)S(1)}, u32[]{:S(2)}, u32[]{:S(2)}) collective-permute-start(bf16[64,1024]{1,0:T(8,128)(2,1)S(1)} %add_convert_fusion.1), channel_id=1, source_target_pairs={{0,4},{4,0},{8,12},{12,8},{16,20},{20,16},{24,28},{28,24},{1,5},{5... | collective-permute-start | bytes 393224 | tf_op jit(solution)/shard_map/ppermute | solution.py:22
  153.5 1.6 collective-permute-start.51
  155.1 5.6 %collective-permute-start.52 = (bf16[64,1024]{1,0:T(8,128)(2,1)S(1)}, bf16[64,1024]{1,0:T(8,128)(2,1)S(1)}, u32[]{:S(2)}, u32[]{:S(2)}) collective-permute-start(bf16[64,1024]{1,0:T(8,128)(2,1)S(1)} %add_convert_fusion), channel_id=1, source_target_pairs={{0,2},{1,3},{2,0},{3,1},{4,6},{5,7},{6,4},{7,5},{8,10},{9,11},{10,... | collective-permute-start | bytes 393224 | tf_op jit(solution)/shard_map/ppermute | solution.py:22
  160.8 1.6 collective-permute-start.53
  (8 other events, 89.3 us)

commit v3 on v2

--- a/solution.py
+++ b/solution.py
@@ -1,3 +1,5 @@
+import functools
+
 import jax
 import jax.numpy as jnp
 from jax import lax
@@ -61,9 +63,8 @@
     return place
 
 
-def one_hot_rows(place, width):
-    hot = place[:, None] == lax.broadcasted_iota(jnp.int32, (place.shape[0], width), 1)
-    return lax.optimization_barrier(hot.astype(BF16))
+def tied(*values):
+    return lax.optimization_barrier(values)
 
 
 TILE = 256
@@ -115,28 +116,54 @@
     )(*pieces, place[None, :], block)
 
 
-def put_kernel(update_ref, place_ref, out_ref):
+def put_kernel(update_ref, place_ref, out_ref, *, first):
     update, place = update_ref[...], place_ref[...]
-    step = out_ref.shape[1]
-    base = pl.program_id(0) * step
-    tile = min(TILE, step)
-    for n in range(0, step, tile):
-        hot = hot_tile(place, base + n, tile)
-        out_ref[:, n : n + tile] = lax.dot_general(update, hot, (((1,), (1,)), ((), ())), preferred_element_type=F32)
-
-
-def put_columns(update, place, width):
+    width = out_ref.shape[1]
+    tile = min(TILE, width)
+    for n in range(0, width, tile):
+        hot = hot_tile(place, first + n, tile)
+        total = lax.dot_general(update, hot, (((1,), (1,)), ((), ())), preferred_element_type=F32)
+        out_ref[:, n : n + tile] = total.astype(out_ref.dtype)
+
+
+def put_columns(update, place, first, width, dtype):
     rows, count = update.shape
-    step = min(width, 2048)
     return pl.pallas_call(
-        put_kernel,
-        grid=(width // step,),
-        in_specs=[pl.BlockSpec((rows, count), lambda i: (0, 0)), pl.BlockSpec((1, count), lambda i: (0, 0))],
-        out_specs=pl.BlockSpec((rows, step), lambda i: (0, i)),
-        out_shape=jax.ShapeDtypeStruct((rows, width), F32),
+        functools.partial(put_kernel, first=first),
+        out_shape=jax.ShapeDtypeStruct((rows, width), dtype),
         compiler_params=pltpu.CompilerParams(vmem_limit_bytes=16 << 20),
-        cost_estimate=pl.CostEstimate(flops=2 * rows * count * width, bytes_accessed=4 * count * width, transcendentals=0),
-    )(update, place[None, :])
+        cost_estimate=pl.CostEstimate(flops=2 * rows * count * width, bytes_accessed=4 * rows * width, transcendentals=0),
+    )(update, place)
+
+
+def join_kernel(core_ref, own_ref, other_ref, out_ref):
+    mine = pl.program_id(0) == core_ref[0]
+
+    @pl.when(mine)
+    def _():
+        out_ref[...] = own_ref[...]
+
+    @pl.when(jnp.logical_not(mine))
+    def _():
+        out_ref[...] = other_ref[...]
+
+
+def join(own, other, core):
+    rows, width = own.shape
+    if width % 128:
+        return jnp.concatenate([jnp.where(core == 0, own, other), jnp.where(core == 0, other, own)], axis=1)
+    return pl.pallas_call(
+        join_kernel,
+        grid_spec=pltpu.PrefetchScalarGridSpec(
+            num_scalar_prefetch=1,
+            grid=(2,),
+            in_specs=[pl.BlockSpec((rows, width), lambda i, core: (0, 0))] * 2,
+            out_specs=pl.BlockSpec((rows, width), lambda i, core: (0, i)),
+        ),
+        out_shape=jax.ShapeDtypeStruct((rows, 2 * width), own.dtype),
+        compiler_params=pltpu.CompilerParams(vmem_limit_bytes=16 << 20),
+        cost_estimate=pl.CostEstimate(flops=0, bytes_accessed=4 * own.size * own.dtype.itemsize, transcendentals=0),
+    )(core[None], own, other)
 
 
 def per_device(
@@ -162,7 +189,8 @@
         width = leaves >> level
         chunk = table.shape[1] // width
         start = (me & width - 1) * chunk
-        return lax.dynamic_slice(table, (me >> (leaf_bits - level), start), (1, chunk))[0]
+        entries = lax.dynamic_slice(table, (me >> (leaf_bits - level), start), (1, chunk))[0]
+        return entries
 
     def split_place(column, level):
         block = sep // (leaves >> level)
@@ -172,53 +200,67 @@
         rel = relative_block(owner, mine, groups[level])
         return ((column // half & 1) ^ core) * (sep // 2) + rel * half + column % half
 
-    def both_halves(own):
-        other = partner(own, "front", 1)
-        return in_order(own, other)
-
-    def front_half(x):
+    def half_of(x, which, dim):
+        size = x.shape[dim] // 2
+        return lax.dynamic_slice_in_dim(x, which * size, size, dim)
+
+    def own_half(x):
         width = x.shape[1] // 2
-        keep = jnp.where(core == 0, x[:, :width], x[:, width:])
-        send = jnp.where(core == 0, x[:, width:], x[:, :width])
-        return exchange_sum(keep + partner(send, "front", 1), "front", away)
+        return jnp.where(core == 0, x[:, :width], x[:, width:])
+
+    def row_total(keep, send, level):
+        return scatter_sum(keep + partner(send, "front", 1).astype(F32), "leaf", groups[level])
+
+    def put_halves(update, place):
+        send = put_columns(update, place, sep // 2, sep // 2, BF16)
+        return put_columns(update, place, 0, sep // 2, F32), send
+
+    def halves(w):
+        return half_of(w, core, 1), half_of(w, 1 - core, 1)
+
+    def front_half(x, split):
+        keep, send = split
+        other = partner(dot(x, send), "front", 1)
+        return exchange_sum(dot(x, keep) + other, "front", away)
+
+    def outputs(own):
+        return join(own, partner(own, "front", 1), core)
 
     def in_order(own, other):
         return jnp.concatenate([jnp.where(core == 0, own, other), jnp.where(core == 0, other, own)], axis=1)
 
-    def known_pieces(half, level):
-        own = gather_blocks(half.astype(BF16), "leaf", groups[level])
+    def both_halves(own):
+        return in_order(own, partner(own, "front", 1))
+
+    def known_pieces(half, within):
+        own = gather_blocks(half.astype(BF16), "leaf", within)
         return own + [partner(piece, "front", 1) for piece in own]
-
-    def row_total(pending, level):
-        width = sep // 2
-        total = pending[:, :width] + partner(pending[:, width:], "front", 1)
-        return scatter_sum(total, "leaf", groups[level])
-
-    def half_columns(x):
-        width = x.shape[1] // 2
-        return jnp.where(core == 0, x[:, :width], x[:, width:])
-
-    def core_slice(index):
-        half = index.shape[0] // 2
-        return lax.dynamic_slice(index, (core * half,), (half,))
 
     index = own_index(2)
     is_root = index < sep
     place_one = jnp.where(is_root, -1, split_place(index - sep, 1))
     place_root = jnp.where(is_root, split_place(index, 0), -1)
+    place_up = split_place(own_index(1), 0)
+    put_one, put_root, put_up = tied(*(half_of(p, core, 0)[None, :] for p in (place_one, place_root, place_up)))
     y_two = exchange_sum(dot(rhs_two.astype(BF16), pivot_two), "leaf", groups[2])
-    hot_one = one_hot_rows(core_slice(place_one), sep)
-    update = front_half(dot(y_two.astype(BF16), lower_two)).astype(BF16)
-    pending_one = dot(update, hot_one)
-    pending_root = put_columns(update, core_slice(place_root), sep)
-
-    place_up = split_place(own_index(1), 0)
-    own_rhs = half_columns(rhs_one)
-    reduced = both_halves((own_rhs - row_total(pending_one, 1)).astype(BF16))
-    y_one = exchange_sum(dot(reduced, pivot_one), "leaf", groups[1])
-    hot_up = one_hot_rows(core_slice(place_up), sep)
-    update = front_half(dot(y_one.astype(BF16), lower_one)).astype(BF16)
-    pending_root = pending_root + dot(update, hot_up)
+    y_two, keep, send = tied(y_two, *halves(lower_two))
+    low = y_two.astype(BF16)
+    other = partner(dot(low, send), "front", 1)
+    total = dot(low, keep) + other
+    update = exchange_sum(total, "front", away).astype(BF16)
+    update, rhs_half = tied(update, own_half(rhs_one))
+    keep, send = put_halves(update, put_one)
+
+    half = (rhs_half - row_total(keep, send, 1)).astype(BF16)
+    y_one = exchange_sum(dot(both_halves(half), pivot_one), "leaf", groups[1])
+    y_one, root_keep, root_send, keep, send = tied(y_one, *put_halves(update, put_root), *halves(lower_one))
+    low = y_one.astype(BF16)
+    total = partner(dot(low, send), "front", 1)
+    total = dot(low, keep) + total
+    update = exchange_sum(total, "front", away).astype(BF16)
+    update, rhs_half = tied(update, own_half(rhs_zero))
+    keep, send = put_halves(update, put_up)
+    keep, send = root_keep + keep, root_send + send
 
     near, far = groups[0][:1], groups[0][1:]
     count = 1 << len(near[0])
@@ -226,22 +268,27 @@
     starts = [((me & count - 1) ^ m) * block for m in range(count)]
     pivot_rel = jnp.concatenate([lax.dynamic_slice_in_dim(pivot_zero, at, block, 1) for at in starts], axis=1)
     back_rel = jnp.concatenate([lax.dynamic_slice_in_dim(back_zero, at, block, 0) for at in starts], axis=0)
-    own_rhs = half_columns(rhs_zero)
-    reduced = both_halves((own_rhs - row_total(pending_root, 0)).astype(BF16))
-    y_zero = exchange_sum(scatter_sum(dot(reduced, pivot_rel), "leaf", near), "leaf", far)
+    half = (rhs_half - row_total(keep, send, 0)).astype(BF16)
+    half, pivot_rel, keep, send = tied(half, pivot_rel, *halves(back_rel))
+    y_zero = exchange_sum(scatter_sum(dot(both_halves(half), pivot_rel), "leaf", near), "leaf", far)
     y_zero = jnp.concatenate(gather_blocks(y_zero.astype(BF16), "leaf", near), axis=1)
-    x_zero = front_half(dot(y_zero, back_rel))
-    known_zero = known_pieces(x_zero, 0)
-
-    coupling = picked_product(known_zero, place_up, upper_one)
-    z_one = y_one - exchange_sum(coupling, "leaf", groups[1])
-    x_one = front_half(dot(z_one.astype(BF16), back_one))
-    known_one = known_pieces(x_one, 1)
-
-    coupling = picked_product(known_zero, place_root, upper_two) + picked_product(known_one, place_one, upper_two)
-    z_two = y_two - exchange_sum(coupling, "leaf", groups[2])
-    x_two = front_half(dot(z_two.astype(BF16), back_two))
-    return both_halves(x_zero), both_halves(x_one), both_halves(x_two)
+    y_zero, *split_one = tied(y_zero, *halves(back_one))
+    x_zero = front_half(y_zero, (keep, send))
+    known_zero = known_pieces(x_zero, groups[0])
+
+    coupling = exchange_sum(picked_product(known_zero, place_up, upper_one), "leaf", groups[1])
+    coupling, coupling_root = tied(coupling, picked_product(known_zero, place_root, upper_two))
+    z_one = y_one - coupling
+    x_one = front_half(z_one.astype(BF16), split_one)
+    x_one, x_zero = tied(x_one, x_zero)
+    known_one = known_pieces(x_one, groups[1])
+    *known_one, solution_zero, keep, send = tied(*known_one, outputs(x_zero), *halves(back_two))
+
+    coupling = coupling_root + picked_product(known_one, place_one, upper_two)
+    coupling, x_one = tied(coupling, x_one)
+    coupling, solution_one = tied(exchange_sum(coupling, "leaf", groups[2]), outputs(x_one))
+    x_two = front_half((y_two - coupling).astype(BF16), (keep, send))
+    return solution_zero, solution_one, outputs(x_two)
 
 
 def solution(mesh):

time: 164 us -> 152 us (0.927)
  waiting for transfers between devices: 76.5 us -> 59.7 us
  other arithmetic: 11.3 us -> 3.94 us
  local copies, waits for them, and re-layouts: 1.1 us -> 7.68 us
  Pallas kernels: 13 us -> 19.5 us
  matrix products: 13.5 us -> 9.23 us
  starting transfers between devices: 46.6 us -> 50 us
    ppermute x54, waiting for transfers between devices: 76.5 us -> 59.7 us  [partner(): lax.ppermute(x, axis, [(i, i ^ mask) for i in range(lax.axis_size(axis))])]
    dynamic_slice x1 -> x6, local copies, waits for them, and re-layouts: 0.08 us -> 6.44 us  [half_of(): return lax.dynamic_slice_in_dim(x, which * size, size, dim)]
    pallas_call x1 -> x9, Pallas kernels: 3.03 us -> 9.36 us  [the longest x6 7.1 us: put_columns(): pl.pallas_call(functools.partial(put_kernel, first=first), out_shape=jax....]
    convert_element_type x5 -> x7, other arithmetic: 6.31 us -> 0.18 us  [the longest x2 0.05 us: per_device(): update = exchange_sum(total, 'front', away).astype(BF16)]
    dot_general x10 -> x13, matrix products: 13.5 us -> 9.23 us  [dot(): return jnp.dot(left, right, preferred_element_type=F32)]
    ppermute x54, starting transfers between devices: 46.6 us -> 50 us  [partner(): lax.ppermute(x, axis, [(i, i ^ mask) for i in range(lax.axis_size(axis))])]
    concatenate x3, other arithmetic: 2.22 us -> 0.21 us  [the longest x1 0.13 us: per_device(): jnp.concatenate([lax.dynamic_slice_in_dim(pivot_zero, at, block, 1) for a...]
  transfers between devices with their start and end apart: 54 -> 54, of which waited for: 45 -> 42; matrix products, arithmetic and copies ran while one was open for 5% -> 6% of each run, Pallas kernels for 4% -> 6%
where the time goes in v3:
time: 152 us; the launch traced here: 151 us
  waiting for transfers between devices  59.7 us (39%)
  starting transfers between devices  50 us (33%)
  Pallas kernels  19.5 us (13%)
  matrix products  9.23 us (6%)
  local copies, waits for them, and re-layouts  7.68 us (5%)
  other arithmetic  3.94 us (3%)
    ppermute x54, waiting for transfers between devices, partner(): lax.ppermute(x, axis, [(i, i ^ mask) for i in range(lax.axis_size(axis))])  59.7 us
    ppermute x54, starting transfers between devices, partner(): lax.ppermute(x, axis, [(i, i ^ mask) for i in range(lax.axis_size(axis))])  50 us
    pallas_call x3, Pallas kernels, picked_product(): pl.pallas_call(pick_kernel, grid=(count // step,), in_specs=[pl.BlockSpec...  10.2 us
    dot_general x13, matrix products, dot(): return jnp.dot(left, right, preferred_element_type=F32)  9.23 us
    pallas_call x6, Pallas kernels, put_columns(): pl.pallas_call(functools.partial(put_kernel, first=first), out_shape=jax....  7.1 us
    dynamic_slice x6, local copies, waits for them, and re-layouts, half_of(): return lax.dynamic_slice_in_dim(x, which * size, size, dim)  6.44 us
  transfers between devices with their start and end apart: 54, of which 42 were waited for; matrix products, arithmetic and copies ran while one was open for 6% of the time, Pallas kernels for 6%

profile of v3, /device:TPU:0, one launch (start us, length us, event | category | flops | bytes accessed | tf_op | source)
XLA Modules:
  0.0 151.4 jit_solution(17620831663715775678)
XLA Ops:
  0.6 3.3 %convolution_convert_fusion = bf16[64,1024]{1,0:T(8,128)(2,1)S(1)} fusion(bf16[2048,1024]{1,0:T(8,128)(2,1)} %param.20, f32[64,2048]{1,0:T(8,128)} %param.17), kind=kOutput, calls=%fused_computation.4 | convolution fusion | flops 268632064 | bytes 4849664 | tf_op jit(solution)/shard_map/dot_general | solution.py:15
  4.0 3.0 %collective-permute-start = (bf16[64,1024]{1,0:T(8,128)(2,1)S(1)}, bf16[64,1024]{1,0:T(8,128)(2,1)S(1)}, u32[]{:S(2)}, u32[]{:S(2)}) collective-permute-start(bf16[64,1024]{1,0:T(8,128)(2,1)S(1)} %convolution_convert_fusion), channel_id=1, source_target_pairs={{0,4},{4,0},{8,12},{12,8},{16,20},{20,16},{24,28},{28,24},{1,5},{5... | collective-permute-start | bytes 393224 | tf_op jit(solution)/shard_map/ppermute | solution.py:24
  8.0 4.0 %constant_dynamic-slice_fusion.16 = (bf16[1024,1024]{1,0:T(8,128)(2,1)S(1)}, bf16[1024,1024]{1,0:T(8,128)(2,1)}) fusion(bf16[1024,2048]{1,0:T(8,128)(2,1)} %param.22, s32[]{:T(128)S(6)} %select_n.171, s32[]{:T(128)S(6)} %select_n.170), kind=kLoop, calls=%fused_computation.144 | loop fusion | bytes 8388616 | tf_op jit(solution)/shard_map/dynamic_slice | solution.py:205
  14.1 2.1 %fusion = bf16[64,1024]{1,0:T(8,128)(2,1)S(1)} fusion(f32[64,1024]{1,0:T(8,128)S(1)} %collective-permute-done.1, bf16[1024,1024]{1,0:T(8,128)(2,1)} %get-tuple-element.45, f32[64,1024]{1,0:T(8,128)S(1)} %convert_add_fusion.4), kind=kOutput, calls=%fused_computation.2 | convolution fusion | flops 134414336 | bytes 2752512 | tf_op jit(solution)/shard_map/dot_general | solution.py:15
  16.2 1.6 %collective-permute-start.2 = (bf16[64,1024]{1,0:T(8,128)(2,1)S(1)}, bf16[64,1024]{1,0:T(8,128)(2,1)S(1)}, u32[]{:S(2)}, u32[]{:S(2)}) collective-permute-start(bf16[64,1024]{1,0:T(8,128)(2,1)S(1)} %fusion), channel_id=1, source_target_pairs={{0,2},{1,3},{2,0},{3,1},{4,6},{5,7},{6,4},{7,5},{8,10},{9,11},{10,... | collective-permute-start | bytes 393224 | tf_op jit(solution)/shard_map/ppermute | solution.py:24
  17.8 4.0 %collective-permute-done.2 = bf16[64,1024]{1,0:T(8,128)(2,1)S(1)} collective-permute-done((bf16[64,1024]{1,0:T(8,128)(2,1)S(1)}, bf16[64,1024]{1,0:T(8,128)(2,1)S(1)}, u32[]{:S(2)}, u32[]{:S(2)}) %collective-permute-start.2) | collective-permute-done | bytes 131104 | tf_op jit(solution)/shard_map/ppermute | solution.py:24
  21.9 1.4 shard_map.167
  23.3 1.4 shard_map.166
  24.9 1.6 %collective-permute-start.6 = (bf16[64,512]{1,0:T(8,128)(2,1)S(1)}, bf16[64,512]{1,0:T(8,128)(2,1)S(1)}, u32[]{:S(2)}, u32[]{:S(2)}) collective-permute-start(bf16[64,512]{1,0:T(8,128)(2,1)S(1)} %get-tuple-element.115), channel_id=1, source_target_pairs={{0,12},{4,8},{8,4},{12,0},{16,28},{20,24},{24,20},{28,16},{1,13},{... | collective-permute-start | bytes 196616 | tf_op jit(solution)/shard_map/ppermute | solution.py:24
  26.8 1.7 %collective-permute-start.4 = (bf16[64,512]{1,0:T(8,128)(2,1)S(1)}, bf16[64,512]{1,0:T(8,128)(2,1)S(1)}, u32[]{:S(2)}, u32[]{:S(2)}) collective-permute-start(bf16[64,512]{1,0:T(8,128)(2,1)S(1)} %get-tuple-element.114), channel_id=1, source_target_pairs={{0,4},{4,0},{8,12},{12,8},{16,20},{20,16},{24,28},{28,24},{1,5},{5... | collective-permute-start | bytes 196616 | tf_op jit(solution)/shard_map/ppermute | solution.py:24
  28.5 1.9 %collective-permute-done.6 = bf16[64,512]{1,0:T(8,128)(2,1)S(1)} collective-permute-done((bf16[64,512]{1,0:T(8,128)(2,1)S(1)}, bf16[64,512]{1,0:T(8,128)(2,1)S(1)}, u32[]{:S(2)}, u32[]{:S(2)}) %collective-permute-start.6) | collective-permute-done | bytes 65568 | tf_op jit(solution)/shard_map/ppermute | solution.py:24
  31.8 1.2 collective-permute-done.7
  33.6 2.2 %collective-permute-start.10 = (bf16[64,1024]{1,0:T(8,128)(2,1)S(1)}, bf16[64,1024]{1,0:T(8,128)(2,1)S(1)}, u32[]{:S(2)}, u32[]{:S(2)}) collective-permute-start(bf16[64,1024]{1,0:T(8,128)(2,1)S(1)} %convolution_convert_fusion.1), channel_id=1, source_target_pairs={{0,12},{4,8},{8,4},{12,0},{16,28},{20,24},{24,20},{28,16},{1,13},{... | collective-permute-start | bytes 393224 | tf_op jit(solution)/shard_map/ppermute | solution.py:24
  37.1 1.5 %constant_dynamic-slice_fusion.14 = (bf16[1024,512]{1,0:T(8,128)(2,1)}, bf16[1024,512]{1,0:T(8,128)(2,1)}) fusion(bf16[1024,1024]{1,0:T(8,128)(2,1)S(1)} %copy-done.8, s32[]{:T(128)S(6)} %select_n.191, s32[]{:T(128)S(6)} %select_n.188), kind=kLoop, calls=%fused_computation.142 | loop fusion | bytes 4194312 | tf_op jit(solution)/shard_map/dynamic_slice | solution.py:205
  38.7 1.4 shard_map.168
  40.1 1.4 shard_map.169
  41.5 1.2 collective-permute-done.9
  43.0 1.0 add_add_fusion.1
  44.5 1.3 collective-permute-done.11
  46.1 1.6 %collective-permute-start.12 = (bf16[64,512]{1,0:T(8,128)(2,1)S(1)}, bf16[64,512]{1,0:T(8,128)(2,1)S(1)}, u32[]{:S(2)}, u32[]{:S(2)}) collective-permute-start(bf16[64,512]{1,0:T(8,128)(2,1)S(1)} %fusion.2), channel_id=1, source_target_pairs={{0,2},{1,3},{2,0},{3,1},{4,6},{5,7},{6,4},{7,5},{8,10},{9,11},{10,... | collective-permute-start | bytes 196616 | tf_op jit(solution)/shard_map/ppermute | solution.py:24
  47.7 1.0 constant_dynamic-slice_fusion.13
  48.7 1.7 %collective-permute-done.12 = bf16[64,512]{1,0:T(8,128)(2,1)S(1)} collective-permute-done((bf16[64,512]{1,0:T(8,128)(2,1)S(1)}, bf16[64,512]{1,0:T(8,128)(2,1)S(1)}, u32[]{:S(2)}, u32[]{:S(2)}) %collective-permute-start.12) | collective-permute-done | bytes 65568 | tf_op jit(solution)/shard_map/ppermute | solution.py:24
  53.0 2.2 %collective-permute-start.16 = (bf16[64,512]{1,0:T(8,128)(2,1)S(1)}, bf16[64,512]{1,0:T(8,128)(2,1)S(1)}, u32[]{:S(2)}, u32[]{:S(2)}) collective-permute-start(bf16[64,512]{1,0:T(8,128)(2,1)S(1)} %get-tuple-element.112), channel_id=1, source_target_pairs={{0,12},{4,8},{8,4},{12,0},{16,28},{20,24},{24,20},{28,16},{1,13},{... | collective-permute-start | bytes 196616 | tf_op jit(solution)/shard_map/ppermute | solution.py:24
  56.6 1.9 %collective-permute-done.16 = bf16[64,512]{1,0:T(8,128)(2,1)S(1)} collective-permute-done((bf16[64,512]{1,0:T(8,128)(2,1)S(1)}, bf16[64,512]{1,0:T(8,128)(2,1)S(1)}, u32[]{:S(2)}, u32[]{:S(2)}) %collective-permute-start.16) | collective-permute-done | bytes 65568 | tf_op jit(solution)/shard_map/ppermute | solution.py:24
  59.9 2.6 %collective-permute-start.17 = (bf16[64,256]{1,0:T(8,128)(2,1)S(1)}, bf16[64,256]{1,0:T(8,128)(2,1)S(1)}, u32[]{:S(2)}, u32[]{:S(2)}) collective-permute-start(bf16[64,256]{1,0:T(8,128)(2,1)S(1)} %slice.127), channel_id=1, source_target_pairs={{0,16},{4,20},{8,24},{12,28},{16,0},{20,4},{24,8},{28,12},{1,17},{... | collective-permute-start | bytes 98312 | tf_op jit(solution)/shard_map/ppermute | solution.py:24
  62.7 2.1 %collective-permute-done.17 = bf16[64,256]{1,0:T(8,128)(2,1)S(1)} collective-permute-done((bf16[64,256]{1,0:T(8,128)(2,1)S(1)}, bf16[64,256]{1,0:T(8,128)(2,1)S(1)}, u32[]{:S(2)}, u32[]{:S(2)}) %collective-permute-start.17) | collective-permute-done | bytes 32800 | tf_op jit(solution)/shard_map/ppermute | solution.py:24
  64.9 1.2 collective-permute-done.18
  66.4 2.0 %collective-permute-start.21 = (bf16[64,256]{1,0:T(8,128)(2,1)S(1)}, bf16[64,256]{1,0:T(8,128)(2,1)S(1)}, u32[]{:S(2)}, u32[]{:S(2)}) collective-permute-start(bf16[64,256]{1,0:T(8,128)(2,1)S(1)} %get-tuple-element.118), channel_id=1, source_target_pairs={{0,12},{4,8},{8,4},{12,0},{16,28},{20,24},{24,20},{28,16},{1,13},{... | collective-permute-start | bytes 98312 | tf_op jit(solution)/shard_map/ppermute | solution.py:24
  68.9 1.1 collective-permute-start.19
  70.0 1.3 collective-permute-done.21
  71.3 1.0 collective-permute-done.20
  72.8 2.7 %collective-permute-start.22 = (bf16[64,256]{1,0:T(8,128)(2,1)S(1)}, bf16[64,256]{1,0:T(8,128)(2,1)S(1)}, u32[]{:S(2)}, u32[]{:S(2)}) collective-permute-start(bf16[64,256]{1,0:T(8,128)(2,1)S(1)} %fusion.17), channel_id=1, source_target_pairs={{0,16},{4,20},{8,24},{12,28},{16,0},{20,4},{24,8},{28,12},{1,17},{... | collective-permute-start | bytes 98312 | tf_op jit(solution)/shard_map/ppermute | solution.py:24
  75.5 2.2 %collective-permute-done.22 = bf16[64,256]{1,0:T(8,128)(2,1)S(1)} collective-permute-done((bf16[64,256]{1,0:T(8,128)(2,1)S(1)}, bf16[64,256]{1,0:T(8,128)(2,1)S(1)}, u32[]{:S(2)}, u32[]{:S(2)}) %collective-permute-start.22) | collective-permute-done | bytes 32800 | tf_op jit(solution)/shard_map/ppermute | solution.py:24
  77.7 2.2 %collective-permute-start.25 = (bf16[64,256]{1,0:T(8,128)(2,1)S(1)}, bf16[64,256]{1,0:T(8,128)(2,1)S(1)}, u32[]{:S(2)}, u32[]{:S(2)}) collective-permute-start(bf16[64,256]{1,0:T(8,128)(2,1)S(1)} %add_convert_fusion.2), channel_id=1, source_target_pairs={{0,12},{4,8},{8,4},{12,0},{16,28},{20,24},{24,20},{28,16},{1,13},{... | collective-permute-start | bytes 98312 | tf_op jit(solution)/shard_map/ppermute | solution.py:24
  81.5 1.1 collective-permute-done.25
  82.6 1.2 collective-permute-done.24
  84.6 1.2 collective-permute-done.26
  86.1 1.6 %collective-permute-start.27 = (bf16[64,256]{1,0:T(8,128)(2,1)S(1)}, bf16[64,256]{1,0:T(8,128)(2,1)S(1)}, u32[]{:S(2)}, u32[]{:S(2)}) collective-permute-start(bf16[64,256]{1,0:T(8,128)(2,1)S(1)} %fusion.4), channel_id=1, source_target_pairs={{0,2},{1,3},{2,0},{3,1},{4,6},{5,7},{6,4},{7,5},{8,10},{9,11},{10,... | collective-permute-start | bytes 98312 | tf_op jit(solution)/shard_map/ppermute | solution.py:24
  87.6 2.4 %collective-permute-done.27 = bf16[64,256]{1,0:T(8,128)(2,1)S(1)} collective-permute-done((bf16[64,256]{1,0:T(8,128)(2,1)S(1)}, bf16[64,256]{1,0:T(8,128)(2,1)S(1)}, u32[]{:S(2)}, u32[]{:S(2)}) %collective-permute-start.27) | collective-permute-done | bytes 32800 | tf_op jit(solution)/shard_map/ppermute | solution.py:24
  90.0 2.7 %collective-permute-start.28 = (bf16[64,256]{1,0:T(8,128)(2,1)S(1)}, bf16[64,256]{1,0:T(8,128)(2,1)S(1)}, u32[]{:S(2)}, u32[]{:S(2)}) collective-permute-start(bf16[64,256]{1,0:T(8,128)(2,1)S(1)} %get-tuple-element.123), channel_id=1, source_target_pairs={{0,16},{4,20},{8,24},{12,28},{16,0},{20,4},{24,8},{28,12},{1,17},{... | collective-permute-start | bytes 98312 | tf_op jit(solution)/shard_map/ppermute | solution.py:24
  92.7 2.2 %collective-permute-done.28 = bf16[64,256]{1,0:T(8,128)(2,1)S(1)} collective-permute-done((bf16[64,256]{1,0:T(8,128)(2,1)S(1)}, bf16[64,256]{1,0:T(8,128)(2,1)S(1)}, u32[]{:S(2)}, u32[]{:S(2)}) %collective-permute-start.28) | collective-permute-done | bytes 32800 | tf_op jit(solution)/shard_map/ppermute | solution.py:24
  95.9 1.6 %collective-permute-start.30 = (bf16[64,512]{1,0:T(8,128)(2,1)S(1)}, bf16[64,512]{1,0:T(8,128)(2,1)S(1)}, u32[]{:S(2)}, u32[]{:S(2)}) collective-permute-start(bf16[64,512]{1,0:T(8,128)(2,1)S(1)} %pad_maximum_fusion.3.refs_0_), channel_id=1, source_target_pairs={{0,8},{4,12},{8,0},{12,4},{16,24},{20,28},{24,16},{28,20},{1,9},{5... | collective-permute-start | bytes 196616 | tf_op jit(solution)/shard_map/ppermute | solution.py:24
  97.4 1.0 collective-permute-start.31
  98.4 1.4 collective-permute-done.29.refs_1_
  100.4 2.2 %collective-permute-done.31.refs_3_ = bf16[64,512]{1,0:T(8,128)(2,1)S(1)} collective-permute-done((bf16[64,512]{1,0:T(8,128)(2,1)S(1)}, bf16[64,512]{1,0:T(8,128)(2,1)S(1)}, u32[]{:S(2)}, u32[]{:S(2)}) %collective-permute-start.31) | collective-permute-done | bytes 65568 | tf_op jit(solution)/shard_map/ppermute | solution.py:24
  102.6 1.2 collective-permute-done.35.refs_7_
  103.9 2.1 %shard_map.172 = f32[64,1024]{1,0:T(8,128)S(1)} custom-call(bf16[64,512]{1,0:T(8,128)(2,1)S(1)} %pad_maximum_fusion.3.refs_0_, bf16[64,512]{1,0:T(8,128)(2,1)S(1)} %collective-permute-done.29.refs_1_, bf16[64,512]{1,0:T(8,128)(2,1)S(1)} %collective-permute-done.30.refs_2_, bf16[64,512]{1,0:T(8,128)(2,1)S(1)} %collective-permute-done.31.refs_3_, ...), custom_call_target="tpu_custom_call" | custom-call | flops 671088640 | bytes 18874368 | tf_op jit(solution)/shard_map/pallas_call | solution.py:105
  106.0 1.1 collective-permute-start.38
  107.1 1.6 %collective-permute-start.37 = (bf16[64,1024]{1,0:T(8,128)(2,1)S(1)}, bf16[64,1024]{1,0:T(8,128)(2,1)S(1)}, u32[]{:S(2)}, u32[]{:S(2)}) collective-permute-start(bf16[64,1024]{1,0:T(8,128)(2,1)S(1)} %convert_element_type.225), channel_id=1, source_target_pairs={{0,8},{4,12},{8,0},{12,4},{16,24},{20,28},{24,16},{28,20},{1,9},{5... | collective-permute-start | bytes 393224 | tf_op jit(solution)/shard_map/ppermute | solution.py:24
  109.7 4.0 %shard_map.173 = f32[64,1024]{1,0:T(8,128)S(1)} custom-call(bf16[64,512]{1,0:T(8,128)(2,1)S(1)} %pad_maximum_fusion.3.refs_0_, bf16[64,512]{1,0:T(8,128)(2,1)S(1)} %collective-permute-done.29.refs_1_, bf16[64,512]{1,0:T(8,128)(2,1)S(1)} %collective-permute-done.30.refs_2_, bf16[64,512]{1,0:T(8,128)(2,1)S(1)} %collective-permute-done.31.refs_3_, ...), custom_call_target="tpu_custom_call" | custom-call | flops 1342177280 | bytes 37748736 | tf_op jit(solution)/shard_map/pallas_call | solution.py:105
  113.7 1.3 collective-permute-done.37
  115.8 1.3 collective-permute-done.39
  117.5 1.6 %collective-permute-start.40 = (bf16[64,512]{1,0:T(8,128)(2,1)S(1)}, bf16[64,512]{1,0:T(8,128)(2,1)S(1)}, u32[]{:S(2)}, u32[]{:S(2)}) collective-permute-start(bf16[64,512]{1,0:T(8,128)(2,1)S(1)} %fusion.3), channel_id=1, source_target_pairs={{0,2},{1,3},{2,0},{3,1},{4,6},{5,7},{6,4},{7,5},{8,10},{9,11},{10,... | collective-permute-start | bytes 196616 | tf_op jit(solution)/shard_map/ppermute | solution.py:24
  119.1 2.7 %collective-permute-done.40 = bf16[64,512]{1,0:T(8,128)(2,1)S(1)} collective-permute-done((bf16[64,512]{1,0:T(8,128)(2,1)S(1)}, bf16[64,512]{1,0:T(8,128)(2,1)S(1)}, u32[]{:S(2)}, u32[]{:S(2)}) %collective-permute-start.40) | collective-permute-done | bytes 65568 | tf_op jit(solution)/shard_map/ppermute | solution.py:24
  121.9 1.2 collective-permute-start.41
  123.5 1.9 %collective-permute-start.43 = (bf16[64,512]{1,0:T(8,128)(2,1)S(1)}, bf16[64,512]{1,0:T(8,128)(2,1)S(1)}, u32[]{:S(2)}, u32[]{:S(2)}) collective-permute-start(bf16[64,512]{1,0:T(8,128)(2,1)S(1)} %convert_element_type.234.refs_0_), channel_id=1, source_target_pairs={{0,12},{4,8},{8,4},{12,0},{16,28},{20,24},{24,20},{28,16},{1,13},{... | collective-permute-start | bytes 196616 | tf_op jit(solution)/shard_map/ppermute | solution.py:24
  127.3 1.3 collective-permute-done.43.refs_3_
  129.9 4.0 %shard_map.175 = f32[64,1024]{1,0:T(8,128)S(1)} custom-call(bf16[64,512]{1,0:T(8,128)(2,1)S(1)} %convert_element_type.234.refs_0_, bf16[64,512]{1,0:T(8,128)(2,1)S(1)} %collective-permute-done.41.refs_1_, bf16[64,512]{1,0:T(8,128)(2,1)S(1)} %collective-permute-done.42.refs_2_, bf16[64,512]{1,0:T(8,128)(2,1)S(1)} %collective-permute-done.43.refs_3_, ...), custom_call_target="tpu_custom_call" | custom-call | flops 1342177280 | bytes 37748736 | tf_op jit(solution)/shard_map/pallas_call | solution.py:105
  134.0 1.0 collective-permute-start.49
  135.2 4.7 %collective-permute-done.49 = bf16[64,1024]{1,0:T(8,128)(2,1)S(1)} collective-permute-done((bf16[64,1024]{1,0:T(8,128)(2,1)S(1)}, bf16[64,1024]{1,0:T(8,128)(2,1)S(1)}, u32[]{:S(2)}, u32[]{:S(2)}) %collective-permute-start.49) | collective-permute-done | bytes 131104 | tf_op jit(solution)/shard_map/ppermute | solution.py:24
  141.3 1.5 %collective-permute-done.51 = f32[64,1024]{1,0:T(8,128)S(1)} collective-permute-done((f32[64,1024]{1,0:T(8,128)S(1)}, f32[64,1024]{1,0:T(8,128)S(1)}, u32[]{:S(2)}, u32[]{:S(2)}) %collective-permute-start.51) | collective-permute-done | bytes 262176 | tf_op jit(solution)/shard_map/ppermute | solution.py:24
  143.4 1.6 %collective-permute-start.52 = (bf16[64,1024]{1,0:T(8,128)(2,1)S(1)}, bf16[64,1024]{1,0:T(8,128)(2,1)S(1)}, u32[]{:S(2)}, u32[]{:S(2)}) collective-permute-start(bf16[64,1024]{1,0:T(8,128)(2,1)S(1)} %fusion.1), channel_id=1, source_target_pairs={{0,2},{1,3},{2,0},{3,1},{4,6},{5,7},{6,4},{7,5},{8,10},{9,11},{10,... | collective-permute-start | bytes 393224 | tf_op jit(solution)/shard_map/ppermute | solution.py:24
  144.9 4.0 %collective-permute-done.52 = bf16[64,1024]{1,0:T(8,128)(2,1)S(1)} collective-permute-done((bf16[64,1024]{1,0:T(8,128)(2,1)S(1)}, bf16[64,1024]{1,0:T(8,128)(2,1)S(1)}, u32[]{:S(2)}, u32[]{:S(2)}) %collective-permute-start.52) | collective-permute-done | bytes 131104 | tf_op jit(solution)/shard_map/ppermute | solution.py:24
  149.1 1.5 %collective-permute-done.53.other_ref = f32[64,1024]{1,0:T(8,128)S(1)} collective-permute-done((f32[64,1024]{1,0:T(8,128)S(1)}, f32[64,1024]{1,0:T(8,128)S(1)}, u32[]{:S(2)}, u32[]{:S(2)}) %collective-permute-start.53) | collective-permute-done | bytes 262176 | tf_op jit(solution)/shard_map/ppermute | solution.py:24
  (153 shorter events, 27.7 us)
Async XLA Ops:
  0.6 32.4 %copy-start = (bf16[1024,1024]{1,0:T(8,128)(2,1)S(1)}, bf16[1024,1024]{1,0:T(8,128)(2,1)}, u32[]{:S(2)}) copy-start(bf16[1024,1024]{1,0:T(8,128)(2,1)} %param.19) | copy-start | bytes 6291460
  4.0 8.0 %collective-permute-start = (bf16[64,1024]{1,0:T(8,128)(2,1)S(1)}, bf16[64,1024]{1,0:T(8,128)(2,1)S(1)}, u32[]{:S(2)}, u32[]{:S(2)}) collective-permute-start(bf16[64,1024]{1,0:T(8,128)(2,1)S(1)} %convolution_convert_fusion), channel_id=1, source_target_pairs={{0,4},{4,0},{8,12},{12,8},{16,20},{20,16},{24,28},{28,24},{1,5},{5... | collective-permute-start | bytes 393224 | tf_op jit(solution)/shard_map/ppermute | solution.py:24
  12.5 1.6 %collective-permute-start.1 = (f32[64,1024]{1,0:T(8,128)S(1)}, f32[64,1024]{1,0:T(8,128)S(1)}, u32[]{:S(2)}, u32[]{:S(2)}) collective-permute-start(f32[64,1024]{1,0:T(8,128)S(1)} %fusion.27), channel_id=1, source_target_pairs={{0,1},{1,0},{2,3},{3,2},{4,5},{5,4},{6,7},{7,6},{8,9},{9,8},{10,11... | collective-permute-start | bytes 786440 | tf_op jit(solution)/shard_map/ppermute | solution.py:24
  16.2 5.6 %collective-permute-start.2 = (bf16[64,1024]{1,0:T(8,128)(2,1)S(1)}, bf16[64,1024]{1,0:T(8,128)(2,1)S(1)}, u32[]{:S(2)}, u32[]{:S(2)}) collective-permute-start(bf16[64,1024]{1,0:T(8,128)(2,1)S(1)} %fusion), channel_id=1, source_target_pairs={{0,2},{1,3},{2,0},{3,1},{4,6},{5,7},{6,4},{7,5},{8,10},{9,11},{10,... | collective-permute-start | bytes 393224 | tf_op jit(solution)/shard_map/ppermute | solution.py:24
  23.3 1.6 %collective-permute-start.3 = (bf16[64,2048]{1,0:T(8,128)(2,1)S(1)}, bf16[64,2048]{1,0:T(8,128)(2,1)S(1)}, u32[]{:S(2)}, u32[]{:S(2)}) collective-permute-start(bf16[64,2048]{1,0:T(8,128)(2,1)S(1)} %shard_map.167), channel_id=1, source_target_pairs={{0,1},{1,0},{2,3},{3,2},{4,5},{5,4},{6,7},{7,6},{8,9},{9,8},{10,11... | collective-permute-start | bytes 786440 | tf_op jit(solution)/shard_map/ppermute | solution.py:24
  24.9 5.5 %collective-permute-start.6 = (bf16[64,512]{1,0:T(8,128)(2,1)S(1)}, bf16[64,512]{1,0:T(8,128)(2,1)S(1)}, u32[]{:S(2)}, u32[]{:S(2)}) collective-permute-start(bf16[64,512]{1,0:T(8,128)(2,1)S(1)} %get-tuple-element.115), channel_id=1, source_target_pairs={{0,12},{4,8},{8,4},{12,0},{16,28},{20,24},{24,20},{28,16},{1,13},{... | collective-permute-start | bytes 196616 | tf_op jit(solution)/shard_map/ppermute | solution.py:24
  26.6 4.3 %collective-permute-start.5 = (bf16[64,512]{1,0:T(8,128)(2,1)S(1)}, bf16[64,512]{1,0:T(8,128)(2,1)S(1)}, u32[]{:S(2)}, u32[]{:S(2)}) collective-permute-start(bf16[64,512]{1,0:T(8,128)(2,1)S(1)} %get-tuple-element.116), channel_id=1, source_target_pairs={{0,8},{4,12},{8,0},{12,4},{16,24},{20,28},{24,16},{28,20},{1,9},{5... | collective-permute-start | bytes 196616 | tf_op jit(solution)/shard_map/ppermute | solution.py:24
  26.8 4.9 %collective-permute-start.4 = (bf16[64,512]{1,0:T(8,128)(2,1)S(1)}, bf16[64,512]{1,0:T(8,128)(2,1)S(1)}, u32[]{:S(2)}, u32[]{:S(2)}) collective-permute-start(bf16[64,512]{1,0:T(8,128)(2,1)S(1)} %get-tuple-element.114), channel_id=1, source_target_pairs={{0,4},{4,0},{8,12},{12,8},{16,20},{20,16},{24,28},{28,24},{1,5},{5... | collective-permute-start | bytes 196616 | tf_op jit(solution)/shard_map/ppermute | solution.py:24
  31.7 1.3 collective-permute-start.7
  33.6 7.9 %collective-permute-start.10 = (bf16[64,1024]{1,0:T(8,128)(2,1)S(1)}, bf16[64,1024]{1,0:T(8,128)(2,1)S(1)}, u32[]{:S(2)}, u32[]{:S(2)}) collective-permute-start(bf16[64,1024]{1,0:T(8,128)(2,1)S(1)} %convolution_convert_fusion.1), channel_id=1, source_target_pairs={{0,12},{4,8},{8,4},{12,0},{16,28},{20,24},{24,20},{28,16},{1,13},{... | collective-permute-start | bytes 393224 | tf_op jit(solution)/shard_map/ppermute | solution.py:24
  35.7 6.9 %collective-permute-start.9 = (bf16[64,1024]{1,0:T(8,128)(2,1)S(1)}, bf16[64,1024]{1,0:T(8,128)(2,1)}, u32[]{:S(2)}, u32[]{:S(2)}) collective-permute-start(bf16[64,1024]{1,0:T(8,128)(2,1)S(1)} %convolution_convert_fusion.1), channel_id=1, source_target_pairs={{0,8},{4,12},{8,0},{12,4},{16,24},{20,28},{24,16},{28,20},{1,9},{5... | collective-permute-start | bytes 393224 | tf_op jit(solution)/shard_map/ppermute | solution.py:24
  36.2 6.8 %collective-permute-start.8 = (bf16[64,1024]{1,0:T(8,128)(2,1)S(1)}, bf16[64,1024]{1,0:T(8,128)(2,1)}, u32[]{:S(2)}, u32[]{:S(2)}) collective-permute-start(bf16[64,1024]{1,0:T(8,128)(2,1)S(1)} %convolution_convert_fusion.1), channel_id=1, source_target_pairs={{0,4},{4,0},{8,12},{12,8},{16,20},{20,16},{24,28},{28,24},{1,5},{5... | collective-permute-start | bytes 393224 | tf_op jit(solution)/shard_map/ppermute | solution.py:24
  44.4 1.4 collective-permute-start.11
  46.1 4.3 %collective-permute-start.12 = (bf16[64,512]{1,0:T(8,128)(2,1)S(1)}, bf16[64,512]{1,0:T(8,128)(2,1)S(1)}, u32[]{:S(2)}, u32[]{:S(2)}) collective-permute-start(bf16[64,512]{1,0:T(8,128)(2,1)S(1)} %fusion.2), channel_id=1, source_target_pairs={{0,2},{1,3},{2,0},{3,1},{4,6},{5,7},{6,4},{7,5},{8,10},{9,11},{10,... | collective-permute-start | bytes 196616 | tf_op jit(solution)/shard_map/ppermute | solution.py:24
  51.3 1.6 %collective-permute-start.13 = (bf16[64,2048]{1,0:T(8,128)(2,1)S(1)}, bf16[64,2048]{1,0:T(8,128)(2,1)S(1)}, u32[]{:S(2)}, u32[]{:S(2)}) collective-permute-start(bf16[64,2048]{1,0:T(8,128)(2,1)S(1)} %add.260), channel_id=1, source_target_pairs={{0,1},{1,0},{2,3},{3,2},{4,5},{5,4},{6,7},{7,6},{8,9},{9,8},{10,11... | collective-permute-start | bytes 786440 | tf_op jit(solution)/shard_map/ppermute | solution.py:24
  52.3 10.3 %copy-start.12 = (bf16[512,256]{1,0:T(8,128)(2,1)S(1)}, bf16[512,256]{1,0:T(8,128)(2,1)}, u32[]{:S(2)}) copy-start(bf16[512,256]{1,0:T(8,128)(2,1)} %get-tuple-element.107) | copy-start | bytes 786436
  52.3 10.3 %copy-start.13 = (bf16[512,256]{1,0:T(8,128)(2,1)S(1)}, bf16[512,256]{1,0:T(8,128)(2,1)}, u32[]{:S(2)}) copy-start(bf16[512,256]{1,0:T(8,128)(2,1)} %get-tuple-element.108) | copy-start | bytes 786436
  52.3 10.3 %copy-start.14 = (bf16[512,256]{1,0:T(8,128)(2,1)S(1)}, bf16[512,256]{1,0:T(8,128)(2,1)}, u32[]{:S(2)}) copy-start(bf16[512,256]{1,0:T(8,128)(2,1)} %get-tuple-element.109) | copy-start | bytes 786436
  52.3 10.3 %copy-start.15 = (bf16[512,256]{1,0:T(8,128)(2,1)S(1)}, bf16[512,256]{1,0:T(8,128)(2,1)}, u32[]{:S(2)}) copy-start(bf16[512,256]{1,0:T(8,128)(2,1)} %get-tuple-element.110) | copy-start | bytes 786436
  53.0 5.5 %collective-permute-start.16 = (bf16[64,512]{1,0:T(8,128)(2,1)S(1)}, bf16[64,512]{1,0:T(8,128)(2,1)S(1)}, u32[]{:S(2)}, u32[]{:S(2)}) collective-permute-start(bf16[64,512]{1,0:T(8,128)(2,1)S(1)} %get-tuple-element.112), channel_id=1, source_target_pairs={{0,12},{4,8},{8,4},{12,0},{16,28},{20,24},{24,20},{28,16},{1,13},{... | collective-permute-start | bytes 196616 | tf_op jit(solution)/shard_map/ppermute | solution.py:24
  55.1 4.3 %collective-permute-start.15 = (bf16[64,512]{1,0:T(8,128)(2,1)S(1)}, bf16[64,512]{1,0:T(8,128)(2,1)S(1)}, u32[]{:S(2)}, u32[]{:S(2)}) collective-permute-start(bf16[64,512]{1,0:T(8,128)(2,1)S(1)} %get-tuple-element.113), channel_id=1, source_target_pairs={{0,8},{4,12},{8,0},{12,4},{16,24},{20,28},{24,16},{28,20},{1,9},{5... | collective-permute-start | bytes 196616 | tf_op jit(solution)/shard_map/ppermute | solution.py:24
  55.6 4.3 %collective-permute-start.14 = (bf16[64,512]{1,0:T(8,128)(2,1)S(1)}, bf16[64,512]{1,0:T(8,128)(2,1)S(1)}, u32[]{:S(2)}, u32[]{:S(2)}) collective-permute-start(bf16[64,512]{1,0:T(8,128)(2,1)S(1)} %get-tuple-element.111), channel_id=1, source_target_pairs={{0,4},{4,0},{8,12},{12,8},{16,20},{20,16},{24,28},{28,24},{1,5},{5... | collective-permute-start | bytes 196616 | tf_op jit(solution)/shard_map/ppermute | solution.py:24
  59.9 4.9 %collective-permute-start.17 = (bf16[64,256]{1,0:T(8,128)(2,1)S(1)}, bf16[64,256]{1,0:T(8,128)(2,1)S(1)}, u32[]{:S(2)}, u32[]{:S(2)}) collective-permute-start(bf16[64,256]{1,0:T(8,128)(2,1)S(1)} %slice.127), channel_id=1, source_target_pairs={{0,16},{4,20},{8,24},{12,28},{16,0},{20,4},{24,8},{28,12},{1,17},{... | collective-permute-start | bytes 98312 | tf_op jit(solution)/shard_map/ppermute | solution.py:24
  62.6 18.7 %copy-start.9 = (bf16[1024,1024]{1,0:T(8,128)(2,1)S(1)}, bf16[1024,1024]{1,0:T(8,128)(2,1)}, u32[]{:S(2)}) copy-start(bf16[1024,1024]{1,0:T(8,128)(2,1)} %param.26) | copy-start | bytes 6291460
  64.8 1.3 collective-permute-start.18
  66.4 4.9 %collective-permute-start.21 = (bf16[64,256]{1,0:T(8,128)(2,1)S(1)}, bf16[64,256]{1,0:T(8,128)(2,1)S(1)}, u32[]{:S(2)}, u32[]{:S(2)}) collective-permute-start(bf16[64,256]{1,0:T(8,128)(2,1)S(1)} %get-tuple-element.118), channel_id=1, source_target_pairs={{0,12},{4,8},{8,4},{12,0},{16,28},{20,24},{24,20},{28,16},{1,13},{... | collective-permute-start | bytes 98312 | tf_op jit(solution)/shard_map/ppermute | solution.py:24
  68.4 3.9 %collective-permute-start.20 = (bf16[64,256]{1,0:T(8,128)(2,1)S(1)}, bf16[64,256]{1,0:T(8,128)(2,1)S(1)}, u32[]{:S(2)}, u32[]{:S(2)}) collective-permute-start(bf16[64,256]{1,0:T(8,128)(2,1)S(1)} %get-tuple-element.119), channel_id=1, source_target_pairs={{0,8},{4,12},{8,0},{12,4},{16,24},{20,28},{24,16},{28,20},{1,9},{5... | collective-permute-start | bytes 98312 | tf_op jit(solution)/shard_map/ppermute | solution.py:24
  68.9 3.9 %collective-permute-start.19 = (bf16[64,256]{1,0:T(8,128)(2,1)S(1)}, bf16[64,256]{1,0:T(8,128)(2,1)S(1)}, u32[]{:S(2)}, u32[]{:S(2)}) collective-permute-start(bf16[64,256]{1,0:T(8,128)(2,1)S(1)} %get-tuple-element.117), channel_id=1, source_target_pairs={{0,4},{4,0},{8,12},{12,8},{16,20},{20,16},{24,28},{28,24},{1,5},{5... | collective-permute-start | bytes 98312 | tf_op jit(solution)/shard_map/ppermute | solution.py:24
  72.8 4.9 %collective-permute-start.22 = (bf16[64,256]{1,0:T(8,128)(2,1)S(1)}, bf16[64,256]{1,0:T(8,128)(2,1)S(1)}, u32[]{:S(2)}, u32[]{:S(2)}) collective-permute-start(bf16[64,256]{1,0:T(8,128)(2,1)S(1)} %fusion.17), channel_id=1, source_target_pairs={{0,16},{4,20},{8,24},{12,28},{16,0},{20,4},{24,8},{28,12},{1,17},{... | collective-permute-start | bytes 98312 | tf_op jit(solution)/shard_map/ppermute | solution.py:24
  77.7 26.1 %copy-start.2 = (bf16[1024,1024]{1,0:T(8,128)(2,1)S(1)}, bf16[1024,1024]{1,0:T(8,128)(2,1)}, u32[]{:S(2)}) copy-start(bf16[1024,1024]{1,0:T(8,128)(2,1)} %refs_9_.3) | copy-start | bytes 6291460
  77.7 4.9 %collective-permute-start.25 = (bf16[64,256]{1,0:T(8,128)(2,1)S(1)}, bf16[64,256]{1,0:T(8,128)(2,1)S(1)}, u32[]{:S(2)}, u32[]{:S(2)}) collective-permute-start(bf16[64,256]{1,0:T(8,128)(2,1)S(1)} %add_convert_fusion.2), channel_id=1, source_target_pairs={{0,12},{4,8},{8,4},{12,0},{16,28},{20,24},{24,20},{28,16},{1,13},{... | collective-permute-start | bytes 98312 | tf_op jit(solution)/shard_map/ppermute | solution.py:24
  79.9 3.9 %collective-permute-start.24 = (bf16[64,256]{1,0:T(8,128)(2,1)S(1)}, bf16[64,256]{1,0:T(8,128)(2,1)S(1)}, u32[]{:S(2)}, u32[]{:S(2)}) collective-permute-start(bf16[64,256]{1,0:T(8,128)(2,1)S(1)} %add_convert_fusion.2), channel_id=1, source_target_pairs={{0,8},{4,12},{8,0},{12,4},{16,24},{20,28},{24,16},{28,20},{1,9},{5... | collective-permute-start | bytes 98312 | tf_op jit(solution)/shard_map/ppermute | solution.py:24
  80.4 3.9 %collective-permute-start.23 = (bf16[64,256]{1,0:T(8,128)(2,1)S(1)}, bf16[64,256]{1,0:T(8,128)(2,1)S(1)}, u32[]{:S(2)}, u32[]{:S(2)}) collective-permute-start(bf16[64,256]{1,0:T(8,128)(2,1)S(1)} %add_convert_fusion.2), channel_id=1, source_target_pairs={{0,4},{4,0},{8,12},{12,8},{16,20},{20,16},{24,28},{28,24},{1,5},{5... | collective-permute-start | bytes 98312 | tf_op jit(solution)/shard_map/ppermute | solution.py:24
  84.5 25.2 %copy-start.1 = (bf16[2048,1024]{1,0:T(8,128)(2,1)S(1)}, bf16[2048,1024]{1,0:T(8,128)(2,1)}, u32[]{:S(2)}) copy-start(bf16[2048,1024]{1,0:T(8,128)(2,1)} %refs_9_.5) | copy-start | bytes 12582916
  84.5 1.3 collective-permute-start.26
  86.1 4.0 %collective-permute-start.27 = (bf16[64,256]{1,0:T(8,128)(2,1)S(1)}, bf16[64,256]{1,0:T(8,128)(2,1)S(1)}, u32[]{:S(2)}, u32[]{:S(2)}) collective-permute-start(bf16[64,256]{1,0:T(8,128)(2,1)S(1)} %fusion.4), channel_id=1, source_target_pairs={{0,2},{1,3},{2,0},{3,1},{4,6},{5,7},{6,4},{7,5},{8,10},{9,11},{10,... | collective-permute-start | bytes 98312 | tf_op jit(solution)/shard_map/ppermute | solution.py:24
  90.0 4.9 %collective-permute-start.28 = (bf16[64,256]{1,0:T(8,128)(2,1)S(1)}, bf16[64,256]{1,0:T(8,128)(2,1)S(1)}, u32[]{:S(2)}, u32[]{:S(2)}) collective-permute-start(bf16[64,256]{1,0:T(8,128)(2,1)S(1)} %get-tuple-element.123), channel_id=1, source_target_pairs={{0,16},{4,20},{8,24},{12,28},{16,0},{20,4},{24,8},{28,12},{1,17},{... | collective-permute-start | bytes 98312 | tf_op jit(solution)/shard_map/ppermute | solution.py:24
  94.9 4.9 %collective-permute-start.29 = (bf16[64,512]{1,0:T(8,128)(2,1)S(1)}, bf16[64,512]{1,0:T(8,128)(2,1)S(1)}, u32[]{:S(2)}, u32[]{:S(2)}) collective-permute-start(bf16[64,512]{1,0:T(8,128)(2,1)S(1)} %pad_maximum_fusion.3.refs_0_), channel_id=1, source_target_pairs={{0,4},{4,0},{8,12},{12,8},{16,20},{20,16},{24,28},{28,24},{1,5},{5... | collective-permute-start | bytes 196616 | tf_op jit(solution)/shard_map/ppermute | solution.py:24
  95.9 4.3 %collective-permute-start.30 = (bf16[64,512]{1,0:T(8,128)(2,1)S(1)}, bf16[64,512]{1,0:T(8,128)(2,1)S(1)}, u32[]{:S(2)}, u32[]{:S(2)}) collective-permute-start(bf16[64,512]{1,0:T(8,128)(2,1)S(1)} %pad_maximum_fusion.3.refs_0_), channel_id=1, source_target_pairs={{0,8},{4,12},{8,0},{12,4},{16,24},{20,28},{24,16},{28,20},{1,9},{5... | collective-permute-start | bytes 196616 | tf_op jit(solution)/shard_map/ppermute | solution.py:24
  97.4 5.2 %collective-permute-start.31 = (bf16[64,512]{1,0:T(8,128)(2,1)S(1)}, bf16[64,512]{1,0:T(8,128)(2,1)S(1)}, u32[]{:S(2)}, u32[]{:S(2)}) collective-permute-start(bf16[64,512]{1,0:T(8,128)(2,1)S(1)} %pad_maximum_fusion.3.refs_0_), channel_id=1, source_target_pairs={{0,12},{4,8},{8,4},{12,0},{16,28},{20,24},{24,20},{28,16},{1,13},{... | collective-permute-start | bytes 196616 | tf_op jit(solution)/shard_map/ppermute | solution.py:24
  98.4 4.2 %collective-permute-start.32 = (bf16[64,512]{1,0:T(8,128)(2,1)S(1)}, bf16[64,512]{1,0:T(8,128)(2,1)S(1)}, u32[]{:S(2)}, u32[]{:S(2)}) collective-permute-start(bf16[64,512]{1,0:T(8,128)(2,1)S(1)} %pad_maximum_fusion.3.refs_0_), channel_id=1, source_target_pairs={{0,1},{1,0},{2,3},{3,2},{4,5},{5,4},{6,7},{7,6},{8,9},{9,8},{10,11... | collective-permute-start | bytes 196616 | tf_op jit(solution)/shard_map/ppermute | solution.py:24
  99.8 2.8 %collective-permute-start.33 = (bf16[64,512]{1,0:T(8,128)(2,1)S(1)}, bf16[64,512]{1,0:T(8,128)(2,1)S(1)}, u32[]{:S(2)}, u32[]{:S(2)}) collective-permute-start(bf16[64,512]{1,0:T(8,128)(2,1)S(1)} %collective-permute-done.29.refs_1_), channel_id=1, source_target_pairs={{0,1},{1,0},{2,3},{3,2},{4,5},{5,4},{6,7},{7,6},{8,9},{9,8},{10,11... | collective-permute-start | bytes 196616 | tf_op jit(solution)/shard_map/ppermute | solution.py:24
  100.1 2.5 %collective-permute-start.34 = (bf16[64,512]{1,0:T(8,128)(2,1)S(1)}, bf16[64,512]{1,0:T(8,128)(2,1)S(1)}, u32[]{:S(2)}, u32[]{:S(2)}) collective-permute-start(bf16[64,512]{1,0:T(8,128)(2,1)S(1)} %collective-permute-done.30.refs_2_), channel_id=1, source_target_pairs={{0,1},{1,0},{2,3},{3,2},{4,5},{5,4},{6,7},{7,6},{8,9},{9,8},{10,11... | collective-permute-start | bytes 196616 | tf_op jit(solution)/shard_map/ppermute | solution.py:24
  102.6 1.3 collective-permute-start.35
  106.0 7.7 %collective-permute-start.38 = (bf16[64,1024]{1,0:T(8,128)(2,1)S(1)}, bf16[64,1024]{1,0:T(8,128)(2,1)S(1)}, u32[]{:S(2)}, u32[]{:S(2)}) collective-permute-start(bf16[64,1024]{1,0:T(8,128)(2,1)S(1)} %convert_element_type.225), channel_id=1, source_target_pairs={{0,12},{4,8},{8,4},{12,0},{16,28},{20,24},{24,20},{28,16},{1,13},{... | collective-permute-start | bytes 393224 | tf_op jit(solution)/shard_map/ppermute | solution.py:24
  107.1 7.9 %collective-permute-start.37 = (bf16[64,1024]{1,0:T(8,128)(2,1)S(1)}, bf16[64,1024]{1,0:T(8,128)(2,1)S(1)}, u32[]{:S(2)}, u32[]{:S(2)}) collective-permute-start(bf16[64,1024]{1,0:T(8,128)(2,1)S(1)} %convert_element_type.225), channel_id=1, source_target_pairs={{0,8},{4,12},{8,0},{12,4},{16,24},{20,28},{24,16},{28,20},{1,9},{5... | collective-permute-start | bytes 393224 | tf_op jit(solution)/shard_map/ppermute | solution.py:24
  108.7 6.7 %collective-permute-start.36 = (bf16[64,1024]{1,0:T(8,128)(2,1)S(1)}, bf16[64,1024]{1,0:T(8,128)(2,1)S(1)}, u32[]{:S(2)}, u32[]{:S(2)}) collective-permute-start(bf16[64,1024]{1,0:T(8,128)(2,1)S(1)} %convert_element_type.225), channel_id=1, source_target_pairs={{0,4},{4,0},{8,12},{12,8},{16,20},{20,16},{24,28},{28,24},{1,5},{5... | collective-permute-start | bytes 393224 | tf_op jit(solution)/shard_map/ppermute | solution.py:24
  115.4 13.3 %copy-start.5 = (bf16[1024,2048]{1,0:T(8,128)(2,1)S(1)}, bf16[1024,2048]{1,0:T(8,128)(2,1)}, u32[]{:S(2)}) copy-start(bf16[1024,2048]{1,0:T(8,128)(2,1)} %param.27) | copy-start | bytes 12582916
  115.8 1.4 collective-permute-start.39
  117.5 4.3 %collective-permute-start.40 = (bf16[64,512]{1,0:T(8,128)(2,1)S(1)}, bf16[64,512]{1,0:T(8,128)(2,1)S(1)}, u32[]{:S(2)}, u32[]{:S(2)}) collective-permute-start(bf16[64,512]{1,0:T(8,128)(2,1)S(1)} %fusion.3), channel_id=1, source_target_pairs={{0,2},{1,3},{2,0},{3,1},{4,6},{5,7},{6,4},{7,5},{8,10},{9,11},{10,... | collective-permute-start | bytes 196616 | tf_op jit(solution)/shard_map/ppermute | solution.py:24
  121.9 4.9 %collective-permute-start.41 = (bf16[64,512]{1,0:T(8,128)(2,1)S(1)}, bf16[64,512]{1,0:T(8,128)(2,1)S(1)}, u32[]{:S(2)}, u32[]{:S(2)}) collective-permute-start(bf16[64,512]{1,0:T(8,128)(2,1)S(1)} %convert_element_type.234.refs_0_), channel_id=1, source_target_pairs={{0,4},{4,0},{8,12},{12,8},{16,20},{20,16},{24,28},{28,24},{1,5},{5... | collective-permute-start | bytes 196616 | tf_op jit(solution)/shard_map/ppermute | solution.py:24
  123.0 4.3 %collective-permute-start.42 = (bf16[64,512]{1,0:T(8,128)(2,1)S(1)}, bf16[64,512]{1,0:T(8,128)(2,1)S(1)}, u32[]{:S(2)}, u32[]{:S(2)}) collective-permute-start(bf16[64,512]{1,0:T(8,128)(2,1)S(1)} %convert_element_type.234.refs_0_), channel_id=1, source_target_pairs={{0,8},{4,12},{8,0},{12,4},{16,24},{20,28},{24,16},{28,20},{1,9},{5... | collective-permute-start | bytes 196616 | tf_op jit(solution)/shard_map/ppermute | solution.py:24
  123.5 5.2 %collective-permute-start.43 = (bf16[64,512]{1,0:T(8,128)(2,1)S(1)}, bf16[64,512]{1,0:T(8,128)(2,1)S(1)}, u32[]{:S(2)}, u32[]{:S(2)}) collective-permute-start(bf16[64,512]{1,0:T(8,128)(2,1)S(1)} %convert_element_type.234.refs_0_), channel_id=1, source_target_pairs={{0,12},{4,8},{8,4},{12,0},{16,28},{20,24},{24,20},{28,16},{1,13},{... | collective-permute-start | bytes 196616 | tf_op jit(solution)/shard_map/ppermute | solution.py:24
  125.4 4.5 %collective-permute-start.44 = (bf16[64,512]{1,0:T(8,128)(2,1)S(1)}, bf16[64,512]{1,0:T(8,128)(2,1)S(1)}, u32[]{:S(2)}, u32[]{:S(2)}) collective-permute-start(bf16[64,512]{1,0:T(8,128)(2,1)S(1)} %convert_element_type.234.refs_0_), channel_id=1, source_target_pairs={{0,1},{1,0},{2,3},{3,2},{4,5},{5,4},{6,7},{7,6},{8,9},{9,8},{10,11... | collective-permute-start | bytes 196616 | tf_op jit(solution)/shard_map/ppermute | solution.py:24
  125.4 3.8 %collective-permute-start.48 = (f32[64,256]{1,0:T(8,128)S(1)}, f32[64,256]{1,0:T(8,128)S(1)}, u32[]{:S(2)}, u32[]{:S(2)}) collective-permute-start(f32[64,256]{1,0:T(8,128)S(1)} %get-tuple-element.68.own_ref), channel_id=1, source_target_pairs={{0,1},{1,0},{2,3},{3,2},{4,5},{5,4},{6,7},{7,6},{8,9},{9,8},{10,11... | collective-permute-start | bytes 196616 | tf_op jit(solution)/shard_map/ppermute | solution.py:24
  126.8 3.1 %collective-permute-start.45 = (bf16[64,512]{1,0:T(8,128)(2,1)S(1)}, bf16[64,512]{1,0:T(8,128)(2,1)S(1)}, u32[]{:S(2)}, u32[]{:S(2)}) collective-permute-start(bf16[64,512]{1,0:T(8,128)(2,1)S(1)} %collective-permute-done.41.refs_1_), channel_id=1, source_target_pairs={{0,1},{1,0},{2,3},{3,2},{4,5},{5,4},{6,7},{7,6},{8,9},{9,8},{10,11... | collective-permute-start | bytes 196616 | tf_op jit(solution)/shard_map/ppermute | solution.py:24
  127.3 2.6 %collective-permute-start.46 = (bf16[64,512]{1,0:T(8,128)(2,1)S(1)}, bf16[64,512]{1,0:T(8,128)(2,1)S(1)}, u32[]{:S(2)}, u32[]{:S(2)}) collective-permute-start(bf16[64,512]{1,0:T(8,128)(2,1)S(1)} %collective-permute-done.42.refs_2_), channel_id=1, source_target_pairs={{0,1},{1,0},{2,3},{3,2},{4,5},{5,4},{6,7},{7,6},{8,9},{9,8},{10,11... | collective-permute-start | bytes 196616 | tf_op jit(solution)/shard_map/ppermute | solution.py:24
  128.6 1.3 collective-permute-start.47
  129.9 10.8 %copy-start.7 = (f32[64,1024]{1,0:T(8,128)S(1)}, f32[64,1024]{1,0:T(8,128)}, u32[]{:S(2)}) copy-start(f32[64,1024]{1,0:T(8,128)} %copy-done.6) | copy-start | bytes 786436
  134.0 6.0 %collective-permute-start.49 = (bf16[64,1024]{1,0:T(8,128)(2,1)S(1)}, bf16[64,1024]{1,0:T(8,128)(2,1)S(1)}, u32[]{:S(2)}, u32[]{:S(2)}) collective-permute-start(bf16[64,1024]{1,0:T(8,128)(2,1)S(1)} %add.292), channel_id=1, source_target_pairs={{0,4},{4,0},{8,12},{12,8},{16,20},{20,16},{24,28},{28,24},{1,5},{5... | collective-permute-start | bytes 393224 | tf_op jit(solution)/shard_map/ppermute | solution.py:24
  135.0 5.0 %collective-permute-start.50 = (f32[64,512]{1,0:T(8,128)S(1)}, f32[64,512]{1,0:T(8,128)S(1)}, u32[]{:S(2)}, u32[]{:S(2)}) collective-permute-start(f32[64,512]{1,0:T(8,128)S(1)} %convert_add_fusion.5.own_ref), channel_id=1, source_target_pairs={{0,1},{1,0},{2,3},{3,2},{4,5},{5,4},{6,7},{7,6},{8,9},{9,8},{10,11... | collective-permute-start | bytes 393224 | tf_op jit(solution)/shard_map/ppermute | solution.py:24
  141.3 1.6 %collective-permute-start.51 = (f32[64,1024]{1,0:T(8,128)S(1)}, f32[64,1024]{1,0:T(8,128)S(1)}, u32[]{:S(2)}, u32[]{:S(2)}) collective-permute-start(f32[64,1024]{1,0:T(8,128)S(1)} %fusion.75), channel_id=1, source_target_pairs={{0,1},{1,0},{2,3},{3,2},{4,5},{5,4},{6,7},{7,6},{8,9},{9,8},{10,11... | collective-permute-start | bytes 786440 | tf_op jit(solution)/shard_map/ppermute | solution.py:24
  143.4 5.6 %collective-permute-start.52 = (bf16[64,1024]{1,0:T(8,128)(2,1)S(1)}, bf16[64,1024]{1,0:T(8,128)(2,1)S(1)}, u32[]{:S(2)}, u32[]{:S(2)}) collective-permute-start(bf16[64,1024]{1,0:T(8,128)(2,1)S(1)} %fusion.1), channel_id=1, source_target_pairs={{0,2},{1,3},{2,0},{3,1},{4,6},{5,7},{6,4},{7,5},{8,10},{9,11},{10,... | collective-permute-start | bytes 393224 | tf_op jit(solution)/shard_map/ppermute | solution.py:24
  149.0 1.6 %collective-permute-start.53 = (f32[64,1024]{1,0:T(8,128)S(1)}, f32[64,1024]{1,0:T(8,128)S(1)}, u32[]{:S(2)}, u32[]{:S(2)}) collective-permute-start(f32[64,1024]{1,0:T(8,128)S(1)} %convert_add_fusion.2.own_ref), channel_id=1, source_target_pairs={{0,1},{1,0},{2,3},{3,2},{4,5},{5,4},{6,7},{7,6},{8,9},{9,8},{10,11... | collective-permute-start | bytes 786440 | tf_op jit(solution)/shard_map/ppermute | solution.py:24
  (8 other events, 42.4 us)

commit v4 on v3

--- a/solution.py
+++ b/solution.py
@@ -109,7 +109,7 @@
         + [pl.BlockSpec((1, step), lambda i: (0, i)), pl.BlockSpec((step, width), lambda i: (i, 0))],
         out_specs=pl.BlockSpec((rows, width), lambda i: (0, 0)),
         out_shape=jax.ShapeDtypeStruct((rows, width), F32),
-        compiler_params=pltpu.CompilerParams(vmem_limit_bytes=16 << 20),
+        compiler_params=pltpu.CompilerParams(vmem_limit_bytes=12 << 20),
         cost_estimate=pl.CostEstimate(
             flops=2 * rows * count * (extent + width), bytes_accessed=2 * count * (width + 2 * extent), transcendentals=0
         ),
@@ -131,7 +131,7 @@
     return pl.pallas_call(
         functools.partial(put_kernel, first=first),
         out_shape=jax.ShapeDtypeStruct((rows, width), dtype),
-        compiler_params=pltpu.CompilerParams(vmem_limit_bytes=16 << 20),
+        compiler_params=pltpu.CompilerParams(vmem_limit_bytes=6 << 20),
         cost_estimate=pl.CostEstimate(flops=2 * rows * count * width, bytes_accessed=4 * rows * width, transcendentals=0),
     )(update, place)
 
@@ -161,8 +161,8 @@
             out_specs=pl.BlockSpec((rows, width), lambda i, core: (0, i)),
         ),
         out_shape=jax.ShapeDtypeStruct((rows, 2 * width), own.dtype),
-        compiler_params=pltpu.CompilerParams(vmem_limit_bytes=16 << 20),
-        cost_estimate=pl.CostEstimate(flops=0, bytes_accessed=4 * own.size * own.dtype.itemsize, transcendentals=0),
+        compiler_params=pltpu.CompilerParams(vmem_limit_bytes=4 << 20),
+        cost_estimate=pl.CostEstimate(flops=0, bytes_accessed=32 * own.size * own.dtype.itemsize, transcendentals=0),
     )(core[None], own, other)
 
 
@@ -242,17 +242,18 @@
     place_root = jnp.where(is_root, split_place(index, 0), -1)
     place_up = split_place(own_index(1), 0)
     put_one, put_root, put_up = tied(*(half_of(p, core, 0)[None, :] for p in (place_one, place_root, place_up)))
-    y_two = exchange_sum(dot(rhs_two.astype(BF16), pivot_two), "leaf", groups[2])
+    y_two = exchange_sum(dot(rhs_two.astype(BF16), pivot_two), "leaf", groups[2]).astype(BF16)
     y_two, keep, send = tied(y_two, *halves(lower_two))
     low = y_two.astype(BF16)
     other = partner(dot(low, send), "front", 1)
-    total = dot(low, keep) + other
+    total, other = tied(dot(low, keep), other)
+    total = total + other
     update = exchange_sum(total, "front", away).astype(BF16)
     update, rhs_half = tied(update, own_half(rhs_one))
     keep, send = put_halves(update, put_one)
 
     half = (rhs_half - row_total(keep, send, 1)).astype(BF16)
-    y_one = exchange_sum(dot(both_halves(half), pivot_one), "leaf", groups[1])
+    y_one = exchange_sum(dot(both_halves(half), pivot_one), "leaf", groups[1]).astype(BF16)
     y_one, root_keep, root_send, keep, send = tied(y_one, *put_halves(update, put_root), *halves(lower_one))
     low = y_one.astype(BF16)
     total = partner(dot(low, send), "front", 1)
@@ -279,14 +280,14 @@
     coupling = exchange_sum(picked_product(known_zero, place_up, upper_one), "leaf", groups[1])
     coupling, coupling_root = tied(coupling, picked_product(known_zero, place_root, upper_two))
     z_one = y_one - coupling
-    x_one = front_half(z_one.astype(BF16), split_one)
-    x_one, x_zero = tied(x_one, x_zero)
+    z_one, x_zero = tied(z_one.astype(BF16), x_zero)
+    x_one, solution_zero = tied(front_half(z_one, split_one), outputs(x_zero))
     known_one = known_pieces(x_one, groups[1])
-    *known_one, solution_zero, keep, send = tied(*known_one, outputs(x_zero), *halves(back_two))
+    *known_one, keep, send = tied(*known_one, *halves(back_two))
 
     coupling = coupling_root + picked_product(known_one, place_one, upper_two)
-    coupling, x_one = tied(coupling, x_one)
-    coupling, solution_one = tied(exchange_sum(coupling, "leaf", groups[2]), outputs(x_one))
+    coupling, other = tied(coupling, partner(x_one, "front", 1))
+    coupling, solution_one = tied(exchange_sum(coupling, "leaf", groups[2]), join(x_one, other, core))
     x_two = front_half((y_two - coupling).astype(BF16), (keep, send))
     return solution_zero, solution_one, outputs(x_two)
 

time: 152 us -> 148 us (0.974)
  waiting for transfers between devices: 59.7 us -> 58 us
  matrix products: 9.23 us -> 7.64 us
    ppermute x54, waiting for transfers between devices: 59.7 us -> 58 us  [partner(): lax.ppermute(x, axis, [(i, i ^ mask) for i in range(lax.axis_size(axis))])]
    dot_general x13, matrix products: 9.23 us -> 7.64 us  [dot(): return jnp.dot(left, right, preferred_element_type=F32)]
  transfers between devices with their start and end apart: 54 -> 54, of which waited for: 42 -> 43; matrix products, arithmetic and copies ran while one was open for 6% -> 7% of each run, Pallas kernels for 6% -> 10%
where the time goes in v4:
time: 148 us
  waiting for transfers between devices  58 us (39%)
  starting transfers between devices  50.3 us (34%)
  Pallas kernels  19.4 us (13%)
  matrix products  7.64 us (5%)
  local copies, waits for them, and re-layouts  6.37 us (4%)
  other arithmetic  4.81 us (3%)
    ppermute x54, waiting for transfers between devices, partner(): lax.ppermute(x, axis, [(i, i ^ mask) for i in range(lax.axis_size(axis))])  58 us
    ppermute x54, starting transfers between devices, partner(): lax.ppermute(x, axis, [(i, i ^ mask) for i in range(lax.axis_size(axis))])  50.3 us
    pallas_call x3, Pallas kernels, picked_product(): pl.pallas_call(pick_kernel, grid=(count // step,), in_specs=[pl.BlockSpec...  10.1 us
    dot_general x13, matrix products, dot(): return jnp.dot(left, right, preferred_element_type=F32)  7.64 us
    pallas_call x6, Pallas kernels, put_columns(): pl.pallas_call(functools.partial(put_kernel, first=first), out_shape=jax....  7.09 us
    dynamic_slice x6, local copies, waits for them, and re-layouts, half_of(): return lax.dynamic_slice_in_dim(x, which * size, size, dim)  5.13 us
  transfers between devices with their start and end apart: 54, of which 43 were waited for; matrix products, arithmetic and copies ran while one was open for 7% of the time, Pallas kernels for 10%

profile of v4, /device:TPU:0, one launch (start us, length us, event | category | flops | bytes accessed | tf_op | source)
XLA Modules:
  0.0 147.8 jit_solution(10997854393834772033)
XLA Ops:
  0.6 3.3 %convolution_convert_fusion = bf16[64,1024]{1,0:T(8,128)(2,1)S(1)} fusion(bf16[2048,1024]{1,0:T(8,128)(2,1)} %param.20, f32[64,2048]{1,0:T(8,128)} %param.17), kind=kOutput, calls=%fused_computation.2 | convolution fusion | flops 268632064 | bytes 4849664 | tf_op jit(solution)/shard_map/dot_general | solution.py:15
  4.0 3.0 %collective-permute-start = (bf16[64,1024]{1,0:T(8,128)(2,1)S(1)}, bf16[64,1024]{1,0:T(8,128)(2,1)S(1)}, u32[]{:S(2)}, u32[]{:S(2)}) collective-permute-start(bf16[64,1024]{1,0:T(8,128)(2,1)S(1)} %convolution_convert_fusion), channel_id=1, source_target_pairs={{0,4},{4,0},{8,12},{12,8},{16,20},{20,16},{24,28},{28,24},{1,5},{5... | collective-permute-start | bytes 393224 | tf_op jit(solution)/shard_map/ppermute | solution.py:24
  7.0 0.9 compare_select_fusion
  9.0 2.7 %constant_dynamic-slice_fusion.16 = (bf16[1024,1024]{1,0:T(8,128)(2,1)S(1)}, bf16[1024,1024]{1,0:T(8,128)(2,1)S(1)}) fusion(bf16[1024,2048]{1,0:T(8,128)(2,1)} %param.22, s32[]{:T(128)S(6)} %select_n.171, s32[]{:T(128)S(6)} %select_n.170), kind=kLoop, calls=%fused_computation.137 | loop fusion | bytes 8388616 | tf_op jit(solution)/shard_map/dynamic_slice | solution.py:205
  12.7 1.0 collective-permute-done.1
  13.8 1.6 %collective-permute-start.2 = (bf16[64,1024]{1,0:T(8,128)(2,1)S(1)}, bf16[64,1024]{1,0:T(8,128)(2,1)S(1)}, u32[]{:S(2)}, u32[]{:S(2)}) collective-permute-start(bf16[64,1024]{1,0:T(8,128)(2,1)S(1)} %add_convert_fusion.2), channel_id=1, source_target_pairs={{0,2},{1,3},{2,0},{3,1},{4,6},{5,7},{6,4},{7,5},{8,10},{9,11},{10,... | collective-permute-start | bytes 393224 | tf_op jit(solution)/shard_map/ppermute | solution.py:24
  15.4 4.0 %collective-permute-done.2 = bf16[64,1024]{1,0:T(8,128)(2,1)S(1)} collective-permute-done((bf16[64,1024]{1,0:T(8,128)(2,1)S(1)}, bf16[64,1024]{1,0:T(8,128)(2,1)S(1)}, u32[]{:S(2)}, u32[]{:S(2)}) %collective-permute-start.2) | collective-permute-done | bytes 131104 | tf_op jit(solution)/shard_map/ppermute | solution.py:24
  19.5 1.4 shard_map.167
  20.9 1.4 shard_map.166
  22.5 1.7 %collective-permute-start.6 = (bf16[64,512]{1,0:T(8,128)(2,1)S(1)}, bf16[64,512]{1,0:T(8,128)(2,1)S(1)}, u32[]{:S(2)}, u32[]{:S(2)}) collective-permute-start(bf16[64,512]{1,0:T(8,128)(2,1)S(1)} %get-tuple-element.121), channel_id=1, source_target_pairs={{0,12},{4,8},{8,4},{12,0},{16,28},{20,24},{24,20},{28,16},{1,13},{... | collective-permute-start | bytes 196616 | tf_op jit(solution)/shard_map/ppermute | solution.py:24
  24.7 1.4 collective-permute-start.4
  26.1 1.9 %collective-permute-done.6 = bf16[64,512]{1,0:T(8,128)(2,1)S(1)} collective-permute-done((bf16[64,512]{1,0:T(8,128)(2,1)S(1)}, bf16[64,512]{1,0:T(8,128)(2,1)S(1)}, u32[]{:S(2)}, u32[]{:S(2)}) %collective-permute-start.6) | collective-permute-done | bytes 65568 | tf_op jit(solution)/shard_map/ppermute | solution.py:24
  29.4 1.2 collective-permute-done.7
  31.2 2.2 %collective-permute-start.10 = (bf16[64,1024]{1,0:T(8,128)(2,1)S(1)}, bf16[64,1024]{1,0:T(8,128)(2,1)S(1)}, u32[]{:S(2)}, u32[]{:S(2)}) collective-permute-start(bf16[64,1024]{1,0:T(8,128)(2,1)S(1)} %convolution_convert_fusion.1), channel_id=1, source_target_pairs={{0,12},{4,8},{8,4},{12,0},{16,28},{20,24},{24,20},{28,16},{1,13},{... | collective-permute-start | bytes 393224 | tf_op jit(solution)/shard_map/ppermute | solution.py:24
  34.7 1.5 %constant_dynamic-slice_fusion.14 = (bf16[1024,512]{1,0:T(8,128)(2,1)}, bf16[1024,512]{1,0:T(8,128)(2,1)}) fusion(bf16[1024,1024]{1,0:T(8,128)(2,1)S(1)} %copy-done.6, s32[]{:T(128)S(6)} %select_n.191, s32[]{:T(128)S(6)} %select_n.188), kind=kLoop, calls=%fused_computation.135 | loop fusion | bytes 4194312 | tf_op jit(solution)/shard_map/dynamic_slice | solution.py:205
  36.3 1.4 shard_map.168
  37.7 1.4 shard_map.169
  39.1 1.2 collective-permute-done.9
  40.6 1.0 add_convert_fusion
  43.7 1.6 %collective-permute-start.12 = (bf16[64,512]{1,0:T(8,128)(2,1)S(1)}, bf16[64,512]{1,0:T(8,128)(2,1)S(1)}, u32[]{:S(2)}, u32[]{:S(2)}) collective-permute-start(bf16[64,512]{1,0:T(8,128)(2,1)S(1)} %fusion.1), channel_id=1, source_target_pairs={{0,2},{1,3},{2,0},{3,1},{4,6},{5,7},{6,4},{7,5},{8,10},{9,11},{10,... | collective-permute-start | bytes 196616 | tf_op jit(solution)/shard_map/ppermute | solution.py:24
  45.2 1.0 constant_dynamic-slice_fusion.13
  46.3 1.7 %collective-permute-done.12 = bf16[64,512]{1,0:T(8,128)(2,1)S(1)} collective-permute-done((bf16[64,512]{1,0:T(8,128)(2,1)S(1)}, bf16[64,512]{1,0:T(8,128)(2,1)S(1)}, u32[]{:S(2)}, u32[]{:S(2)}) %collective-permute-start.12) | collective-permute-done | bytes 65568 | tf_op jit(solution)/shard_map/ppermute | solution.py:24
  50.6 2.2 %collective-permute-start.16 = (bf16[64,512]{1,0:T(8,128)(2,1)S(1)}, bf16[64,512]{1,0:T(8,128)(2,1)S(1)}, u32[]{:S(2)}, u32[]{:S(2)}) collective-permute-start(bf16[64,512]{1,0:T(8,128)(2,1)S(1)} %get-tuple-element.118), channel_id=1, source_target_pairs={{0,12},{4,8},{8,4},{12,0},{16,28},{20,24},{24,20},{28,16},{1,13},{... | collective-permute-start | bytes 196616 | tf_op jit(solution)/shard_map/ppermute | solution.py:24
  54.2 1.9 %collective-permute-done.16 = bf16[64,512]{1,0:T(8,128)(2,1)S(1)} collective-permute-done((bf16[64,512]{1,0:T(8,128)(2,1)S(1)}, bf16[64,512]{1,0:T(8,128)(2,1)S(1)}, u32[]{:S(2)}, u32[]{:S(2)}) %collective-permute-start.16) | collective-permute-done | bytes 65568 | tf_op jit(solution)/shard_map/ppermute | solution.py:24
  57.5 2.7 %collective-permute-start.17 = (bf16[64,256]{1,0:T(8,128)(2,1)S(1)}, bf16[64,256]{1,0:T(8,128)(2,1)S(1)}, u32[]{:S(2)}, u32[]{:S(2)}) collective-permute-start(bf16[64,256]{1,0:T(8,128)(2,1)S(1)} %slice.127), channel_id=1, source_target_pairs={{0,16},{4,20},{8,24},{12,28},{16,0},{20,4},{24,8},{28,12},{1,17},{... | collective-permute-start | bytes 98312 | tf_op jit(solution)/shard_map/ppermute | solution.py:24
  60.3 2.1 %collective-permute-done.17 = bf16[64,256]{1,0:T(8,128)(2,1)S(1)} collective-permute-done((bf16[64,256]{1,0:T(8,128)(2,1)S(1)}, bf16[64,256]{1,0:T(8,128)(2,1)S(1)}, u32[]{:S(2)}, u32[]{:S(2)}) %collective-permute-start.17) | collective-permute-done | bytes 32800 | tf_op jit(solution)/shard_map/ppermute | solution.py:24
  62.5 1.2 collective-permute-done.18
  64.0 2.0 %collective-permute-start.21 = (bf16[64,256]{1,0:T(8,128)(2,1)S(1)}, bf16[64,256]{1,0:T(8,128)(2,1)S(1)}, u32[]{:S(2)}, u32[]{:S(2)}) collective-permute-start(bf16[64,256]{1,0:T(8,128)(2,1)S(1)} %get-tuple-element.124), channel_id=1, source_target_pairs={{0,12},{4,8},{8,4},{12,0},{16,28},{20,24},{24,20},{28,16},{1,13},{... | collective-permute-start | bytes 98312 | tf_op jit(solution)/shard_map/ppermute | solution.py:24
  66.5 1.1 collective-permute-start.19
  67.6 1.3 collective-permute-done.21
  68.9 1.0 collective-permute-done.20
  70.4 2.7 %collective-permute-start.22 = (bf16[64,256]{1,0:T(8,128)(2,1)S(1)}, bf16[64,256]{1,0:T(8,128)(2,1)S(1)}, u32[]{:S(2)}, u32[]{:S(2)}) collective-permute-start(bf16[64,256]{1,0:T(8,128)(2,1)S(1)} %fusion.16), channel_id=1, source_target_pairs={{0,16},{4,20},{8,24},{12,28},{16,0},{20,4},{24,8},{28,12},{1,17},{... | collective-permute-start | bytes 98312 | tf_op jit(solution)/shard_map/ppermute | solution.py:24
  73.1 2.2 %collective-permute-done.22 = bf16[64,256]{1,0:T(8,128)(2,1)S(1)} collective-permute-done((bf16[64,256]{1,0:T(8,128)(2,1)S(1)}, bf16[64,256]{1,0:T(8,128)(2,1)S(1)}, u32[]{:S(2)}, u32[]{:S(2)}) %collective-permute-start.22) | collective-permute-done | bytes 32800 | tf_op jit(solution)/shard_map/ppermute | solution.py:24
  75.3 2.2 %collective-permute-start.25 = (bf16[64,256]{1,0:T(8,128)(2,1)S(1)}, bf16[64,256]{1,0:T(8,128)(2,1)S(1)}, u32[]{:S(2)}, u32[]{:S(2)}) collective-permute-start(bf16[64,256]{1,0:T(8,128)(2,1)S(1)} %add_convert_fusion.5), channel_id=1, source_target_pairs={{0,12},{4,8},{8,4},{12,0},{16,28},{20,24},{24,20},{28,16},{1,13},{... | collective-permute-start | bytes 98312 | tf_op jit(solution)/shard_map/ppermute | solution.py:24
  79.1 1.1 collective-permute-done.25
  80.2 1.2 collective-permute-done.24
  82.2 1.2 collective-permute-done.26
  83.7 1.6 %collective-permute-start.27 = (bf16[64,256]{1,0:T(8,128)(2,1)S(1)}, bf16[64,256]{1,0:T(8,128)(2,1)S(1)}, u32[]{:S(2)}, u32[]{:S(2)}) collective-permute-start(bf16[64,256]{1,0:T(8,128)(2,1)S(1)} %fusion.3), channel_id=1, source_target_pairs={{0,2},{1,3},{2,0},{3,1},{4,6},{5,7},{6,4},{7,5},{8,10},{9,11},{10,... | collective-permute-start | bytes 98312 | tf_op jit(solution)/shard_map/ppermute | solution.py:24
  85.2 2.4 %collective-permute-done.27 = bf16[64,256]{1,0:T(8,128)(2,1)S(1)} collective-permute-done((bf16[64,256]{1,0:T(8,128)(2,1)S(1)}, bf16[64,256]{1,0:T(8,128)(2,1)S(1)}, u32[]{:S(2)}, u32[]{:S(2)}) %collective-permute-start.27) | collective-permute-done | bytes 32800 | tf_op jit(solution)/shard_map/ppermute | solution.py:24
  87.6 2.7 %collective-permute-start.28 = (bf16[64,256]{1,0:T(8,128)(2,1)S(1)}, bf16[64,256]{1,0:T(8,128)(2,1)S(1)}, u32[]{:S(2)}, u32[]{:S(2)}) collective-permute-start(bf16[64,256]{1,0:T(8,128)(2,1)S(1)} %get-tuple-element.129), channel_id=1, source_target_pairs={{0,16},{4,20},{8,24},{12,28},{16,0},{20,4},{24,8},{28,12},{1,17},{... | collective-permute-start | bytes 98312 | tf_op jit(solution)/shard_map/ppermute | solution.py:24
  90.3 2.2 %collective-permute-done.28 = bf16[64,256]{1,0:T(8,128)(2,1)S(1)} collective-permute-done((bf16[64,256]{1,0:T(8,128)(2,1)S(1)}, bf16[64,256]{1,0:T(8,128)(2,1)S(1)}, u32[]{:S(2)}, u32[]{:S(2)}) %collective-permute-start.28) | collective-permute-done | bytes 32800 | tf_op jit(solution)/shard_map/ppermute | solution.py:24
  92.5 0.9 collective-permute-start.29
  93.5 1.6 %collective-permute-start.30 = (bf16[64,512]{1,0:T(8,128)(2,1)S(1)}, bf16[64,512]{1,0:T(8,128)(2,1)S(1)}, u32[]{:S(2)}, u32[]{:S(2)}) collective-permute-start(bf16[64,512]{1,0:T(8,128)(2,1)S(1)} %pad_maximum_fusion.3.refs_0_), channel_id=1, source_target_pairs={{0,8},{4,12},{8,0},{12,4},{16,24},{20,28},{24,16},{28,20},{1,9},{5... | collective-permute-start | bytes 196616 | tf_op jit(solution)/shard_map/ppermute | solution.py:24
  95.0 1.0 collective-permute-start.31
  96.0 1.4 collective-permute-done.29.refs_1_
  98.0 2.2 %collective-permute-done.31.refs_3_ = bf16[64,512]{1,0:T(8,128)(2,1)S(1)} collective-permute-done((bf16[64,512]{1,0:T(8,128)(2,1)S(1)}, bf16[64,512]{1,0:T(8,128)(2,1)S(1)}, u32[]{:S(2)}, u32[]{:S(2)}) %collective-permute-start.31) | collective-permute-done | bytes 65568 | tf_op jit(solution)/shard_map/ppermute | solution.py:24
  100.2 1.2 collective-permute-done.35.refs_7_
  101.5 2.1 %shard_map.172 = f32[64,1024]{1,0:T(8,128)S(1)} custom-call(bf16[64,512]{1,0:T(8,128)(2,1)S(1)} %pad_maximum_fusion.3.refs_0_, bf16[64,512]{1,0:T(8,128)(2,1)S(1)} %collective-permute-done.29.refs_1_, bf16[64,512]{1,0:T(8,128)(2,1)S(1)} %collective-permute-done.30.refs_2_, bf16[64,512]{1,0:T(8,128)(2,1)S(1)} %collective-permute-done.31.refs_3_, ...), custom_call_target="tpu_custom_call" | custom-call | flops 671088640 | bytes 18874368 | tf_op jit(solution)/shard_map/pallas_call | solution.py:105
  103.6 1.0 collective-permute-start.38
  104.7 1.6 %collective-permute-start.37 = (bf16[64,1024]{1,0:T(8,128)(2,1)S(1)}, bf16[64,1024]{1,0:T(8,128)(2,1)S(1)}, u32[]{:S(2)}, u32[]{:S(2)}) collective-permute-start(bf16[64,1024]{1,0:T(8,128)(2,1)S(1)} %convert_element_type.232), channel_id=1, source_target_pairs={{0,8},{4,12},{8,0},{12,4},{16,24},{20,28},{24,16},{28,20},{1,9},{5... | collective-permute-start | bytes 393224 | tf_op jit(solution)/shard_map/ppermute | solution.py:24
  107.3 4.0 %shard_map.173 = f32[64,1024]{1,0:T(8,128)S(1)} custom-call(bf16[64,512]{1,0:T(8,128)(2,1)S(1)} %pad_maximum_fusion.3.refs_0_, bf16[64,512]{1,0:T(8,128)(2,1)S(1)} %collective-permute-done.29.refs_1_, bf16[64,512]{1,0:T(8,128)(2,1)S(1)} %collective-permute-done.30.refs_2_, bf16[64,512]{1,0:T(8,128)(2,1)S(1)} %collective-permute-done.31.refs_3_, ...), custom_call_target="tpu_custom_call" | custom-call | flops 1342177280 | bytes 37748736 | tf_op jit(solution)/shard_map/pallas_call | solution.py:105
  111.3 1.3 collective-permute-done.37
  115.1 1.6 %collective-permute-start.40 = (bf16[64,512]{1,0:T(8,128)(2,1)S(1)}, bf16[64,512]{1,0:T(8,128)(2,1)S(1)}, u32[]{:S(2)}, u32[]{:S(2)}) collective-permute-start(bf16[64,512]{1,0:T(8,128)(2,1)S(1)} %fusion.2), channel_id=1, source_target_pairs={{0,2},{1,3},{2,0},{3,1},{4,6},{5,7},{6,4},{7,5},{8,10},{9,11},{10,... | collective-permute-start | bytes 196616 | tf_op jit(solution)/shard_map/ppermute | solution.py:24
  117.3 2.1 %collective-permute-done.40 = bf16[64,512]{1,0:T(8,128)(2,1)S(1)} collective-permute-done((bf16[64,512]{1,0:T(8,128)(2,1)S(1)}, bf16[64,512]{1,0:T(8,128)(2,1)S(1)}, u32[]{:S(2)}, u32[]{:S(2)}) %collective-permute-start.40) | collective-permute-done | bytes 65568 | tf_op jit(solution)/shard_map/ppermute | solution.py:24
  119.4 1.2 collective-permute-start.42
  121.0 1.9 %collective-permute-start.44 = (bf16[64,512]{1,0:T(8,128)(2,1)S(1)}, bf16[64,512]{1,0:T(8,128)(2,1)S(1)}, u32[]{:S(2)}, u32[]{:S(2)}) collective-permute-start(bf16[64,512]{1,0:T(8,128)(2,1)S(1)} %convert_element_type.241.refs_0_), channel_id=1, source_target_pairs={{0,12},{4,8},{8,4},{12,0},{16,28},{20,24},{24,20},{28,16},{1,13},{... | collective-permute-start | bytes 196616 | tf_op jit(solution)/shard_map/ppermute | solution.py:24
  124.9 1.3 collective-permute-done.44.refs_3_
  127.5 4.0 %shard_map.175 = f32[64,1024]{1,0:T(8,128)S(1)} custom-call(bf16[64,512]{1,0:T(8,128)(2,1)S(1)} %convert_element_type.241.refs_0_, bf16[64,512]{1,0:T(8,128)(2,1)S(1)} %collective-permute-done.42.refs_1_, bf16[64,512]{1,0:T(8,128)(2,1)S(1)} %collective-permute-done.43.refs_2_, bf16[64,512]{1,0:T(8,128)(2,1)S(1)} %collective-permute-done.44.refs_3_, ...), custom_call_target="tpu_custom_call" | custom-call | flops 1342177280 | bytes 37748736 | tf_op jit(solution)/shard_map/pallas_call | solution.py:105
  131.5 1.0 collective-permute-start.50
  133.2 3.9 %collective-permute-done.50 = bf16[64,1024]{1,0:T(8,128)(2,1)S(1)} collective-permute-done((bf16[64,1024]{1,0:T(8,128)(2,1)S(1)}, bf16[64,1024]{1,0:T(8,128)(2,1)S(1)}, u32[]{:S(2)}, u32[]{:S(2)}) %collective-permute-start.50) | collective-permute-done | bytes 131104 | tf_op jit(solution)/shard_map/ppermute | solution.py:24
  137.7 1.5 %collective-permute-done.51 = f32[64,1024]{1,0:T(8,128)S(1)} collective-permute-done((f32[64,1024]{1,0:T(8,128)S(1)}, f32[64,1024]{1,0:T(8,128)S(1)}, u32[]{:S(2)}, u32[]{:S(2)}) %collective-permute-start.51) | collective-permute-done | bytes 262176 | tf_op jit(solution)/shard_map/ppermute | solution.py:24
  139.8 1.6 %collective-permute-start.52 = (bf16[64,1024]{1,0:T(8,128)(2,1)S(1)}, bf16[64,1024]{1,0:T(8,128)(2,1)S(1)}, u32[]{:S(2)}, u32[]{:S(2)}) collective-permute-start(bf16[64,1024]{1,0:T(8,128)(2,1)S(1)} %fusion), channel_id=1, source_target_pairs={{0,2},{1,3},{2,0},{3,1},{4,6},{5,7},{6,4},{7,5},{8,10},{9,11},{10,... | collective-permute-start | bytes 393224 | tf_op jit(solution)/shard_map/ppermute | solution.py:24
  141.4 4.0 %collective-permute-done.52 = bf16[64,1024]{1,0:T(8,128)(2,1)S(1)} collective-permute-done((bf16[64,1024]{1,0:T(8,128)(2,1)S(1)}, bf16[64,1024]{1,0:T(8,128)(2,1)S(1)}, u32[]{:S(2)}, u32[]{:S(2)}) %collective-permute-start.52) | collective-permute-done | bytes 131104 | tf_op jit(solution)/shard_map/ppermute | solution.py:24
  145.5 1.5 %collective-permute-done.53.other_ref = f32[64,1024]{1,0:T(8,128)S(1)} collective-permute-done((f32[64,1024]{1,0:T(8,128)S(1)}, f32[64,1024]{1,0:T(8,128)S(1)}, u32[]{:S(2)}, u32[]{:S(2)}) %collective-permute-start.53) | collective-permute-done | bytes 262176 | tf_op jit(solution)/shard_map/ppermute | solution.py:24
  (151 shorter events, 28.9 us)
Async XLA Ops:
  0.6 30.0 %copy-start = (bf16[1024,1024]{1,0:T(8,128)(2,1)S(1)}, bf16[1024,1024]{1,0:T(8,128)(2,1)}, u32[]{:S(2)}) copy-start(bf16[1024,1024]{1,0:T(8,128)(2,1)} %param.19) | copy-start | bytes 6291460
  4.0 7.6 %collective-permute-start = (bf16[64,1024]{1,0:T(8,128)(2,1)S(1)}, bf16[64,1024]{1,0:T(8,128)(2,1)S(1)}, u32[]{:S(2)}, u32[]{:S(2)}) collective-permute-start(bf16[64,1024]{1,0:T(8,128)(2,1)S(1)} %convolution_convert_fusion), channel_id=1, source_target_pairs={{0,4},{4,0},{8,12},{12,8},{16,20},{20,16},{24,28},{28,24},{1,5},{5... | collective-permute-start | bytes 393224 | tf_op jit(solution)/shard_map/ppermute | solution.py:24
  12.2 1.6 %collective-permute-start.1 = (f32[64,1024]{1,0:T(8,128)S(1)}, f32[64,1024]{1,0:T(8,128)S(1)}, u32[]{:S(2)}, u32[]{:S(2)}) collective-permute-start(f32[64,1024]{1,0:T(8,128)S(1)} %fusion.68), channel_id=1, source_target_pairs={{0,1},{1,0},{2,3},{3,2},{4,5},{5,4},{6,7},{7,6},{8,9},{9,8},{10,11... | collective-permute-start | bytes 786440 | tf_op jit(solution)/shard_map/ppermute | solution.py:24
  13.8 5.6 %collective-permute-start.2 = (bf16[64,1024]{1,0:T(8,128)(2,1)S(1)}, bf16[64,1024]{1,0:T(8,128)(2,1)S(1)}, u32[]{:S(2)}, u32[]{:S(2)}) collective-permute-start(bf16[64,1024]{1,0:T(8,128)(2,1)S(1)} %add_convert_fusion.2), channel_id=1, source_target_pairs={{0,2},{1,3},{2,0},{3,1},{4,6},{5,7},{6,4},{7,5},{8,10},{9,11},{10,... | collective-permute-start | bytes 393224 | tf_op jit(solution)/shard_map/ppermute | solution.py:24
  20.8 1.6 %collective-permute-start.3 = (bf16[64,2048]{1,0:T(8,128)(2,1)S(1)}, bf16[64,2048]{1,0:T(8,128)(2,1)S(1)}, u32[]{:S(2)}, u32[]{:S(2)}) collective-permute-start(bf16[64,2048]{1,0:T(8,128)(2,1)S(1)} %shard_map.167), channel_id=1, source_target_pairs={{0,1},{1,0},{2,3},{3,2},{4,5},{5,4},{6,7},{7,6},{8,9},{9,8},{10,11... | collective-permute-start | bytes 786440 | tf_op jit(solution)/shard_map/ppermute | solution.py:24
  22.5 5.5 %collective-permute-start.6 = (bf16[64,512]{1,0:T(8,128)(2,1)S(1)}, bf16[64,512]{1,0:T(8,128)(2,1)S(1)}, u32[]{:S(2)}, u32[]{:S(2)}) collective-permute-start(bf16[64,512]{1,0:T(8,128)(2,1)S(1)} %get-tuple-element.121), channel_id=1, source_target_pairs={{0,12},{4,8},{8,4},{12,0},{16,28},{20,24},{24,20},{28,16},{1,13},{... | collective-permute-start | bytes 196616 | tf_op jit(solution)/shard_map/ppermute | solution.py:24
  24.2 4.3 %collective-permute-start.5 = (bf16[64,512]{1,0:T(8,128)(2,1)S(1)}, bf16[64,512]{1,0:T(8,128)(2,1)S(1)}, u32[]{:S(2)}, u32[]{:S(2)}) collective-permute-start(bf16[64,512]{1,0:T(8,128)(2,1)S(1)} %get-tuple-element.122), channel_id=1, source_target_pairs={{0,8},{4,12},{8,0},{12,4},{16,24},{20,28},{24,16},{28,20},{1,9},{5... | collective-permute-start | bytes 196616 | tf_op jit(solution)/shard_map/ppermute | solution.py:24
  24.7 4.6 %collective-permute-start.4 = (bf16[64,512]{1,0:T(8,128)(2,1)S(1)}, bf16[64,512]{1,0:T(8,128)(2,1)S(1)}, u32[]{:S(2)}, u32[]{:S(2)}) collective-permute-start(bf16[64,512]{1,0:T(8,128)(2,1)S(1)} %get-tuple-element.120), channel_id=1, source_target_pairs={{0,4},{4,0},{8,12},{12,8},{16,20},{20,16},{24,28},{28,24},{1,5},{5... | collective-permute-start | bytes 196616 | tf_op jit(solution)/shard_map/ppermute | solution.py:24
  29.3 1.3 collective-permute-start.7
  31.2 7.9 %collective-permute-start.10 = (bf16[64,1024]{1,0:T(8,128)(2,1)S(1)}, bf16[64,1024]{1,0:T(8,128)(2,1)S(1)}, u32[]{:S(2)}, u32[]{:S(2)}) collective-permute-start(bf16[64,1024]{1,0:T(8,128)(2,1)S(1)} %convolution_convert_fusion.1), channel_id=1, source_target_pairs={{0,12},{4,8},{8,4},{12,0},{16,28},{20,24},{24,20},{28,16},{1,13},{... | collective-permute-start | bytes 393224 | tf_op jit(solution)/shard_map/ppermute | solution.py:24
  33.3 6.9 %collective-permute-start.9 = (bf16[64,1024]{1,0:T(8,128)(2,1)S(1)}, bf16[64,1024]{1,0:T(8,128)(2,1)}, u32[]{:S(2)}, u32[]{:S(2)}) collective-permute-start(bf16[64,1024]{1,0:T(8,128)(2,1)S(1)} %convolution_convert_fusion.1), channel_id=1, source_target_pairs={{0,8},{4,12},{8,0},{12,4},{16,24},{20,28},{24,16},{28,20},{1,9},{5... | collective-permute-start | bytes 393224 | tf_op jit(solution)/shard_map/ppermute | solution.py:24
  33.8 6.8 %collective-permute-start.8 = (bf16[64,1024]{1,0:T(8,128)(2,1)S(1)}, bf16[64,1024]{1,0:T(8,128)(2,1)}, u32[]{:S(2)}, u32[]{:S(2)}) collective-permute-start(bf16[64,1024]{1,0:T(8,128)(2,1)S(1)} %convolution_convert_fusion.1), channel_id=1, source_target_pairs={{0,4},{4,0},{8,12},{12,8},{16,20},{20,16},{24,28},{28,24},{1,5},{5... | collective-permute-start | bytes 393224 | tf_op jit(solution)/shard_map/ppermute | solution.py:24
  41.9 1.4 collective-permute-start.11
  43.7 4.3 %collective-permute-start.12 = (bf16[64,512]{1,0:T(8,128)(2,1)S(1)}, bf16[64,512]{1,0:T(8,128)(2,1)S(1)}, u32[]{:S(2)}, u32[]{:S(2)}) collective-permute-start(bf16[64,512]{1,0:T(8,128)(2,1)S(1)} %fusion.1), channel_id=1, source_target_pairs={{0,2},{1,3},{2,0},{3,1},{4,6},{5,7},{6,4},{7,5},{8,10},{9,11},{10,... | collective-permute-start | bytes 196616 | tf_op jit(solution)/shard_map/ppermute | solution.py:24
  48.8 1.6 %collective-permute-start.13 = (bf16[64,2048]{1,0:T(8,128)(2,1)S(1)}, bf16[64,2048]{1,0:T(8,128)(2,1)S(1)}, u32[]{:S(2)}, u32[]{:S(2)}) collective-permute-start(bf16[64,2048]{1,0:T(8,128)(2,1)S(1)} %add.260), channel_id=1, source_target_pairs={{0,1},{1,0},{2,3},{3,2},{4,5},{5,4},{6,7},{7,6},{8,9},{9,8},{10,11... | collective-permute-start | bytes 786440 | tf_op jit(solution)/shard_map/ppermute | solution.py:24
  49.9 10.3 %copy-start.10 = (bf16[512,256]{1,0:T(8,128)(2,1)S(1)}, bf16[512,256]{1,0:T(8,128)(2,1)}, u32[]{:S(2)}) copy-start(bf16[512,256]{1,0:T(8,128)(2,1)} %get-tuple-element.113) | copy-start | bytes 786436
  49.9 10.3 %copy-start.11 = (bf16[512,256]{1,0:T(8,128)(2,1)S(1)}, bf16[512,256]{1,0:T(8,128)(2,1)}, u32[]{:S(2)}) copy-start(bf16[512,256]{1,0:T(8,128)(2,1)} %get-tuple-element.114) | copy-start | bytes 786436
  49.9 10.3 %copy-start.12 = (bf16[512,256]{1,0:T(8,128)(2,1)S(1)}, bf16[512,256]{1,0:T(8,128)(2,1)}, u32[]{:S(2)}) copy-start(bf16[512,256]{1,0:T(8,128)(2,1)} %get-tuple-element.115) | copy-start | bytes 786436
  49.9 10.3 %copy-start.13 = (bf16[512,256]{1,0:T(8,128)(2,1)S(1)}, bf16[512,256]{1,0:T(8,128)(2,1)}, u32[]{:S(2)}) copy-start(bf16[512,256]{1,0:T(8,128)(2,1)} %get-tuple-element.116) | copy-start | bytes 786436
  50.6 5.5 %collective-permute-start.16 = (bf16[64,512]{1,0:T(8,128)(2,1)S(1)}, bf16[64,512]{1,0:T(8,128)(2,1)S(1)}, u32[]{:S(2)}, u32[]{:S(2)}) collective-permute-start(bf16[64,512]{1,0:T(8,128)(2,1)S(1)} %get-tuple-element.118), channel_id=1, source_target_pairs={{0,12},{4,8},{8,4},{12,0},{16,28},{20,24},{24,20},{28,16},{1,13},{... | collective-permute-start | bytes 196616 | tf_op jit(solution)/shard_map/ppermute | solution.py:24
  52.7 4.3 %collective-permute-start.15 = (bf16[64,512]{1,0:T(8,128)(2,1)S(1)}, bf16[64,512]{1,0:T(8,128)(2,1)S(1)}, u32[]{:S(2)}, u32[]{:S(2)}) collective-permute-start(bf16[64,512]{1,0:T(8,128)(2,1)S(1)} %get-tuple-element.119), channel_id=1, source_target_pairs={{0,8},{4,12},{8,0},{12,4},{16,24},{20,28},{24,16},{28,20},{1,9},{5... | collective-permute-start | bytes 196616 | tf_op jit(solution)/shard_map/ppermute | solution.py:24
  53.2 4.3 %collective-permute-start.14 = (bf16[64,512]{1,0:T(8,128)(2,1)S(1)}, bf16[64,512]{1,0:T(8,128)(2,1)S(1)}, u32[]{:S(2)}, u32[]{:S(2)}) collective-permute-start(bf16[64,512]{1,0:T(8,128)(2,1)S(1)} %get-tuple-element.117), channel_id=1, source_target_pairs={{0,4},{4,0},{8,12},{12,8},{16,20},{20,16},{24,28},{28,24},{1,5},{5... | collective-permute-start | bytes 196616 | tf_op jit(solution)/shard_map/ppermute | solution.py:24
  57.5 4.9 %collective-permute-start.17 = (bf16[64,256]{1,0:T(8,128)(2,1)S(1)}, bf16[64,256]{1,0:T(8,128)(2,1)S(1)}, u32[]{:S(2)}, u32[]{:S(2)}) collective-permute-start(bf16[64,256]{1,0:T(8,128)(2,1)S(1)} %slice.127), channel_id=1, source_target_pairs={{0,16},{4,20},{8,24},{12,28},{16,0},{20,4},{24,8},{28,12},{1,17},{... | collective-permute-start | bytes 98312 | tf_op jit(solution)/shard_map/ppermute | solution.py:24
  60.2 18.7 %copy-start.7 = (bf16[1024,1024]{1,0:T(8,128)(2,1)S(1)}, bf16[1024,1024]{1,0:T(8,128)(2,1)}, u32[]{:S(2)}) copy-start(bf16[1024,1024]{1,0:T(8,128)(2,1)} %param.26) | copy-start | bytes 6291460
  62.4 1.3 collective-permute-start.18
  64.0 4.9 %collective-permute-start.21 = (bf16[64,256]{1,0:T(8,128)(2,1)S(1)}, bf16[64,256]{1,0:T(8,128)(2,1)S(1)}, u32[]{:S(2)}, u32[]{:S(2)}) collective-permute-start(bf16[64,256]{1,0:T(8,128)(2,1)S(1)} %get-tuple-element.124), channel_id=1, source_target_pairs={{0,12},{4,8},{8,4},{12,0},{16,28},{20,24},{24,20},{28,16},{1,13},{... | collective-permute-start | bytes 98312 | tf_op jit(solution)/shard_map/ppermute | solution.py:24
  66.0 3.9 %collective-permute-start.20 = (bf16[64,256]{1,0:T(8,128)(2,1)S(1)}, bf16[64,256]{1,0:T(8,128)(2,1)S(1)}, u32[]{:S(2)}, u32[]{:S(2)}) collective-permute-start(bf16[64,256]{1,0:T(8,128)(2,1)S(1)} %get-tuple-element.125), channel_id=1, source_target_pairs={{0,8},{4,12},{8,0},{12,4},{16,24},{20,28},{24,16},{28,20},{1,9},{5... | collective-permute-start | bytes 98312 | tf_op jit(solution)/shard_map/ppermute | solution.py:24
  66.5 3.9 %collective-permute-start.19 = (bf16[64,256]{1,0:T(8,128)(2,1)S(1)}, bf16[64,256]{1,0:T(8,128)(2,1)S(1)}, u32[]{:S(2)}, u32[]{:S(2)}) collective-permute-start(bf16[64,256]{1,0:T(8,128)(2,1)S(1)} %get-tuple-element.123), channel_id=1, source_target_pairs={{0,4},{4,0},{8,12},{12,8},{16,20},{20,16},{24,28},{28,24},{1,5},{5... | collective-permute-start | bytes 98312 | tf_op jit(solution)/shard_map/ppermute | solution.py:24
  70.4 4.9 %collective-permute-start.22 = (bf16[64,256]{1,0:T(8,128)(2,1)S(1)}, bf16[64,256]{1,0:T(8,128)(2,1)S(1)}, u32[]{:S(2)}, u32[]{:S(2)}) collective-permute-start(bf16[64,256]{1,0:T(8,128)(2,1)S(1)} %fusion.16), channel_id=1, source_target_pairs={{0,16},{4,20},{8,24},{12,28},{16,0},{20,4},{24,8},{28,12},{1,17},{... | collective-permute-start | bytes 98312 | tf_op jit(solution)/shard_map/ppermute | solution.py:24
  75.3 26.2 %copy-start.2 = (bf16[1024,1024]{1,0:T(8,128)(2,1)S(1)}, bf16[1024,1024]{1,0:T(8,128)(2,1)}, u32[]{:S(2)}) copy-start(bf16[1024,1024]{1,0:T(8,128)(2,1)} %refs_9_.3) | copy-start | bytes 6291460
  75.3 4.9 %collective-permute-start.25 = (bf16[64,256]{1,0:T(8,128)(2,1)S(1)}, bf16[64,256]{1,0:T(8,128)(2,1)S(1)}, u32[]{:S(2)}, u32[]{:S(2)}) collective-permute-start(bf16[64,256]{1,0:T(8,128)(2,1)S(1)} %add_convert_fusion.5), channel_id=1, source_target_pairs={{0,12},{4,8},{8,4},{12,0},{16,28},{20,24},{24,20},{28,16},{1,13},{... | collective-permute-start | bytes 98312 | tf_op jit(solution)/shard_map/ppermute | solution.py:24
  77.5 3.9 %collective-permute-start.24 = (bf16[64,256]{1,0:T(8,128)(2,1)S(1)}, bf16[64,256]{1,0:T(8,128)(2,1)S(1)}, u32[]{:S(2)}, u32[]{:S(2)}) collective-permute-start(bf16[64,256]{1,0:T(8,128)(2,1)S(1)} %add_convert_fusion.5), channel_id=1, source_target_pairs={{0,8},{4,12},{8,0},{12,4},{16,24},{20,28},{24,16},{28,20},{1,9},{5... | collective-permute-start | bytes 98312 | tf_op jit(solution)/shard_map/ppermute | solution.py:24
  77.9 3.9 %collective-permute-start.23 = (bf16[64,256]{1,0:T(8,128)(2,1)S(1)}, bf16[64,256]{1,0:T(8,128)(2,1)S(1)}, u32[]{:S(2)}, u32[]{:S(2)}) collective-permute-start(bf16[64,256]{1,0:T(8,128)(2,1)S(1)} %add_convert_fusion.5), channel_id=1, source_target_pairs={{0,4},{4,0},{8,12},{12,8},{16,20},{20,16},{24,28},{28,24},{1,5},{5... | collective-permute-start | bytes 98312 | tf_op jit(solution)/shard_map/ppermute | solution.py:24
  82.1 25.1 %copy-start.16 = (s32[1,2048]{1,0:T(1,128)S(1)}, s32[1,2048]{1,0:T(1,128)}, u32[]{:S(2)}) copy-start(s32[1,2048]{1,0:T(1,128)} %copy-done.15) | copy-start | bytes 24580
  82.1 25.2 %copy-start.1 = (bf16[2048,1024]{1,0:T(8,128)(2,1)S(1)}, bf16[2048,1024]{1,0:T(8,128)(2,1)}, u32[]{:S(2)}) copy-start(bf16[2048,1024]{1,0:T(8,128)(2,1)} %refs_9_.5) | copy-start | bytes 12582916
  82.1 1.3 collective-permute-start.26
  83.7 4.0 %collective-permute-start.27 = (bf16[64,256]{1,0:T(8,128)(2,1)S(1)}, bf16[64,256]{1,0:T(8,128)(2,1)S(1)}, u32[]{:S(2)}, u32[]{:S(2)}) collective-permute-start(bf16[64,256]{1,0:T(8,128)(2,1)S(1)} %fusion.3), channel_id=1, source_target_pairs={{0,2},{1,3},{2,0},{3,1},{4,6},{5,7},{6,4},{7,5},{8,10},{9,11},{10,... | collective-permute-start | bytes 98312 | tf_op jit(solution)/shard_map/ppermute | solution.py:24
  87.6 4.9 %collective-permute-start.28 = (bf16[64,256]{1,0:T(8,128)(2,1)S(1)}, bf16[64,256]{1,0:T(8,128)(2,1)S(1)}, u32[]{:S(2)}, u32[]{:S(2)}) collective-permute-start(bf16[64,256]{1,0:T(8,128)(2,1)S(1)} %get-tuple-element.129), channel_id=1, source_target_pairs={{0,16},{4,20},{8,24},{12,28},{16,0},{20,4},{24,8},{28,12},{1,17},{... | collective-permute-start | bytes 98312 | tf_op jit(solution)/shard_map/ppermute | solution.py:24
  92.5 4.9 %collective-permute-start.29 = (bf16[64,512]{1,0:T(8,128)(2,1)S(1)}, bf16[64,512]{1,0:T(8,128)(2,1)S(1)}, u32[]{:S(2)}, u32[]{:S(2)}) collective-permute-start(bf16[64,512]{1,0:T(8,128)(2,1)S(1)} %pad_maximum_fusion.3.refs_0_), channel_id=1, source_target_pairs={{0,4},{4,0},{8,12},{12,8},{16,20},{20,16},{24,28},{28,24},{1,5},{5... | collective-permute-start | bytes 196616 | tf_op jit(solution)/shard_map/ppermute | solution.py:24
  93.5 4.3 %collective-permute-start.30 = (bf16[64,512]{1,0:T(8,128)(2,1)S(1)}, bf16[64,512]{1,0:T(8,128)(2,1)S(1)}, u32[]{:S(2)}, u32[]{:S(2)}) collective-permute-start(bf16[64,512]{1,0:T(8,128)(2,1)S(1)} %pad_maximum_fusion.3.refs_0_), channel_id=1, source_target_pairs={{0,8},{4,12},{8,0},{12,4},{16,24},{20,28},{24,16},{28,20},{1,9},{5... | collective-permute-start | bytes 196616 | tf_op jit(solution)/shard_map/ppermute | solution.py:24
  95.0 5.2 %collective-permute-start.31 = (bf16[64,512]{1,0:T(8,128)(2,1)S(1)}, bf16[64,512]{1,0:T(8,128)(2,1)S(1)}, u32[]{:S(2)}, u32[]{:S(2)}) collective-permute-start(bf16[64,512]{1,0:T(8,128)(2,1)S(1)} %pad_maximum_fusion.3.refs_0_), channel_id=1, source_target_pairs={{0,12},{4,8},{8,4},{12,0},{16,28},{20,24},{24,20},{28,16},{1,13},{... | collective-permute-start | bytes 196616 | tf_op jit(solution)/shard_map/ppermute | solution.py:24
  96.0 4.2 %collective-permute-start.32 = (bf16[64,512]{1,0:T(8,128)(2,1)S(1)}, bf16[64,512]{1,0:T(8,128)(2,1)S(1)}, u32[]{:S(2)}, u32[]{:S(2)}) collective-permute-start(bf16[64,512]{1,0:T(8,128)(2,1)S(1)} %pad_maximum_fusion.3.refs_0_), channel_id=1, source_target_pairs={{0,1},{1,0},{2,3},{3,2},{4,5},{5,4},{6,7},{7,6},{8,9},{9,8},{10,11... | collective-permute-start | bytes 196616 | tf_op jit(solution)/shard_map/ppermute | solution.py:24
  97.5 2.8 %collective-permute-start.33 = (bf16[64,512]{1,0:T(8,128)(2,1)S(1)}, bf16[64,512]{1,0:T(8,128)(2,1)S(1)}, u32[]{:S(2)}, u32[]{:S(2)}) collective-permute-start(bf16[64,512]{1,0:T(8,128)(2,1)S(1)} %collective-permute-done.29.refs_1_), channel_id=1, source_target_pairs={{0,1},{1,0},{2,3},{3,2},{4,5},{5,4},{6,7},{7,6},{8,9},{9,8},{10,11... | collective-permute-start | bytes 196616 | tf_op jit(solution)/shard_map/ppermute | solution.py:24
  97.7 2.5 %collective-permute-start.34 = (bf16[64,512]{1,0:T(8,128)(2,1)S(1)}, bf16[64,512]{1,0:T(8,128)(2,1)S(1)}, u32[]{:S(2)}, u32[]{:S(2)}) collective-permute-start(bf16[64,512]{1,0:T(8,128)(2,1)S(1)} %collective-permute-done.30.refs_2_), channel_id=1, source_target_pairs={{0,1},{1,0},{2,3},{3,2},{4,5},{5,4},{6,7},{7,6},{8,9},{9,8},{10,11... | collective-permute-start | bytes 196616 | tf_op jit(solution)/shard_map/ppermute | solution.py:24
  100.2 1.3 collective-permute-start.35
  103.6 7.7 %collective-permute-start.38 = (bf16[64,1024]{1,0:T(8,128)(2,1)S(1)}, bf16[64,1024]{1,0:T(8,128)(2,1)S(1)}, u32[]{:S(2)}, u32[]{:S(2)}) collective-permute-start(bf16[64,1024]{1,0:T(8,128)(2,1)S(1)} %convert_element_type.232), channel_id=1, source_target_pairs={{0,12},{4,8},{8,4},{12,0},{16,28},{20,24},{24,20},{28,16},{1,13},{... | collective-permute-start | bytes 393224 | tf_op jit(solution)/shard_map/ppermute | solution.py:24
  104.7 7.9 %collective-permute-start.37 = (bf16[64,1024]{1,0:T(8,128)(2,1)S(1)}, bf16[64,1024]{1,0:T(8,128)(2,1)S(1)}, u32[]{:S(2)}, u32[]{:S(2)}) collective-permute-start(bf16[64,1024]{1,0:T(8,128)(2,1)S(1)} %convert_element_type.232), channel_id=1, source_target_pairs={{0,8},{4,12},{8,0},{12,4},{16,24},{20,28},{24,16},{28,20},{1,9},{5... | collective-permute-start | bytes 393224 | tf_op jit(solution)/shard_map/ppermute | solution.py:24
  106.2 6.7 %collective-permute-start.36 = (bf16[64,1024]{1,0:T(8,128)(2,1)S(1)}, bf16[64,1024]{1,0:T(8,128)(2,1)S(1)}, u32[]{:S(2)}, u32[]{:S(2)}) collective-permute-start(bf16[64,1024]{1,0:T(8,128)(2,1)S(1)} %convert_element_type.232), channel_id=1, source_target_pairs={{0,4},{4,0},{8,12},{12,8},{16,20},{20,16},{24,28},{28,24},{1,5},{5... | collective-permute-start | bytes 393224 | tf_op jit(solution)/shard_map/ppermute | solution.py:24
  113.0 13.3 %copy-start.5 = (bf16[1024,2048]{1,0:T(8,128)(2,1)S(1)}, bf16[1024,2048]{1,0:T(8,128)(2,1)}, u32[]{:S(2)}) copy-start(bf16[1024,2048]{1,0:T(8,128)(2,1)} %param.27) | copy-start | bytes 12582916
  113.4 1.4 collective-permute-start.39
  113.4 3.2 %collective-permute-start.41 = (f32[64,256]{1,0:T(8,128)S(1)}, f32[64,256]{1,0:T(8,128)S(1)}, u32[]{:S(2)}, u32[]{:S(2)}) collective-permute-start(f32[64,256]{1,0:T(8,128)S(1)} %get-tuple-element.73.own_ref), channel_id=1, source_target_pairs={{0,1},{1,0},{2,3},{3,2},{4,5},{5,4},{6,7},{7,6},{8,9},{9,8},{10,11... | collective-permute-start | bytes 196616 | tf_op jit(solution)/shard_map/ppermute | solution.py:24
  115.1 4.3 %collective-permute-start.40 = (bf16[64,512]{1,0:T(8,128)(2,1)S(1)}, bf16[64,512]{1,0:T(8,128)(2,1)S(1)}, u32[]{:S(2)}, u32[]{:S(2)}) collective-permute-start(bf16[64,512]{1,0:T(8,128)(2,1)S(1)} %fusion.2), channel_id=1, source_target_pairs={{0,2},{1,3},{2,0},{3,1},{4,6},{5,7},{6,4},{7,5},{8,10},{9,11},{10,... | collective-permute-start | bytes 196616 | tf_op jit(solution)/shard_map/ppermute | solution.py:24
  119.4 4.9 %collective-permute-start.42 = (bf16[64,512]{1,0:T(8,128)(2,1)S(1)}, bf16[64,512]{1,0:T(8,128)(2,1)S(1)}, u32[]{:S(2)}, u32[]{:S(2)}) collective-permute-start(bf16[64,512]{1,0:T(8,128)(2,1)S(1)} %convert_element_type.241.refs_0_), channel_id=1, source_target_pairs={{0,4},{4,0},{8,12},{12,8},{16,20},{20,16},{24,28},{28,24},{1,5},{5... | collective-permute-start | bytes 196616 | tf_op jit(solution)/shard_map/ppermute | solution.py:24
  120.6 4.3 %collective-permute-start.43 = (bf16[64,512]{1,0:T(8,128)(2,1)S(1)}, bf16[64,512]{1,0:T(8,128)(2,1)S(1)}, u32[]{:S(2)}, u32[]{:S(2)}) collective-permute-start(bf16[64,512]{1,0:T(8,128)(2,1)S(1)} %convert_element_type.241.refs_0_), channel_id=1, source_target_pairs={{0,8},{4,12},{8,0},{12,4},{16,24},{20,28},{24,16},{28,20},{1,9},{5... | collective-permute-start | bytes 196616 | tf_op jit(solution)/shard_map/ppermute | solution.py:24
  121.0 5.2 %collective-permute-start.44 = (bf16[64,512]{1,0:T(8,128)(2,1)S(1)}, bf16[64,512]{1,0:T(8,128)(2,1)S(1)}, u32[]{:S(2)}, u32[]{:S(2)}) collective-permute-start(bf16[64,512]{1,0:T(8,128)(2,1)S(1)} %convert_element_type.241.refs_0_), channel_id=1, source_target_pairs={{0,12},{4,8},{8,4},{12,0},{16,28},{20,24},{24,20},{28,16},{1,13},{... | collective-permute-start | bytes 196616 | tf_op jit(solution)/shard_map/ppermute | solution.py:24
  123.0 3.8 %collective-permute-start.45 = (bf16[64,512]{1,0:T(8,128)(2,1)S(1)}, bf16[64,512]{1,0:T(8,128)(2,1)S(1)}, u32[]{:S(2)}, u32[]{:S(2)}) collective-permute-start(bf16[64,512]{1,0:T(8,128)(2,1)S(1)} %convert_element_type.241.refs_0_), channel_id=1, source_target_pairs={{0,1},{1,0},{2,3},{3,2},{4,5},{5,4},{6,7},{7,6},{8,9},{9,8},{10,11... | collective-permute-start | bytes 196616 | tf_op jit(solution)/shard_map/ppermute | solution.py:24
  123.0 8.5 %collective-permute-start.49 = (f32[64,512]{1,0:T(8,128)S(1)}, f32[64,512]{1,0:T(8,128)S(1)}, u32[]{:S(2)}, u32[]{:S(2)}) collective-permute-start(f32[64,512]{1,0:T(8,128)S(1)} %convert_add_fusion.4.own_ref), channel_id=1, source_target_pairs={{0,1},{1,0},{2,3},{3,2},{4,5},{5,4},{6,7},{7,6},{8,9},{9,8},{10,11... | collective-permute-start | bytes 393224 | tf_op jit(solution)/shard_map/ppermute | solution.py:24
  124.4 2.4 %collective-permute-start.46 = (bf16[64,512]{1,0:T(8,128)(2,1)S(1)}, bf16[64,512]{1,0:T(8,128)(2,1)S(1)}, u32[]{:S(2)}, u32[]{:S(2)}) collective-permute-start(bf16[64,512]{1,0:T(8,128)(2,1)S(1)} %collective-permute-done.42.refs_1_), channel_id=1, source_target_pairs={{0,1},{1,0},{2,3},{3,2},{4,5},{5,4},{6,7},{7,6},{8,9},{9,8},{10,11... | collective-permute-start | bytes 196616 | tf_op jit(solution)/shard_map/ppermute | solution.py:24
  124.9 1.9 %collective-permute-start.47 = (bf16[64,512]{1,0:T(8,128)(2,1)S(1)}, bf16[64,512]{1,0:T(8,128)(2,1)S(1)}, u32[]{:S(2)}, u32[]{:S(2)}) collective-permute-start(bf16[64,512]{1,0:T(8,128)(2,1)S(1)} %collective-permute-done.43.refs_2_), channel_id=1, source_target_pairs={{0,1},{1,0},{2,3},{3,2},{4,5},{5,4},{6,7},{7,6},{8,9},{9,8},{10,11... | collective-permute-start | bytes 196616 | tf_op jit(solution)/shard_map/ppermute | solution.py:24
  126.2 1.3 collective-permute-start.48
  131.5 5.6 %collective-permute-start.50 = (bf16[64,1024]{1,0:T(8,128)(2,1)S(1)}, bf16[64,1024]{1,0:T(8,128)(2,1)S(1)}, u32[]{:S(2)}, u32[]{:S(2)}) collective-permute-start(bf16[64,1024]{1,0:T(8,128)(2,1)S(1)} %add.292), channel_id=1, source_target_pairs={{0,4},{4,0},{8,12},{12,8},{16,20},{20,16},{24,28},{28,24},{1,5},{5... | collective-permute-start | bytes 393224 | tf_op jit(solution)/shard_map/ppermute | solution.py:24
  137.7 1.6 %collective-permute-start.51 = (f32[64,1024]{1,0:T(8,128)S(1)}, f32[64,1024]{1,0:T(8,128)S(1)}, u32[]{:S(2)}, u32[]{:S(2)}) collective-permute-start(f32[64,1024]{1,0:T(8,128)S(1)} %fusion.60), channel_id=1, source_target_pairs={{0,1},{1,0},{2,3},{3,2},{4,5},{5,4},{6,7},{7,6},{8,9},{9,8},{10,11... | collective-permute-start | bytes 786440 | tf_op jit(solution)/shard_map/ppermute | solution.py:24
  139.8 5.6 %collective-permute-start.52 = (bf16[64,1024]{1,0:T(8,128)(2,1)S(1)}, bf16[64,1024]{1,0:T(8,128)(2,1)S(1)}, u32[]{:S(2)}, u32[]{:S(2)}) collective-permute-start(bf16[64,1024]{1,0:T(8,128)(2,1)S(1)} %fusion), channel_id=1, source_target_pairs={{0,2},{1,3},{2,0},{3,1},{4,6},{5,7},{6,4},{7,5},{8,10},{9,11},{10,... | collective-permute-start | bytes 393224 | tf_op jit(solution)/shard_map/ppermute | solution.py:24
  145.4 1.6 %collective-permute-start.53 = (f32[64,1024]{1,0:T(8,128)S(1)}, f32[64,1024]{1,0:T(8,128)S(1)}, u32[]{:S(2)}, u32[]{:S(2)}) collective-permute-start(f32[64,1024]{1,0:T(8,128)S(1)} %convert_add_fusion.2.own_ref), channel_id=1, source_target_pairs={{0,1},{1,0},{2,3},{3,2},{4,5},{5,4},{6,7},{7,6},{8,9},{9,8},{10,11... | collective-permute-start | bytes 786440 | tf_op jit(solution)/shard_map/ppermute | solution.py:24
  (7 other events, 35.0 us)

commit v5 on v4

--- a/solution.py
+++ b/solution.py
@@ -223,6 +223,20 @@
         other = partner(dot(x, send), "front", 1)
         return exchange_sum(dot(x, keep) + other, "front", away)
 
+    def front_half_at_once(x, split):
+        if len(away) != 1:
+            return front_half(x, split)
+        keep, send = split
+        own, given = dot(x, keep).astype(BF16), dot(x, send).astype(BF16)
+        terms = []
+        for m in range(1 << len(away[0])):
+            terms.append(own if m == 0 else partner(own, "front", m << 1))
+            terms.append(partner(given, "front", m << 1 | 1))
+        terms = [t.astype(F32) for t in terms]
+        while len(terms) > 1:
+            terms = [terms[i] + terms[i + 1] for i in range(0, len(terms), 2)]
+        return terms[0]
+
     def outputs(own):
         return join(own, partner(own, "front", 1), core)
 
@@ -274,7 +288,7 @@
     y_zero = exchange_sum(scatter_sum(dot(both_halves(half), pivot_rel), "leaf", near), "leaf", far)
     y_zero = jnp.concatenate(gather_blocks(y_zero.astype(BF16), "leaf", near), axis=1)
     y_zero, *split_one = tied(y_zero, *halves(back_one))
-    x_zero = front_half(y_zero, (keep, send))
+    x_zero = front_half_at_once(y_zero, (keep, send))
     known_zero = known_pieces(x_zero, groups[0])
 
     coupling = exchange_sum(picked_product(known_zero, place_up, upper_one), "leaf", groups[1])

time: 148 us -> 147 us (level)
    ppermute x54 -> x55, waiting for transfers between devices: 58 us -> 56.6 us  [partner(): lax.ppermute(x, axis, [(i, i ^ mask) for i in range(lax.axis_size(axis))])]
    ppermute x54 -> x55, starting transfers between devices: 50.3 us -> 50.4 us  [partner(): lax.ppermute(x, axis, [(i, i ^ mask) for i in range(lax.axis_size(axis))])]
  transfers between devices with their start and end apart: 54 -> 55, of which waited for: 43 -> 43; matrix products, arithmetic and copies ran while one was open for 7% -> 7% of each run, Pallas kernels for 10% -> 10%
where the time goes in v5:
time: 147 us
  waiting for transfers between devices  56.6 us (39%)
  starting transfers between devices  50.4 us (34%)
  Pallas kernels  19.4 us (13%)
  matrix products  7.63 us (5%)
  local copies, waits for them, and re-layouts  6.37 us (4%)
  other arithmetic  4.84 us (3%)
    ppermute x55, waiting for transfers between devices, partner(): lax.ppermute(x, axis, [(i, i ^ mask) for i in range(lax.axis_size(axis))])  56.6 us
    ppermute x55, starting transfers between devices, partner(): lax.ppermute(x, axis, [(i, i ^ mask) for i in range(lax.axis_size(axis))])  50.4 us
    pallas_call x3, Pallas kernels, picked_product(): pl.pallas_call(pick_kernel, grid=(count // step,), in_specs=[pl.BlockSpec...  10.1 us
    dot_general x13, matrix products, dot(): return jnp.dot(left, right, preferred_element_type=F32)  7.63 us
    pallas_call x6, Pallas kernels, put_columns(): pl.pallas_call(functools.partial(put_kernel, first=first), out_shape=jax....  7.1 us
    dynamic_slice x6, local copies, waits for them, and re-layouts, half_of(): return lax.dynamic_slice_in_dim(x, which * size, size, dim)  5.12 us
  transfers between devices with their start and end apart: 55, of which 43 were waited for; matrix products, arithmetic and copies ran while one was open for 7% of the time, Pallas kernels for 10%

profile of v5, /device:TPU:0, one launch (start us, length us, event | category | flops | bytes accessed | tf_op | source)
XLA Modules:
  0.0 146.6 jit_solution(2686217232260356245)
XLA Ops:
  0.6 3.3 %convolution_convert_fusion = bf16[64,1024]{1,0:T(8,128)(2,1)S(1)} fusion(bf16[2048,1024]{1,0:T(8,128)(2,1)} %param.20, f32[64,2048]{1,0:T(8,128)} %param.17), kind=kOutput, calls=%fused_computation.2 | convolution fusion | flops 268632064 | bytes 4849664 | tf_op jit(solution)/shard_map/dot_general | solution.py:15
  4.0 3.0 %collective-permute-start = (bf16[64,1024]{1,0:T(8,128)(2,1)S(1)}, bf16[64,1024]{1,0:T(8,128)(2,1)S(1)}, u32[]{:S(2)}, u32[]{:S(2)}) collective-permute-start(bf16[64,1024]{1,0:T(8,128)(2,1)S(1)} %convolution_convert_fusion), channel_id=1, source_target_pairs={{0,4},{4,0},{8,12},{12,8},{16,20},{20,16},{24,28},{28,24},{1,5},{5... | collective-permute-start | bytes 393224 | tf_op jit(solution)/shard_map/ppermute | solution.py:24
  7.0 0.9 compare_select_fusion
  9.0 2.7 %constant_dynamic-slice_fusion.16 = (bf16[1024,1024]{1,0:T(8,128)(2,1)S(1)}, bf16[1024,1024]{1,0:T(8,128)(2,1)S(1)}) fusion(bf16[1024,2048]{1,0:T(8,128)(2,1)} %param.22, s32[]{:T(128)S(6)} %select_n.171, s32[]{:T(128)S(6)} %select_n.170), kind=kLoop, calls=%fused_computation.137 | loop fusion | bytes 8388616 | tf_op jit(solution)/shard_map/dynamic_slice | solution.py:205
  12.7 1.0 collective-permute-done.1
  13.8 1.6 %collective-permute-start.2 = (bf16[64,1024]{1,0:T(8,128)(2,1)S(1)}, bf16[64,1024]{1,0:T(8,128)(2,1)S(1)}, u32[]{:S(2)}, u32[]{:S(2)}) collective-permute-start(bf16[64,1024]{1,0:T(8,128)(2,1)S(1)} %add_convert_fusion.2), channel_id=1, source_target_pairs={{0,2},{1,3},{2,0},{3,1},{4,6},{5,7},{6,4},{7,5},{8,10},{9,11},{10,... | collective-permute-start | bytes 393224 | tf_op jit(solution)/shard_map/ppermute | solution.py:24
  15.4 4.0 %collective-permute-done.2 = bf16[64,1024]{1,0:T(8,128)(2,1)S(1)} collective-permute-done((bf16[64,1024]{1,0:T(8,128)(2,1)S(1)}, bf16[64,1024]{1,0:T(8,128)(2,1)S(1)}, u32[]{:S(2)}, u32[]{:S(2)}) %collective-permute-start.2) | collective-permute-done | bytes 131104 | tf_op jit(solution)/shard_map/ppermute | solution.py:24
  19.5 1.4 shard_map.167
  20.9 1.4 shard_map.166
  22.5 1.7 %collective-permute-start.6 = (bf16[64,512]{1,0:T(8,128)(2,1)S(1)}, bf16[64,512]{1,0:T(8,128)(2,1)S(1)}, u32[]{:S(2)}, u32[]{:S(2)}) collective-permute-start(bf16[64,512]{1,0:T(8,128)(2,1)S(1)} %get-tuple-element.123), channel_id=1, source_target_pairs={{0,12},{4,8},{8,4},{12,0},{16,28},{20,24},{24,20},{28,16},{1,13},{... | collective-permute-start | bytes 196616 | tf_op jit(solution)/shard_map/ppermute | solution.py:24
  24.7 1.4 collective-permute-start.4
  26.1 1.9 %collective-permute-done.6 = bf16[64,512]{1,0:T(8,128)(2,1)S(1)} collective-permute-done((bf16[64,512]{1,0:T(8,128)(2,1)S(1)}, bf16[64,512]{1,0:T(8,128)(2,1)S(1)}, u32[]{:S(2)}, u32[]{:S(2)}) %collective-permute-start.6) | collective-permute-done | bytes 65568 | tf_op jit(solution)/shard_map/ppermute | solution.py:24
  29.4 1.2 collective-permute-done.7
  31.2 2.2 %collective-permute-start.10 = (bf16[64,1024]{1,0:T(8,128)(2,1)S(1)}, bf16[64,1024]{1,0:T(8,128)(2,1)S(1)}, u32[]{:S(2)}, u32[]{:S(2)}) collective-permute-start(bf16[64,1024]{1,0:T(8,128)(2,1)S(1)} %convolution_convert_fusion.1), channel_id=1, source_target_pairs={{0,12},{4,8},{8,4},{12,0},{16,28},{20,24},{24,20},{28,16},{1,13},{... | collective-permute-start | bytes 393224 | tf_op jit(solution)/shard_map/ppermute | solution.py:24
  33.8 0.9 collective-permute-start.8
  34.7 1.5 %constant_dynamic-slice_fusion.14 = (bf16[1024,512]{1,0:T(8,128)(2,1)}, bf16[1024,512]{1,0:T(8,128)(2,1)}) fusion(bf16[1024,1024]{1,0:T(8,128)(2,1)S(1)} %copy-done.6, s32[]{:T(128)S(6)} %select_n.191, s32[]{:T(128)S(6)} %select_n.188), kind=kLoop, calls=%fused_computation.135 | loop fusion | bytes 4194312 | tf_op jit(solution)/shard_map/dynamic_slice | solution.py:205
  36.3 1.4 shard_map.168
  37.7 1.4 shard_map.169
  39.1 1.2 collective-permute-done.9
  40.6 1.0 add_convert_fusion
  43.7 1.6 %collective-permute-start.12 = (bf16[64,512]{1,0:T(8,128)(2,1)S(1)}, bf16[64,512]{1,0:T(8,128)(2,1)S(1)}, u32[]{:S(2)}, u32[]{:S(2)}) collective-permute-start(bf16[64,512]{1,0:T(8,128)(2,1)S(1)} %fusion.1), channel_id=1, source_target_pairs={{0,2},{1,3},{2,0},{3,1},{4,6},{5,7},{6,4},{7,5},{8,10},{9,11},{10,... | collective-permute-start | bytes 196616 | tf_op jit(solution)/shard_map/ppermute | solution.py:24
  45.2 1.0 constant_dynamic-slice_fusion.13
  46.3 1.7 %collective-permute-done.12 = bf16[64,512]{1,0:T(8,128)(2,1)S(1)} collective-permute-done((bf16[64,512]{1,0:T(8,128)(2,1)S(1)}, bf16[64,512]{1,0:T(8,128)(2,1)S(1)}, u32[]{:S(2)}, u32[]{:S(2)}) %collective-permute-start.12) | collective-permute-done | bytes 65568 | tf_op jit(solution)/shard_map/ppermute | solution.py:24
  50.6 2.2 %collective-permute-start.16 = (bf16[64,512]{1,0:T(8,128)(2,1)S(1)}, bf16[64,512]{1,0:T(8,128)(2,1)S(1)}, u32[]{:S(2)}, u32[]{:S(2)}) collective-permute-start(bf16[64,512]{1,0:T(8,128)(2,1)S(1)} %get-tuple-element.120), channel_id=1, source_target_pairs={{0,12},{4,8},{8,4},{12,0},{16,28},{20,24},{24,20},{28,16},{1,13},{... | collective-permute-start | bytes 196616 | tf_op jit(solution)/shard_map/ppermute | solution.py:24
  53.2 0.9 collective-permute-start.14
  54.2 1.9 %collective-permute-done.16 = bf16[64,512]{1,0:T(8,128)(2,1)S(1)} collective-permute-done((bf16[64,512]{1,0:T(8,128)(2,1)S(1)}, bf16[64,512]{1,0:T(8,128)(2,1)S(1)}, u32[]{:S(2)}, u32[]{:S(2)}) %collective-permute-start.16) | collective-permute-done | bytes 65568 | tf_op jit(solution)/shard_map/ppermute | solution.py:24
  57.5 2.7 %collective-permute-start.17 = (bf16[64,256]{1,0:T(8,128)(2,1)S(1)}, bf16[64,256]{1,0:T(8,128)(2,1)S(1)}, u32[]{:S(2)}, u32[]{:S(2)}) collective-permute-start(bf16[64,256]{1,0:T(8,128)(2,1)S(1)} %slice.127), channel_id=1, source_target_pairs={{0,16},{4,20},{8,24},{12,28},{16,0},{20,4},{24,8},{28,12},{1,17},{... | collective-permute-start | bytes 98312 | tf_op jit(solution)/shard_map/ppermute | solution.py:24
  60.3 2.1 %collective-permute-done.17 = bf16[64,256]{1,0:T(8,128)(2,1)S(1)} collective-permute-done((bf16[64,256]{1,0:T(8,128)(2,1)S(1)}, bf16[64,256]{1,0:T(8,128)(2,1)S(1)}, u32[]{:S(2)}, u32[]{:S(2)}) %collective-permute-start.17) | collective-permute-done | bytes 32800 | tf_op jit(solution)/shard_map/ppermute | solution.py:24
  62.5 1.2 collective-permute-done.18
  64.0 2.0 %collective-permute-start.21 = (bf16[64,256]{1,0:T(8,128)(2,1)S(1)}, bf16[64,256]{1,0:T(8,128)(2,1)S(1)}, u32[]{:S(2)}, u32[]{:S(2)}) collective-permute-start(bf16[64,256]{1,0:T(8,128)(2,1)S(1)} %get-tuple-element.126), channel_id=1, source_target_pairs={{0,12},{4,8},{8,4},{12,0},{16,28},{20,24},{24,20},{28,16},{1,13},{... | collective-permute-start | bytes 98312 | tf_op jit(solution)/shard_map/ppermute | solution.py:24
  66.5 1.1 collective-permute-start.19
  67.6 1.3 collective-permute-done.21
  68.9 1.0 collective-permute-done.20
  70.4 2.7 %collective-permute-start.22 = (bf16[64,256]{1,0:T(8,128)(2,1)S(1)}, bf16[64,256]{1,0:T(8,128)(2,1)S(1)}, u32[]{:S(2)}, u32[]{:S(2)}) collective-permute-start(bf16[64,256]{1,0:T(8,128)(2,1)S(1)} %fusion.15), channel_id=1, source_target_pairs={{0,16},{4,20},{8,24},{12,28},{16,0},{20,4},{24,8},{28,12},{1,17},{... | collective-permute-start | bytes 98312 | tf_op jit(solution)/shard_map/ppermute | solution.py:24
  73.1 2.2 %collective-permute-done.22 = bf16[64,256]{1,0:T(8,128)(2,1)S(1)} collective-permute-done((bf16[64,256]{1,0:T(8,128)(2,1)S(1)}, bf16[64,256]{1,0:T(8,128)(2,1)S(1)}, u32[]{:S(2)}, u32[]{:S(2)}) %collective-permute-start.22) | collective-permute-done | bytes 32800 | tf_op jit(solution)/shard_map/ppermute | solution.py:24
  75.3 2.2 %collective-permute-start.25 = (bf16[64,256]{1,0:T(8,128)(2,1)S(1)}, bf16[64,256]{1,0:T(8,128)(2,1)S(1)}, u32[]{:S(2)}, u32[]{:S(2)}) collective-permute-start(bf16[64,256]{1,0:T(8,128)(2,1)S(1)} %add_convert_fusion.5), channel_id=1, source_target_pairs={{0,12},{4,8},{8,4},{12,0},{16,28},{20,24},{24,20},{28,16},{1,13},{... | collective-permute-start | bytes 98312 | tf_op jit(solution)/shard_map/ppermute | solution.py:24
  79.1 1.1 collective-permute-done.25
  80.2 1.2 collective-permute-done.24
  82.4 1.6 %collective-permute-start.27 = (bf16[64,256]{1,0:T(8,128)(2,1)S(1)}, bf16[64,256]{1,0:T(8,128)(2,1)S(1)}, u32[]{:S(2)}, u32[]{:S(2)}) collective-permute-start(bf16[64,256]{1,0:T(8,128)(2,1)S(1)} %convolution_convert_fusion.3), channel_id=1, source_target_pairs={{0,2},{1,3},{2,0},{3,1},{4,6},{5,7},{6,4},{7,5},{8,10},{9,11},{10,... | collective-permute-start | bytes 98312 | tf_op jit(solution)/shard_map/ppermute | solution.py:24
  84.3 1.5 %collective-permute-done.28 = bf16[64,256]{1,0:T(8,128)(2,1)S(1)} collective-permute-done((bf16[64,256]{1,0:T(8,128)(2,1)S(1)}, bf16[64,256]{1,0:T(8,128)(2,1)S(1)}, u32[]{:S(2)}, u32[]{:S(2)}) %collective-permute-start.28) | collective-permute-done | bytes 32800 | tf_op jit(solution)/shard_map/ppermute | solution.py:24
  86.4 2.7 %collective-permute-start.29 = (bf16[64,256]{1,0:T(8,128)(2,1)S(1)}, bf16[64,256]{1,0:T(8,128)(2,1)S(1)}, u32[]{:S(2)}, u32[]{:S(2)}) collective-permute-start(bf16[64,256]{1,0:T(8,128)(2,1)S(1)} %get-tuple-element.95), channel_id=1, source_target_pairs={{0,16},{4,20},{8,24},{12,28},{16,0},{20,4},{24,8},{28,12},{1,17},{... | collective-permute-start | bytes 98312 | tf_op jit(solution)/shard_map/ppermute | solution.py:24
  89.1 2.2 %collective-permute-done.29 = bf16[64,256]{1,0:T(8,128)(2,1)S(1)} collective-permute-done((bf16[64,256]{1,0:T(8,128)(2,1)S(1)}, bf16[64,256]{1,0:T(8,128)(2,1)S(1)}, u32[]{:S(2)}, u32[]{:S(2)}) %collective-permute-start.29) | collective-permute-done | bytes 32800 | tf_op jit(solution)/shard_map/ppermute | solution.py:24
  92.3 1.6 %collective-permute-start.31 = (bf16[64,512]{1,0:T(8,128)(2,1)S(1)}, bf16[64,512]{1,0:T(8,128)(2,1)S(1)}, u32[]{:S(2)}, u32[]{:S(2)}) collective-permute-start(bf16[64,512]{1,0:T(8,128)(2,1)S(1)} %pad_maximum_fusion.3.refs_0_), channel_id=1, source_target_pairs={{0,8},{4,12},{8,0},{12,4},{16,24},{20,28},{24,16},{28,20},{1,9},{5... | collective-permute-start | bytes 196616 | tf_op jit(solution)/shard_map/ppermute | solution.py:24
  95.6 1.3 collective-permute-done.31.refs_2_
  96.8 2.2 %collective-permute-done.32.refs_3_ = bf16[64,512]{1,0:T(8,128)(2,1)S(1)} collective-permute-done((bf16[64,512]{1,0:T(8,128)(2,1)S(1)}, bf16[64,512]{1,0:T(8,128)(2,1)S(1)}, u32[]{:S(2)}, u32[]{:S(2)}) %collective-permute-start.32) | collective-permute-done | bytes 65568 | tf_op jit(solution)/shard_map/ppermute | solution.py:24
  99.1 1.2 collective-permute-done.36.refs_7_
  100.3 2.1 %shard_map.172 = f32[64,1024]{1,0:T(8,128)S(1)} custom-call(bf16[64,512]{1,0:T(8,128)(2,1)S(1)} %pad_maximum_fusion.3.refs_0_, bf16[64,512]{1,0:T(8,128)(2,1)S(1)} %collective-permute-done.30.refs_1_, bf16[64,512]{1,0:T(8,128)(2,1)S(1)} %collective-permute-done.31.refs_2_, bf16[64,512]{1,0:T(8,128)(2,1)S(1)} %collective-permute-done.32.refs_3_, ...), custom_call_target="tpu_custom_call" | custom-call | flops 671088640 | bytes 18874368 | tf_op jit(solution)/shard_map/pallas_call | solution.py:105
  102.5 1.0 collective-permute-start.39
  103.5 1.6 %collective-permute-start.38 = (bf16[64,1024]{1,0:T(8,128)(2,1)S(1)}, bf16[64,1024]{1,0:T(8,128)(2,1)S(1)}, u32[]{:S(2)}, u32[]{:S(2)}) collective-permute-start(bf16[64,1024]{1,0:T(8,128)(2,1)S(1)} %convert_element_type.244), channel_id=1, source_target_pairs={{0,8},{4,12},{8,0},{12,4},{16,24},{20,28},{24,16},{28,20},{1,9},{5... | collective-permute-start | bytes 393224 | tf_op jit(solution)/shard_map/ppermute | solution.py:24
  105.1 0.9 collective-permute-start.37
  106.2 4.0 %shard_map.173 = f32[64,1024]{1,0:T(8,128)S(1)} custom-call(bf16[64,512]{1,0:T(8,128)(2,1)S(1)} %pad_maximum_fusion.3.refs_0_, bf16[64,512]{1,0:T(8,128)(2,1)S(1)} %collective-permute-done.30.refs_1_, bf16[64,512]{1,0:T(8,128)(2,1)S(1)} %collective-permute-done.31.refs_2_, bf16[64,512]{1,0:T(8,128)(2,1)S(1)} %collective-permute-done.32.refs_3_, ...), custom_call_target="tpu_custom_call" | custom-call | flops 1342177280 | bytes 37748736 | tf_op jit(solution)/shard_map/pallas_call | solution.py:105
  110.2 1.3 collective-permute-done.38
  113.9 1.5 %collective-permute-start.41 = (bf16[64,512]{1,0:T(8,128)(2,1)S(1)}, bf16[64,512]{1,0:T(8,128)(2,1)S(1)}, u32[]{:S(2)}, u32[]{:S(2)}) collective-permute-start(bf16[64,512]{1,0:T(8,128)(2,1)S(1)} %fusion.2), channel_id=1, source_target_pairs={{0,2},{1,3},{2,0},{3,1},{4,6},{5,7},{6,4},{7,5},{8,10},{9,11},{10,... | collective-permute-start | bytes 196616 | tf_op jit(solution)/shard_map/ppermute | solution.py:24
  116.1 2.1 %collective-permute-done.41 = bf16[64,512]{1,0:T(8,128)(2,1)S(1)} collective-permute-done((bf16[64,512]{1,0:T(8,128)(2,1)S(1)}, bf16[64,512]{1,0:T(8,128)(2,1)S(1)}, u32[]{:S(2)}, u32[]{:S(2)}) %collective-permute-start.41) | collective-permute-done | bytes 65568 | tf_op jit(solution)/shard_map/ppermute | solution.py:24
  118.3 1.2 collective-permute-start.43
  119.9 2.0 %collective-permute-start.45 = (bf16[64,512]{1,0:T(8,128)(2,1)S(1)}, bf16[64,512]{1,0:T(8,128)(2,1)S(1)}, u32[]{:S(2)}, u32[]{:S(2)}) collective-permute-start(bf16[64,512]{1,0:T(8,128)(2,1)S(1)} %convert_element_type.253.refs_0_), channel_id=1, source_target_pairs={{0,12},{4,8},{8,4},{12,0},{16,28},{20,24},{24,20},{28,16},{1,13},{... | collective-permute-start | bytes 196616 | tf_op jit(solution)/shard_map/ppermute | solution.py:24
  123.8 1.2 collective-permute-done.45.refs_3_
  126.3 4.0 %shard_map.175 = f32[64,1024]{1,0:T(8,128)S(1)} custom-call(bf16[64,512]{1,0:T(8,128)(2,1)S(1)} %convert_element_type.253.refs_0_, bf16[64,512]{1,0:T(8,128)(2,1)S(1)} %collective-permute-done.43.refs_1_, bf16[64,512]{1,0:T(8,128)(2,1)S(1)} %collective-permute-done.44.refs_2_, bf16[64,512]{1,0:T(8,128)(2,1)S(1)} %collective-permute-done.45.refs_3_, ...), custom_call_target="tpu_custom_call" | custom-call | flops 1342177280 | bytes 37748736 | tf_op jit(solution)/shard_map/pallas_call | solution.py:105
  130.3 1.0 collective-permute-start.51
  132.0 3.9 %collective-permute-done.51 = bf16[64,1024]{1,0:T(8,128)(2,1)S(1)} collective-permute-done((bf16[64,1024]{1,0:T(8,128)(2,1)S(1)}, bf16[64,1024]{1,0:T(8,128)(2,1)S(1)}, u32[]{:S(2)}, u32[]{:S(2)}) %collective-permute-start.51) | collective-permute-done | bytes 131104 | tf_op jit(solution)/shard_map/ppermute | solution.py:24
  136.5 1.5 %collective-permute-done.52 = f32[64,1024]{1,0:T(8,128)S(1)} collective-permute-done((f32[64,1024]{1,0:T(8,128)S(1)}, f32[64,1024]{1,0:T(8,128)S(1)}, u32[]{:S(2)}, u32[]{:S(2)}) %collective-permute-start.52) | collective-permute-done | bytes 262176 | tf_op jit(solution)/shard_map/ppermute | solution.py:24
  138.6 1.6 %collective-permute-start.53 = (bf16[64,1024]{1,0:T(8,128)(2,1)S(1)}, bf16[64,1024]{1,0:T(8,128)(2,1)S(1)}, u32[]{:S(2)}, u32[]{:S(2)}) collective-permute-start(bf16[64,1024]{1,0:T(8,128)(2,1)S(1)} %fusion), channel_id=1, source_target_pairs={{0,2},{1,3},{2,0},{3,1},{4,6},{5,7},{6,4},{7,5},{8,10},{9,11},{10,... | collective-permute-start | bytes 393224 | tf_op jit(solution)/shard_map/ppermute | solution.py:24
  140.2 4.0 %collective-permute-done.53 = bf16[64,1024]{1,0:T(8,128)(2,1)S(1)} collective-permute-done((bf16[64,1024]{1,0:T(8,128)(2,1)S(1)}, bf16[64,1024]{1,0:T(8,128)(2,1)S(1)}, u32[]{:S(2)}, u32[]{:S(2)}) %collective-permute-start.53) | collective-permute-done | bytes 131104 | tf_op jit(solution)/shard_map/ppermute | solution.py:24
  144.3 1.5 %collective-permute-done.54.other_ref = f32[64,1024]{1,0:T(8,128)S(1)} collective-permute-done((f32[64,1024]{1,0:T(8,128)S(1)}, f32[64,1024]{1,0:T(8,128)S(1)}, u32[]{:S(2)}, u32[]{:S(2)}) %collective-permute-start.54) | collective-permute-done | bytes 262176 | tf_op jit(solution)/shard_map/ppermute | solution.py:24
  (153 shorter events, 29.1 us)
Async XLA Ops:
  0.6 30.0 %copy-start = (bf16[1024,1024]{1,0:T(8,128)(2,1)S(1)}, bf16[1024,1024]{1,0:T(8,128)(2,1)}, u32[]{:S(2)}) copy-start(bf16[1024,1024]{1,0:T(8,128)(2,1)} %param.19) | copy-start | bytes 6291460
  4.0 7.6 %collective-permute-start = (bf16[64,1024]{1,0:T(8,128)(2,1)S(1)}, bf16[64,1024]{1,0:T(8,128)(2,1)S(1)}, u32[]{:S(2)}, u32[]{:S(2)}) collective-permute-start(bf16[64,1024]{1,0:T(8,128)(2,1)S(1)} %convolution_convert_fusion), channel_id=1, source_target_pairs={{0,4},{4,0},{8,12},{12,8},{16,20},{20,16},{24,28},{28,24},{1,5},{5... | collective-permute-start | bytes 393224 | tf_op jit(solution)/shard_map/ppermute | solution.py:24
  12.2 1.6 %collective-permute-start.1 = (f32[64,1024]{1,0:T(8,128)S(1)}, f32[64,1024]{1,0:T(8,128)S(1)}, u32[]{:S(2)}, u32[]{:S(2)}) collective-permute-start(f32[64,1024]{1,0:T(8,128)S(1)} %fusion.67), channel_id=1, source_target_pairs={{0,1},{1,0},{2,3},{3,2},{4,5},{5,4},{6,7},{7,6},{8,9},{9,8},{10,11... | collective-permute-start | bytes 786440 | tf_op jit(solution)/shard_map/ppermute | solution.py:24
  13.8 5.6 %collective-permute-start.2 = (bf16[64,1024]{1,0:T(8,128)(2,1)S(1)}, bf16[64,1024]{1,0:T(8,128)(2,1)S(1)}, u32[]{:S(2)}, u32[]{:S(2)}) collective-permute-start(bf16[64,1024]{1,0:T(8,128)(2,1)S(1)} %add_convert_fusion.2), channel_id=1, source_target_pairs={{0,2},{1,3},{2,0},{3,1},{4,6},{5,7},{6,4},{7,5},{8,10},{9,11},{10,... | collective-permute-start | bytes 393224 | tf_op jit(solution)/shard_map/ppermute | solution.py:24
  20.8 1.6 %collective-permute-start.3 = (bf16[64,2048]{1,0:T(8,128)(2,1)S(1)}, bf16[64,2048]{1,0:T(8,128)(2,1)S(1)}, u32[]{:S(2)}, u32[]{:S(2)}) collective-permute-start(bf16[64,2048]{1,0:T(8,128)(2,1)S(1)} %shard_map.167), channel_id=1, source_target_pairs={{0,1},{1,0},{2,3},{3,2},{4,5},{5,4},{6,7},{7,6},{8,9},{9,8},{10,11... | collective-permute-start | bytes 786440 | tf_op jit(solution)/shard_map/ppermute | solution.py:24
  22.5 5.5 %collective-permute-start.6 = (bf16[64,512]{1,0:T(8,128)(2,1)S(1)}, bf16[64,512]{1,0:T(8,128)(2,1)S(1)}, u32[]{:S(2)}, u32[]{:S(2)}) collective-permute-start(bf16[64,512]{1,0:T(8,128)(2,1)S(1)} %get-tuple-element.123), channel_id=1, source_target_pairs={{0,12},{4,8},{8,4},{12,0},{16,28},{20,24},{24,20},{28,16},{1,13},{... | collective-permute-start | bytes 196616 | tf_op jit(solution)/shard_map/ppermute | solution.py:24
  24.2 4.3 %collective-permute-start.5 = (bf16[64,512]{1,0:T(8,128)(2,1)S(1)}, bf16[64,512]{1,0:T(8,128)(2,1)S(1)}, u32[]{:S(2)}, u32[]{:S(2)}) collective-permute-start(bf16[64,512]{1,0:T(8,128)(2,1)S(1)} %get-tuple-element.124), channel_id=1, source_target_pairs={{0,8},{4,12},{8,0},{12,4},{16,24},{20,28},{24,16},{28,20},{1,9},{5... | collective-permute-start | bytes 196616 | tf_op jit(solution)/shard_map/ppermute | solution.py:24
  24.7 4.6 %collective-permute-start.4 = (bf16[64,512]{1,0:T(8,128)(2,1)S(1)}, bf16[64,512]{1,0:T(8,128)(2,1)S(1)}, u32[]{:S(2)}, u32[]{:S(2)}) collective-permute-start(bf16[64,512]{1,0:T(8,128)(2,1)S(1)} %get-tuple-element.122), channel_id=1, source_target_pairs={{0,4},{4,0},{8,12},{12,8},{16,20},{20,16},{24,28},{28,24},{1,5},{5... | collective-permute-start | bytes 196616 | tf_op jit(solution)/shard_map/ppermute | solution.py:24
  29.3 1.3 collective-permute-start.7
  31.2 7.9 %collective-permute-start.10 = (bf16[64,1024]{1,0:T(8,128)(2,1)S(1)}, bf16[64,1024]{1,0:T(8,128)(2,1)S(1)}, u32[]{:S(2)}, u32[]{:S(2)}) collective-permute-start(bf16[64,1024]{1,0:T(8,128)(2,1)S(1)} %convolution_convert_fusion.1), channel_id=1, source_target_pairs={{0,12},{4,8},{8,4},{12,0},{16,28},{20,24},{24,20},{28,16},{1,13},{... | collective-permute-start | bytes 393224 | tf_op jit(solution)/shard_map/ppermute | solution.py:24
  33.3 6.9 %collective-permute-start.9 = (bf16[64,1024]{1,0:T(8,128)(2,1)S(1)}, bf16[64,1024]{1,0:T(8,128)(2,1)}, u32[]{:S(2)}, u32[]{:S(2)}) collective-permute-start(bf16[64,1024]{1,0:T(8,128)(2,1)S(1)} %convolution_convert_fusion.1), channel_id=1, source_target_pairs={{0,8},{4,12},{8,0},{12,4},{16,24},{20,28},{24,16},{28,20},{1,9},{5... | collective-permute-start | bytes 393224 | tf_op jit(solution)/shard_map/ppermute | solution.py:24
  33.8 6.8 %collective-permute-start.8 = (bf16[64,1024]{1,0:T(8,128)(2,1)S(1)}, bf16[64,1024]{1,0:T(8,128)(2,1)}, u32[]{:S(2)}, u32[]{:S(2)}) collective-permute-start(bf16[64,1024]{1,0:T(8,128)(2,1)S(1)} %convolution_convert_fusion.1), channel_id=1, source_target_pairs={{0,4},{4,0},{8,12},{12,8},{16,20},{20,16},{24,28},{28,24},{1,5},{5... | collective-permute-start | bytes 393224 | tf_op jit(solution)/shard_map/ppermute | solution.py:24
  41.9 1.4 collective-permute-start.11
  43.7 4.3 %collective-permute-start.12 = (bf16[64,512]{1,0:T(8,128)(2,1)S(1)}, bf16[64,512]{1,0:T(8,128)(2,1)S(1)}, u32[]{:S(2)}, u32[]{:S(2)}) collective-permute-start(bf16[64,512]{1,0:T(8,128)(2,1)S(1)} %fusion.1), channel_id=1, source_target_pairs={{0,2},{1,3},{2,0},{3,1},{4,6},{5,7},{6,4},{7,5},{8,10},{9,11},{10,... | collective-permute-start | bytes 196616 | tf_op jit(solution)/shard_map/ppermute | solution.py:24
  48.8 1.6 %collective-permute-start.13 = (bf16[64,2048]{1,0:T(8,128)(2,1)S(1)}, bf16[64,2048]{1,0:T(8,128)(2,1)S(1)}, u32[]{:S(2)}, u32[]{:S(2)}) collective-permute-start(bf16[64,2048]{1,0:T(8,128)(2,1)S(1)} %add.263), channel_id=1, source_target_pairs={{0,1},{1,0},{2,3},{3,2},{4,5},{5,4},{6,7},{7,6},{8,9},{9,8},{10,11... | collective-permute-start | bytes 786440 | tf_op jit(solution)/shard_map/ppermute | solution.py:24
  49.9 10.3 %copy-start.10 = (bf16[512,256]{1,0:T(8,128)(2,1)S(1)}, bf16[512,256]{1,0:T(8,128)(2,1)}, u32[]{:S(2)}) copy-start(bf16[512,256]{1,0:T(8,128)(2,1)} %get-tuple-element.115) | copy-start | bytes 786436
  49.9 10.3 %copy-start.11 = (bf16[512,256]{1,0:T(8,128)(2,1)S(1)}, bf16[512,256]{1,0:T(8,128)(2,1)}, u32[]{:S(2)}) copy-start(bf16[512,256]{1,0:T(8,128)(2,1)} %get-tuple-element.116) | copy-start | bytes 786436
  49.9 10.3 %copy-start.12 = (bf16[512,256]{1,0:T(8,128)(2,1)S(1)}, bf16[512,256]{1,0:T(8,128)(2,1)}, u32[]{:S(2)}) copy-start(bf16[512,256]{1,0:T(8,128)(2,1)} %get-tuple-element.117) | copy-start | bytes 786436
  50.6 5.5 %collective-permute-start.16 = (bf16[64,512]{1,0:T(8,128)(2,1)S(1)}, bf16[64,512]{1,0:T(8,128)(2,1)S(1)}, u32[]{:S(2)}, u32[]{:S(2)}) collective-permute-start(bf16[64,512]{1,0:T(8,128)(2,1)S(1)} %get-tuple-element.120), channel_id=1, source_target_pairs={{0,12},{4,8},{8,4},{12,0},{16,28},{20,24},{24,20},{28,16},{1,13},{... | collective-permute-start | bytes 196616 | tf_op jit(solution)/shard_map/ppermute | solution.py:24
  52.8 4.3 %collective-permute-start.15 = (bf16[64,512]{1,0:T(8,128)(2,1)S(1)}, bf16[64,512]{1,0:T(8,128)(2,1)S(1)}, u32[]{:S(2)}, u32[]{:S(2)}) collective-permute-start(bf16[64,512]{1,0:T(8,128)(2,1)S(1)} %get-tuple-element.121), channel_id=1, source_target_pairs={{0,8},{4,12},{8,0},{12,4},{16,24},{20,28},{24,16},{28,20},{1,9},{5... | collective-permute-start | bytes 196616 | tf_op jit(solution)/shard_map/ppermute | solution.py:24
  53.2 4.3 %collective-permute-start.14 = (bf16[64,512]{1,0:T(8,128)(2,1)S(1)}, bf16[64,512]{1,0:T(8,128)(2,1)S(1)}, u32[]{:S(2)}, u32[]{:S(2)}) collective-permute-start(bf16[64,512]{1,0:T(8,128)(2,1)S(1)} %get-tuple-element.119), channel_id=1, source_target_pairs={{0,4},{4,0},{8,12},{12,8},{16,20},{20,16},{24,28},{28,24},{1,5},{5... | collective-permute-start | bytes 196616 | tf_op jit(solution)/shard_map/ppermute | solution.py:24
  57.5 4.9 %collective-permute-start.17 = (bf16[64,256]{1,0:T(8,128)(2,1)S(1)}, bf16[64,256]{1,0:T(8,128)(2,1)S(1)}, u32[]{:S(2)}, u32[]{:S(2)}) collective-permute-start(bf16[64,256]{1,0:T(8,128)(2,1)S(1)} %slice.127), channel_id=1, source_target_pairs={{0,16},{4,20},{8,24},{12,28},{16,0},{20,4},{24,8},{28,12},{1,17},{... | collective-permute-start | bytes 98312 | tf_op jit(solution)/shard_map/ppermute | solution.py:24
  60.2 18.7 %copy-start.7 = (bf16[1024,1024]{1,0:T(8,128)(2,1)S(1)}, bf16[1024,1024]{1,0:T(8,128)(2,1)}, u32[]{:S(2)}) copy-start(bf16[1024,1024]{1,0:T(8,128)(2,1)} %param.26) | copy-start | bytes 6291460
  62.4 1.3 collective-permute-start.18
  64.0 4.9 %collective-permute-start.21 = (bf16[64,256]{1,0:T(8,128)(2,1)S(1)}, bf16[64,256]{1,0:T(8,128)(2,1)S(1)}, u32[]{:S(2)}, u32[]{:S(2)}) collective-permute-start(bf16[64,256]{1,0:T(8,128)(2,1)S(1)} %get-tuple-element.126), channel_id=1, source_target_pairs={{0,12},{4,8},{8,4},{12,0},{16,28},{20,24},{24,20},{28,16},{1,13},{... | collective-permute-start | bytes 98312 | tf_op jit(solution)/shard_map/ppermute | solution.py:24
  66.0 3.9 %collective-permute-start.20 = (bf16[64,256]{1,0:T(8,128)(2,1)S(1)}, bf16[64,256]{1,0:T(8,128)(2,1)S(1)}, u32[]{:S(2)}, u32[]{:S(2)}) collective-permute-start(bf16[64,256]{1,0:T(8,128)(2,1)S(1)} %get-tuple-element.127), channel_id=1, source_target_pairs={{0,8},{4,12},{8,0},{12,4},{16,24},{20,28},{24,16},{28,20},{1,9},{5... | collective-permute-start | bytes 98312 | tf_op jit(solution)/shard_map/ppermute | solution.py:24
  66.5 3.9 %collective-permute-start.19 = (bf16[64,256]{1,0:T(8,128)(2,1)S(1)}, bf16[64,256]{1,0:T(8,128)(2,1)S(1)}, u32[]{:S(2)}, u32[]{:S(2)}) collective-permute-start(bf16[64,256]{1,0:T(8,128)(2,1)S(1)} %get-tuple-element.125), channel_id=1, source_target_pairs={{0,4},{4,0},{8,12},{12,8},{16,20},{20,16},{24,28},{28,24},{1,5},{5... | collective-permute-start | bytes 98312 | tf_op jit(solution)/shard_map/ppermute | solution.py:24
  70.4 4.9 %collective-permute-start.22 = (bf16[64,256]{1,0:T(8,128)(2,1)S(1)}, bf16[64,256]{1,0:T(8,128)(2,1)S(1)}, u32[]{:S(2)}, u32[]{:S(2)}) collective-permute-start(bf16[64,256]{1,0:T(8,128)(2,1)S(1)} %fusion.15), channel_id=1, source_target_pairs={{0,16},{4,20},{8,24},{12,28},{16,0},{20,4},{24,8},{28,12},{1,17},{... | collective-permute-start | bytes 98312 | tf_op jit(solution)/shard_map/ppermute | solution.py:24
  75.3 25.0 %copy-start.2 = (bf16[1024,1024]{1,0:T(8,128)(2,1)S(1)}, bf16[1024,1024]{1,0:T(8,128)(2,1)}, u32[]{:S(2)}) copy-start(bf16[1024,1024]{1,0:T(8,128)(2,1)} %refs_9_.3) | copy-start | bytes 6291460
  75.3 4.9 %collective-permute-start.25 = (bf16[64,256]{1,0:T(8,128)(2,1)S(1)}, bf16[64,256]{1,0:T(8,128)(2,1)S(1)}, u32[]{:S(2)}, u32[]{:S(2)}) collective-permute-start(bf16[64,256]{1,0:T(8,128)(2,1)S(1)} %add_convert_fusion.5), channel_id=1, source_target_pairs={{0,12},{4,8},{8,4},{12,0},{16,28},{20,24},{24,20},{28,16},{1,13},{... | collective-permute-start | bytes 98312 | tf_op jit(solution)/shard_map/ppermute | solution.py:24
  77.5 3.9 %collective-permute-start.24 = (bf16[64,256]{1,0:T(8,128)(2,1)S(1)}, bf16[64,256]{1,0:T(8,128)(2,1)S(1)}, u32[]{:S(2)}, u32[]{:S(2)}) collective-permute-start(bf16[64,256]{1,0:T(8,128)(2,1)S(1)} %add_convert_fusion.5), channel_id=1, source_target_pairs={{0,8},{4,12},{8,0},{12,4},{16,24},{20,28},{24,16},{28,20},{1,9},{5... | collective-permute-start | bytes 98312 | tf_op jit(solution)/shard_map/ppermute | solution.py:24
  78.0 3.9 %collective-permute-start.23 = (bf16[64,256]{1,0:T(8,128)(2,1)S(1)}, bf16[64,256]{1,0:T(8,128)(2,1)S(1)}, u32[]{:S(2)}, u32[]{:S(2)}) collective-permute-start(bf16[64,256]{1,0:T(8,128)(2,1)S(1)} %add_convert_fusion.5), channel_id=1, source_target_pairs={{0,4},{4,0},{8,12},{12,8},{16,20},{20,16},{24,28},{28,24},{1,5},{5... | collective-permute-start | bytes 98312 | tf_op jit(solution)/shard_map/ppermute | solution.py:24
  82.1 23.9 %copy-start.16 = (s32[1,2048]{1,0:T(1,128)S(1)}, s32[1,2048]{1,0:T(1,128)}, u32[]{:S(2)}) copy-start(s32[1,2048]{1,0:T(1,128)} %copy-done.15) | copy-start | bytes 24580
  82.1 24.1 %copy-start.1 = (bf16[2048,1024]{1,0:T(8,128)(2,1)S(1)}, bf16[2048,1024]{1,0:T(8,128)(2,1)}, u32[]{:S(2)}) copy-start(bf16[2048,1024]{1,0:T(8,128)(2,1)} %refs_9_.5) | copy-start | bytes 12582916
  82.1 3.7 %collective-permute-start.28 = (bf16[64,256]{1,0:T(8,128)(2,1)S(1)}, bf16[64,256]{1,0:T(8,128)(2,1)S(1)}, u32[]{:S(2)}, u32[]{:S(2)}) collective-permute-start(bf16[64,256]{1,0:T(8,128)(2,1)S(1)} %convolution_convert_fusion.2), channel_id=1, source_target_pairs={{0,3},{1,2},{2,1},{3,0},{4,7},{5,6},{6,5},{7,4},{8,11},{9,10},{10,... | collective-permute-start | bytes 98312 | tf_op jit(solution)/shard_map/ppermute | solution.py:24
  82.4 4.0 %collective-permute-start.27 = (bf16[64,256]{1,0:T(8,128)(2,1)S(1)}, bf16[64,256]{1,0:T(8,128)(2,1)S(1)}, u32[]{:S(2)}, u32[]{:S(2)}) collective-permute-start(bf16[64,256]{1,0:T(8,128)(2,1)S(1)} %convolution_convert_fusion.3), channel_id=1, source_target_pairs={{0,2},{1,3},{2,0},{3,1},{4,6},{5,7},{6,4},{7,5},{8,10},{9,11},{10,... | collective-permute-start | bytes 98312 | tf_op jit(solution)/shard_map/ppermute | solution.py:24
  84.0 2.4 %collective-permute-start.26 = (bf16[64,256]{1,0:T(8,128)(2,1)S(1)}, bf16[64,256]{1,0:T(8,128)(2,1)S(1)}, u32[]{:S(2)}, u32[]{:S(2)}) collective-permute-start(bf16[64,256]{1,0:T(8,128)(2,1)S(1)} %convolution_convert_fusion.2), channel_id=1, source_target_pairs={{0,1},{1,0},{2,3},{3,2},{4,5},{5,4},{6,7},{7,6},{8,9},{9,8},{10,11... | collective-permute-start | bytes 98312 | tf_op jit(solution)/shard_map/ppermute | solution.py:24
  86.4 4.9 %collective-permute-start.29 = (bf16[64,256]{1,0:T(8,128)(2,1)S(1)}, bf16[64,256]{1,0:T(8,128)(2,1)S(1)}, u32[]{:S(2)}, u32[]{:S(2)}) collective-permute-start(bf16[64,256]{1,0:T(8,128)(2,1)S(1)} %get-tuple-element.95), channel_id=1, source_target_pairs={{0,16},{4,20},{8,24},{12,28},{16,0},{20,4},{24,8},{28,12},{1,17},{... | collective-permute-start | bytes 98312 | tf_op jit(solution)/shard_map/ppermute | solution.py:24
  91.3 4.3 %collective-permute-start.30 = (bf16[64,512]{1,0:T(8,128)(2,1)S(1)}, bf16[64,512]{1,0:T(8,128)(2,1)S(1)}, u32[]{:S(2)}, u32[]{:S(2)}) collective-permute-start(bf16[64,512]{1,0:T(8,128)(2,1)S(1)} %pad_maximum_fusion.3.refs_0_), channel_id=1, source_target_pairs={{0,4},{4,0},{8,12},{12,8},{16,20},{20,16},{24,28},{28,24},{1,5},{5... | collective-permute-start | bytes 196616 | tf_op jit(solution)/shard_map/ppermute | solution.py:24
  92.3 4.6 %collective-permute-start.31 = (bf16[64,512]{1,0:T(8,128)(2,1)S(1)}, bf16[64,512]{1,0:T(8,128)(2,1)S(1)}, u32[]{:S(2)}, u32[]{:S(2)}) collective-permute-start(bf16[64,512]{1,0:T(8,128)(2,1)S(1)} %pad_maximum_fusion.3.refs_0_), channel_id=1, source_target_pairs={{0,8},{4,12},{8,0},{12,4},{16,24},{20,28},{24,16},{28,20},{1,9},{5... | collective-permute-start | bytes 196616 | tf_op jit(solution)/shard_map/ppermute | solution.py:24
  93.9 5.2 %collective-permute-start.32 = (bf16[64,512]{1,0:T(8,128)(2,1)S(1)}, bf16[64,512]{1,0:T(8,128)(2,1)S(1)}, u32[]{:S(2)}, u32[]{:S(2)}) collective-permute-start(bf16[64,512]{1,0:T(8,128)(2,1)S(1)} %pad_maximum_fusion.3.refs_0_), channel_id=1, source_target_pairs={{0,12},{4,8},{8,4},{12,0},{16,28},{20,24},{24,20},{28,16},{1,13},{... | collective-permute-start | bytes 196616 | tf_op jit(solution)/shard_map/ppermute | solution.py:24
  94.8 4.3 %collective-permute-start.33 = (bf16[64,512]{1,0:T(8,128)(2,1)S(1)}, bf16[64,512]{1,0:T(8,128)(2,1)S(1)}, u32[]{:S(2)}, u32[]{:S(2)}) collective-permute-start(bf16[64,512]{1,0:T(8,128)(2,1)S(1)} %pad_maximum_fusion.3.refs_0_), channel_id=1, source_target_pairs={{0,1},{1,0},{2,3},{3,2},{4,5},{5,4},{6,7},{7,6},{8,9},{9,8},{10,11... | collective-permute-start | bytes 196616 | tf_op jit(solution)/shard_map/ppermute | solution.py:24
  95.6 3.5 %collective-permute-start.34 = (bf16[64,512]{1,0:T(8,128)(2,1)S(1)}, bf16[64,512]{1,0:T(8,128)(2,1)S(1)}, u32[]{:S(2)}, u32[]{:S(2)}) collective-permute-start(bf16[64,512]{1,0:T(8,128)(2,1)S(1)} %collective-permute-done.30.refs_1_), channel_id=1, source_target_pairs={{0,1},{1,0},{2,3},{3,2},{4,5},{5,4},{6,7},{7,6},{8,9},{9,8},{10,11... | collective-permute-start | bytes 196616 | tf_op jit(solution)/shard_map/ppermute | solution.py:24
  96.8 2.2 %collective-permute-start.35 = (bf16[64,512]{1,0:T(8,128)(2,1)S(1)}, bf16[64,512]{1,0:T(8,128)(2,1)S(1)}, u32[]{:S(2)}, u32[]{:S(2)}) collective-permute-start(bf16[64,512]{1,0:T(8,128)(2,1)S(1)} %collective-permute-done.31.refs_2_), channel_id=1, source_target_pairs={{0,1},{1,0},{2,3},{3,2},{4,5},{5,4},{6,7},{7,6},{8,9},{9,8},{10,11... | collective-permute-start | bytes 196616 | tf_op jit(solution)/shard_map/ppermute | solution.py:24
  99.1 1.3 collective-permute-start.36
  102.5 7.7 %collective-permute-start.39 = (bf16[64,1024]{1,0:T(8,128)(2,1)S(1)}, bf16[64,1024]{1,0:T(8,128)(2,1)S(1)}, u32[]{:S(2)}, u32[]{:S(2)}) collective-permute-start(bf16[64,1024]{1,0:T(8,128)(2,1)S(1)} %convert_element_type.244), channel_id=1, source_target_pairs={{0,12},{4,8},{8,4},{12,0},{16,28},{20,24},{24,20},{28,16},{1,13},{... | collective-permute-start | bytes 393224 | tf_op jit(solution)/shard_map/ppermute | solution.py:24
  103.5 8.0 %collective-permute-start.38 = (bf16[64,1024]{1,0:T(8,128)(2,1)S(1)}, bf16[64,1024]{1,0:T(8,128)(2,1)S(1)}, u32[]{:S(2)}, u32[]{:S(2)}) collective-permute-start(bf16[64,1024]{1,0:T(8,128)(2,1)S(1)} %convert_element_type.244), channel_id=1, source_target_pairs={{0,8},{4,12},{8,0},{12,4},{16,24},{20,28},{24,16},{28,20},{1,9},{5... | collective-permute-start | bytes 393224 | tf_op jit(solution)/shard_map/ppermute | solution.py:24
  105.1 6.7 %collective-permute-start.37 = (bf16[64,1024]{1,0:T(8,128)(2,1)S(1)}, bf16[64,1024]{1,0:T(8,128)(2,1)S(1)}, u32[]{:S(2)}, u32[]{:S(2)}) collective-permute-start(bf16[64,1024]{1,0:T(8,128)(2,1)S(1)} %convert_element_type.244), channel_id=1, source_target_pairs={{0,4},{4,0},{8,12},{12,8},{16,20},{20,16},{24,28},{28,24},{1,5},{5... | collective-permute-start | bytes 393224 | tf_op jit(solution)/shard_map/ppermute | solution.py:24
  111.8 13.2 %copy-start.5 = (bf16[1024,2048]{1,0:T(8,128)(2,1)S(1)}, bf16[1024,2048]{1,0:T(8,128)(2,1)}, u32[]{:S(2)}) copy-start(bf16[1024,2048]{1,0:T(8,128)(2,1)} %param.27) | copy-start | bytes 12582916
  112.2 1.4 collective-permute-start.40
  112.3 3.2 %collective-permute-start.42 = (f32[64,256]{1,0:T(8,128)S(1)}, f32[64,256]{1,0:T(8,128)S(1)}, u32[]{:S(2)}, u32[]{:S(2)}) collective-permute-start(f32[64,256]{1,0:T(8,128)S(1)} %get-tuple-element.73.own_ref), channel_id=1, source_target_pairs={{0,1},{1,0},{2,3},{3,2},{4,5},{5,4},{6,7},{7,6},{8,9},{9,8},{10,11... | collective-permute-start | bytes 196616 | tf_op jit(solution)/shard_map/ppermute | solution.py:24
  113.9 4.3 %collective-permute-start.41 = (bf16[64,512]{1,0:T(8,128)(2,1)S(1)}, bf16[64,512]{1,0:T(8,128)(2,1)S(1)}, u32[]{:S(2)}, u32[]{:S(2)}) collective-permute-start(bf16[64,512]{1,0:T(8,128)(2,1)S(1)} %fusion.2), channel_id=1, source_target_pairs={{0,2},{1,3},{2,0},{3,1},{4,6},{5,7},{6,4},{7,5},{8,10},{9,11},{10,... | collective-permute-start | bytes 196616 | tf_op jit(solution)/shard_map/ppermute | solution.py:24
  118.3 4.9 %collective-permute-start.43 = (bf16[64,512]{1,0:T(8,128)(2,1)S(1)}, bf16[64,512]{1,0:T(8,128)(2,1)S(1)}, u32[]{:S(2)}, u32[]{:S(2)}) collective-permute-start(bf16[64,512]{1,0:T(8,128)(2,1)S(1)} %convert_element_type.253.refs_0_), channel_id=1, source_target_pairs={{0,4},{4,0},{8,12},{12,8},{16,20},{20,16},{24,28},{28,24},{1,5},{5... | collective-permute-start | bytes 196616 | tf_op jit(solution)/shard_map/ppermute | solution.py:24
  119.5 4.3 %collective-permute-start.44 = (bf16[64,512]{1,0:T(8,128)(2,1)S(1)}, bf16[64,512]{1,0:T(8,128)(2,1)S(1)}, u32[]{:S(2)}, u32[]{:S(2)}) collective-permute-start(bf16[64,512]{1,0:T(8,128)(2,1)S(1)} %convert_element_type.253.refs_0_), channel_id=1, source_target_pairs={{0,8},{4,12},{8,0},{12,4},{16,24},{20,28},{24,16},{28,20},{1,9},{5... | collective-permute-start | bytes 196616 | tf_op jit(solution)/shard_map/ppermute | solution.py:24
  119.9 5.2 %collective-permute-start.45 = (bf16[64,512]{1,0:T(8,128)(2,1)S(1)}, bf16[64,512]{1,0:T(8,128)(2,1)S(1)}, u32[]{:S(2)}, u32[]{:S(2)}) collective-permute-start(bf16[64,512]{1,0:T(8,128)(2,1)S(1)} %convert_element_type.253.refs_0_), channel_id=1, source_target_pairs={{0,12},{4,8},{8,4},{12,0},{16,28},{20,24},{24,20},{28,16},{1,13},{... | collective-permute-start | bytes 196616 | tf_op jit(solution)/shard_map/ppermute | solution.py:24
  121.9 3.7 %collective-permute-start.46 = (bf16[64,512]{1,0:T(8,128)(2,1)S(1)}, bf16[64,512]{1,0:T(8,128)(2,1)S(1)}, u32[]{:S(2)}, u32[]{:S(2)}) collective-permute-start(bf16[64,512]{1,0:T(8,128)(2,1)S(1)} %convert_element_type.253.refs_0_), channel_id=1, source_target_pairs={{0,1},{1,0},{2,3},{3,2},{4,5},{5,4},{6,7},{7,6},{8,9},{9,8},{10,11... | collective-permute-start | bytes 196616 | tf_op jit(solution)/shard_map/ppermute | solution.py:24
  121.9 8.4 %collective-permute-start.50 = (f32[64,512]{1,0:T(8,128)S(1)}, f32[64,512]{1,0:T(8,128)S(1)}, u32[]{:S(2)}, u32[]{:S(2)}) collective-permute-start(f32[64,512]{1,0:T(8,128)S(1)} %convert_add_fusion.4.own_ref), channel_id=1, source_target_pairs={{0,1},{1,0},{2,3},{3,2},{4,5},{5,4},{6,7},{7,6},{8,9},{9,8},{10,11... | collective-permute-start | bytes 393224 | tf_op jit(solution)/shard_map/ppermute | solution.py:24
  123.3 2.3 %collective-permute-start.47 = (bf16[64,512]{1,0:T(8,128)(2,1)S(1)}, bf16[64,512]{1,0:T(8,128)(2,1)S(1)}, u32[]{:S(2)}, u32[]{:S(2)}) collective-permute-start(bf16[64,512]{1,0:T(8,128)(2,1)S(1)} %collective-permute-done.43.refs_1_), channel_id=1, source_target_pairs={{0,1},{1,0},{2,3},{3,2},{4,5},{5,4},{6,7},{7,6},{8,9},{9,8},{10,11... | collective-permute-start | bytes 196616 | tf_op jit(solution)/shard_map/ppermute | solution.py:24
  123.7 1.9 %collective-permute-start.48 = (bf16[64,512]{1,0:T(8,128)(2,1)S(1)}, bf16[64,512]{1,0:T(8,128)(2,1)S(1)}, u32[]{:S(2)}, u32[]{:S(2)}) collective-permute-start(bf16[64,512]{1,0:T(8,128)(2,1)S(1)} %collective-permute-done.44.refs_2_), channel_id=1, source_target_pairs={{0,1},{1,0},{2,3},{3,2},{4,5},{5,4},{6,7},{7,6},{8,9},{9,8},{10,11... | collective-permute-start | bytes 196616 | tf_op jit(solution)/shard_map/ppermute | solution.py:24
  125.0 1.3 collective-permute-start.49
  130.3 5.6 %collective-permute-start.51 = (bf16[64,1024]{1,0:T(8,128)(2,1)S(1)}, bf16[64,1024]{1,0:T(8,128)(2,1)S(1)}, u32[]{:S(2)}, u32[]{:S(2)}) collective-permute-start(bf16[64,1024]{1,0:T(8,128)(2,1)S(1)} %add.296), channel_id=1, source_target_pairs={{0,4},{4,0},{8,12},{12,8},{16,20},{20,16},{24,28},{28,24},{1,5},{5... | collective-permute-start | bytes 393224 | tf_op jit(solution)/shard_map/ppermute | solution.py:24
  136.5 1.6 %collective-permute-start.52 = (f32[64,1024]{1,0:T(8,128)S(1)}, f32[64,1024]{1,0:T(8,128)S(1)}, u32[]{:S(2)}, u32[]{:S(2)}) collective-permute-start(f32[64,1024]{1,0:T(8,128)S(1)} %fusion.58), channel_id=1, source_target_pairs={{0,1},{1,0},{2,3},{3,2},{4,5},{5,4},{6,7},{7,6},{8,9},{9,8},{10,11... | collective-permute-start | bytes 786440 | tf_op jit(solution)/shard_map/ppermute | solution.py:24
  138.6 5.6 %collective-permute-start.53 = (bf16[64,1024]{1,0:T(8,128)(2,1)S(1)}, bf16[64,1024]{1,0:T(8,128)(2,1)S(1)}, u32[]{:S(2)}, u32[]{:S(2)}) collective-permute-start(bf16[64,1024]{1,0:T(8,128)(2,1)S(1)} %fusion), channel_id=1, source_target_pairs={{0,2},{1,3},{2,0},{3,1},{4,6},{5,7},{6,4},{7,5},{8,10},{9,11},{10,... | collective-permute-start | bytes 393224 | tf_op jit(solution)/shard_map/ppermute | solution.py:24
  144.2 1.6 %collective-permute-start.54 = (f32[64,1024]{1,0:T(8,128)S(1)}, f32[64,1024]{1,0:T(8,128)S(1)}, u32[]{:S(2)}, u32[]{:S(2)}) collective-permute-start(f32[64,1024]{1,0:T(8,128)S(1)} %convert_add_fusion.2.own_ref), channel_id=1, source_target_pairs={{0,1},{1,0},{2,3},{3,2},{4,5},{5,4},{6,7},{7,6},{8,9},{9,8},{10,11... | collective-permute-start | bytes 786440 | tf_op jit(solution)/shard_map/ppermute | solution.py:24
  (8 other events, 45.2 us)

commit v6 on v5

--- a/solution.py
+++ b/solution.py
@@ -295,9 +295,8 @@
     coupling, coupling_root = tied(coupling, picked_product(known_zero, place_root, upper_two))
     z_one = y_one - coupling
     z_one, x_zero = tied(z_one.astype(BF16), x_zero)
-    x_one, solution_zero = tied(front_half(z_one, split_one), outputs(x_zero))
+    x_one, solution_zero, keep, send = tied(front_half(z_one, split_one), outputs(x_zero), *halves(back_two))
     known_one = known_pieces(x_one, groups[1])
-    *known_one, keep, send = tied(*known_one, *halves(back_two))
 
     coupling = coupling_root + picked_product(known_one, place_one, upper_two)
     coupling, other = tied(coupling, partner(x_one, "front", 1))

time: 147 us -> 147 us (level)
  no operation moved by 1% of the time
where the time goes in v6:
time: 147 us
  waiting for transfers between devices  56.6 us (39%)
  starting transfers between devices  50.4 us (34%)
  Pallas kernels  19.4 us (13%)
  matrix products  7.63 us (5%)
  local copies, waits for them, and re-layouts  6.37 us (4%)
  other arithmetic  4.85 us (3%)
    ppermute x55, waiting for transfers between devices, partner(): lax.ppermute(x, axis, [(i, i ^ mask) for i in range(lax.axis_size(axis))])  56.6 us
    ppermute x55, starting transfers between devices, partner(): lax.ppermute(x, axis, [(i, i ^ mask) for i in range(lax.axis_size(axis))])  50.4 us
    pallas_call x3, Pallas kernels, picked_product(): pl.pallas_call(pick_kernel, grid=(count // step,), in_specs=[pl.BlockSpec...  10.1 us
    dot_general x13, matrix products, dot(): return jnp.dot(left, right, preferred_element_type=F32)  7.63 us
    pallas_call x6, Pallas kernels, put_columns(): pl.pallas_call(functools.partial(put_kernel, first=first), out_shape=jax....  7.1 us
    dynamic_slice x6, local copies, waits for them, and re-layouts, half_of(): return lax.dynamic_slice_in_dim(x, which * size, size, dim)  5.12 us
  transfers between devices with their start and end apart: 55, of which 43 were waited for; matrix products, arithmetic and copies ran while one was open for 7% of the time, Pallas kernels for 10%

profile of v6, /device:TPU:0, one launch (start us, length us, event | category | flops | bytes accessed | tf_op | source)
XLA Modules:
  0.0 146.6 jit_solution(6869363089633018905)
XLA Ops:
  0.6 3.3 %convolution_convert_fusion = bf16[64,1024]{1,0:T(8,128)(2,1)S(1)} fusion(bf16[2048,1024]{1,0:T(8,128)(2,1)} %param.20, f32[64,2048]{1,0:T(8,128)} %param.17), kind=kOutput, calls=%fused_computation.2 | convolution fusion | flops 268632064 | bytes 4849664 | tf_op jit(solution)/shard_map/dot_general | solution.py:15
  4.0 3.0 %collective-permute-start = (bf16[64,1024]{1,0:T(8,128)(2,1)S(1)}, bf16[64,1024]{1,0:T(8,128)(2,1)S(1)}, u32[]{:S(2)}, u32[]{:S(2)}) collective-permute-start(bf16[64,1024]{1,0:T(8,128)(2,1)S(1)} %convolution_convert_fusion), channel_id=1, source_target_pairs={{0,4},{4,0},{8,12},{12,8},{16,20},{20,16},{24,28},{28,24},{1,5},{5... | collective-permute-start | bytes 393224 | tf_op jit(solution)/shard_map/ppermute | solution.py:24
  7.0 0.9 compare_select_fusion
  9.0 2.7 %constant_dynamic-slice_fusion.16 = (bf16[1024,1024]{1,0:T(8,128)(2,1)S(1)}, bf16[1024,1024]{1,0:T(8,128)(2,1)S(1)}) fusion(bf16[1024,2048]{1,0:T(8,128)(2,1)} %param.22, s32[]{:T(128)S(6)} %select_n.171, s32[]{:T(128)S(6)} %select_n.170), kind=kLoop, calls=%fused_computation.137 | loop fusion | bytes 8388616 | tf_op jit(solution)/shard_map/dynamic_slice | solution.py:205
  12.7 1.0 collective-permute-done.1
  13.8 1.6 %collective-permute-start.2 = (bf16[64,1024]{1,0:T(8,128)(2,1)S(1)}, bf16[64,1024]{1,0:T(8,128)(2,1)S(1)}, u32[]{:S(2)}, u32[]{:S(2)}) collective-permute-start(bf16[64,1024]{1,0:T(8,128)(2,1)S(1)} %add_convert_fusion.2), channel_id=1, source_target_pairs={{0,2},{1,3},{2,0},{3,1},{4,6},{5,7},{6,4},{7,5},{8,10},{9,11},{10,... | collective-permute-start | bytes 393224 | tf_op jit(solution)/shard_map/ppermute | solution.py:24
  15.4 4.0 %collective-permute-done.2 = bf16[64,1024]{1,0:T(8,128)(2,1)S(1)} collective-permute-done((bf16[64,1024]{1,0:T(8,128)(2,1)S(1)}, bf16[64,1024]{1,0:T(8,128)(2,1)S(1)}, u32[]{:S(2)}, u32[]{:S(2)}) %collective-permute-start.2) | collective-permute-done | bytes 131104 | tf_op jit(solution)/shard_map/ppermute | solution.py:24
  19.5 1.4 shard_map.167
  20.9 1.4 shard_map.166
  22.5 1.7 %collective-permute-start.6 = (bf16[64,512]{1,0:T(8,128)(2,1)S(1)}, bf16[64,512]{1,0:T(8,128)(2,1)S(1)}, u32[]{:S(2)}, u32[]{:S(2)}) collective-permute-start(bf16[64,512]{1,0:T(8,128)(2,1)S(1)} %get-tuple-element.107), channel_id=1, source_target_pairs={{0,12},{4,8},{8,4},{12,0},{16,28},{20,24},{24,20},{28,16},{1,13},{... | collective-permute-start | bytes 196616 | tf_op jit(solution)/shard_map/ppermute | solution.py:24
  24.7 1.4 collective-permute-start.4
  26.1 1.9 %collective-permute-done.6 = bf16[64,512]{1,0:T(8,128)(2,1)S(1)} collective-permute-done((bf16[64,512]{1,0:T(8,128)(2,1)S(1)}, bf16[64,512]{1,0:T(8,128)(2,1)S(1)}, u32[]{:S(2)}, u32[]{:S(2)}) %collective-permute-start.6) | collective-permute-done | bytes 65568 | tf_op jit(solution)/shard_map/ppermute | solution.py:24
  29.4 1.2 collective-permute-done.7
  31.2 2.2 %collective-permute-start.10 = (bf16[64,1024]{1,0:T(8,128)(2,1)S(1)}, bf16[64,1024]{1,0:T(8,128)(2,1)S(1)}, u32[]{:S(2)}, u32[]{:S(2)}) collective-permute-start(bf16[64,1024]{1,0:T(8,128)(2,1)S(1)} %convolution_convert_fusion.1), channel_id=1, source_target_pairs={{0,12},{4,8},{8,4},{12,0},{16,28},{20,24},{24,20},{28,16},{1,13},{... | collective-permute-start | bytes 393224 | tf_op jit(solution)/shard_map/ppermute | solution.py:24
  34.7 1.5 %constant_dynamic-slice_fusion.14 = (bf16[1024,512]{1,0:T(8,128)(2,1)}, bf16[1024,512]{1,0:T(8,128)(2,1)}) fusion(bf16[1024,1024]{1,0:T(8,128)(2,1)S(1)} %copy-done.6, s32[]{:T(128)S(6)} %select_n.191, s32[]{:T(128)S(6)} %select_n.188), kind=kLoop, calls=%fused_computation.135 | loop fusion | bytes 4194312 | tf_op jit(solution)/shard_map/dynamic_slice | solution.py:205
  36.3 1.4 shard_map.168
  37.7 1.4 shard_map.169
  39.1 1.2 collective-permute-done.9
  40.6 1.0 add_convert_fusion
  43.7 1.6 %collective-permute-start.12 = (bf16[64,512]{1,0:T(8,128)(2,1)S(1)}, bf16[64,512]{1,0:T(8,128)(2,1)S(1)}, u32[]{:S(2)}, u32[]{:S(2)}) collective-permute-start(bf16[64,512]{1,0:T(8,128)(2,1)S(1)} %fusion.1), channel_id=1, source_target_pairs={{0,2},{1,3},{2,0},{3,1},{4,6},{5,7},{6,4},{7,5},{8,10},{9,11},{10,... | collective-permute-start | bytes 196616 | tf_op jit(solution)/shard_map/ppermute | solution.py:24
  45.2 1.0 constant_dynamic-slice_fusion.13
  46.3 1.7 %collective-permute-done.12 = bf16[64,512]{1,0:T(8,128)(2,1)S(1)} collective-permute-done((bf16[64,512]{1,0:T(8,128)(2,1)S(1)}, bf16[64,512]{1,0:T(8,128)(2,1)S(1)}, u32[]{:S(2)}, u32[]{:S(2)}) %collective-permute-start.12) | collective-permute-done | bytes 65568 | tf_op jit(solution)/shard_map/ppermute | solution.py:24
  50.6 2.2 %collective-permute-start.16 = (bf16[64,512]{1,0:T(8,128)(2,1)S(1)}, bf16[64,512]{1,0:T(8,128)(2,1)S(1)}, u32[]{:S(2)}, u32[]{:S(2)}) collective-permute-start(bf16[64,512]{1,0:T(8,128)(2,1)S(1)} %get-tuple-element.104), channel_id=1, source_target_pairs={{0,12},{4,8},{8,4},{12,0},{16,28},{20,24},{24,20},{28,16},{1,13},{... | collective-permute-start | bytes 196616 | tf_op jit(solution)/shard_map/ppermute | solution.py:24
  53.2 0.9 collective-permute-start.14
  54.2 1.9 %collective-permute-done.16 = bf16[64,512]{1,0:T(8,128)(2,1)S(1)} collective-permute-done((bf16[64,512]{1,0:T(8,128)(2,1)S(1)}, bf16[64,512]{1,0:T(8,128)(2,1)S(1)}, u32[]{:S(2)}, u32[]{:S(2)}) %collective-permute-start.16) | collective-permute-done | bytes 65568 | tf_op jit(solution)/shard_map/ppermute | solution.py:24
  57.5 2.7 %collective-permute-start.17 = (bf16[64,256]{1,0:T(8,128)(2,1)S(1)}, bf16[64,256]{1,0:T(8,128)(2,1)S(1)}, u32[]{:S(2)}, u32[]{:S(2)}) collective-permute-start(bf16[64,256]{1,0:T(8,128)(2,1)S(1)} %slice.127), channel_id=1, source_target_pairs={{0,16},{4,20},{8,24},{12,28},{16,0},{20,4},{24,8},{28,12},{1,17},{... | collective-permute-start | bytes 98312 | tf_op jit(solution)/shard_map/ppermute | solution.py:24
  60.3 2.1 %collective-permute-done.17 = bf16[64,256]{1,0:T(8,128)(2,1)S(1)} collective-permute-done((bf16[64,256]{1,0:T(8,128)(2,1)S(1)}, bf16[64,256]{1,0:T(8,128)(2,1)S(1)}, u32[]{:S(2)}, u32[]{:S(2)}) %collective-permute-start.17) | collective-permute-done | bytes 32800 | tf_op jit(solution)/shard_map/ppermute | solution.py:24
  62.5 1.2 collective-permute-done.18
  64.0 2.0 %collective-permute-start.21 = (bf16[64,256]{1,0:T(8,128)(2,1)S(1)}, bf16[64,256]{1,0:T(8,128)(2,1)S(1)}, u32[]{:S(2)}, u32[]{:S(2)}) collective-permute-start(bf16[64,256]{1,0:T(8,128)(2,1)S(1)} %get-tuple-element.110), channel_id=1, source_target_pairs={{0,12},{4,8},{8,4},{12,0},{16,28},{20,24},{24,20},{28,16},{1,13},{... | collective-permute-start | bytes 98312 | tf_op jit(solution)/shard_map/ppermute | solution.py:24
  66.5 1.1 collective-permute-start.19
  67.6 1.3 collective-permute-done.21
  68.9 1.0 collective-permute-done.20
  70.4 2.7 %collective-permute-start.22 = (bf16[64,256]{1,0:T(8,128)(2,1)S(1)}, bf16[64,256]{1,0:T(8,128)(2,1)S(1)}, u32[]{:S(2)}, u32[]{:S(2)}) collective-permute-start(bf16[64,256]{1,0:T(8,128)(2,1)S(1)} %fusion.15), channel_id=1, source_target_pairs={{0,16},{4,20},{8,24},{12,28},{16,0},{20,4},{24,8},{28,12},{1,17},{... | collective-permute-start | bytes 98312 | tf_op jit(solution)/shard_map/ppermute | solution.py:24
  73.1 2.2 %collective-permute-done.22 = bf16[64,256]{1,0:T(8,128)(2,1)S(1)} collective-permute-done((bf16[64,256]{1,0:T(8,128)(2,1)S(1)}, bf16[64,256]{1,0:T(8,128)(2,1)S(1)}, u32[]{:S(2)}, u32[]{:S(2)}) %collective-permute-start.22) | collective-permute-done | bytes 32800 | tf_op jit(solution)/shard_map/ppermute | solution.py:24
  75.3 2.2 %collective-permute-start.25 = (bf16[64,256]{1,0:T(8,128)(2,1)S(1)}, bf16[64,256]{1,0:T(8,128)(2,1)S(1)}, u32[]{:S(2)}, u32[]{:S(2)}) collective-permute-start(bf16[64,256]{1,0:T(8,128)(2,1)S(1)} %add_convert_fusion.5), channel_id=1, source_target_pairs={{0,12},{4,8},{8,4},{12,0},{16,28},{20,24},{24,20},{28,16},{1,13},{... | collective-permute-start | bytes 98312 | tf_op jit(solution)/shard_map/ppermute | solution.py:24
  79.1 1.1 collective-permute-done.25
  80.2 1.2 collective-permute-done.24
  82.4 1.6 %collective-permute-start.27 = (bf16[64,256]{1,0:T(8,128)(2,1)S(1)}, bf16[64,256]{1,0:T(8,128)(2,1)S(1)}, u32[]{:S(2)}, u32[]{:S(2)}) collective-permute-start(bf16[64,256]{1,0:T(8,128)(2,1)S(1)} %convolution_convert_fusion.3), channel_id=1, source_target_pairs={{0,2},{1,3},{2,0},{3,1},{4,6},{5,7},{6,4},{7,5},{8,10},{9,11},{10,... | collective-permute-start | bytes 98312 | tf_op jit(solution)/shard_map/ppermute | solution.py:24
  84.3 1.5 %collective-permute-done.28 = bf16[64,256]{1,0:T(8,128)(2,1)S(1)} collective-permute-done((bf16[64,256]{1,0:T(8,128)(2,1)S(1)}, bf16[64,256]{1,0:T(8,128)(2,1)S(1)}, u32[]{:S(2)}, u32[]{:S(2)}) %collective-permute-start.28) | collective-permute-done | bytes 32800 | tf_op jit(solution)/shard_map/ppermute | solution.py:24
  86.4 2.7 %collective-permute-start.29 = (bf16[64,256]{1,0:T(8,128)(2,1)S(1)}, bf16[64,256]{1,0:T(8,128)(2,1)S(1)}, u32[]{:S(2)}, u32[]{:S(2)}) collective-permute-start(bf16[64,256]{1,0:T(8,128)(2,1)S(1)} %get-tuple-element.79), channel_id=1, source_target_pairs={{0,16},{4,20},{8,24},{12,28},{16,0},{20,4},{24,8},{28,12},{1,17},{... | collective-permute-start | bytes 98312 | tf_op jit(solution)/shard_map/ppermute | solution.py:24
  89.1 2.2 %collective-permute-done.29 = bf16[64,256]{1,0:T(8,128)(2,1)S(1)} collective-permute-done((bf16[64,256]{1,0:T(8,128)(2,1)S(1)}, bf16[64,256]{1,0:T(8,128)(2,1)S(1)}, u32[]{:S(2)}, u32[]{:S(2)}) %collective-permute-start.29) | collective-permute-done | bytes 32800 | tf_op jit(solution)/shard_map/ppermute | solution.py:24
  92.3 1.6 %collective-permute-start.31 = (bf16[64,512]{1,0:T(8,128)(2,1)S(1)}, bf16[64,512]{1,0:T(8,128)(2,1)S(1)}, u32[]{:S(2)}, u32[]{:S(2)}) collective-permute-start(bf16[64,512]{1,0:T(8,128)(2,1)S(1)} %pad_maximum_fusion.3.refs_0_), channel_id=1, source_target_pairs={{0,8},{4,12},{8,0},{12,4},{16,24},{20,28},{24,16},{28,20},{1,9},{5... | collective-permute-start | bytes 196616 | tf_op jit(solution)/shard_map/ppermute | solution.py:24
  95.6 1.3 collective-permute-done.31.refs_2_
  96.8 2.2 %collective-permute-done.32.refs_3_ = bf16[64,512]{1,0:T(8,128)(2,1)S(1)} collective-permute-done((bf16[64,512]{1,0:T(8,128)(2,1)S(1)}, bf16[64,512]{1,0:T(8,128)(2,1)S(1)}, u32[]{:S(2)}, u32[]{:S(2)}) %collective-permute-start.32) | collective-permute-done | bytes 65568 | tf_op jit(solution)/shard_map/ppermute | solution.py:24
  99.1 1.2 collective-permute-done.36.refs_7_
  100.3 2.1 %shard_map.172 = f32[64,1024]{1,0:T(8,128)S(1)} custom-call(bf16[64,512]{1,0:T(8,128)(2,1)S(1)} %pad_maximum_fusion.3.refs_0_, bf16[64,512]{1,0:T(8,128)(2,1)S(1)} %collective-permute-done.30.refs_1_, bf16[64,512]{1,0:T(8,128)(2,1)S(1)} %collective-permute-done.31.refs_2_, bf16[64,512]{1,0:T(8,128)(2,1)S(1)} %collective-permute-done.32.refs_3_, ...), custom_call_target="tpu_custom_call" | custom-call | flops 671088640 | bytes 18874368 | tf_op jit(solution)/shard_map/pallas_call | solution.py:105
  102.5 1.0 collective-permute-start.39
  103.5 1.6 %collective-permute-start.38 = (bf16[64,1024]{1,0:T(8,128)(2,1)S(1)}, bf16[64,1024]{1,0:T(8,128)(2,1)S(1)}, u32[]{:S(2)}, u32[]{:S(2)}) collective-permute-start(bf16[64,1024]{1,0:T(8,128)(2,1)S(1)} %convert_element_type.244), channel_id=1, source_target_pairs={{0,8},{4,12},{8,0},{12,4},{16,24},{20,28},{24,16},{28,20},{1,9},{5... | collective-permute-start | bytes 393224 | tf_op jit(solution)/shard_map/ppermute | solution.py:24
  105.1 0.9 collective-permute-start.37
  106.2 4.0 %shard_map.173 = f32[64,1024]{1,0:T(8,128)S(1)} custom-call(bf16[64,512]{1,0:T(8,128)(2,1)S(1)} %pad_maximum_fusion.3.refs_0_, bf16[64,512]{1,0:T(8,128)(2,1)S(1)} %collective-permute-done.30.refs_1_, bf16[64,512]{1,0:T(8,128)(2,1)S(1)} %collective-permute-done.31.refs_2_, bf16[64,512]{1,0:T(8,128)(2,1)S(1)} %collective-permute-done.32.refs_3_, ...), custom_call_target="tpu_custom_call" | custom-call | flops 1342177280 | bytes 37748736 | tf_op jit(solution)/shard_map/pallas_call | solution.py:105
  110.2 1.2 collective-permute-done.38
  113.9 1.5 %collective-permute-start.41 = (bf16[64,512]{1,0:T(8,128)(2,1)S(1)}, bf16[64,512]{1,0:T(8,128)(2,1)S(1)}, u32[]{:S(2)}, u32[]{:S(2)}) collective-permute-start(bf16[64,512]{1,0:T(8,128)(2,1)S(1)} %fusion.2), channel_id=1, source_target_pairs={{0,2},{1,3},{2,0},{3,1},{4,6},{5,7},{6,4},{7,5},{8,10},{9,11},{10,... | collective-permute-start | bytes 196616 | tf_op jit(solution)/shard_map/ppermute | solution.py:24
  116.7 1.5 %collective-permute-done.41 = bf16[64,512]{1,0:T(8,128)(2,1)S(1)} collective-permute-done((bf16[64,512]{1,0:T(8,128)(2,1)S(1)}, bf16[64,512]{1,0:T(8,128)(2,1)S(1)}, u32[]{:S(2)}, u32[]{:S(2)}) %collective-permute-start.41) | collective-permute-done | bytes 65568 | tf_op jit(solution)/shard_map/ppermute | solution.py:24
  118.3 1.2 collective-permute-start.43
  119.9 2.0 %collective-permute-start.45 = (bf16[64,512]{1,0:T(8,128)(2,1)S(1)}, bf16[64,512]{1,0:T(8,128)(2,1)S(1)}, u32[]{:S(2)}, u32[]{:S(2)}) collective-permute-start(bf16[64,512]{1,0:T(8,128)(2,1)S(1)} %convert_element_type.253.refs_0_), channel_id=1, source_target_pairs={{0,12},{4,8},{8,4},{12,0},{16,28},{20,24},{24,20},{28,16},{1,13},{... | collective-permute-start | bytes 196616 | tf_op jit(solution)/shard_map/ppermute | solution.py:24
  121.9 1.4 collective-permute-done.43.refs_1_
  123.8 1.3 collective-permute-done.45.refs_3_
  126.3 4.0 %shard_map.175 = f32[64,1024]{1,0:T(8,128)S(1)} custom-call(bf16[64,512]{1,0:T(8,128)(2,1)S(1)} %convert_element_type.253.refs_0_, bf16[64,512]{1,0:T(8,128)(2,1)S(1)} %collective-permute-done.43.refs_1_, bf16[64,512]{1,0:T(8,128)(2,1)S(1)} %collective-permute-done.44.refs_2_, bf16[64,512]{1,0:T(8,128)(2,1)S(1)} %collective-permute-done.45.refs_3_, ...), custom_call_target="tpu_custom_call" | custom-call | flops 1342177280 | bytes 37748736 | tf_op jit(solution)/shard_map/pallas_call | solution.py:105
  130.3 1.0 collective-permute-start.51
  132.0 3.9 %collective-permute-done.51 = bf16[64,1024]{1,0:T(8,128)(2,1)S(1)} collective-permute-done((bf16[64,1024]{1,0:T(8,128)(2,1)S(1)}, bf16[64,1024]{1,0:T(8,128)(2,1)S(1)}, u32[]{:S(2)}, u32[]{:S(2)}) %collective-permute-start.51) | collective-permute-done | bytes 131104 | tf_op jit(solution)/shard_map/ppermute | solution.py:24
  136.5 1.5 %collective-permute-done.52 = f32[64,1024]{1,0:T(8,128)S(1)} collective-permute-done((f32[64,1024]{1,0:T(8,128)S(1)}, f32[64,1024]{1,0:T(8,128)S(1)}, u32[]{:S(2)}, u32[]{:S(2)}) %collective-permute-start.52) | collective-permute-done | bytes 262176 | tf_op jit(solution)/shard_map/ppermute | solution.py:24
  138.6 1.6 %collective-permute-start.53 = (bf16[64,1024]{1,0:T(8,128)(2,1)S(1)}, bf16[64,1024]{1,0:T(8,128)(2,1)S(1)}, u32[]{:S(2)}, u32[]{:S(2)}) collective-permute-start(bf16[64,1024]{1,0:T(8,128)(2,1)S(1)} %fusion), channel_id=1, source_target_pairs={{0,2},{1,3},{2,0},{3,1},{4,6},{5,7},{6,4},{7,5},{8,10},{9,11},{10,... | collective-permute-start | bytes 393224 | tf_op jit(solution)/shard_map/ppermute | solution.py:24
  140.2 4.0 %collective-permute-done.53 = bf16[64,1024]{1,0:T(8,128)(2,1)S(1)} collective-permute-done((bf16[64,1024]{1,0:T(8,128)(2,1)S(1)}, bf16[64,1024]{1,0:T(8,128)(2,1)S(1)}, u32[]{:S(2)}, u32[]{:S(2)}) %collective-permute-start.53) | collective-permute-done | bytes 131104 | tf_op jit(solution)/shard_map/ppermute | solution.py:24
  144.3 1.5 %collective-permute-done.54.other_ref = f32[64,1024]{1,0:T(8,128)S(1)} collective-permute-done((f32[64,1024]{1,0:T(8,128)S(1)}, f32[64,1024]{1,0:T(8,128)S(1)}, u32[]{:S(2)}, u32[]{:S(2)}) %collective-permute-start.54) | collective-permute-done | bytes 262176 | tf_op jit(solution)/shard_map/ppermute | solution.py:24
  (153 shorter events, 29.3 us)
Async XLA Ops:
  0.6 30.0 %copy-start = (bf16[1024,1024]{1,0:T(8,128)(2,1)S(1)}, bf16[1024,1024]{1,0:T(8,128)(2,1)}, u32[]{:S(2)}) copy-start(bf16[1024,1024]{1,0:T(8,128)(2,1)} %param.19) | copy-start | bytes 6291460
  4.0 7.6 %collective-permute-start = (bf16[64,1024]{1,0:T(8,128)(2,1)S(1)}, bf16[64,1024]{1,0:T(8,128)(2,1)S(1)}, u32[]{:S(2)}, u32[]{:S(2)}) collective-permute-start(bf16[64,1024]{1,0:T(8,128)(2,1)S(1)} %convolution_convert_fusion), channel_id=1, source_target_pairs={{0,4},{4,0},{8,12},{12,8},{16,20},{20,16},{24,28},{28,24},{1,5},{5... | collective-permute-start | bytes 393224 | tf_op jit(solution)/shard_map/ppermute | solution.py:24
  12.2 1.6 %collective-permute-start.1 = (f32[64,1024]{1,0:T(8,128)S(1)}, f32[64,1024]{1,0:T(8,128)S(1)}, u32[]{:S(2)}, u32[]{:S(2)}) collective-permute-start(f32[64,1024]{1,0:T(8,128)S(1)} %fusion.67), channel_id=1, source_target_pairs={{0,1},{1,0},{2,3},{3,2},{4,5},{5,4},{6,7},{7,6},{8,9},{9,8},{10,11... | collective-permute-start | bytes 786440 | tf_op jit(solution)/shard_map/ppermute | solution.py:24
  13.8 5.6 %collective-permute-start.2 = (bf16[64,1024]{1,0:T(8,128)(2,1)S(1)}, bf16[64,1024]{1,0:T(8,128)(2,1)S(1)}, u32[]{:S(2)}, u32[]{:S(2)}) collective-permute-start(bf16[64,1024]{1,0:T(8,128)(2,1)S(1)} %add_convert_fusion.2), channel_id=1, source_target_pairs={{0,2},{1,3},{2,0},{3,1},{4,6},{5,7},{6,4},{7,5},{8,10},{9,11},{10,... | collective-permute-start | bytes 393224 | tf_op jit(solution)/shard_map/ppermute | solution.py:24
  20.8 1.6 %collective-permute-start.3 = (bf16[64,2048]{1,0:T(8,128)(2,1)S(1)}, bf16[64,2048]{1,0:T(8,128)(2,1)S(1)}, u32[]{:S(2)}, u32[]{:S(2)}) collective-permute-start(bf16[64,2048]{1,0:T(8,128)(2,1)S(1)} %shard_map.167), channel_id=1, source_target_pairs={{0,1},{1,0},{2,3},{3,2},{4,5},{5,4},{6,7},{7,6},{8,9},{9,8},{10,11... | collective-permute-start | bytes 786440 | tf_op jit(solution)/shard_map/ppermute | solution.py:24
  22.5 5.5 %collective-permute-start.6 = (bf16[64,512]{1,0:T(8,128)(2,1)S(1)}, bf16[64,512]{1,0:T(8,128)(2,1)S(1)}, u32[]{:S(2)}, u32[]{:S(2)}) collective-permute-start(bf16[64,512]{1,0:T(8,128)(2,1)S(1)} %get-tuple-element.107), channel_id=1, source_target_pairs={{0,12},{4,8},{8,4},{12,0},{16,28},{20,24},{24,20},{28,16},{1,13},{... | collective-permute-start | bytes 196616 | tf_op jit(solution)/shard_map/ppermute | solution.py:24
  24.2 4.3 %collective-permute-start.5 = (bf16[64,512]{1,0:T(8,128)(2,1)S(1)}, bf16[64,512]{1,0:T(8,128)(2,1)S(1)}, u32[]{:S(2)}, u32[]{:S(2)}) collective-permute-start(bf16[64,512]{1,0:T(8,128)(2,1)S(1)} %get-tuple-element.108), channel_id=1, source_target_pairs={{0,8},{4,12},{8,0},{12,4},{16,24},{20,28},{24,16},{28,20},{1,9},{5... | collective-permute-start | bytes 196616 | tf_op jit(solution)/shard_map/ppermute | solution.py:24
  24.7 4.6 %collective-permute-start.4 = (bf16[64,512]{1,0:T(8,128)(2,1)S(1)}, bf16[64,512]{1,0:T(8,128)(2,1)S(1)}, u32[]{:S(2)}, u32[]{:S(2)}) collective-permute-start(bf16[64,512]{1,0:T(8,128)(2,1)S(1)} %get-tuple-element.106), channel_id=1, source_target_pairs={{0,4},{4,0},{8,12},{12,8},{16,20},{20,16},{24,28},{28,24},{1,5},{5... | collective-permute-start | bytes 196616 | tf_op jit(solution)/shard_map/ppermute | solution.py:24
  29.3 1.3 collective-permute-start.7
  31.2 7.9 %collective-permute-start.10 = (bf16[64,1024]{1,0:T(8,128)(2,1)S(1)}, bf16[64,1024]{1,0:T(8,128)(2,1)S(1)}, u32[]{:S(2)}, u32[]{:S(2)}) collective-permute-start(bf16[64,1024]{1,0:T(8,128)(2,1)S(1)} %convolution_convert_fusion.1), channel_id=1, source_target_pairs={{0,12},{4,8},{8,4},{12,0},{16,28},{20,24},{24,20},{28,16},{1,13},{... | collective-permute-start | bytes 393224 | tf_op jit(solution)/shard_map/ppermute | solution.py:24
  33.3 6.9 %collective-permute-start.9 = (bf16[64,1024]{1,0:T(8,128)(2,1)S(1)}, bf16[64,1024]{1,0:T(8,128)(2,1)}, u32[]{:S(2)}, u32[]{:S(2)}) collective-permute-start(bf16[64,1024]{1,0:T(8,128)(2,1)S(1)} %convolution_convert_fusion.1), channel_id=1, source_target_pairs={{0,8},{4,12},{8,0},{12,4},{16,24},{20,28},{24,16},{28,20},{1,9},{5... | collective-permute-start | bytes 393224 | tf_op jit(solution)/shard_map/ppermute | solution.py:24
  33.8 6.8 %collective-permute-start.8 = (bf16[64,1024]{1,0:T(8,128)(2,1)S(1)}, bf16[64,1024]{1,0:T(8,128)(2,1)}, u32[]{:S(2)}, u32[]{:S(2)}) collective-permute-start(bf16[64,1024]{1,0:T(8,128)(2,1)S(1)} %convolution_convert_fusion.1), channel_id=1, source_target_pairs={{0,4},{4,0},{8,12},{12,8},{16,20},{20,16},{24,28},{28,24},{1,5},{5... | collective-permute-start | bytes 393224 | tf_op jit(solution)/shard_map/ppermute | solution.py:24
  41.9 1.4 collective-permute-start.11
  43.7 4.3 %collective-permute-start.12 = (bf16[64,512]{1,0:T(8,128)(2,1)S(1)}, bf16[64,512]{1,0:T(8,128)(2,1)S(1)}, u32[]{:S(2)}, u32[]{:S(2)}) collective-permute-start(bf16[64,512]{1,0:T(8,128)(2,1)S(1)} %fusion.1), channel_id=1, source_target_pairs={{0,2},{1,3},{2,0},{3,1},{4,6},{5,7},{6,4},{7,5},{8,10},{9,11},{10,... | collective-permute-start | bytes 196616 | tf_op jit(solution)/shard_map/ppermute | solution.py:24
  48.8 1.6 %collective-permute-start.13 = (bf16[64,2048]{1,0:T(8,128)(2,1)S(1)}, bf16[64,2048]{1,0:T(8,128)(2,1)S(1)}, u32[]{:S(2)}, u32[]{:S(2)}) collective-permute-start(bf16[64,2048]{1,0:T(8,128)(2,1)S(1)} %add.263), channel_id=1, source_target_pairs={{0,1},{1,0},{2,3},{3,2},{4,5},{5,4},{6,7},{7,6},{8,9},{9,8},{10,11... | collective-permute-start | bytes 786440 | tf_op jit(solution)/shard_map/ppermute | solution.py:24
  49.9 10.3 %copy-start.10 = (bf16[512,256]{1,0:T(8,128)(2,1)S(1)}, bf16[512,256]{1,0:T(8,128)(2,1)}, u32[]{:S(2)}) copy-start(bf16[512,256]{1,0:T(8,128)(2,1)} %get-tuple-element.99) | copy-start | bytes 786436
  49.9 10.3 %copy-start.11 = (bf16[512,256]{1,0:T(8,128)(2,1)S(1)}, bf16[512,256]{1,0:T(8,128)(2,1)}, u32[]{:S(2)}) copy-start(bf16[512,256]{1,0:T(8,128)(2,1)} %get-tuple-element.100) | copy-start | bytes 786436
  49.9 10.3 %copy-start.12 = (bf16[512,256]{1,0:T(8,128)(2,1)S(1)}, bf16[512,256]{1,0:T(8,128)(2,1)}, u32[]{:S(2)}) copy-start(bf16[512,256]{1,0:T(8,128)(2,1)} %get-tuple-element.101) | copy-start | bytes 786436
  49.9 10.3 %copy-start.13 = (bf16[512,256]{1,0:T(8,128)(2,1)S(1)}, bf16[512,256]{1,0:T(8,128)(2,1)}, u32[]{:S(2)}) copy-start(bf16[512,256]{1,0:T(8,128)(2,1)} %get-tuple-element.102) | copy-start | bytes 786436
  50.6 5.5 %collective-permute-start.16 = (bf16[64,512]{1,0:T(8,128)(2,1)S(1)}, bf16[64,512]{1,0:T(8,128)(2,1)S(1)}, u32[]{:S(2)}, u32[]{:S(2)}) collective-permute-start(bf16[64,512]{1,0:T(8,128)(2,1)S(1)} %get-tuple-element.104), channel_id=1, source_target_pairs={{0,12},{4,8},{8,4},{12,0},{16,28},{20,24},{24,20},{28,16},{1,13},{... | collective-permute-start | bytes 196616 | tf_op jit(solution)/shard_map/ppermute | solution.py:24
  52.8 4.3 %collective-permute-start.15 = (bf16[64,512]{1,0:T(8,128)(2,1)S(1)}, bf16[64,512]{1,0:T(8,128)(2,1)S(1)}, u32[]{:S(2)}, u32[]{:S(2)}) collective-permute-start(bf16[64,512]{1,0:T(8,128)(2,1)S(1)} %get-tuple-element.105), channel_id=1, source_target_pairs={{0,8},{4,12},{8,0},{12,4},{16,24},{20,28},{24,16},{28,20},{1,9},{5... | collective-permute-start | bytes 196616 | tf_op jit(solution)/shard_map/ppermute | solution.py:24
  53.2 4.3 %collective-permute-start.14 = (bf16[64,512]{1,0:T(8,128)(2,1)S(1)}, bf16[64,512]{1,0:T(8,128)(2,1)S(1)}, u32[]{:S(2)}, u32[]{:S(2)}) collective-permute-start(bf16[64,512]{1,0:T(8,128)(2,1)S(1)} %get-tuple-element.103), channel_id=1, source_target_pairs={{0,4},{4,0},{8,12},{12,8},{16,20},{20,16},{24,28},{28,24},{1,5},{5... | collective-permute-start | bytes 196616 | tf_op jit(solution)/shard_map/ppermute | solution.py:24
  57.5 4.9 %collective-permute-start.17 = (bf16[64,256]{1,0:T(8,128)(2,1)S(1)}, bf16[64,256]{1,0:T(8,128)(2,1)S(1)}, u32[]{:S(2)}, u32[]{:S(2)}) collective-permute-start(bf16[64,256]{1,0:T(8,128)(2,1)S(1)} %slice.127), channel_id=1, source_target_pairs={{0,16},{4,20},{8,24},{12,28},{16,0},{20,4},{24,8},{28,12},{1,17},{... | collective-permute-start | bytes 98312 | tf_op jit(solution)/shard_map/ppermute | solution.py:24
  60.2 18.7 %copy-start.7 = (bf16[1024,1024]{1,0:T(8,128)(2,1)S(1)}, bf16[1024,1024]{1,0:T(8,128)(2,1)}, u32[]{:S(2)}) copy-start(bf16[1024,1024]{1,0:T(8,128)(2,1)} %param.26) | copy-start | bytes 6291460
  62.4 1.3 collective-permute-start.18
  64.0 4.9 %collective-permute-start.21 = (bf16[64,256]{1,0:T(8,128)(2,1)S(1)}, bf16[64,256]{1,0:T(8,128)(2,1)S(1)}, u32[]{:S(2)}, u32[]{:S(2)}) collective-permute-start(bf16[64,256]{1,0:T(8,128)(2,1)S(1)} %get-tuple-element.110), channel_id=1, source_target_pairs={{0,12},{4,8},{8,4},{12,0},{16,28},{20,24},{24,20},{28,16},{1,13},{... | collective-permute-start | bytes 98312 | tf_op jit(solution)/shard_map/ppermute | solution.py:24
  66.0 3.9 %collective-permute-start.20 = (bf16[64,256]{1,0:T(8,128)(2,1)S(1)}, bf16[64,256]{1,0:T(8,128)(2,1)S(1)}, u32[]{:S(2)}, u32[]{:S(2)}) collective-permute-start(bf16[64,256]{1,0:T(8,128)(2,1)S(1)} %get-tuple-element.111), channel_id=1, source_target_pairs={{0,8},{4,12},{8,0},{12,4},{16,24},{20,28},{24,16},{28,20},{1,9},{5... | collective-permute-start | bytes 98312 | tf_op jit(solution)/shard_map/ppermute | solution.py:24
  66.5 3.9 %collective-permute-start.19 = (bf16[64,256]{1,0:T(8,128)(2,1)S(1)}, bf16[64,256]{1,0:T(8,128)(2,1)S(1)}, u32[]{:S(2)}, u32[]{:S(2)}) collective-permute-start(bf16[64,256]{1,0:T(8,128)(2,1)S(1)} %get-tuple-element.109), channel_id=1, source_target_pairs={{0,4},{4,0},{8,12},{12,8},{16,20},{20,16},{24,28},{28,24},{1,5},{5... | collective-permute-start | bytes 98312 | tf_op jit(solution)/shard_map/ppermute | solution.py:24
  70.4 4.9 %collective-permute-start.22 = (bf16[64,256]{1,0:T(8,128)(2,1)S(1)}, bf16[64,256]{1,0:T(8,128)(2,1)S(1)}, u32[]{:S(2)}, u32[]{:S(2)}) collective-permute-start(bf16[64,256]{1,0:T(8,128)(2,1)S(1)} %fusion.15), channel_id=1, source_target_pairs={{0,16},{4,20},{8,24},{12,28},{16,0},{20,4},{24,8},{28,12},{1,17},{... | collective-permute-start | bytes 98312 | tf_op jit(solution)/shard_map/ppermute | solution.py:24
  75.3 25.0 %copy-start.2 = (bf16[1024,1024]{1,0:T(8,128)(2,1)S(1)}, bf16[1024,1024]{1,0:T(8,128)(2,1)}, u32[]{:S(2)}) copy-start(bf16[1024,1024]{1,0:T(8,128)(2,1)} %refs_9_.3) | copy-start | bytes 6291460
  75.3 4.9 %collective-permute-start.25 = (bf16[64,256]{1,0:T(8,128)(2,1)S(1)}, bf16[64,256]{1,0:T(8,128)(2,1)S(1)}, u32[]{:S(2)}, u32[]{:S(2)}) collective-permute-start(bf16[64,256]{1,0:T(8,128)(2,1)S(1)} %add_convert_fusion.5), channel_id=1, source_target_pairs={{0,12},{4,8},{8,4},{12,0},{16,28},{20,24},{24,20},{28,16},{1,13},{... | collective-permute-start | bytes 98312 | tf_op jit(solution)/shard_map/ppermute | solution.py:24
  77.5 3.9 %collective-permute-start.24 = (bf16[64,256]{1,0:T(8,128)(2,1)S(1)}, bf16[64,256]{1,0:T(8,128)(2,1)S(1)}, u32[]{:S(2)}, u32[]{:S(2)}) collective-permute-start(bf16[64,256]{1,0:T(8,128)(2,1)S(1)} %add_convert_fusion.5), channel_id=1, source_target_pairs={{0,8},{4,12},{8,0},{12,4},{16,24},{20,28},{24,16},{28,20},{1,9},{5... | collective-permute-start | bytes 98312 | tf_op jit(solution)/shard_map/ppermute | solution.py:24
  78.0 3.9 %collective-permute-start.23 = (bf16[64,256]{1,0:T(8,128)(2,1)S(1)}, bf16[64,256]{1,0:T(8,128)(2,1)S(1)}, u32[]{:S(2)}, u32[]{:S(2)}) collective-permute-start(bf16[64,256]{1,0:T(8,128)(2,1)S(1)} %add_convert_fusion.5), channel_id=1, source_target_pairs={{0,4},{4,0},{8,12},{12,8},{16,20},{20,16},{24,28},{28,24},{1,5},{5... | collective-permute-start | bytes 98312 | tf_op jit(solution)/shard_map/ppermute | solution.py:24
  82.1 23.9 %copy-start.16 = (s32[1,2048]{1,0:T(1,128)S(1)}, s32[1,2048]{1,0:T(1,128)}, u32[]{:S(2)}) copy-start(s32[1,2048]{1,0:T(1,128)} %copy-done.15) | copy-start | bytes 24580
  82.1 24.1 %copy-start.1 = (bf16[2048,1024]{1,0:T(8,128)(2,1)S(1)}, bf16[2048,1024]{1,0:T(8,128)(2,1)}, u32[]{:S(2)}) copy-start(bf16[2048,1024]{1,0:T(8,128)(2,1)} %refs_9_.5) | copy-start | bytes 12582916
  82.1 3.7 %collective-permute-start.28 = (bf16[64,256]{1,0:T(8,128)(2,1)S(1)}, bf16[64,256]{1,0:T(8,128)(2,1)S(1)}, u32[]{:S(2)}, u32[]{:S(2)}) collective-permute-start(bf16[64,256]{1,0:T(8,128)(2,1)S(1)} %convolution_convert_fusion.2), channel_id=1, source_target_pairs={{0,3},{1,2},{2,1},{3,0},{4,7},{5,6},{6,5},{7,4},{8,11},{9,10},{10,... | collective-permute-start | bytes 98312 | tf_op jit(solution)/shard_map/ppermute | solution.py:24
  82.4 4.0 %collective-permute-start.27 = (bf16[64,256]{1,0:T(8,128)(2,1)S(1)}, bf16[64,256]{1,0:T(8,128)(2,1)S(1)}, u32[]{:S(2)}, u32[]{:S(2)}) collective-permute-start(bf16[64,256]{1,0:T(8,128)(2,1)S(1)} %convolution_convert_fusion.3), channel_id=1, source_target_pairs={{0,2},{1,3},{2,0},{3,1},{4,6},{5,7},{6,4},{7,5},{8,10},{9,11},{10,... | collective-permute-start | bytes 98312 | tf_op jit(solution)/shard_map/ppermute | solution.py:24
  84.0 2.4 %collective-permute-start.26 = (bf16[64,256]{1,0:T(8,128)(2,1)S(1)}, bf16[64,256]{1,0:T(8,128)(2,1)S(1)}, u32[]{:S(2)}, u32[]{:S(2)}) collective-permute-start(bf16[64,256]{1,0:T(8,128)(2,1)S(1)} %convolution_convert_fusion.2), channel_id=1, source_target_pairs={{0,1},{1,0},{2,3},{3,2},{4,5},{5,4},{6,7},{7,6},{8,9},{9,8},{10,11... | collective-permute-start | bytes 98312 | tf_op jit(solution)/shard_map/ppermute | solution.py:24
  86.4 4.9 %collective-permute-start.29 = (bf16[64,256]{1,0:T(8,128)(2,1)S(1)}, bf16[64,256]{1,0:T(8,128)(2,1)S(1)}, u32[]{:S(2)}, u32[]{:S(2)}) collective-permute-start(bf16[64,256]{1,0:T(8,128)(2,1)S(1)} %get-tuple-element.79), channel_id=1, source_target_pairs={{0,16},{4,20},{8,24},{12,28},{16,0},{20,4},{24,8},{28,12},{1,17},{... | collective-permute-start | bytes 98312 | tf_op jit(solution)/shard_map/ppermute | solution.py:24
  91.3 4.3 %collective-permute-start.30 = (bf16[64,512]{1,0:T(8,128)(2,1)S(1)}, bf16[64,512]{1,0:T(8,128)(2,1)S(1)}, u32[]{:S(2)}, u32[]{:S(2)}) collective-permute-start(bf16[64,512]{1,0:T(8,128)(2,1)S(1)} %pad_maximum_fusion.3.refs_0_), channel_id=1, source_target_pairs={{0,4},{4,0},{8,12},{12,8},{16,20},{20,16},{24,28},{28,24},{1,5},{5... | collective-permute-start | bytes 196616 | tf_op jit(solution)/shard_map/ppermute | solution.py:24
  92.3 4.6 %collective-permute-start.31 = (bf16[64,512]{1,0:T(8,128)(2,1)S(1)}, bf16[64,512]{1,0:T(8,128)(2,1)S(1)}, u32[]{:S(2)}, u32[]{:S(2)}) collective-permute-start(bf16[64,512]{1,0:T(8,128)(2,1)S(1)} %pad_maximum_fusion.3.refs_0_), channel_id=1, source_target_pairs={{0,8},{4,12},{8,0},{12,4},{16,24},{20,28},{24,16},{28,20},{1,9},{5... | collective-permute-start | bytes 196616 | tf_op jit(solution)/shard_map/ppermute | solution.py:24
  93.9 5.2 %collective-permute-start.32 = (bf16[64,512]{1,0:T(8,128)(2,1)S(1)}, bf16[64,512]{1,0:T(8,128)(2,1)S(1)}, u32[]{:S(2)}, u32[]{:S(2)}) collective-permute-start(bf16[64,512]{1,0:T(8,128)(2,1)S(1)} %pad_maximum_fusion.3.refs_0_), channel_id=1, source_target_pairs={{0,12},{4,8},{8,4},{12,0},{16,28},{20,24},{24,20},{28,16},{1,13},{... | collective-permute-start | bytes 196616 | tf_op jit(solution)/shard_map/ppermute | solution.py:24
  94.8 4.3 %collective-permute-start.33 = (bf16[64,512]{1,0:T(8,128)(2,1)S(1)}, bf16[64,512]{1,0:T(8,128)(2,1)S(1)}, u32[]{:S(2)}, u32[]{:S(2)}) collective-permute-start(bf16[64,512]{1,0:T(8,128)(2,1)S(1)} %pad_maximum_fusion.3.refs_0_), channel_id=1, source_target_pairs={{0,1},{1,0},{2,3},{3,2},{4,5},{5,4},{6,7},{7,6},{8,9},{9,8},{10,11... | collective-permute-start | bytes 196616 | tf_op jit(solution)/shard_map/ppermute | solution.py:24
  95.6 3.5 %collective-permute-start.34 = (bf16[64,512]{1,0:T(8,128)(2,1)S(1)}, bf16[64,512]{1,0:T(8,128)(2,1)S(1)}, u32[]{:S(2)}, u32[]{:S(2)}) collective-permute-start(bf16[64,512]{1,0:T(8,128)(2,1)S(1)} %collective-permute-done.30.refs_1_), channel_id=1, source_target_pairs={{0,1},{1,0},{2,3},{3,2},{4,5},{5,4},{6,7},{7,6},{8,9},{9,8},{10,11... | collective-permute-start | bytes 196616 | tf_op jit(solution)/shard_map/ppermute | solution.py:24
  96.8 2.2 %collective-permute-start.35 = (bf16[64,512]{1,0:T(8,128)(2,1)S(1)}, bf16[64,512]{1,0:T(8,128)(2,1)S(1)}, u32[]{:S(2)}, u32[]{:S(2)}) collective-permute-start(bf16[64,512]{1,0:T(8,128)(2,1)S(1)} %collective-permute-done.31.refs_2_), channel_id=1, source_target_pairs={{0,1},{1,0},{2,3},{3,2},{4,5},{5,4},{6,7},{7,6},{8,9},{9,8},{10,11... | collective-permute-start | bytes 196616 | tf_op jit(solution)/shard_map/ppermute | solution.py:24
  99.1 1.3 collective-permute-start.36
  102.5 7.7 %collective-permute-start.39 = (bf16[64,1024]{1,0:T(8,128)(2,1)S(1)}, bf16[64,1024]{1,0:T(8,128)(2,1)S(1)}, u32[]{:S(2)}, u32[]{:S(2)}) collective-permute-start(bf16[64,1024]{1,0:T(8,128)(2,1)S(1)} %convert_element_type.244), channel_id=1, source_target_pairs={{0,12},{4,8},{8,4},{12,0},{16,28},{20,24},{24,20},{28,16},{1,13},{... | collective-permute-start | bytes 393224 | tf_op jit(solution)/shard_map/ppermute | solution.py:24
  103.5 8.0 %collective-permute-start.38 = (bf16[64,1024]{1,0:T(8,128)(2,1)S(1)}, bf16[64,1024]{1,0:T(8,128)(2,1)S(1)}, u32[]{:S(2)}, u32[]{:S(2)}) collective-permute-start(bf16[64,1024]{1,0:T(8,128)(2,1)S(1)} %convert_element_type.244), channel_id=1, source_target_pairs={{0,8},{4,12},{8,0},{12,4},{16,24},{20,28},{24,16},{28,20},{1,9},{5... | collective-permute-start | bytes 393224 | tf_op jit(solution)/shard_map/ppermute | solution.py:24
  105.1 6.7 %collective-permute-start.37 = (bf16[64,1024]{1,0:T(8,128)(2,1)S(1)}, bf16[64,1024]{1,0:T(8,128)(2,1)S(1)}, u32[]{:S(2)}, u32[]{:S(2)}) collective-permute-start(bf16[64,1024]{1,0:T(8,128)(2,1)S(1)} %convert_element_type.244), channel_id=1, source_target_pairs={{0,4},{4,0},{8,12},{12,8},{16,20},{20,16},{24,28},{28,24},{1,5},{5... | collective-permute-start | bytes 393224 | tf_op jit(solution)/shard_map/ppermute | solution.py:24
  112.2 1.4 collective-permute-start.40
  112.3 3.7 %collective-permute-start.42 = (f32[64,256]{1,0:T(8,128)S(1)}, f32[64,256]{1,0:T(8,128)S(1)}, u32[]{:S(2)}, u32[]{:S(2)}) collective-permute-start(f32[64,256]{1,0:T(8,128)S(1)} %get-tuple-element.65.own_ref), channel_id=1, source_target_pairs={{0,1},{1,0},{2,3},{3,2},{4,5},{5,4},{6,7},{7,6},{8,9},{9,8},{10,11... | collective-permute-start | bytes 196616 | tf_op jit(solution)/shard_map/ppermute | solution.py:24
  113.9 4.3 %collective-permute-start.41 = (bf16[64,512]{1,0:T(8,128)(2,1)S(1)}, bf16[64,512]{1,0:T(8,128)(2,1)S(1)}, u32[]{:S(2)}, u32[]{:S(2)}) collective-permute-start(bf16[64,512]{1,0:T(8,128)(2,1)S(1)} %fusion.2), channel_id=1, source_target_pairs={{0,2},{1,3},{2,0},{3,1},{4,6},{5,7},{6,4},{7,5},{8,10},{9,11},{10,... | collective-permute-start | bytes 196616 | tf_op jit(solution)/shard_map/ppermute | solution.py:24
  118.3 4.9 %collective-permute-start.43 = (bf16[64,512]{1,0:T(8,128)(2,1)S(1)}, bf16[64,512]{1,0:T(8,128)(2,1)S(1)}, u32[]{:S(2)}, u32[]{:S(2)}) collective-permute-start(bf16[64,512]{1,0:T(8,128)(2,1)S(1)} %convert_element_type.253.refs_0_), channel_id=1, source_target_pairs={{0,4},{4,0},{8,12},{12,8},{16,20},{20,16},{24,28},{28,24},{1,5},{5... | collective-permute-start | bytes 196616 | tf_op jit(solution)/shard_map/ppermute | solution.py:24
  119.5 4.3 %collective-permute-start.44 = (bf16[64,512]{1,0:T(8,128)(2,1)S(1)}, bf16[64,512]{1,0:T(8,128)(2,1)S(1)}, u32[]{:S(2)}, u32[]{:S(2)}) collective-permute-start(bf16[64,512]{1,0:T(8,128)(2,1)S(1)} %convert_element_type.253.refs_0_), channel_id=1, source_target_pairs={{0,8},{4,12},{8,0},{12,4},{16,24},{20,28},{24,16},{28,20},{1,9},{5... | collective-permute-start | bytes 196616 | tf_op jit(solution)/shard_map/ppermute | solution.py:24
  119.9 5.2 %collective-permute-start.45 = (bf16[64,512]{1,0:T(8,128)(2,1)S(1)}, bf16[64,512]{1,0:T(8,128)(2,1)S(1)}, u32[]{:S(2)}, u32[]{:S(2)}) collective-permute-start(bf16[64,512]{1,0:T(8,128)(2,1)S(1)} %convert_element_type.253.refs_0_), channel_id=1, source_target_pairs={{0,12},{4,8},{8,4},{12,0},{16,28},{20,24},{24,20},{28,16},{1,13},{... | collective-permute-start | bytes 196616 | tf_op jit(solution)/shard_map/ppermute | solution.py:24
  121.9 3.7 %collective-permute-start.46 = (bf16[64,512]{1,0:T(8,128)(2,1)S(1)}, bf16[64,512]{1,0:T(8,128)(2,1)S(1)}, u32[]{:S(2)}, u32[]{:S(2)}) collective-permute-start(bf16[64,512]{1,0:T(8,128)(2,1)S(1)} %convert_element_type.253.refs_0_), channel_id=1, source_target_pairs={{0,1},{1,0},{2,3},{3,2},{4,5},{5,4},{6,7},{7,6},{8,9},{9,8},{10,11... | collective-permute-start | bytes 196616 | tf_op jit(solution)/shard_map/ppermute | solution.py:24
  123.3 2.3 %collective-permute-start.47 = (bf16[64,512]{1,0:T(8,128)(2,1)S(1)}, bf16[64,512]{1,0:T(8,128)(2,1)S(1)}, u32[]{:S(2)}, u32[]{:S(2)}) collective-permute-start(bf16[64,512]{1,0:T(8,128)(2,1)S(1)} %collective-permute-done.43.refs_1_), channel_id=1, source_target_pairs={{0,1},{1,0},{2,3},{3,2},{4,5},{5,4},{6,7},{7,6},{8,9},{9,8},{10,11... | collective-permute-start | bytes 196616 | tf_op jit(solution)/shard_map/ppermute | solution.py:24
  123.7 1.8 %collective-permute-start.48 = (bf16[64,512]{1,0:T(8,128)(2,1)S(1)}, bf16[64,512]{1,0:T(8,128)(2,1)S(1)}, u32[]{:S(2)}, u32[]{:S(2)}) collective-permute-start(bf16[64,512]{1,0:T(8,128)(2,1)S(1)} %collective-permute-done.44.refs_2_), channel_id=1, source_target_pairs={{0,1},{1,0},{2,3},{3,2},{4,5},{5,4},{6,7},{7,6},{8,9},{9,8},{10,11... | collective-permute-start | bytes 196616 | tf_op jit(solution)/shard_map/ppermute | solution.py:24
  125.0 1.3 collective-permute-start.49
  125.0 5.3 %collective-permute-start.50 = (f32[64,512]{1,0:T(8,128)S(1)}, f32[64,512]{1,0:T(8,128)S(1)}, u32[]{:S(2)}, u32[]{:S(2)}) collective-permute-start(f32[64,512]{1,0:T(8,128)S(1)} %convert_add_fusion.4.own_ref), channel_id=1, source_target_pairs={{0,1},{1,0},{2,3},{3,2},{4,5},{5,4},{6,7},{7,6},{8,9},{9,8},{10,11... | collective-permute-start | bytes 393224 | tf_op jit(solution)/shard_map/ppermute | solution.py:24
  130.3 5.6 %collective-permute-start.51 = (bf16[64,1024]{1,0:T(8,128)(2,1)S(1)}, bf16[64,1024]{1,0:T(8,128)(2,1)S(1)}, u32[]{:S(2)}, u32[]{:S(2)}) collective-permute-start(bf16[64,1024]{1,0:T(8,128)(2,1)S(1)} %add.296), channel_id=1, source_target_pairs={{0,4},{4,0},{8,12},{12,8},{16,20},{20,16},{24,28},{28,24},{1,5},{5... | collective-permute-start | bytes 393224 | tf_op jit(solution)/shard_map/ppermute | solution.py:24
  136.5 1.6 %collective-permute-start.52 = (f32[64,1024]{1,0:T(8,128)S(1)}, f32[64,1024]{1,0:T(8,128)S(1)}, u32[]{:S(2)}, u32[]{:S(2)}) collective-permute-start(f32[64,1024]{1,0:T(8,128)S(1)} %fusion.58), channel_id=1, source_target_pairs={{0,1},{1,0},{2,3},{3,2},{4,5},{5,4},{6,7},{7,6},{8,9},{9,8},{10,11... | collective-permute-start | bytes 786440 | tf_op jit(solution)/shard_map/ppermute | solution.py:24
  138.6 5.6 %collective-permute-start.53 = (bf16[64,1024]{1,0:T(8,128)(2,1)S(1)}, bf16[64,1024]{1,0:T(8,128)(2,1)S(1)}, u32[]{:S(2)}, u32[]{:S(2)}) collective-permute-start(bf16[64,1024]{1,0:T(8,128)(2,1)S(1)} %fusion), channel_id=1, source_target_pairs={{0,2},{1,3},{2,0},{3,1},{4,6},{5,7},{6,4},{7,5},{8,10},{9,11},{10,... | collective-permute-start | bytes 393224 | tf_op jit(solution)/shard_map/ppermute | solution.py:24
  144.2 1.6 %collective-permute-start.54 = (f32[64,1024]{1,0:T(8,128)S(1)}, f32[64,1024]{1,0:T(8,128)S(1)}, u32[]{:S(2)}, u32[]{:S(2)}) collective-permute-start(f32[64,1024]{1,0:T(8,128)S(1)} %convert_add_fusion.2.own_ref), channel_id=1, source_target_pairs={{0,1},{1,0},{2,3},{3,2},{4,5},{5,4},{6,7},{7,6},{8,9},{9,8},{10,11... | collective-permute-start | bytes 786440 | tf_op jit(solution)/shard_map/ppermute | solution.py:24
  (8 other events, 44.2 us)
